TPU v7x, 32 devices: a whole 2x2x4 slice. The times are simulated.
32 devices in a mesh: wide: 4 (over y, x), rows: 4 (over z), cols: 2 (over core).
Axes of the slice: x: 2, y: 2, z: 4, core: 2. Of those that a mesh axis runs over, the one named last changes fastest.
Arguments:
- latent: bfloat16 [16, 4, 64, 32], P('wide', None, 'rows', 'cols'), may hold values from -6 to 6
- pred_grad: bfloat16 [16, 8, 64, 32], P('wide', None, 'rows', 'cols'), may hold values from -6 to 6
- timesteps: int32 [16], P('wide'), may hold values from 0 to 999
- labels: int32 [16], P('wide'), may hold values from 0 to 1000
- offsets: int32 [16], P('wide'), may hold values from 0 to 1
- counts: int32 [4], P('wide'), may hold values from 1 to 4, as said below
- patch_weight: bfloat16 [16, 384], replicated, may hold values from -1.5 to 1.5
- time_in: bfloat16 [256, 384], replicated, may hold values from -0.375 to 0.375
- time_out: bfloat16 [384, 384], replicated, may hold values from -0.3125 to 0.3125
- label_table: bfloat16 [1001, 384], replicated, may hold values from -6 to 6
- modulation: bfloat16 [2, 384, 2304], replicated, may hold values from -0.3125 to 0.3125
- qkv_weight: bfloat16 [2, 384, 1152], replicated, may hold values from -0.3125 to 0.3125
- proj_weight: bfloat16 [2, 384, 384], replicated, may hold values from -2.5 to 2.5
- up_weight: bfloat16 [2, 384, 1536], replicated, may hold values from -0.3125 to 0.3125
- down_weight: bfloat16 [2, 1536, 384], replicated, may hold values from -0.15625 to 0.15625
- final_mod: bfloat16 [384, 768], replicated, may hold values from -0.3125 to 0.3125
- final_weight: bfloat16 [384, 32], replicated, may hold values from -0.3125 to 0.3125
Outputs:
- prediction: bfloat16 [16, 8, 64, 32], P('wide', None, 'rows', 'cols')
- latent_grad: float32 [16, 4, 64, 32], P('wide', None, 'rows', 'cols')
- grad_patch: float32 [16, 384], replicated
- grad_time_in: float32 [256, 384], replicated
- grad_time_out: float32 [384, 384], replicated
- grad_table: float32 [1001, 384], replicated
- grad_modulation: float32 [2, 384, 2304], P(None, ('rows', 'cols'))
- grad_qkv: float32 [2, 384, 1152], P(None, ('rows', 'cols'))
- grad_proj: float32 [2, 384, 384], P(None, ('rows', 'cols'))
- grad_up: float32 [2, 384, 1536], P(None, ('rows', 'cols'))
- grad_down: float32 [2, 1536, 384], P(None, ('rows', 'cols'))
- grad_final_mod: float32 [384, 768], replicated
- grad_final: float32 [384, 32], replicated
Inputs may be any that keep to these rules, and one draw needn't show every extreme that they name: Index w of wide holds live samples in its slots 0 to counts[w] - 1 and empty ones after; some index has all 4 slots filled. `labels`: label 1000 is the unconditional class.
All inputs are finite; a program needn't handle non-finite values.
Results may differ from a plain program's by a relative error of at most 0.02.
Values may be sent and summed in bfloat16 or wider, within the bound.
No kernel may reach another device: no remote copies, remote signals or barrier semaphores. Data moves between devices by JAX's collectives and lax.ppermute only.
A program may use at most 128 MiB of HBM per device.

v0:
```python
from functools import partial
import math

import jax
import jax.numpy as jnp
import numpy as np
from jax import lax
from jax.experimental import pallas as pl
from jax.experimental.pallas import tpu as pltpu
from jax.sharding import PartitionSpec as P

HEADS = 6
HEAD_DIM = 64
PAIRS = HEADS // 2
LANES = 2 * HEAD_DIM
EPS = 1e-06
F32 = jnp.float32
BF16 = jnp.bfloat16
ROWS = 24
ROW_F, ROW_SHARED, ROW_ACT, ROW_COND, ROW_HID, ROW_FEAT = 12, 14, 15, 16, 17, 18

def dot(a, b):
    return jnp.dot(a, b, preferred_element_type=F32)


def dot_nt(a, b):
    return lax.dot_general(a, b, (((1,), (1,)), ((), ())), preferred_element_type=F32)


def dot_tn(a, b):
    return lax.dot_general(a, b, (((0,), (0,)), ((), ())), preferred_element_type=F32)


def sds(shape, dtype):
    return jax.ShapeDtypeStruct(shape, dtype)


def layer_norm(states):
    centred = states - jnp.mean(states, axis=-1, keepdims=True)
    inverse = lax.rsqrt(jnp.mean(centred * centred, axis=-1, keepdims=True) + EPS)
    return centred * inverse, inverse


def norm_back(grad, normed, inverse):
    mean_grad = jnp.mean(grad, axis=-1, keepdims=True)
    mean_cross = jnp.mean(grad * normed, axis=-1, keepdims=True)
    return inverse * (grad - mean_grad - normed * mean_cross)


def token_sum(values):
    return jnp.sum(values, axis=0, keepdims=True)


def head_masks(dtype):
    lane = lax.broadcasted_iota(jnp.int32, (1, LANES), 1)
    first = (lane < HEAD_DIM).astype(F32)
    return first.astype(dtype), (1.0 - first).astype(dtype)


def unit_place(zz, ww, cc):
    x, y = ww % 2, ww // 2
    return (x * 8 + y * 4 + zz) if cc == 0 else (y * 8 + x * 4 + zz)


def kernel_call(body, ins, outs, scratch=(), us=1.0, after=None):
    spaces = {"v": pltpu.VMEM, "p": pltpu.VMEM, "s": pltpu.SMEM, "h": pltpu.HBM}
    specs, arrays = [], []
    for kind, array in ins:
        specs.append(pl.BlockSpec(memory_space=spaces[kind]))
        if kind in "ph":
            array = pltpu.with_memory_space_constraint(array, spaces[kind])
        arrays.append(array)
    if after is not None:
        specs.append(pl.BlockSpec(memory_space=pl.ANY))
        arrays.append(after)

    def kernel(*refs):
        body(*refs[: len(ins)], *refs[len(arrays) :])

    return pl.pallas_call(
        kernel,
        in_specs=specs,
        out_specs=[pl.BlockSpec(memory_space=pltpu.VMEM)] * len(outs),
        out_shape=[sds(o[0], o[1]) if len(o) > 2 else pltpu.VMEM(o[0], o[1]) for o in outs],
        scratch_shapes=list(scratch),
        compiler_params=pltpu.CompilerParams(vmem_limit_bytes=24 * 1024 * 1024),
        cost_estimate=pl.CostEstimate(
            flops=int(us * 1.5e9), bytes_accessed=int(us * 1e6), transcendentals=0
        ),
    )(*arrays)


def one_hot(shape, test):
    first = lax.broadcasted_iota(jnp.int32, shape, 0)
    second = lax.broadcasted_iota(jnp.int32, shape, 1)
    return test(first, second).astype(F32).astype(BF16)


def places():
    return lax.axis_index("rows"), lax.axis_index("cols"), lax.axis_index("wide")


def wide_bits():
    _, c, w = places()
    x, y = lax.rem(w, 2), lax.rem(lax.div(w, 2), 2)
    return jnp.where(c == 0, x, y), jnp.where(c == 0, y, x)


def rows_at(index, count):
    return pl.ds(pl.multiple_of(index * count, 16), count)


def tiles_body(latent, pred_grad, *tiles):
    z, _, _ = places()
    _, lat_ch, height, wide = latent.shape
    out_ch = pred_grad.shape[1]
    chans, tok = lat_ch + out_ch, height * wide // 4
    half = wide // 2
    lanes = 2 * chans
    spread = [one_hot((tok, wide), lambda t, v: v == 2 * (t % half) + u) for u in range(2)]
    inside = [
        one_hot((tok, chans * height), lambda t, v: v % height == 2 * (t // half) + par).astype(F32)
        for par in range(2)
    ]

    def lane_of(channel, u):
        return jnp.where(
            channel < lat_ch, u * lat_ch + channel, 2 * lat_ch + u * out_ch + channel - lat_ch
        )

    fold = [
        one_hot((chans * height, lanes), lambda v, lane: lane == lane_of(v // height, u))
        for u in range(2)
    ]
    for k, tile in enumerate(tiles):
        image = jnp.concatenate(
            [
                latent[z ^ k].reshape(lat_ch * height, wide),
                pred_grad[z ^ k].reshape(out_ch * height, wide),
            ],
            axis=0,
        )
        wide_rows = [dot_nt(spread[u], image) for u in range(2)]
        for par in range(2):
            tile[par] = sum(
                dot((wide_rows[u] * inside[par]).astype(BF16), fold[u]) for u in range(2)
            ).astype(BF16)


def packed_tile(parities, lanes, order):
    tok = parities[0].shape[0]
    across = tok // order
    total = order * 2 * lanes
    block = 0.0
    for par in range(2):
        copy = one_hot((lanes, total), lambda a, b: b % (2 * lanes) == par * lanes + a)
        block = block + dot(parities[par].astype(BF16), copy)
    own = one_hot((tok, total), lambda t, b: b // (2 * lanes) == t // across).astype(F32)
    gather = one_hot((across, tok), lambda j, t: t % across == j)
    return dot(gather, (block * own).astype(BF16))


def unpacked_tile(block, chans, height, wide):
    lanes = 2 * chans
    half = wide // 2
    image = 0.0
    for u in range(2):
        chosen = one_hot(
            (chans * height, block.shape[1]),
            lambda v, b: b
            == (v % height) // 2 * 2 * lanes + v % 2 * lanes + u * chans + v // height,
        )
        column = dot_nt(chosen, block).astype(BF16)
        image = image + dot(column, one_hot((half, wide), lambda j, v: v == 2 * j + u))
    return image


def by_parity(first, second, offset):
    step = first.shape[0] // 32
    moved = jnp.concatenate([jnp.zeros((step, second.shape[1]), F32), second[:-step]], axis=0)
    return jnp.where(offset == 1, moved, first), jnp.where(offset == 1, first, second)


def cond_body(
    timesteps, labels, freqs, label_table, time_in, final_weight, positions, *rest,
):
    sources, (mods, cond, final_copy, pos), held = rest[:7], rest[7:11], rest[11:18]
    sem = rest[18]
    final_copy[...] = final_weight[...]
    sources, held = sources + (positions.at[lax.axis_index("cols")],), held + (pos,)
    copies = [
        pltpu.make_async_copy(source, target, sem.at[i])
        for i, (source, target) in enumerate(zip(sources, held))
    ]
    for copy in copies:
        copy.start()
    time_out, modulation, final_mod = held[:3]
    z, _, _ = places()
    label = labels[z]
    count, width = time_in.shape
    angles = jnp.full((8, count // 2), timesteps[z].astype(F32)) * freqs[...]
    feats = jnp.concatenate([jnp.cos(angles), jnp.sin(angles)], axis=-1).astype(BF16)
    hidden = dot(feats, time_in[...])
    act = (hidden * jax.nn.sigmoid(hidden)).astype(BF16)
    chosen = one_hot((8, label_table.shape[0]), lambda a, b: b == label)
    copies[0].wait()
    condition = dot(act, time_out[...]) + dot(chosen, label_table[...])
    shared = (condition * jax.nn.sigmoid(condition)).astype(BF16)
    mods[...] = jnp.zeros_like(mods)
    copies[1].wait()
    for layer in range(2):
        values = dot(shared, modulation[layer])
        for k in range(6):
            mods[layer, k : k + 1, :] = values[0:1, k * width : (k + 1) * width]
    copies[2].wait()
    values = dot(shared, final_mod[...])
    for k in range(2):
        mods[2, k : k + 1, :] = values[0:1, k * width : (k + 1) * width]
    lane = lax.broadcasted_iota(jnp.int32, (1, width - count), 1)
    marks = jnp.where(
        lane == 0, lax.div(label, 32), jnp.where(lane == 1, lax.rem(label, 32), 0)
    ).astype(F32)
    cond[...] = jnp.zeros_like(cond)
    cond[0:1, :] = shared[0:1].astype(F32)
    cond[1:2, :] = act[0:1].astype(F32)
    cond[2:3, :] = condition[0:1]
    cond[3:4, :] = hidden[0:1]
    cond[4:5, :] = jnp.concatenate([feats[0:1].astype(F32), marks], axis=-1)
    for copy in copies[3:]:
        copy.wait()


def qkv_forward(state, mods, layer, weight):
    width = state.shape[-1]
    normed, _ = layer_norm(state)
    inner = (normed * (1.0 + mods[layer, 1:2]) + mods[layer, 0:1]).astype(BF16)
    projected = dot(inner, weight[layer]).astype(BF16)
    return projected[:, :width], projected[:, width:]


def attend_forward(q, kv, kvp, probs, attended):
    width = q.shape[-1]
    masks = head_masks(BF16)
    for p in range(PAIRS):
        at = slice(p * LANES, (p + 1) * LANES)
        av = slice(width + p * LANES, width + (p + 1) * LANES)
        qp = q[:, at] * BF16(HEAD_DIM**-0.5)
        k0, v0, k1, v1 = kv[:, at], kv[:, av], kvp[:, at], kvp[:, av]
        total = None
        for h in range(2):
            qh = qp * masks[h]
            s0, s1 = dot_nt(qh, k0), dot_nt(qh, k1)
            peak = jnp.maximum(
                jnp.max(s0, axis=-1, keepdims=True), jnp.max(s1, axis=-1, keepdims=True)
            )
            e0, e1 = jnp.exp(s0 - peak), jnp.exp(s1 - peak)
            scale = 1.0 / (
                jnp.sum(e0, axis=-1, keepdims=True) + jnp.sum(e1, axis=-1, keepdims=True)
            )
            p0, p1 = (e0 * scale).astype(BF16), (e1 * scale).astype(BF16)
            probs[2 * p + h, 0] = p0
            probs[2 * p + h, 1] = p1
            part = dot(p0, v0 * masks[h]) + dot(p1, v1 * masks[h])
            total = part if total is None else total + part
        attended[:, at] = total.astype(BF16)


def mlp_forward(middle, mods, layer, up, down, gp, act):
    normed, _ = layer_norm(middle)
    inner = (normed * (1.0 + mods[layer, 4:5]) + mods[layer, 3:4]).astype(BF16)
    width = middle.shape[-1]
    branch = None
    for i in range(up.shape[-1] // width):
        at = slice(i * width, (i + 1) * width)
        hidden = dot(inner, up[layer, :, at])
        square = hidden * hidden
        root = math.sqrt(2.0 / math.pi)
        bent = jnp.tanh(root * hidden * (1.0 + 0.044715 * square))
        half = 0.5 * (1.0 + bent)
        activated = (hidden * half).astype(BF16)
        act[:, at] = activated
        slope = half + 0.5 * hidden * (1.0 - bent * bent) * (root * (1.0 + 3 * 0.044715 * square))
        gp[:, at] = slope.astype(BF16)
        part = dot(activated, down[layer, at, :])
        branch = part if branch is None else branch + part
    return branch


def put_units(keep, send, pair, place, size, at_row):
    first = lax.axis_index("cols") == 0
    block = pair[0].shape[0]
    own = jnp.where(first, place[0], place[1]) * size + at_row
    other = jnp.where(first, place[1], place[0]) * size + at_row
    keep[pl.ds(pl.multiple_of(own, 16), block), :] = jnp.where(first, pair[0], pair[1])
    send[pl.ds(pl.multiple_of(other, 16), block), :] = jnp.where(first, pair[1], pair[0])


def mlp_backward(grad, middle, branch, mods, layer, gp, act, up, down, keep, send, size, rows, first):
    width = middle.shape[-1]
    normed, inverse = layer_norm(middle)
    scale = 1.0 + mods[layer, 4:5]
    inner_t = (normed * scale + mods[layer, 3:4]).astype(BF16).T
    branch_grad = (mods[layer, 5:6] * grad).astype(BF16)
    inner_grad = None
    pieces = up.shape[-1] // width
    block = width // 8
    for i in range(pieces):
        at = slice(i * width, (i + 1) * width)
        act_grad = dot_nt(branch_grad, down[layer, at, :])
        hidden_grad = (act_grad * gp[:, at].astype(F32)).astype(BF16)
        part = dot_nt(hidden_grad, up[layer, :, at])
        inner_grad = part if inner_grad is None else inner_grad + part
        grad_up = dot(inner_t, hidden_grad).astype(BF16)
        for b in range(4):
            pair = [grad_up[(2 * b + cc) * block : (2 * b + cc + 1) * block] for cc in range(2)]
            put_units(keep, send, pair, [unit_place(b, i, cc) for cc in range(2)], size, 0)
        grad_down = dot_tn(act[:, at], branch_grad).astype(BF16)
        for j in range(4):
            pair = [grad_down[(4 * cc + j) * block : (4 * cc + j + 1) * block] for cc in range(2)]
            put_units(keep, send, pair, [unit_place(i, j, cc) for cc in range(2)], size, block)
    rows[first : first + 1, :] = token_sum(inner_grad)
    rows[first + 1 : first + 2, :] = token_sum(inner_grad * normed)
    rows[first + 2 : first + 3, :] = token_sum(grad * branch.astype(F32))
    return grad + norm_back(inner_grad * scale, normed, inverse)


def qkv_backward(
    state, middle_grad, dq, dkv, dkvr, mods, layer, weight, gproj, keep, send, size, at_row, flip, rows
):
    width = state.shape[-1]
    block = width // 8
    normed, inverse = layer_norm(state)
    scale = 1.0 + mods[layer, 1:2]
    inner_t = (normed * scale + mods[layer, 0:1]).astype(BF16).T
    dkv_sum = dkv[...] + dkvr[...]
    pieces = (dq[...], dkv_sum[:, :width], dkv_sum[:, width:])
    inner_grad = None

    def put(values, i):
        for b in range(4):
            pair = [values[(2 * b + cc) * block : (2 * b + cc + 1) * block] for cc in range(2)]
            place = [unit_place(b, i, cc ^ flip) for cc in range(2)]
            put_units(keep, send, pair, place, size, at_row)

    for i, piece in enumerate(pieces):
        part = dot_nt(piece, weight[layer, :, i * width : (i + 1) * width])
        inner_grad = part if inner_grad is None else inner_grad + part
        put(dot(inner_t, piece).astype(BF16), i)
    put(gproj[...], 3)
    rows[0:1, :] = token_sum(inner_grad)
    rows[1:2, :] = token_sum(inner_grad * normed)
    return middle_grad + norm_back(inner_grad * scale, normed, inverse)


def embed_body(
    offsets, t0, t1, t2, t3, pos, mods, patch_weight, qkv,
    state, q, kv, patches, tiles,
):
    z, _, _ = places()
    offset = offsets[z]
    for k, tile in enumerate((t0, t1, t2, t3)):
        tiles[k] = tile[...]
    count = tiles.shape[0]
    even = jnp.concatenate([tiles[z ^ t, 0] for t in range(count)], axis=0).astype(F32)
    odd = jnp.concatenate([tiles[z ^ t, 1] for t in range(count)], axis=0).astype(F32)
    step = even.shape[0] // 32
    later = jnp.concatenate([even[step:], jnp.zeros((step, even.shape[1]), F32)], axis=0)
    first = jnp.where(offset == 1, odd, even).astype(BF16)
    second = jnp.where(offset == 1, later, odd).astype(BF16)
    patches[0] = first
    patches[1] = second
    weight = patch_weight[...].astype(F32)
    lanes = weight.shape[0] // 2
    fill = jnp.zeros((even.shape[1] - lanes, weight.shape[1]), F32)
    upper = jnp.concatenate([weight[:lanes], fill], axis=0).astype(BF16)
    lower = jnp.concatenate([weight[lanes:], fill], axis=0).astype(BF16)
    values = dot(first, upper) + dot(second, lower) + pos[...]
    state[...] = values
    q[...], kv[...] = qkv_forward(values, mods, 0, qkv)


def block_body(
    state, q, kv, kvp, mods, proj, up, down, qkv,
    state1, q1, kv1, probs, attended, attn_out, middle, gp, act, branch,
):
    attend_forward(q, kv, kvp, probs, attended)
    m = mods
    attn = dot(attended[...], proj[0])
    attn_out[...] = attn.astype(BF16)
    mid = state[...] + m[0, 2:3] * attn
    middle[...] = mid
    out = mlp_forward(mid, m, 0, up, down, gp, act)
    branch[...] = out.astype(BF16)
    new = mid + m[0, 5:6] * out
    state1[...] = new
    q1[...], kv1[...] = qkv_forward(new, m, 1, qkv)


def turn_body(
    offsets, counts, state, q, kv, kvp, mods, patches, final_weight, proj, up, down,
    probs, attended, attn_out, middle_grad, keep, send, rows, gfinal, predt,
    gp, act, preds,
):
    z, _, _ = places()
    offset = offsets[z]
    live = (z < counts[0]).astype(F32)
    attend_forward(q, kv, kvp, probs, attended)
    m = mods
    attn = dot(attended[...], proj[1])
    attn_out[...] = attn.astype(BF16)
    middle = state[...] + m[1, 2:3] * attn
    branch = mlp_forward(middle, m, 1, up, down, gp, act)
    last = middle + m[1, 5:6] * branch
    normed, inverse = layer_norm(last)
    scale = 1.0 + m[2, 1:2]
    inner = (normed * scale + m[2, 0:1]).astype(BF16)
    weight = final_weight[...]
    lanes = weight.shape[1] // 2
    out = dot(inner, weight) * live
    preds[0], preds[1] = by_parity(out[:, :lanes], out[:, lanes:], offset)
    tok = preds.shape[1] // 4
    for k in range(4):
        cut = pl.ds(pl.multiple_of((z ^ k) * tok, 8), tok)
        predt[k] = packed_tile([preds[0, cut, :], preds[1, cut, :]], lanes, 8)
    across = weight.astype(F32).T
    chosen = patches
    fill = jnp.zeros((chosen.shape[2] - lanes, across.shape[1]), F32)
    upper = jnp.concatenate([fill, across[:lanes]], axis=0).astype(BF16)
    lower = jnp.concatenate([fill, across[lanes:]], axis=0).astype(BF16)
    inner_grad = (dot(chosen[0], upper) + dot(chosen[1], lower)) * live
    gfinal[0] = dot_tn(chosen[0], inner) * live
    gfinal[1] = dot_tn(chosen[1], inner) * live
    rows[...] = jnp.zeros_like(rows)
    rows[3:4, :] = token_sum(inner_grad)
    rows[4:5, :] = token_sum(inner_grad * normed)
    grad = norm_back(inner_grad * scale, normed, inverse)
    size = 2 * (weight.shape[0] // 8)
    middle_grad[...] = mlp_backward(
        grad, middle, branch, m, 1, gp, act, up, down, keep, send, size, rows, 0
    )


def attend_back_body(
    layer, q, kv, kvp, probs, attended, attn_out, middle_grad, mods, proj,
    dq, dkv, gproj, dkvs, rows,
):
    grad = middle_grad[...]
    attn_grad = (mods[layer, 2:3] * grad).astype(BF16)
    attended_grad = dot_nt(attn_grad, proj[layer]).astype(BF16)
    masks = head_masks(BF16)
    width = q.shape[-1]
    for p in range(PAIRS):
        at = slice(p * LANES, (p + 1) * LANES)
        av = slice(width + p * LANES, width + (p + 1) * LANES)
        qp = q[:, at] * BF16(HEAD_DIM**-0.5)
        dop = attended_grad[:, at]
        ks, vs = (kv[:, at], kvp[:, at]), (kv[:, av], kvp[:, av])
        total = None
        parts = [None] * 4
        for h in range(2):
            doh = dop * masks[h]
            qh = qp * masks[h]
            ps = [probs[2 * p + h, i] for i in range(2)]
            dps = [dot_nt(doh, vs[i]) for i in range(2)]
            pfs = [ps[i].astype(F32) for i in range(2)]
            inner = sum(jnp.sum(dps[i] * pfs[i], axis=-1, keepdims=True) for i in range(2))
            for i in range(2):
                ds = (pfs[i] * (dps[i] - inner)).astype(BF16)
                part = dot(ds, ks[i] * masks[h])
                total = part if total is None else total + part
                dk, dv = dot_tn(ds, qh), dot_tn(ps[i], doh)
                parts[2 * i] = dk if h == 0 else parts[2 * i] + dk
                parts[2 * i + 1] = dv if h == 0 else parts[2 * i + 1] + dv
        dq[:, at] = (total * HEAD_DIM**-0.5).astype(BF16)
        dkv[:, at] = parts[0].astype(BF16)
        dkv[:, av] = parts[1].astype(BF16)
        dkvs[:, at] = parts[2].astype(BF16)
        dkvs[:, av] = parts[3].astype(BF16)
    rows[...] = jnp.zeros_like(rows)
    rows[0:1, :] = token_sum(grad * attn_out[...].astype(F32))
    gproj[...] = dot_tn(attended[...], attn_grad).astype(BF16)


def middle_body(
    state1, middle_grad1, dq, dkv, dkvr, gproj, middle, branch, gp, act, mods, qkv, up, down,
    middle_grad, keep, send, rows,
):
    width = dq.shape[-1]
    size = 3 * (width // 8)
    rows[...] = jnp.zeros_like(rows)
    m = mods
    grad = qkv_backward(
        state1[...], middle_grad1[...], dq, dkv, dkvr, m, 1, qkv, gproj, keep, send, size,
        2 * (width // 8), 0, rows,
    )
    middle_grad[...] = mlp_backward(
        grad, middle[...], branch[...], m, 0, gp, act, up, down, keep, send, size,
        rows, 2,
    )


def last_body(
    offsets, state0, middle_grad, dq, dkv, dkvr, gproj, mods, patches, patch_weight, cond,
    rows_turn, rows_a1, rows_mid, rows_a0, gfinal, qkv,
    keep, send, lgradt, rows, lgrads, table,
):
    z, _, _ = places()
    offset = offsets[z]
    width = dq.shape[-1]
    block = width // 8
    grad = qkv_backward(
        state0[...], middle_grad[...], dq, dkv, dkvr, mods, 0, qkv, gproj, keep, send, block,
        0, 1, rows,
    )
    embed_grad = grad.astype(BF16)
    chosen = patches
    gp0, gp1 = dot_tn(chosen[0], embed_grad), dot_tn(chosen[1], embed_grad)
    chans = patch_weight.shape[0] // 2
    window = dot_nt(embed_grad, patch_weight[...])
    lgrads[0], lgrads[1] = by_parity(window[:, :chans], window[:, chans:], offset)
    tok = lgrads.shape[1] // 4
    for k in range(4):
        cut = pl.ds(pl.multiple_of((z ^ k) * tok, 8), tok)
        parts = [lgrads[0, cut, :], lgrads[1, cut, :]]
        leading = [part.astype(BF16).astype(F32) for part in parts]
        lgradt[k, :, 0:128] = packed_tile(leading, chans, 8)
        lgradt[k, :, 128:256] = packed_tile([a - b for a, b in zip(parts, leading)], chans, 8)
    table[...] = jnp.zeros_like(table)
    table[0:2, :] = rows[0:2, :]
    table[2:3, :] = rows_a0[0:1, :]
    table[3:6, :] = rows_mid[2:5, :]
    table[6:8, :] = rows_mid[0:2, :]
    table[8:9, :] = rows_a1[0:1, :]
    table[9:12, :] = rows_turn[0:3, :]
    table[12:14, :] = rows_turn[3:5, :]
    table[14:19, :] = 0.5 * cond[0:5, :]
    table[ROWS : ROWS + chans, :] = gp0[:chans]
    table[ROWS + chans : ROWS + 2 * chans, :] = gp1[:chans]
    final = gfinal
    outs = final.shape[1] - chans
    base = ROWS + 2 * chans
    table[base : base + outs, :] = final[0, chans:, :]
    table[base + outs : base + 2 * outs, :] = final[1, chans:, :]
    keep[16 * block :] = table[...].astype(BF16)
    send[16 * block :] = table[...].astype(BF16)


def split_body(keep, recv, keep_out, send_out, bit_at):
    half = keep.shape[0] // 2
    bit = wide_bits()[bit_at]
    keep_out[...] = keep[rows_at(bit, half)] + recv[rows_at(bit, half)]
    send_out[...] = keep[rows_at(1 - bit, half)] + recv[rows_at(1 - bit, half)]


def one_split_body(bit_at, keep, recv, keep_out, send_out):
    split_body(keep, recv, keep_out, send_out, bit_at)


def to_chips(held, recv, outs):
    z, _, _ = places()
    size = held.shape[0] // 4
    for k, out in enumerate(outs):
        out[...] = held[rows_at(z ^ k, size)] + recv[rows_at(z ^ k, size)]


def second_body(keep2, recv2, held1, recv1, keep2_out, send2_out, *units1):
    split_body(keep2, recv2, keep2_out, send2_out, 0)
    to_chips(held1, recv1, units1)


def third_body(keep2, recv2, keep3, recv3, u0, u1, u2, u3, keep2_out, keep3_out, table, unit1, send):
    half2 = keep2.shape[0] // 2
    size3 = keep3.shape[0] - 80
    half3 = size3 // 2
    bit = wide_bits()[1]
    keep2_out[...] = keep2[rows_at(bit, half2)] + recv2[rows_at(bit, half2)]
    send[0:half2] = keep2[rows_at(1 - bit, half2)] + recv2[rows_at(1 - bit, half2)]
    keep3_out[...] = keep3[rows_at(bit, half3)] + recv3[rows_at(bit, half3)]
    send[half2 : half2 + half3] = keep3[rows_at(1 - bit, half3)] + recv3[rows_at(1 - bit, half3)]
    rows = keep3[size3:] + recv3[size3:]
    table[...] = rows
    send[half2 + half3 :] = rows
    unit1[...] = (
        u0[...].astype(F32) + u1[...].astype(F32) + u2[...].astype(F32) + u3[...].astype(F32)
    ).astype(BF16)


def fourth_body(keep2, keep3, table, recv, z0, z1, z2, z3, keep3_out, pair_out, send):
    z, _, _ = places()
    size2, size3 = keep2.shape[0], keep3.shape[0]
    unit2, half3 = size2 // 4, size3 // 2
    for k, out in enumerate((z0, z1, z2, z3)):
        out[...] = keep2[rows_at(z ^ k, unit2)] + recv[rows_at(z ^ k, unit2)]
    bit = wide_bits()[0]

    def half(index):
        start = pl.multiple_of(index * half3, 16)
        return keep3[pl.ds(start, half3)] + recv[pl.ds(pl.multiple_of(start + size2, 16), half3)]

    keep3_out[...] = half(bit)
    send[0:half3] = half(1 - bit)
    mine = table[...].astype(F32)
    other = recv[size2 + size3 :].astype(F32)
    pair = jnp.concatenate(
        [mine[:ROWS], other[:ROWS], mine[ROWS : ROWS + 48] + other[ROWS : ROWS + 48]], axis=0
    ).astype(BF16)
    pair_out[...] = pair
    send[half3:] = pair


def fifth_body(keep3, pair, recv, predt, lgradt, z0, z1, z2, z3, four):
    z, c, w = places()
    size3 = keep3.shape[0]
    unit3 = size3 // 4
    first = jnp.where(c == 0, 2, 1)
    second = 3 - first
    spot = lax.rem(w, 4)
    mine, other = pair[...].astype(F32), recv[size3:].astype(F32)
    four[spot] = mine[:ROWS]
    four[spot ^ first] = mine[ROWS : 2 * ROWS]
    four[spot ^ second] = other[:ROWS]
    four[spot ^ first ^ second] = other[ROWS : 2 * ROWS]
    rows = jnp.concatenate([four[2 * c], four[2 * c + 1]], axis=0).astype(BF16)
    sums = (mine[2 * ROWS :] + other[2 * ROWS :]).astype(BF16)
    base = unit3 + 2 * ROWS
    for k, out in enumerate((z0, z1, z2, z3)):
        out[0:unit3] = keep3[rows_at(z ^ k, unit3)] + recv[rows_at(z ^ k, unit3)]
        out[unit3:base] = rows
        out[base : base + 48] = sums
        tile = jnp.concatenate([lgradt[k], predt[k]], axis=0)
        out[base + 48 : base + 64, 0:256] = tile.astype(BF16)
        out[base + 48 : base + 64, 256:384] = jnp.zeros((16, 128), BF16)


def sixth_body(*refs):
    twos, threes = refs[:4], refs[4:8]
    unit, half, sums, tiles = refs[8:]
    size2 = twos[0].shape[0]
    size3 = threes[0].shape[0] - 2 * ROWS - 64
    base = size3 + 2 * ROWS
    unit[0:size2] = sum(t[...].astype(F32) for t in twos).astype(BF16)
    unit[size2:] = sum(t[0:size3].astype(F32) for t in threes).astype(BF16)
    sums[...] = sum(t[base : base + 48].astype(F32) for t in threes)
    for k, t in enumerate(threes):
        half[2 * ROWS * k : 2 * ROWS * (k + 1)] = t[size3:base]
        tiles[k] = t[base + 48 :]


def silu_slope(values):
    sigmoid = jax.nn.sigmoid(values)
    return sigmoid * (1.0 + values * (1.0 - sigmoid))


def sums_body(
    own, other, sums, modulation, final_mod, time_out,
    g_time_in, g_time_out, g_table, g_mod, g_final_mod, g_patch, g_final,
    table, shared_t,
):
    z, c, _ = places()
    half = own.shape[0]
    parts = table.shape[0]
    for i in range(parts):
        at = slice(128 * i, 128 * (i + 1))
        table[i, 0:half] = own[:, at].astype(F32)
        table[i, half:] = other[:, at].astype(F32)
    samples = table.shape[1] // ROWS

    def rows(r):
        pieces = [table[i, pl.ds(r, samples, stride=ROWS), :] for i in range(parts)]
        return jnp.concatenate(pieces, axis=-1)

    mods = [
        jnp.concatenate([rows(6 * layer + k) for k in range(6)], axis=-1).astype(BF16)
        for layer in range(2)
    ]
    fmods = jnp.concatenate([rows(ROW_F), rows(ROW_F + 1)], axis=-1).astype(BF16)
    shared_t[...] = rows(ROW_SHARED).T
    block = g_mod.shape[1]
    start = pl.multiple_of((z * 2 + c) * block, 8)
    mine = shared_t[pl.ds(start, block), :].astype(BF16)
    for layer in range(2):
        g_mod[layer] = dot(mine, mods[layer])
    g_final_mod[...] = dot(shared_t[...].astype(BF16), fmods)
    patch = g_patch.shape[0]
    g_patch[...] = sums[:patch, :]
    g_final[...] = sums[patch:, :].T
    shared_grad = dot_nt(fmods, final_mod[...])
    for layer in range(2):
        shared_grad += dot_nt(mods[layer], modulation[layer])
    cond_grad = shared_grad * silu_slope(rows(ROW_COND))
    cond_low = cond_grad.astype(BF16)
    feats = rows(ROW_FEAT)
    count = g_time_in.shape[0]
    label = (feats[:, count : count + 1] * 32.0 + feats[:, count + 1 : count + 2]).astype(jnp.int32)
    classes = g_table.shape[0]
    padded = (classes + 127) // 128 * 128
    lane = lax.broadcasted_iota(jnp.int32, (samples, padded), 1)
    hot = (lane == label).astype(F32).T[:classes].astype(BF16)
    cond_rest = (cond_grad - cond_low.astype(F32)).astype(BF16)
    g_table[...] = dot(hot, cond_low) + dot(hot, cond_rest)
    g_time_out[...] = dot(rows(ROW_ACT).T.astype(BF16), cond_low)
    time_grad = dot_nt(cond_low, time_out[...]) * silu_slope(rows(ROW_HID))
    g_time_in[...] = dot(feats[:, :count].T.astype(BF16), time_grad.astype(BF16))


def spread_body(*refs):
    ones, others, tiles = refs[:4], refs[4:8], refs[8]
    g_qkv, g_proj, g_up, g_down, prediction, latent_grad = refs[9:]
    z, _, w = places()
    width = g_proj.shape[-1]
    block = g_proj.shape[1]
    spot = lax.rem(w, 4)

    def place_mlp(layer, piece, unit):
        cols = pl.ds(pl.multiple_of(unit * width, 128), width)
        g_up[layer, :, cols] = piece[0:block].astype(F32)
        down_rows = pl.ds(pl.multiple_of(unit * block, 8), block)
        g_down[layer, down_rows, :] = piece[block : 2 * block].astype(F32)

    def place_attn(layer, piece, unit):
        @pl.when(unit < 3)
        def _():
            cols = pl.ds(pl.multiple_of(unit * width, 128), width)
            g_qkv[layer, :, cols] = piece.astype(F32)

        @pl.when(unit == 3)
        def _():
            g_proj[layer] = piece.astype(F32)

    for k in range(4):
        unit = spot ^ k
        place_mlp(1, ones[k][...], unit)
        both = others[k]
        place_mlp(0, both[0 : 2 * block], unit)
        place_attn(1, both[2 * block : 3 * block], unit)
        place_attn(0, both[3 * block :], unit)
        _, out_ch, height, wide = prediction.shape
        lat_ch = latent_grad.shape[1]
        tile = tiles[k].astype(F32)
        image = unpacked_tile(tile[8:16, 0:256].astype(BF16), out_ch, height, wide)
        prediction[z ^ k] = image.astype(BF16).reshape(out_ch, height, wide)
        image = unpacked_tile(tile[0:8, 0:128].astype(BF16), lat_ch, height, wide)
        image = image + unpacked_tile(tile[0:8, 128:256].astype(BF16), lat_ch, height, wide)
        latent_grad[z ^ k] = image.reshape(lat_ch, height, wide)


def swap(value, axis, bit):
    count = lax.axis_size(axis)
    return lax.ppermute(value, axis, [(i, i ^ bit) for i in range(count)])


def swap_by_core(value, bits):
    wide, cores = lax.axis_size("wide"), lax.axis_size("cols")
    pairs = [
        (w * cores + c, (w ^ bits[c % 2]) * cores + c) for w in range(wide) for c in range(cores)
    ]
    return lax.ppermute(value, ("wide", "cols"), pairs)


FIRST, SECOND = (1, 2), (2, 1)


def rest_sum(value):
    bit = 4
    while bit < lax.axis_size("wide"):
        value = (value.astype(F32) + swap(value, "wide", bit).astype(F32)).astype(value.dtype)
        bit *= 2
    return value


def rest_gather(value):
    bit = 4
    while bit < lax.axis_size("wide"):
        value = jnp.concatenate([value, swap(value, "wide", bit)])
        bit *= 2
    return value


def position_tables(row_count, col_count, cores, width):
    quarter = width // 4
    omega = np.exp(-math.log(10000.0) * np.arange(quarter) / quarter)
    row_angle = np.arange(row_count)[:, None] * omega[None, :]
    col_angle = np.arange(col_count * cores)[:, None] * omega[None, :]
    row_part = np.concatenate([np.sin(row_angle), np.cos(row_angle)], axis=-1)
    col_part = np.concatenate([np.sin(col_angle), np.cos(col_angle)], axis=-1)
    col_part = col_part.reshape(cores, 1, col_count, width // 2)
    table = np.concatenate(
        [
            np.broadcast_to(row_part[None, :, None, :], (cores, row_count, col_count, width // 2)),
            np.broadcast_to(col_part, (cores, row_count, col_count, width // 2)),
        ],
        axis=-1,
    )
    return table.reshape(cores, row_count * col_count, width).astype(np.float32)


def shards(
    latent, pred_grad, timesteps, labels, offsets, counts, patch_weight, time_in, time_out,
    label_table, modulation, qkv_weight, proj_weight, up_weight, down_weight, final_mod, final_weight,
):
    slots, lat_ch, tile_h, tile_w = latent.shape
    out_ch = pred_grad.shape[1]
    width = patch_weight.shape[1]
    ff = up_weight.shape[2]
    n_rows, n_cols = lax.axis_size("rows"), lax.axis_size("cols")
    hp, wp = tile_h // 2, tile_w // 2
    tile_tok = hp * wp
    tokens = n_rows * tile_tok
    lanes = 2 * (lat_ch + out_ch)
    block = width // 8
    tok, wide_tok, double = (tokens, width), (tokens, ff), (tokens, 2 * width)

    tiles = kernel_call(
        tiles_body, [("v", latent), ("v", pred_grad)], [((2, tile_tok, lanes), BF16)] * n_rows, us=1
    )
    tiles = [tiles[0]] + [swap(tiles[k], "rows", k) for k in range(1, n_rows)]
    half = time_in.shape[0] // 2
    freqs = np.exp(-math.log(10000.0) * np.arange(half, dtype=np.float32) / np.float32(half))
    positions = jnp.asarray(position_tables(n_rows * hp, wp, n_cols, width))
    weights = (time_out, modulation, final_mod, qkv_weight, proj_weight, up_weight, down_weight)
    mods, cond, final_v, pos, time_out_v, modulation_v, final_mod_v, qkv, proj, up, down = kernel_call(
        cond_body,
        [("s", timesteps), ("s", labels), ("v", jnp.asarray(freqs.astype(np.float32))[None])]
        + [("v", label_table), ("v", time_in), ("v", final_weight), ("h", positions)]
        + [("h", weight) for weight in weights],
        [((3, 8, width), F32), ((8, width), F32), (final_weight.shape, BF16), (tok, F32)]
        + [(weight.shape, BF16) for weight in weights],
        [pltpu.SemaphoreType.DMA((len(weights) + 1,))],
        us=5,
    )
    probs_shape = (HEADS, 2, tokens, tokens)
    state0, q0, kv0, patches = kernel_call(
        embed_body,
        [("s", offsets)]
        + [("v", t) for t in tiles]
        + [("p", pos), ("p", mods), ("v", patch_weight), ("p", qkv)],
        [(tok, F32), (tok, BF16), (double, BF16), ((2, tokens, lanes), BF16)],
        [pltpu.VMEM((n_rows, 2, tile_tok, lanes), BF16)],
        us=2,
    )
    kv0p = swap(kv0, "cols", 1)
    state1, q1, kv1, probs0, attended0, attn_out0, middle0, gp0, act0, branch0 = kernel_call(
        block_body,
        [("p", state0), ("p", q0), ("p", kv0), ("v", kv0p)]
        + [("p", a) for a in (mods, proj, up, down, qkv)],
        [
            (tok, F32), (tok, BF16), (double, BF16), (probs_shape, BF16), (tok, BF16), (tok, BF16),
            (tok, F32), (wide_tok, BF16), (wide_tok, BF16), (tok, BF16),
        ],
        us=7,
    )
    kv1p = swap(kv1, "cols", 1)
    probs1, attended1, attn_out1, mgrad1, keep1, send1, rows_turn, gfinal, predt = kernel_call(
        turn_body,
        [("s", offsets), ("s", counts), ("p", state1), ("p", q1), ("p", kv1), ("v", kv1p)]
        + [("p", mods), ("p", patches), ("p", final_v), ("p", proj), ("p", up), ("p", down)],
        [
            (probs_shape, BF16), (tok, BF16), (tok, BF16), (tok, F32), ((16 * 2 * block, width), BF16),
            ((16 * 2 * block, width), BF16), ((8, width), F32), ((2, lanes, width), F32),
            ((4, wp, 4 * out_ch * hp), F32),
        ],
        [
            pltpu.VMEM(wide_tok, BF16), pltpu.VMEM(wide_tok, BF16),
            pltpu.VMEM((2, tokens, 2 * out_ch), F32),
        ],
        us=10,
    )
    recv1 = swap(send1, "cols", 1)

    def attend_back(layer, q, kv, kvp, *saved, after):
        return kernel_call(
            partial(attend_back_body, layer),
            [("p", q), ("p", kv), ("v", kvp)] + [("p", a) for a in saved + (mods, proj)],
            [
                (tok, BF16), (double, BF16), ((width, width), BF16), (double, BF16), ((8, width), F32),
            ],
            us=5,
            after=after,
        )

    dq1, dkv1, gproj1, dkvs1, rows_a1 = attend_back(
        1, q1, kv1, kv1p, probs1, attended1, attn_out1, mgrad1, after=None
    )
    dkvr1 = swap(dkvs1, "cols", 1)
    keep1, send1 = kernel_call(
        partial(one_split_body, 0),
        [("p", keep1), ("v", recv1)],
        [((8 * 2 * block, width), BF16)] * 2,
        us=0.5,
        after=rows_a1,
    )
    recv1 = swap_by_core(send1, FIRST)
    mgrad0, keep2, send2, rows_mid = kernel_call(
        middle_body,
        [("p", a) for a in (state1, mgrad1, dq1, dkv1)]
        + [("v", dkvr1)]
        + [("p", a) for a in (gproj1, middle0, branch0, gp0, act0, mods, qkv, up, down)],
        [
            (tok, F32), ((16 * 3 * block, width), BF16), ((16 * 3 * block, width), BF16),
            ((8, width), F32),
        ],
        us=6,
        after=keep1,
    )
    recv2 = swap(send2, "cols", 1)
    keep1, send1 = kernel_call(
        partial(one_split_body, 1),
        [("p", keep1), ("v", recv1)],
        [((4 * 2 * block, width), BF16)] * 2,
        us=0.5,
        after=rows_mid,
    )
    recv1 = swap_by_core(send1, SECOND)
    dq0, dkv0, gproj0, dkvs0, rows_a0 = attend_back(
        0, q0, kv0, kv0p, probs0, attended0, attn_out0, mgrad0, after=keep1
    )
    dkvr0 = swap(dkvs0, "cols", 1)
    keep2, send2, *units1 = kernel_call(
        second_body,
        [("p", keep2), ("v", recv2), ("p", keep1), ("v", recv1)],
        [((8 * 3 * block, width), BF16)] * 2 + [((2 * block, width), BF16)] * 4,
        us=1,
        after=rows_a0,
    )
    recv2 = swap_by_core(send2, FIRST)
    units1 = [units1[0]] + [swap(units1[k], "rows", k) for k in range(1, n_rows)]
    keep3, send3, lgradt = kernel_call(
        last_body,
        [("s", offsets), ("p", state0), ("p", mgrad0), ("p", dq0), ("p", dkv0), ("v", dkvr0)]
        + [("p", gproj0), ("p", mods), ("p", patches), ("v", patch_weight), ("p", cond)]
        + [("p", a) for a in (rows_turn, rows_a1, rows_mid, rows_a0, gfinal, qkv)],
        [
            ((16 * block + 80, width), BF16), ((16 * block + 80, width), BF16),
            ((4, wp, 4 * lat_ch * hp * 2), F32),
        ],
        [
            pltpu.VMEM((8, width), F32), pltpu.VMEM((2, tokens, 2 * lat_ch), F32),
            pltpu.VMEM((80, width), F32),
        ],
        us=3,
        after=keep2,
    )
    recv3 = swap(send3, "cols", 1)
    keep2, keep3, table, unit1, send = kernel_call(
        third_body,
        [("p", keep2), ("v", recv2), ("p", keep3), ("v", recv3), ("p", units1[0])]
        + [("v", u) for u in units1[1:]],
        [
            ((4 * 3 * block, width), BF16), ((8 * block, width), BF16), ((80, width), BF16),
            ((2 * block, width), BF16), ((4 * 3 * block + 8 * block + 80, width), BF16),
        ],
        us=1,
    )
    recv = swap_by_core(send, SECOND)
    unit1 = rest_sum(unit1)
    ones = [unit1] + [swap(unit1, "wide", k) for k in range(1, 4)]
    *twos, keep3, pair, send = kernel_call(
        fourth_body,
        [("p", keep2), ("p", keep3), ("p", table), ("v", recv)],
        [((3 * block, width), BF16)] * 4
        + [
            ((4 * block, width), BF16), ((2 * ROWS + 48, width), BF16),
            ((4 * block + 2 * ROWS + 48, width), BF16),
        ],
        us=1,
    )
    recv = swap_by_core(send, FIRST)
    twos = [twos[0]] + [swap(twos[k], "rows", k) for k in range(1, n_rows)]
    threes = kernel_call(
        fifth_body,
        [("p", keep3), ("p", pair), ("v", recv), ("p", predt), ("p", lgradt)],
        [((block + 2 * ROWS + 64, width), BF16)] * 4,
        [pltpu.VMEM((4, ROWS, width), F32)],
        us=1,
    )
    threes = [threes[0]] + [swap(threes[k], "rows", k) for k in range(1, n_rows)]
    unit, rows, sums, tiles = kernel_call(
        sixth_body,
        [("v", t) for t in twos + threes],
        [
            ((4 * block, width), BF16), ((4 * 2 * ROWS, width), BF16), ((48, width), F32),
            ((4, 16, width), BF16),
        ],
        us=1,
    )
    unit, sums = rest_sum(unit), rest_sum(sums)
    others = [unit] + [swap(unit, "wide", k) for k in range(1, 4)]
    rows_other = rest_gather(swap(rows, "cols", 1))
    rows = rest_gather(rows)
    classes = label_table.shape[0]
    g_time_in, g_time_out, g_table, g_mod, g_final_mod, g_patch, g_final = kernel_call(
        sums_body,
        [("v", rows), ("v", rows_other), ("v", sums)]
        + [("p", a) for a in (modulation_v, final_mod_v, time_out_v)],
        [
            (shape, F32, 0)
            for shape in (
                time_in.shape, time_out.shape, (classes, width), (2, block, 6 * width), final_mod.shape,
                patch_weight.shape, final_weight.shape,
            )
        ],
        [
            pltpu.VMEM((width // 128, 2 * rows.shape[0], 128), F32),
            pltpu.VMEM((width, 2 * rows.shape[0] // ROWS), F32),
        ],
        us=5,
    )
    g_qkv, g_proj, g_up, g_down, prediction, latent_grad = kernel_call(
        spread_body,
        [("v", a) for a in ones + others] + [("v", tiles)],
        [
            ((2, block, 3 * width), F32, 0), ((2, block, width), F32, 0), ((2, block, ff), F32, 0),
            ((2, ff // 8, width), F32, 0), ((slots, out_ch, tile_h, tile_w), BF16, 0),
            (latent.shape, F32, 0),
        ],
        us=2,
    )
    return (
        prediction, latent_grad, g_patch, g_time_in, g_time_out, g_table, g_mod, g_qkv, g_proj,
        g_up, g_down, g_final_mod, g_final,
    )


def solution(mesh):
    tiled, split = P("wide", None, "rows", "cols"), P(None, ("rows", "cols"), None)
    return jax.shard_map(
        shards,
        mesh=mesh,
        in_specs=(tiled, tiled, P("wide"), P("wide"), P("wide"), P("wide")) + (P(),) * 11,
        out_specs=(tiled, tiled, P(), P(), P(), P(), split, split, split, split, split, P(), P()),
        check_vma=False,
    )
```

profile of v0, /device:TPU:0, one launch (start us, length us, event | category | flops | bytes accessed | tf_op | source)
XLA Modules:
  0.0 133.0 jit_solution(17808792375883873665)
XLA Ops:
  3.5 3.1 %collective-permute-start = (bf16[2,64,24]{2,1,0:T(8,128)(2,1)S(1)}, bf16[2,64,24]{2,1,0:T(8,128)(2,1)S(1)}, u32[]{:S(2)}, u32[]{:S(2)}) collective-permute-start(bf16[2,64,24]{2,1,0:T(8,128)(2,1)S(1)} %get-tuple-element.112), channel_id=1, source_target_pairs={{0,2},{2,0},{4,6},{6,4},{1,3},{3,1},{5,7},{7,5},{8,10},{10,8},{12,... | collective-permute-start | bytes 18440 | tf_op jit(solution)/shard_map/ppermute | solution.py:749
  6.6 2.6 %collective-permute-start.1 = (bf16[2,64,24]{2,1,0:T(8,128)(2,1)S(1)}, bf16[2,64,24]{2,1,0:T(8,128)(2,1)S(1)}, u32[]{:S(2)}, u32[]{:S(2)}) collective-permute-start(bf16[2,64,24]{2,1,0:T(8,128)(2,1)S(1)} %get-tuple-element.113), channel_id=1, source_target_pairs={{0,4},{2,6},{4,0},{6,2},{1,5},{3,7},{5,1},{7,3},{8,12},{10,14},{12... | collective-permute-start | bytes 18440 | tf_op jit(solution)/shard_map/ppermute | solution.py:749
  9.4 5.1 %shard_map.283 = (f32[3,8,384]{2,1,0:T(8,128)S(1)}, f32[8,384]{1,0:T(8,128)S(1)}, bf16[384,32]{1,0:T(8,128)(2,1)S(1)}, f32[256,384]{1,0:T(8,128)S(1)}, bf16[384,...) custom-call(s32[4]{0:T(128)S(1)} %copy-done.5, ...), custom_call_target="tpu_custom_call" | custom-call | flops 7500000256 | bytes 5000000 | tf_op jit(solution)/shard_map/pallas_call | solution.py:80
  16.5 1.7 %collective-permute-done.3.refs_3_.refs_2_ = bf16[256,768]{1,0:T(8,128)(2,1)S(1)} collective-permute-done((bf16[256,768]{1,0:T(8,128)(2,1)S(1)}, bf16[256,768]{1,0:T(8,128)(2,1)S(1)}, u32[]{:S(2)}, u32[]{:S(2)}) %collective-permute-start.3) | collective-permute-done | bytes 393248 | tf_op jit(solution)/shard_map/ppermute | solution.py:749
  18.2 5.4 %shard_map.285 = (f32[256,384]{1,0:T(8,128)S(1)}, bf16[256,384]{1,0:T(8,128)(2,1)S(1)}, bf16[256,768]{1,0:T(8,128)(2,1)S(1)}, bf16[6,2,256,256]{3,2,1,0:T(8,128)...) custom-call(f32[256,384]{1,0:T(8,128)S(1)} %get-tuple-element.118.re, ...), custom_call_target="tpu_custom_call" | custom-call | flops 10499999744 | bytes 7000000 | tf_op jit(solution)/shard_map/pallas_call | solution.py:80
  25.4 9.1 %shard_map.286 = (bf16[6,2,256,256]{3,2,1,0:T(8,128)(2,1)S(1)}, bf16[256,384]{1,0:T(8,128)(2,1)S(1)}, bf16[256,384]{1,0:T(8,128)(2,1)S(1)}, f32[256,384]{1,0:T(8...) custom-call(s32[4]{0:T(128)S(1)} %copy-done.7, ...), custom_call_target="tpu_custom_call" | custom-call | flops 15000000512 | bytes 10000000 | tf_op jit(solution)/shard_map/pallas_call | solution.py:80
  34.7 3.4 %shard_map.287 = (bf16[256,384]{1,0:T(8,128)(2,1)S(1)}, bf16[256,768]{1,0:T(8,128)(2,1)S(1)}, bf16[384,384]{1,0:T(8,128)(2,1)S(1)}, bf16[256,768]{1,0:T(8,128)(2,1)S(1)}, f32[8,384]{1,0:T(8,128)S(1)}) custom-call(bf16[256,384]{1,0:T(8,128)(2,1)S(1)} %get-tuple-element.125.refs_3_.refs_0_, bf16[256,768]{1,0:T(8,128)(2,1)S(1)} %get-tuple-element.126.refs_4_.refs_1_, ...), custom_call_target="tpu_custom_call" | custom-call | flops 7500000256 | bytes 5000000 | tf_op jit(solution)/shard_map/pallas_call | solution.py:80
  39.9 3.5 %shard_map.289 = (f32[256,384]{1,0:T(8,128)S(1)}, bf16[2304,384]{1,0:T(8,128)(2,1)S(1)}, bf16[2304,384]{1,0:T(8,128)(2,1)S(1)}, f32[8,384]{1,0:T(8,128)S(1)}) custom-call(f32[256,384]{1,0:T(8,128)S(1)} %get-tuple-element.124.refs_2_.refs_0_, f32[256,384]{1,0:T(8,128)S(1)} %get-tuple-element.129.refs_6_.refs_1_, ...), custom_call_target="tpu_custom_call" | custom-call | flops 8999999488 | bytes 6000000 | tf_op jit(solution)/shard_map/pallas_call | solution.py:80
  45.4 8.4 %collective-permute-done.8.refs_1_ = bf16[768,384]{1,0:T(8,128)(2,1)S(1)} collective-permute-done((bf16[768,384]{1,0:T(8,128)(2,1)S(1)}, bf16[768,384]{1,0:T(8,128)(2,1)S(1)}, u32[]{:S(2)}, u32[]{:S(2)}) %collective-permute-start.8) | collective-permute-done | bytes 589856 | tf_op jit(solution)/shard_map/ppermute | solution.py:757
  55.4 3.4 %shard_map.291 = (bf16[256,384]{1,0:T(8,128)(2,1)S(1)}, bf16[256,768]{1,0:T(8,128)(2,1)S(1)}, bf16[384,384]{1,0:T(8,128)(2,1)S(1)}, bf16[256,768]{1,0:T(8,128)(2,1)S(1)}, f32[8,384]{1,0:T(8,128)S(1)}) custom-call(bf16[256,384]{1,0:T(8,128)(2,1)S(1)} %get-tuple-element.119.refs_1_.refs_0_, bf16[256,768]{1,0:T(8,128)(2,1)S(1)} %get-tuple-element.120.refs_2_.refs_1_, ...), custom_call_target="tpu_custom_call" | custom-call | flops 7500000256 | bytes 5000000 | tf_op jit(solution)/shard_map/pallas_call | solution.py:80
  58.9 1.8 %collective-permute-done.9.refs_3_ = bf16[384,384]{1,0:T(8,128)(2,1)S(1)} collective-permute-done((bf16[384,384]{1,0:T(8,128)(2,1)S(1)}, bf16[384,384]{1,0:T(8,128)(2,1)S(1)}, u32[]{:S(2)}, u32[]{:S(2)}) %collective-permute-start.9) | collective-permute-done | bytes 294944 | tf_op jit(solution)/shard_map/ppermute | solution.py:757
  62.5 3.3 %shard_map.293 = (bf16[848,384]{1,0:T(8,128)(2,1)S(1)}, bf16[848,384]{1,0:T(8,128)(2,1)S(1)}, f32[4,8,256]{2,1,0:T(8,128)S(1)}) custom-call(s32[4]{0:T(128)S(1)} %copy-done.7, f32[256,384]{1,0:T(8,128)S(1)} %get-tuple-element.118.refs_0_.refs_1_, f32[256,384]{1,0:T(8,128)S(1)} %get-tuple-element.154.refs_6_.refs_2_, ...), custom_call_target="tpu_custom_call" | custom-call | flops 4499999744 | bytes 3000000 | tf_op jit(solution)/shard_map/pallas_call | solution.py:80
  66.4 3.5 %collective-permute-start.14 = (bf16[96,384]{1,0:T(8,128)(2,1)S(1)}, bf16[96,384]{1,0:T(8,128)(2,1)S(1)}, u32[]{:S(2)}, u32[]{:S(2)}) collective-permute-start(bf16[96,384]{1,0:T(8,128)(2,1)S(1)} %get-tuple-element.169), channel_id=1, source_target_pairs={{0,4},{2,6},{4,0},{6,2},{1,5},{3,7},{5,1},{7,3},{8,12},{10,14},{12... | collective-permute-start | bytes 221192 | tf_op jit(solution)/shard_map/ppermute | solution.py:749
  70.5 5.6 %collective-permute-done.14.refs_6_ = bf16[96,384]{1,0:T(8,128)(2,1)S(1)} collective-permute-done((bf16[96,384]{1,0:T(8,128)(2,1)S(1)}, bf16[96,384]{1,0:T(8,128)(2,1)S(1)}, u32[]{:S(2)}, u32[]{:S(2)}) %collective-permute-start.14) | collective-permute-done | bytes 73760 | tf_op jit(solution)/shard_map/ppermute | solution.py:749
  76.4 1.6 %collective-permute-start.19 = (bf16[1040,384]{1,0:T(8,128)(2,1)S(1)}, bf16[1040,384]{1,0:T(8,128)(2,1)S(1)}, u32[]{:S(2)}, u32[]{:S(2)}) collective-permute-start(bf16[1040,384]{1,0:T(8,128)(2,1)S(1)} %get-tuple-element.175), channel_id=1, source_target_pairs={{0,16},{1,9},{8,24},{9,1},{16,0},{17,25},{24,8},{25,17},{2,18},{3,... | collective-permute-start | bytes 2396168 | tf_op jit(solution)/shard_map/ppermute | solution.py:757
  78.0 10.6 %collective-permute-done.19.refs_3_ = bf16[1040,384]{1,0:T(8,128)(2,1)S(1)} collective-permute-done((bf16[1040,384]{1,0:T(8,128)(2,1)S(1)}, bf16[1040,384]{1,0:T(8,128)(2,1)S(1)}, u32[]{:S(2)}, u32[]{:S(2)}) %collective-permute-start.19) | collective-permute-done | bytes 798752 | tf_op jit(solution)/shard_map/ppermute | solution.py:757
  89.3 1.7 %collective-permute-start.20 = (bf16[144,384]{1,0:T(8,128)(2,1)S(1)}, bf16[144,384]{1,0:T(8,128)(2,1)S(1)}, u32[]{:S(2)}, u32[]{:S(2)}) collective-permute-start(bf16[144,384]{1,0:T(8,128)(2,1)S(1)} %get-tuple-element.177), channel_id=1, source_target_pairs={{0,2},{2,0},{4,6},{6,4},{1,3},{3,1},{5,7},{7,5},{8,10},{10,8},{12,... | collective-permute-start | bytes 331784 | tf_op jit(solution)/shard_map/ppermute | solution.py:749
  91.0 3.7 %collective-permute-done.23.refs_2_ = bf16[288,384]{1,0:T(8,128)(2,1)S(1)} collective-permute-done((bf16[288,384]{1,0:T(8,128)(2,1)S(1)}, bf16[288,384]{1,0:T(8,128)(2,1)S(1)}, u32[]{:S(2)}, u32[]{:S(2)}) %collective-permute-start.23) | collective-permute-done | bytes 221216 | tf_op jit(solution)/shard_map/ppermute | solution.py:757
  94.8 1.8 %collective-permute-start.24 = (bf16[160,384]{1,0:T(8,128)(2,1)S(1)}, bf16[160,384]{1,0:T(8,128)(2,1)S(1)}, u32[]{:S(2)}, u32[]{:S(2)}) collective-permute-start(bf16[160,384]{1,0:T(8,128)(2,1)S(1)} %get-tuple-element.186), channel_id=1, source_target_pairs={{0,2},{2,0},{4,6},{6,4},{1,3},{3,1},{5,7},{7,5},{8,10},{10,8},{12,... | collective-permute-start | bytes 368648 | tf_op jit(solution)/shard_map/ppermute | solution.py:749
  99.3 1.8 %collective-permute-start.21 = (bf16[144,384]{1,0:T(8,128)(2,1)S(1)}, bf16[144,384]{1,0:T(8,128)(2,1)S(1)}, u32[]{:S(2)}, u32[]{:S(2)}) collective-permute-start(bf16[144,384]{1,0:T(8,128)(2,1)S(1)} %get-tuple-element.178), channel_id=1, source_target_pairs={{0,4},{2,6},{4,0},{6,2},{1,5},{3,7},{5,1},{7,3},{8,12},{10,14},{12... | collective-permute-start | bytes 331784 | tf_op jit(solution)/shard_map/ppermute | solution.py:749
  102.4 14.2 %collective-permute-done.21.refs_2_ = bf16[144,384]{1,0:T(8,128)(2,1)S(1)} collective-permute-done((bf16[144,384]{1,0:T(8,128)(2,1)S(1)}, bf16[144,384]{1,0:T(8,128)(2,1)S(1)}, u32[]{:S(2)}, u32[]{:S(2)}) %collective-permute-start.21) | collective-permute-done | bytes 110624 | tf_op jit(solution)/shard_map/ppermute | solution.py:749
  122.5 1.9 %collective-permute-start.28 = (bf16[192,384]{1,0:T(8,128)(2,1)S(1)}, bf16[192,384]{1,0:T(8,128)(2,1)S(1)}, u32[]{:S(2)}, u32[]{:S(2)}) collective-permute-start(bf16[192,384]{1,0:T(8,128)(2,1)S(1)} %get-tuple-element.189.refs_4_), channel_id=1, source_target_pairs={{0,16},{8,24},{16,0},{24,8},{1,17},{9,25},{17,1},{25,9},{2,18},{10... | collective-permute-start | bytes 442376 | tf_op jit(solution)/shard_map/ppermute | solution.py:749
  124.6 4.3 %shard_map.299 = (f32[256,384]{1,0:T(8,128)}, f32[384,384]{1,0:T(8,128)}, f32[1001,384]{1,0:T(8,128)}, f32[2,48,2304]{2,1,0:T(8,128)}, f32[384,768]{1,0:T(8,128)...) custom-call(bf16[192,384]{1,0:T(8,128)(2,1)S(1)} %get-tuple-element.193.refs_0_, ...), custom_call_target="tpu_custom_call" | custom-call | flops 7500000256 | bytes 5000000 | tf_op jit(solution)/shard_map/pallas_call | solution.py:80
  130.4 2.6 %shard_map.298 = (f32[2,48,1152]{2,1,0:T(8,128)}, f32[2,48,384]{2,1,0:T(8,128)}, f32[2,48,1536]{2,1,0:T(8,128)}, f32[2,192,384]{2,1,0:T(8,128)}, bf16[4,8,16,16]...) custom-call(bf16[96,384]{1,0:T(8,128)(2,1)S(1)} %get-tuple-element.171.refs_0_, ...), custom_call_target="tpu_custom_call" | custom-call | flops 3000000000 | bytes 2000000 | tf_op jit(solution)/shard_map/pallas_call | solution.py:80
  (78 shorter events, 27.5 us)
Async XLA Ops:
  3.5 11.0 %collective-permute-start = (bf16[2,64,24]{2,1,0:T(8,128)(2,1)S(1)}, bf16[2,64,24]{2,1,0:T(8,128)(2,1)S(1)}, u32[]{:S(2)}, u32[]{:S(2)}) collective-permute-start(bf16[2,64,24]{2,1,0:T(8,128)(2,1)S(1)} %get-tuple-element.112), channel_id=1, source_target_pairs={{0,2},{2,0},{4,6},{6,4},{1,3},{3,1},{5,7},{7,5},{8,10},{10,8},{12,... | collective-permute-start | bytes 18440 | tf_op jit(solution)/shard_map/ppermute | solution.py:749
  6.6 7.9 %collective-permute-start.1 = (bf16[2,64,24]{2,1,0:T(8,128)(2,1)S(1)}, bf16[2,64,24]{2,1,0:T(8,128)(2,1)S(1)}, u32[]{:S(2)}, u32[]{:S(2)}) collective-permute-start(bf16[2,64,24]{2,1,0:T(8,128)(2,1)S(1)} %get-tuple-element.113), channel_id=1, source_target_pairs={{0,4},{2,6},{4,0},{6,2},{1,5},{3,7},{5,1},{7,3},{8,12},{10,14},{12... | collective-permute-start | bytes 18440 | tf_op jit(solution)/shard_map/ppermute | solution.py:749
  9.2 5.7 %collective-permute-start.2 = (bf16[2,64,24]{2,1,0:T(8,128)(2,1)S(1)}, bf16[2,64,24]{2,1,0:T(8,128)(2,1)S(1)}, u32[]{:S(2)}, u32[]{:S(2)}) collective-permute-start(bf16[2,64,24]{2,1,0:T(8,128)(2,1)S(1)} %get-tuple-element.114), channel_id=1, source_target_pairs={{0,6},{2,4},{4,2},{6,0},{1,7},{3,5},{5,3},{7,1},{8,14},{10,12},{12... | collective-permute-start | bytes 18440 | tf_op jit(solution)/shard_map/ppermute | solution.py:749
  43.4 17.2 %collective-permute-start.7 = (bf16[2304,384]{1,0:T(8,128)(2,1)S(1)}, bf16[2304,384]{1,0:T(8,128)(2,1)S(1)}, u32[]{:S(2)}, u32[]{:S(2)}) collective-permute-start(bf16[2304,384]{1,0:T(8,128)(2,1)S(1)} %get-tuple-element.146), channel_id=1, source_target_pairs={{0,1},{1,0},{2,3},{3,2},{4,5},{5,4},{6,7},{7,6},{8,9},{9,8},{10,11... | collective-permute-start | bytes 5308424 | tf_op jit(solution)/shard_map/ppermute | solution.py:749
  43.9 9.9 %collective-permute-start.8 = (bf16[768,384]{1,0:T(8,128)(2,1)S(1)}, bf16[768,384]{1,0:T(8,128)(2,1)S(1)}, u32[]{:S(2)}, u32[]{:S(2)}) collective-permute-start(bf16[768,384]{1,0:T(8,128)(2,1)S(1)} %get-tuple-element.147), channel_id=1, source_target_pairs={{0,8},{1,17},{8,0},{9,25},{16,24},{17,1},{24,16},{25,9},{2,10},{3,... | collective-permute-start | bytes 1769480 | tf_op jit(solution)/shard_map/ppermute | solution.py:757
  53.9 6.8 %collective-permute-start.9 = (bf16[384,384]{1,0:T(8,128)(2,1)S(1)}, bf16[384,384]{1,0:T(8,128)(2,1)S(1)}, u32[]{:S(2)}, u32[]{:S(2)}) collective-permute-start(bf16[384,384]{1,0:T(8,128)(2,1)S(1)} %get-tuple-element.150), channel_id=1, source_target_pairs={{0,16},{1,9},{8,24},{9,1},{16,0},{17,25},{24,8},{25,17},{2,18},{3,... | collective-permute-start | bytes 884744 | tf_op jit(solution)/shard_map/ppermute | solution.py:757
  61.0 15.1 %collective-permute-start.10 = (bf16[1152,384]{1,0:T(8,128)(2,1)S(1)}, bf16[1152,384]{1,0:T(8,128)(2,1)S(1)}, u32[]{:S(2)}, u32[]{:S(2)}) collective-permute-start(bf16[1152,384]{1,0:T(8,128)(2,1)S(1)} %get-tuple-element.157), channel_id=1, source_target_pairs={{0,8},{1,17},{8,0},{9,25},{16,24},{17,1},{24,16},{25,9},{2,10},{3,... | collective-permute-start | bytes 2654216 | tf_op jit(solution)/shard_map/ppermute | solution.py:757
  65.8 10.3 %collective-permute-start.12 = (bf16[848,384]{1,0:T(8,128)(2,1)S(1)}, bf16[848,384]{1,0:T(8,128)(2,1)S(1)}, u32[]{:S(2)}, u32[]{:S(2)}) collective-permute-start(bf16[848,384]{1,0:T(8,128)(2,1)S(1)} %get-tuple-element.166), channel_id=1, source_target_pairs={{0,1},{1,0},{2,3},{3,2},{4,5},{5,4},{6,7},{7,6},{8,9},{9,8},{10,11... | collective-permute-start | bytes 1953800 | tf_op jit(solution)/shard_map/ppermute | solution.py:749
  66.4 9.7 %collective-permute-start.14 = (bf16[96,384]{1,0:T(8,128)(2,1)S(1)}, bf16[96,384]{1,0:T(8,128)(2,1)S(1)}, u32[]{:S(2)}, u32[]{:S(2)}) collective-permute-start(bf16[96,384]{1,0:T(8,128)(2,1)S(1)} %get-tuple-element.169), channel_id=1, source_target_pairs={{0,4},{2,6},{4,0},{6,2},{1,5},{3,7},{5,1},{7,3},{8,12},{10,14},{12... | collective-permute-start | bytes 221192 | tf_op jit(solution)/shard_map/ppermute | solution.py:749
  69.9 6.2 %collective-permute-start.15 = (bf16[96,384]{1,0:T(8,128)(2,1)S(1)}, bf16[96,384]{1,0:T(8,128)(2,1)S(1)}, u32[]{:S(2)}, u32[]{:S(2)}) collective-permute-start(bf16[96,384]{1,0:T(8,128)(2,1)S(1)} %get-tuple-element.170), channel_id=1, source_target_pairs={{0,6},{2,4},{4,2},{6,0},{1,7},{3,5},{5,3},{7,1},{8,14},{10,12},{12... | collective-permute-start | bytes 221192 | tf_op jit(solution)/shard_map/ppermute | solution.py:749
  76.4 12.2 %collective-permute-start.19 = (bf16[1040,384]{1,0:T(8,128)(2,1)S(1)}, bf16[1040,384]{1,0:T(8,128)(2,1)S(1)}, u32[]{:S(2)}, u32[]{:S(2)}) collective-permute-start(bf16[1040,384]{1,0:T(8,128)(2,1)S(1)} %get-tuple-element.175), channel_id=1, source_target_pairs={{0,16},{1,9},{8,24},{9,1},{16,0},{17,25},{24,8},{25,17},{2,18},{3,... | collective-permute-start | bytes 2396168 | tf_op jit(solution)/shard_map/ppermute | solution.py:757
  88.7 6.0 %collective-permute-start.23 = (bf16[288,384]{1,0:T(8,128)(2,1)S(1)}, bf16[288,384]{1,0:T(8,128)(2,1)S(1)}, u32[]{:S(2)}, u32[]{:S(2)}) collective-permute-start(bf16[288,384]{1,0:T(8,128)(2,1)S(1)} %get-tuple-element.182), channel_id=1, source_target_pairs={{0,8},{1,17},{8,0},{9,25},{16,24},{17,1},{24,16},{25,9},{2,10},{3,... | collective-permute-start | bytes 663560 | tf_op jit(solution)/shard_map/ppermute | solution.py:757
  89.3 11.7 %collective-permute-start.20 = (bf16[144,384]{1,0:T(8,128)(2,1)S(1)}, bf16[144,384]{1,0:T(8,128)(2,1)S(1)}, u32[]{:S(2)}, u32[]{:S(2)}) collective-permute-start(bf16[144,384]{1,0:T(8,128)(2,1)S(1)} %get-tuple-element.177), channel_id=1, source_target_pairs={{0,2},{2,0},{4,6},{6,4},{1,3},{3,1},{5,7},{7,5},{8,10},{10,8},{12,... | collective-permute-start | bytes 331784 | tf_op jit(solution)/shard_map/ppermute | solution.py:749
  94.8 21.8 %collective-permute-start.24 = (bf16[160,384]{1,0:T(8,128)(2,1)S(1)}, bf16[160,384]{1,0:T(8,128)(2,1)S(1)}, u32[]{:S(2)}, u32[]{:S(2)}) collective-permute-start(bf16[160,384]{1,0:T(8,128)(2,1)S(1)} %get-tuple-element.186), channel_id=1, source_target_pairs={{0,2},{2,0},{4,6},{6,4},{1,3},{3,1},{5,7},{7,5},{8,10},{10,8},{12,... | collective-permute-start | bytes 368648 | tf_op jit(solution)/shard_map/ppermute | solution.py:749
  96.6 20.0 %collective-permute-start.25 = (bf16[160,384]{1,0:T(8,128)(2,1)S(1)}, bf16[160,384]{1,0:T(8,128)(2,1)S(1)}, u32[]{:S(2)}, u32[]{:S(2)}) collective-permute-start(bf16[160,384]{1,0:T(8,128)(2,1)S(1)} %get-tuple-element.187), channel_id=1, source_target_pairs={{0,4},{2,6},{4,0},{6,2},{1,5},{3,7},{5,1},{7,3},{8,12},{10,14},{12... | collective-permute-start | bytes 368648 | tf_op jit(solution)/shard_map/ppermute | solution.py:749
  97.9 18.7 %collective-permute-start.26 = (bf16[160,384]{1,0:T(8,128)(2,1)S(1)}, bf16[160,384]{1,0:T(8,128)(2,1)S(1)}, u32[]{:S(2)}, u32[]{:S(2)}) collective-permute-start(bf16[160,384]{1,0:T(8,128)(2,1)S(1)} %get-tuple-element.188), channel_id=1, source_target_pairs={{0,6},{2,4},{4,2},{6,0},{1,7},{3,5},{5,3},{7,1},{8,14},{10,12},{12... | collective-permute-start | bytes 368648 | tf_op jit(solution)/shard_map/ppermute | solution.py:749
  99.3 17.3 %collective-permute-start.21 = (bf16[144,384]{1,0:T(8,128)(2,1)S(1)}, bf16[144,384]{1,0:T(8,128)(2,1)S(1)}, u32[]{:S(2)}, u32[]{:S(2)}) collective-permute-start(bf16[144,384]{1,0:T(8,128)(2,1)S(1)} %get-tuple-element.178), channel_id=1, source_target_pairs={{0,4},{2,6},{4,0},{6,2},{1,5},{3,7},{5,1},{7,3},{8,12},{10,14},{12... | collective-permute-start | bytes 331784 | tf_op jit(solution)/shard_map/ppermute | solution.py:749
  101.0 15.6 %collective-permute-start.22 = (bf16[144,384]{1,0:T(8,128)(2,1)S(1)}, bf16[144,384]{1,0:T(8,128)(2,1)S(1)}, u32[]{:S(2)}, u32[]{:S(2)}) collective-permute-start(bf16[144,384]{1,0:T(8,128)(2,1)S(1)} %get-tuple-element.179), channel_id=1, source_target_pairs={{0,6},{2,4},{4,2},{6,0},{1,7},{3,5},{5,3},{7,1},{8,14},{10,12},{12... | collective-permute-start | bytes 331784 | tf_op jit(solution)/shard_map/ppermute | solution.py:749
  116.7 7.7 %collective-permute-start.30 = (bf16[192,384]{1,0:T(8,128)(2,1)S(1)}, bf16[192,384]{1,0:T(8,128)(2,1)S(1)}, u32[]{:S(2)}, u32[]{:S(2)}) collective-permute-start(bf16[192,384]{1,0:T(8,128)(2,1)S(1)} %get-tuple-element.193.refs_0_), channel_id=1, source_target_pairs={{0,1},{1,0},{2,3},{3,2},{4,5},{5,4},{6,7},{7,6},{8,9},{9,8},{10,11... | collective-permute-start | bytes 442376 | tf_op jit(solution)/shard_map/ppermute | solution.py:749
  118.4 11.3 %collective-permute-start.17 = (bf16[96,384]{1,0:T(8,128)(2,1)S(1)}, bf16[96,384]{1,0:T(8,128)(2,1)S(1)}, u32[]{:S(2)}, u32[]{:S(2)}) collective-permute-start(bf16[96,384]{1,0:T(8,128)(2,1)S(1)} %get-tuple-element.171.refs_0_), channel_id=1, source_target_pairs={{0,16},{8,24},{16,0},{24,8},{1,17},{9,25},{17,1},{25,9},{2,18},{10... | collective-permute-start | bytes 221192 | tf_op jit(solution)/shard_map/ppermute | solution.py:749
  118.9 10.8 %collective-permute-start.16 = (bf16[96,384]{1,0:T(8,128)(2,1)S(1)}, bf16[96,384]{1,0:T(8,128)(2,1)S(1)}, u32[]{:S(2)}, u32[]{:S(2)}) collective-permute-start(bf16[96,384]{1,0:T(8,128)(2,1)S(1)} %get-tuple-element.171.refs_0_), channel_id=1, source_target_pairs={{0,8},{8,0},{16,24},{24,16},{1,9},{9,1},{17,25},{25,17},{2,10},{10... | collective-permute-start | bytes 221192 | tf_op jit(solution)/shard_map/ppermute | solution.py:749
  120.4 9.3 %collective-permute-start.29 = (bf16[192,384]{1,0:T(8,128)(2,1)S(1)}, bf16[192,384]{1,0:T(8,128)(2,1)S(1)}, u32[]{:S(2)}, u32[]{:S(2)}) collective-permute-start(bf16[192,384]{1,0:T(8,128)(2,1)S(1)} %get-tuple-element.189.refs_4_), channel_id=1, source_target_pairs={{0,24},{8,16},{16,8},{24,0},{1,25},{9,17},{17,9},{25,1},{2,26},{10... | collective-permute-start | bytes 442376 | tf_op jit(solution)/shard_map/ppermute | solution.py:749
  122.5 7.9 %collective-permute-start.28 = (bf16[192,384]{1,0:T(8,128)(2,1)S(1)}, bf16[192,384]{1,0:T(8,128)(2,1)S(1)}, u32[]{:S(2)}, u32[]{:S(2)}) collective-permute-start(bf16[192,384]{1,0:T(8,128)(2,1)S(1)} %get-tuple-element.189.refs_4_), channel_id=1, source_target_pairs={{0,16},{8,24},{16,0},{24,8},{1,17},{9,25},{17,1},{25,9},{2,18},{10... | collective-permute-start | bytes 442376 | tf_op jit(solution)/shard_map/ppermute | solution.py:749
  124.4 6.0 %collective-permute-start.27 = (bf16[192,384]{1,0:T(8,128)(2,1)S(1)}, bf16[192,384]{1,0:T(8,128)(2,1)S(1)}, u32[]{:S(2)}, u32[]{:S(2)}) collective-permute-start(bf16[192,384]{1,0:T(8,128)(2,1)S(1)} %get-tuple-element.189.refs_4_), channel_id=1, source_target_pairs={{0,8},{8,0},{16,24},{24,16},{1,9},{9,1},{17,25},{25,17},{2,10},{10... | collective-permute-start | bytes 442376 | tf_op jit(solution)/shard_map/ppermute | solution.py:749
  (17 other events, 82.9 us)
where the time goes:
time: 133 us
  waiting for transfers between devices  50.1 us (38%)
  Pallas kernels  43.8 us (33%)
  starting transfers between devices  34.9 us (26%)
  local copies, waits for them, and re-layouts  2.71 us (2%)
  between operations  1.54 us (1%)
    pallas_call x18, Pallas kernels, kernel_call(): pl.pallas_call(kernel, in_specs=specs, out_specs=[pl.BlockSpec(memory_spa...  43.8 us
    ppermute x26, starting transfers between devices, swap(): return lax.ppermute(value, axis, [(i, i ^ bit) for i in range(count)])  28 us
    ppermute x26, waiting for transfers between devices, swap(): return lax.ppermute(value, axis, [(i, i ^ bit) for i in range(count)])  25.6 us
    ppermute x5, waiting for transfers between devices, swap_by_core(): return lax.ppermute(value, ('wide', 'cols'), pairs)  24.4 us
    ppermute x5, starting transfers between devices, swap_by_core(): return lax.ppermute(value, ('wide', 'cols'), pairs)  6.83 us
    unnamed x22, local copies, waits for them, and re-layouts  2.71 us
  transfers between devices with their start and end apart: 31, of which 13 were waited for; matrix products, arithmetic and copies ran while one was open for 1% of the time, Pallas kernels for 15%

commit v1 on v0

--- a/solution.py
+++ b/solution.py
@@ -16,8 +16,14 @@
 EPS = 1e-06
 F32 = jnp.float32
 BF16 = jnp.bfloat16
-ROWS = 24
-ROW_F, ROW_SHARED, ROW_ACT, ROW_COND, ROW_HID, ROW_FEAT = 12, 14, 15, 16, 17, 18
+ROWS = 12
+ROW_SHARED, ROW_ACT, ROW_COND, ROW_HID, ROW_FEAT = 5, 6, 7, 8, 9
+US = {
+    "cond": 5, "embed": 2, "block": 6, "turn": 9, "back": 20, "middle": 4, "last": 4, "sums": 5, "spread": 2,
+    "A1": 0.05, "A2": 0.05, "A2b": 0.05, "A3": 0.05, "A3b": 0.05, "A4": 30, "A4b": 0.05, "A5": 0.05, "A6": 0.05, "S1": 0.05, "U2": 0.05,
+    "U1": 20,
+}
+
 
 def dot(a, b):
     return jnp.dot(a, b, preferred_element_type=F32)
@@ -98,6 +104,11 @@
 
 def places():
     return lax.axis_index("rows"), lax.axis_index("cols"), lax.axis_index("wide")
+
+
+def chip_place(zz, ww, cc):
+    x, y = ww % 2, ww // 2
+    return zz * 4 + ((2 * y + x) if cc == 0 else (2 * x + y))
 
 
 def wide_bits():
@@ -325,7 +336,7 @@
 
 
 def qkv_backward(
-    state, middle_grad, dq, dkv, dkvr, mods, layer, weight, gproj, keep, send, size, at_row, flip, rows
+    state, middle_grad, dq, dkv, dkvr, mods, layer, weight, gproj, keep, send, at_row, place_of, rows
 ):
     width = state.shape[-1]
     block = width // 8
@@ -339,8 +350,8 @@
     def put(values, i):
         for b in range(4):
             pair = [values[(2 * b + cc) * block : (2 * b + cc + 1) * block] for cc in range(2)]
-            place = [unit_place(b, i, cc ^ flip) for cc in range(2)]
-            put_units(keep, send, pair, place, size, at_row)
+            place = [place_of(b, i, cc) for cc in range(2)]
+            put_units(keep, send, pair, place, block, at_row)
 
     for i, piece in enumerate(pieces):
         part = dot_nt(piece, weight[layer, :, i * width : (i + 1) * width])
@@ -397,9 +408,9 @@
 
 
 def turn_body(
-    offsets, counts, state, q, kv, kvp, mods, patches, final_weight, proj, up, down,
-    probs, attended, attn_out, middle_grad, keep, send, rows, gfinal, predt,
-    gp, act, preds,
+    offsets, counts, state, q, kv, kvp, mods, cond, patches, final_weight, proj, up, down,
+    probs, attended, attn_out, middle_grad, keep, send, preds,
+    gp, act, table,
 ):
     z, _, _ = places()
     offset = offsets[z]
@@ -418,26 +429,28 @@
     lanes = weight.shape[1] // 2
     out = dot(inner, weight) * live
     preds[0], preds[1] = by_parity(out[:, :lanes], out[:, lanes:], offset)
-    tok = preds.shape[1] // 4
-    for k in range(4):
-        cut = pl.ds(pl.multiple_of((z ^ k) * tok, 8), tok)
-        predt[k] = packed_tile([preds[0, cut, :], preds[1, cut, :]], lanes, 8)
     across = weight.astype(F32).T
     chosen = patches
     fill = jnp.zeros((chosen.shape[2] - lanes, across.shape[1]), F32)
     upper = jnp.concatenate([fill, across[:lanes]], axis=0).astype(BF16)
     lower = jnp.concatenate([fill, across[lanes:]], axis=0).astype(BF16)
     inner_grad = (dot(chosen[0], upper) + dot(chosen[1], lower)) * live
-    gfinal[0] = dot_tn(chosen[0], inner) * live
-    gfinal[1] = dot_tn(chosen[1], inner) * live
-    rows[...] = jnp.zeros_like(rows)
-    rows[3:4, :] = token_sum(inner_grad)
-    rows[4:5, :] = token_sum(inner_grad * normed)
+    table[...] = jnp.zeros_like(table)
+    table[0:1, :] = token_sum(inner_grad)
+    table[1:2, :] = token_sum(inner_grad * normed)
+    table[5:10, :] = 0.5 * cond[0:5, :]
+    skip = chosen.shape[2] - lanes
+    for r in range(2):
+        at = ROWS + r * lanes
+        table[at : at + lanes, :] = (dot_tn(chosen[r], inner) * live)[skip:]
     grad = norm_back(inner_grad * scale, normed, inverse)
     size = 2 * (weight.shape[0] // 8)
     middle_grad[...] = mlp_backward(
-        grad, middle, branch, m, 1, gp, act, up, down, keep, send, size, rows, 0
-    )
+        grad, middle, branch, m, 1, gp, act, up, down, keep, send, size, table, 2
+    )
+    base = 4 * weight.shape[0]
+    keep[base:] = table[...].astype(BF16)
+    send[base:] = table[...].astype(BF16)
 
 
 def attend_back_body(
@@ -486,12 +499,12 @@
     middle_grad, keep, send, rows,
 ):
     width = dq.shape[-1]
-    size = 3 * (width // 8)
+    size = 2 * (width // 8)
     rows[...] = jnp.zeros_like(rows)
     m = mods
     grad = qkv_backward(
-        state1[...], middle_grad1[...], dq, dkv, dkvr, m, 1, qkv, gproj, keep, send, size,
-        2 * (width // 8), 0, rows,
+        state1[...], middle_grad1[...], dq, dkv, dkvr, m, 1, qkv, gproj, keep, send,
+        16 * size, chip_place, rows,
     )
     middle_grad[...] = mlp_backward(
         grad, middle[...], branch[...], m, 0, gp, act, up, down, keep, send, size,
@@ -500,17 +513,17 @@
 
 
 def last_body(
-    offsets, state0, middle_grad, dq, dkv, dkvr, gproj, mods, patches, patch_weight, cond,
-    rows_turn, rows_a1, rows_mid, rows_a0, gfinal, qkv,
-    keep, send, lgradt, rows, lgrads, table,
+    offsets, state0, middle_grad, dq, dkv, dkvr, gproj, mods, patches, patch_weight,
+    rows_a1, rows_mid, rows_a0, qkv,
+    keep, send, lgrads, rows, table,
 ):
     z, _, _ = places()
     offset = offsets[z]
     width = dq.shape[-1]
     block = width // 8
     grad = qkv_backward(
-        state0[...], middle_grad[...], dq, dkv, dkvr, mods, 0, qkv, gproj, keep, send, block,
-        0, 1, rows,
+        state0[...], middle_grad[...], dq, dkv, dkvr, mods, 0, qkv, gproj, keep, send,
+        0, lambda zz, ww, cc: unit_place(zz, ww, 1 - cc), rows,
     )
     embed_grad = grad.astype(BF16)
     chosen = patches
@@ -518,132 +531,195 @@
     chans = patch_weight.shape[0] // 2
     window = dot_nt(embed_grad, patch_weight[...])
     lgrads[0], lgrads[1] = by_parity(window[:, :chans], window[:, chans:], offset)
-    tok = lgrads.shape[1] // 4
-    for k in range(4):
-        cut = pl.ds(pl.multiple_of((z ^ k) * tok, 8), tok)
-        parts = [lgrads[0, cut, :], lgrads[1, cut, :]]
-        leading = [part.astype(BF16).astype(F32) for part in parts]
-        lgradt[k, :, 0:128] = packed_tile(leading, chans, 8)
-        lgradt[k, :, 128:256] = packed_tile([a - b for a, b in zip(parts, leading)], chans, 8)
     table[...] = jnp.zeros_like(table)
     table[0:2, :] = rows[0:2, :]
     table[2:3, :] = rows_a0[0:1, :]
     table[3:6, :] = rows_mid[2:5, :]
     table[6:8, :] = rows_mid[0:2, :]
     table[8:9, :] = rows_a1[0:1, :]
-    table[9:12, :] = rows_turn[0:3, :]
-    table[12:14, :] = rows_turn[3:5, :]
-    table[14:19, :] = 0.5 * cond[0:5, :]
     table[ROWS : ROWS + chans, :] = gp0[:chans]
     table[ROWS + chans : ROWS + 2 * chans, :] = gp1[:chans]
-    final = gfinal
-    outs = final.shape[1] - chans
-    base = ROWS + 2 * chans
-    table[base : base + outs, :] = final[0, chans:, :]
-    table[base + outs : base + 2 * outs, :] = final[1, chans:, :]
     keep[16 * block :] = table[...].astype(BF16)
     send[16 * block :] = table[...].astype(BF16)
 
 
-def split_body(keep, recv, keep_out, send_out, bit_at):
-    half = keep.shape[0] // 2
-    bit = wide_bits()[bit_at]
+def second_body(keep, recv, keep_out, send_out):
+    half = keep_out.shape[0]
+    bit = wide_bits()[0]
     keep_out[...] = keep[rows_at(bit, half)] + recv[rows_at(bit, half)]
     send_out[...] = keep[rows_at(1 - bit, half)] + recv[rows_at(1 - bit, half)]
 
 
-def one_split_body(bit_at, keep, recv, keep_out, send_out):
-    split_body(keep, recv, keep_out, send_out, bit_at)
-
-
-def to_chips(held, recv, outs):
+def beta_body(keep, recv, *chips):
     z, _, _ = places()
-    size = held.shape[0] // 4
-    for k, out in enumerate(outs):
-        out[...] = held[rows_at(z ^ k, size)] + recv[rows_at(z ^ k, size)]
-
-
-def second_body(keep2, recv2, held1, recv1, keep2_out, send2_out, *units1):
-    split_body(keep2, recv2, keep2_out, send2_out, 0)
-    to_chips(held1, recv1, units1)
-
-
-def third_body(keep2, recv2, keep3, recv3, u0, u1, u2, u3, keep2_out, keep3_out, table, unit1, send):
-    half2 = keep2.shape[0] // 2
-    size3 = keep3.shape[0] - 80
-    half3 = size3 // 2
-    bit = wide_bits()[1]
-    keep2_out[...] = keep2[rows_at(bit, half2)] + recv2[rows_at(bit, half2)]
-    send[0:half2] = keep2[rows_at(1 - bit, half2)] + recv2[rows_at(1 - bit, half2)]
-    keep3_out[...] = keep3[rows_at(bit, half3)] + recv3[rows_at(bit, half3)]
-    send[half2 : half2 + half3] = keep3[rows_at(1 - bit, half3)] + recv3[rows_at(1 - bit, half3)]
-    rows = keep3[size3:] + recv3[size3:]
-    table[...] = rows
-    send[half2 + half3 :] = rows
-    unit1[...] = (
-        u0[...].astype(F32) + u1[...].astype(F32) + u2[...].astype(F32) + u3[...].astype(F32)
-    ).astype(BF16)
-
-
-def fourth_body(keep2, keep3, table, recv, z0, z1, z2, z3, keep3_out, pair_out, send):
-    z, _, _ = places()
-    size2, size3 = keep2.shape[0], keep3.shape[0]
-    unit2, half3 = size2 // 4, size3 // 2
-    for k, out in enumerate((z0, z1, z2, z3)):
-        out[...] = keep2[rows_at(z ^ k, unit2)] + recv[rows_at(z ^ k, unit2)]
-    bit = wide_bits()[0]
-
-    def half(index):
-        start = pl.multiple_of(index * half3, 16)
-        return keep3[pl.ds(start, half3)] + recv[pl.ds(pl.multiple_of(start + size2, 16), half3)]
-
-    keep3_out[...] = half(bit)
-    send[0:half3] = half(1 - bit)
-    mine = table[...].astype(F32)
-    other = recv[size2 + size3 :].astype(F32)
-    pair = jnp.concatenate(
-        [mine[:ROWS], other[:ROWS], mine[ROWS : ROWS + 48] + other[ROWS : ROWS + 48]], axis=0
-    ).astype(BF16)
-    pair_out[...] = pair
-    send[half3:] = pair
-
-
-def fifth_body(keep3, pair, recv, predt, lgradt, z0, z1, z2, z3, four):
-    z, c, w = places()
-    size3 = keep3.shape[0]
-    unit3 = size3 // 4
-    first = jnp.where(c == 0, 2, 1)
+    size = chips[0].shape[0]
+    base = keep.shape[0] - 4 * size
+    for k, out in enumerate(chips):
+        at = pl.ds(pl.multiple_of(base + (z ^ k) * size, 16), size)
+        out[...] = keep[at] + recv[at]
+
+
+def padded(*pieces):
+    rows = jnp.concatenate(pieces, axis=0)
+    fill = -rows.shape[0] % 16
+    if fill:
+        rows = jnp.concatenate([rows, jnp.zeros((fill, rows.shape[1]), F32)], axis=0)
+    return rows.astype(BF16)
+
+
+def paired(mine, other, sums):
+    return padded(
+        mine[:ROWS], other[:ROWS], mine[ROWS : ROWS + sums] + other[ROWS : ROWS + sums]
+    )
+
+
+def half_of_four(mine, other, sums, flip, four, total):
+    _, c, w = places()
+    first = jnp.where(c == flip, 1, 2)
     second = 3 - first
     spot = lax.rem(w, 4)
-    mine, other = pair[...].astype(F32), recv[size3:].astype(F32)
     four[spot] = mine[:ROWS]
     four[spot ^ first] = mine[ROWS : 2 * ROWS]
     four[spot ^ second] = other[:ROWS]
     four[spot ^ first ^ second] = other[ROWS : 2 * ROWS]
-    rows = jnp.concatenate([four[2 * c], four[2 * c + 1]], axis=0).astype(BF16)
-    sums = (mine[2 * ROWS :] + other[2 * ROWS :]).astype(BF16)
-    base = unit3 + 2 * ROWS
+    at = slice(2 * ROWS, 2 * ROWS + sums)
+    total[...] = mine[at] + other[at]
+    half = sums // 2
+    return padded(four[2 * c], four[2 * c + 1], total[pl.ds(pl.multiple_of(c * half, 8), half), :])
+
+
+def first_body(keep, recv, keep_out, table, send):
+    half = (keep.shape[0] - table.shape[0]) // 2
+    bit = wide_bits()[0]
+    keep_out[...] = keep[rows_at(bit, half)] + recv[rows_at(bit, half)]
+    send[0:half] = keep[rows_at(1 - bit, half)] + recv[rows_at(1 - bit, half)]
+    rows = keep[2 * half :] + recv[2 * half :]
+    table[...] = rows
+    send[half:] = rows
+
+
+def first_pair_body(sums, keep, table, recv, keep_out, pair_out, send):
+    size = keep.shape[0]
+    half = size // 2
+    bit = wide_bits()[1]
+    keep_out[...] = keep[rows_at(bit, half)] + recv[rows_at(bit, half)]
+    send[0:half] = keep[rows_at(1 - bit, half)] + recv[rows_at(1 - bit, half)]
+    pair = paired(table[...].astype(F32), recv[size:].astype(F32), sums)
+    pair_out[...] = pair
+    send[half:] = pair
+
+
+def first_chip_body(
+    sums, keep, pair, recv, preds, lgrads, z0, z1, z2, z3, tiles, four, total
+):
+    z, _, _ = places()
+    size = keep.shape[0]
+    unit = size // 4
+    rows = half_of_four(pair[...].astype(F32), recv[size:].astype(F32), sums, 0, four, total)
     for k, out in enumerate((z0, z1, z2, z3)):
-        out[0:unit3] = keep3[rows_at(z ^ k, unit3)] + recv[rows_at(z ^ k, unit3)]
-        out[unit3:base] = rows
-        out[base : base + 48] = sums
-        tile = jnp.concatenate([lgradt[k], predt[k]], axis=0)
-        out[base + 48 : base + 64, 0:256] = tile.astype(BF16)
-        out[base + 48 : base + 64, 256:384] = jnp.zeros((16, 128), BF16)
-
-
-def sixth_body(*refs):
-    twos, threes = refs[:4], refs[4:8]
-    unit, half, sums, tiles = refs[8:]
-    size2 = twos[0].shape[0]
-    size3 = threes[0].shape[0] - 2 * ROWS - 64
-    base = size3 + 2 * ROWS
-    unit[0:size2] = sum(t[...].astype(F32) for t in twos).astype(BF16)
-    unit[size2:] = sum(t[0:size3].astype(F32) for t in threes).astype(BF16)
-    sums[...] = sum(t[base : base + 48].astype(F32) for t in threes)
-    for k, t in enumerate(threes):
-        half[2 * ROWS * k : 2 * ROWS * (k + 1)] = t[size3:base]
-        tiles[k] = t[base + 48 :]
+        out[0:unit] = keep[rows_at(z ^ k, unit)] + recv[rows_at(z ^ k, unit)]
+        out[unit:] = rows
+    tok = preds.shape[1] // 4
+    tiles[:, :, 256:] = jnp.zeros((4, 16, 128), BF16)
+    for k in range(4):
+        cut = pl.ds(pl.multiple_of((z ^ k) * tok, 8), tok)
+        parts = [lgrads[0, cut, :], lgrads[1, cut, :]]
+        leading = [part.astype(BF16).astype(F32) for part in parts]
+        chans = lgrads.shape[2]
+        latents = jnp.concatenate(
+            [
+                packed_tile(leading, chans, 8),
+                packed_tile([a - b for a, b in zip(parts, leading)], chans, 8),
+            ],
+            axis=1,
+        )
+        predicted = packed_tile([preds[0, cut, :], preds[1, cut, :]], preds.shape[2], 8)
+        tiles[k, :, 0:256] = jnp.concatenate([latents, predicted], axis=0).astype(BF16)
+
+
+def chip_sum(parts, at):
+    return sum(part[at].astype(F32) for part in parts)
+
+
+def third_body(keep2, recv2, b0, b1, b2, b3, keep2_out, keepb, part, whole):
+    half2, halfb = keep2.shape[0] // 2, keepb.shape[0]
+    bit = wide_bits()[1]
+    keep2_out[...] = keep2[rows_at(bit, half2)] + recv2[rows_at(bit, half2)]
+    part[0:half2] = keep2[rows_at(1 - bit, half2)] + recv2[rows_at(1 - bit, half2)]
+    whole[...] = chip_sum((b0, b1, b2, b3), slice(None)).astype(BF16)
+    keepb[...] = whole[rows_at(bit, halfb)]
+    part[half2:] = whole[rows_at(1 - bit, halfb)]
+
+
+def third_send_body(keep3, recv3, part, keep3_out, table, send):
+    size = part.shape[0]
+    size3 = keep3.shape[0] - table.shape[0]
+    half3 = size3 // 2
+    bit = wide_bits()[1]
+    send[0:size] = part[...]
+    keep3_out[...] = keep3[rows_at(bit, half3)] + recv3[rows_at(bit, half3)]
+    send[size : size + half3] = keep3[rows_at(1 - bit, half3)] + recv3[rows_at(1 - bit, half3)]
+    rows = keep3[size3:] + recv3[size3:]
+    table[...] = rows
+    send[size + half3 :] = rows
+
+
+def fourth_body(sums, keep2, keep3, keepb, table, recv, whole2, keep3_out, keepb_out, pair_out, send):
+    size2, size3, sizeb = keep2.shape[0], keep3.shape[0], keepb.shape[0]
+    half3, halfb = size3 // 2, sizeb // 2
+    whole2[...] = keep2[...] + recv[0:size2]
+    bit = wide_bits()[0]
+
+    def half(held, index, size, base):
+        start = pl.multiple_of(index * size, 16)
+        return held[pl.ds(start, size)] + recv[pl.ds(pl.multiple_of(start + base, 16), size)]
+
+    keep3_out[...] = half(keep3, bit, half3, size2 + sizeb)
+    send[0:half3] = half(keep3, 1 - bit, half3, size2 + sizeb)
+    keepb_out[...] = half(keepb, bit, halfb, size2)
+    send[half3 : half3 + halfb] = half(keepb, 1 - bit, halfb, size2)
+    pair = paired(table[...].astype(F32), recv[size2 + size3 + sizeb :].astype(F32), sums)
+    pair_out[...] = pair
+    send[half3 + halfb :] = pair
+
+
+def fifth_body(sums, whole2, keep3, keepb, pair, recv, tiles, z0, z1, z2, z3, unitb, four, total):
+    z, _, _ = places()
+    unit2, size3, sizeb = whole2.shape[0] // 4, keep3.shape[0], keepb.shape[0]
+    unit3 = size3 // 4
+    other = recv[size3 + sizeb :].astype(F32)
+    rows = half_of_four(pair[...].astype(F32), other, sums, 1, four, total)
+    start = unit2 + unit3
+    end = start + rows.shape[0]
+    for k, out in enumerate((z0, z1, z2, z3)):
+        out[0:unit2] = whole2[rows_at(z ^ k, unit2)]
+        out[unit2:start] = keep3[rows_at(z ^ k, unit3)] + recv[rows_at(z ^ k, unit3)]
+        out[start:end] = rows
+        out[end:] = tiles[k]
+    unitb[...] = keepb[...] + recv[size3 : size3 + sizeb]
+
+
+def chip_rows(sums, parts, size, pack):
+    rows = [part[size : size + 48 if sums > 8 else size + 32].astype(F32) for part in parts]
+    total = sum(r[2 * ROWS : 2 * ROWS + sums] for r in rows)
+    pack[...] = padded(*[r[: 2 * ROWS] for r in rows], total)
+
+
+def unit1_body(sums, z0, z1, z2, z3, unit, pack):
+    parts = (z0, z1, z2, z3)
+    size = unit.shape[0]
+    unit[...] = chip_sum(parts, slice(0, size)).astype(BF16)
+    chip_rows(sums, parts, size, pack)
+
+
+def unit2_body(sums, z0, z1, z2, z3, unitb, unit, pack, tiles):
+    parts = (z0, z1, z2, z3)
+    size = unit.shape[0] - unitb.shape[0]
+    unit[0:size] = chip_sum(parts, slice(0, size)).astype(BF16)
+    unit[size:] = unitb[...]
+    chip_rows(sums, parts, size, pack)
+    for k, part in enumerate(parts):
+        tiles[k] = part[size + 32 :]
 
 
 def silu_slope(values):
@@ -652,28 +728,37 @@
 
 
 def sums_body(
-    own, other, sums, modulation, final_mod, time_out,
+    pack_a, other_a, pack_b, other_b, modulation, final_mod, time_out,
     g_time_in, g_time_out, g_table, g_mod, g_final_mod, g_patch, g_final,
-    table, shared_t,
+    table, shared_t, total,
 ):
     z, c, _ = places()
-    half = own.shape[0]
-    parts = table.shape[0]
-    for i in range(parts):
-        at = slice(128 * i, 128 * (i + 1))
-        table[i, 0:half] = own[:, at].astype(F32)
-        table[i, half:] = other[:, at].astype(F32)
-    samples = table.shape[1] // ROWS
-
-    def rows(r):
-        pieces = [table[i, pl.ds(r, samples, stride=ROWS), :] for i in range(parts)]
+    parts = table.shape[1]
+    half = table.shape[2] // 2
+    for which, pair in enumerate(((pack_a, other_a), (pack_b, other_b))):
+        for side, pack in enumerate(pair):
+            for i in range(parts):
+                at = slice(128 * i, 128 * (i + 1))
+                table[which, i, half * side : half * (side + 1)] = pack[0:half, at].astype(F32)
+    count = g_patch.shape[0] // 2
+    for side, pack in enumerate((pack_b, other_b)):
+        at = pl.ds(pl.multiple_of((c ^ side) * count, 8), count)
+        g_patch[at, :] = pack[half : half + 16].astype(F32)[:count]
+    count = total.shape[0] // 2
+    for side, pack in enumerate((pack_a, other_a)):
+        at = pl.ds(pl.multiple_of((c ^ side) * count, 8), count)
+        total[at, :] = pack[half : half + count].astype(F32)
+    g_final[...] = total[...].T
+    samples = table.shape[2] // ROWS
+
+    def rows(r, which=0):
+        pieces = [table[which, i, pl.ds(r, samples, stride=ROWS), :] for i in range(parts)]
         return jnp.concatenate(pieces, axis=-1)
 
-    mods = [
-        jnp.concatenate([rows(6 * layer + k) for k in range(6)], axis=-1).astype(BF16)
-        for layer in range(2)
-    ]
-    fmods = jnp.concatenate([rows(ROW_F), rows(ROW_F + 1)], axis=-1).astype(BF16)
+    low = [rows(k, 1) for k in range(6)]
+    high = [rows(k, 1) for k in range(6, 9)] + [rows(k) for k in range(2, 5)]
+    mods = [jnp.concatenate(pieces, axis=-1).astype(BF16) for pieces in (low, high)]
+    fmods = jnp.concatenate([rows(0), rows(1)], axis=-1).astype(BF16)
     shared_t[...] = rows(ROW_SHARED).T
     block = g_mod.shape[1]
     start = pl.multiple_of((z * 2 + c) * block, 8)
@@ -681,9 +766,6 @@
     for layer in range(2):
         g_mod[layer] = dot(mine, mods[layer])
     g_final_mod[...] = dot(shared_t[...].astype(BF16), fmods)
-    patch = g_patch.shape[0]
-    g_patch[...] = sums[:patch, :]
-    g_final[...] = sums[patch:, :].T
     shared_grad = dot_nt(fmods, final_mod[...])
     for layer in range(2):
         shared_grad += dot_nt(mods[layer], modulation[layer])
@@ -703,45 +785,56 @@
     g_time_in[...] = dot(feats[:, :count].T.astype(BF16), time_grad.astype(BF16))
 
 
+def place_mlp(g_up, g_down, layer, piece, unit):
+    block, width = g_up.shape[1], g_down.shape[2]
+    cols = pl.ds(pl.multiple_of(unit * width, 128), width)
+    g_up[layer, :, cols] = piece[0:block].astype(F32)
+    down_rows = pl.ds(pl.multiple_of(unit * block, 8), block)
+    g_down[layer, down_rows, :] = piece[block : 2 * block].astype(F32)
+
+
+def place_attn(g_qkv, g_proj, layer, piece, unit):
+    width = g_proj.shape[2]
+
+    @pl.when(unit < 3)
+    def _():
+        cols = pl.ds(pl.multiple_of(unit * width, 128), width)
+        g_qkv[layer, :, cols] = piece.astype(F32)
+
+    @pl.when(unit == 3)
+    def _():
+        g_proj[layer] = piece.astype(F32)
+
+
+def first_spread_body(*refs):
+    ones, (g_up, g_down) = refs[:4], refs[4:]
+    spot = lax.rem(lax.axis_index("wide"), 4)
+    for k in range(4):
+        place_mlp(g_up, g_down, 1, ones[k][...], spot ^ k)
+
+
 def spread_body(*refs):
-    ones, others, tiles = refs[:4], refs[4:8], refs[8]
-    g_qkv, g_proj, g_up, g_down, prediction, latent_grad = refs[9:]
+    twos, tiles, up, down = refs[:4], refs[4], refs[5], refs[6]
+    g_qkv, g_proj, g_up, g_down, prediction, latent_grad = refs[7:]
     z, _, w = places()
-    width = g_proj.shape[-1]
     block = g_proj.shape[1]
     spot = lax.rem(w, 4)
-
-    def place_mlp(layer, piece, unit):
-        cols = pl.ds(pl.multiple_of(unit * width, 128), width)
-        g_up[layer, :, cols] = piece[0:block].astype(F32)
-        down_rows = pl.ds(pl.multiple_of(unit * block, 8), block)
-        g_down[layer, down_rows, :] = piece[block : 2 * block].astype(F32)
-
-    def place_attn(layer, piece, unit):
-        @pl.when(unit < 3)
-        def _():
-            cols = pl.ds(pl.multiple_of(unit * width, 128), width)
-            g_qkv[layer, :, cols] = piece.astype(F32)
-
-        @pl.when(unit == 3)
-        def _():
-            g_proj[layer] = piece.astype(F32)
-
+    g_up[1] = up[1]
+    g_down[1] = down[1]
+    _, out_ch, height, wide = prediction.shape
+    lat_ch = latent_grad.shape[1]
     for k in range(4):
-        unit = spot ^ k
-        place_mlp(1, ones[k][...], unit)
-        both = others[k]
-        place_mlp(0, both[0 : 2 * block], unit)
-        place_attn(1, both[2 * block : 3 * block], unit)
-        place_attn(0, both[3 * block :], unit)
-        _, out_ch, height, wide = prediction.shape
-        lat_ch = latent_grad.shape[1]
         tile = tiles[k].astype(F32)
         image = unpacked_tile(tile[8:16, 0:256].astype(BF16), out_ch, height, wide)
         prediction[z ^ k] = image.astype(BF16).reshape(out_ch, height, wide)
         image = unpacked_tile(tile[0:8, 0:128].astype(BF16), lat_ch, height, wide)
         image = image + unpacked_tile(tile[0:8, 128:256].astype(BF16), lat_ch, height, wide)
         latent_grad[z ^ k] = image.reshape(lat_ch, height, wide)
+    for k in range(4):
+        unit = spot ^ k
+        place_mlp(g_up, g_down, 0, twos[k][0 : 2 * block], unit)
+        place_attn(g_qkv, g_proj, 0, twos[k][2 * block : 3 * block], unit)
+        place_attn(g_qkv, g_proj, 1, twos[k][3 * block :], unit)
 
 
 def swap(value, axis, bit):
@@ -813,7 +906,21 @@
     tiles = kernel_call(
         tiles_body, [("v", latent), ("v", pred_grad)], [((2, tile_tok, lanes), BF16)] * n_rows, us=1
     )
-    tiles = [tiles[0]] + [swap(tiles[k], "rows", k) for k in range(1, n_rows)]
+
+    def along_z(parts):
+        return [parts[0]] + [swap(parts[k], "rows", k) for k in range(1, n_rows)]
+
+    def along_wide(unit):
+        unit = rest_sum(unit)
+        return [unit] + [swap(unit, "wide", k) for k in range(1, 4)]
+
+    def both_halves(pack):
+        if lax.axis_size("wide") > 4:
+            rows, sums = rest_gather(pack[: 8 * ROWS]), rest_sum(pack[8 * ROWS :])
+            pack = jnp.concatenate([rows, sums])
+        return pack, swap(pack, "cols", 1)
+
+    tiles = along_z(tiles)
     half = time_in.shape[0] // 2
     freqs = np.exp(-math.log(10000.0) * np.arange(half, dtype=np.float32) / np.float32(half))
     positions = jnp.asarray(position_tables(n_rows * hp, wp, n_cols, width))
@@ -826,7 +933,7 @@
         [((3, 8, width), F32), ((8, width), F32), (final_weight.shape, BF16), (tok, F32)]
         + [(weight.shape, BF16) for weight in weights],
         [pltpu.SemaphoreType.DMA((len(weights) + 1,))],
-        us=5,
+        us=US["cond"],
     )
     probs_shape = (HEADS, 2, tokens, tokens)
     state0, q0, kv0, patches = kernel_call(
@@ -836,7 +943,7 @@
         + [("p", pos), ("p", mods), ("v", patch_weight), ("p", qkv)],
         [(tok, F32), (tok, BF16), (double, BF16), ((2, tokens, lanes), BF16)],
         [pltpu.VMEM((n_rows, 2, tile_tok, lanes), BF16)],
-        us=2,
+        us=US["embed"],
     )
     kv0p = swap(kv0, "cols", 1)
     state1, q1, kv1, probs0, attended0, attn_out0, middle0, gp0, act0, branch0 = kernel_call(
@@ -847,23 +954,21 @@
             (tok, F32), (tok, BF16), (double, BF16), (probs_shape, BF16), (tok, BF16), (tok, BF16),
             (tok, F32), (wide_tok, BF16), (wide_tok, BF16), (tok, BF16),
         ],
-        us=7,
+        us=US["block"],
     )
     kv1p = swap(kv1, "cols", 1)
-    probs1, attended1, attn_out1, mgrad1, keep1, send1, rows_turn, gfinal, predt = kernel_call(
+    sums_a, sums_b = 4 * out_ch, 4 * lat_ch
+    rows_1 = 16 * 2 * block + 48
+    probs1, attended1, attn_out1, mgrad1, keep1, send1, preds = kernel_call(
         turn_body,
         [("s", offsets), ("s", counts), ("p", state1), ("p", q1), ("p", kv1), ("v", kv1p)]
-        + [("p", mods), ("p", patches), ("p", final_v), ("p", proj), ("p", up), ("p", down)],
+        + [("p", a) for a in (mods, cond, patches, final_v, proj, up, down)],
         [
-            (probs_shape, BF16), (tok, BF16), (tok, BF16), (tok, F32), ((16 * 2 * block, width), BF16),
-            ((16 * 2 * block, width), BF16), ((8, width), F32), ((2, lanes, width), F32),
-            ((4, wp, 4 * out_ch * hp), F32),
+            (probs_shape, BF16), (tok, BF16), (tok, BF16), (tok, F32), ((rows_1, width), BF16),
+            ((rows_1, width), BF16), ((2, tokens, 2 * out_ch), F32),
         ],
-        [
-            pltpu.VMEM(wide_tok, BF16), pltpu.VMEM(wide_tok, BF16),
-            pltpu.VMEM((2, tokens, 2 * out_ch), F32),
-        ],
-        us=10,
+        [pltpu.VMEM(wide_tok, BF16), pltpu.VMEM(wide_tok, BF16), pltpu.VMEM((48, width), F32)],
+        us=US["turn"],
     )
     recv1 = swap(send1, "cols", 1)
 
@@ -874,7 +979,7 @@
             [
                 (tok, BF16), (double, BF16), ((width, width), BF16), (double, BF16), ((8, width), F32),
             ],
-            us=5,
+            us=US["back"],
             after=after,
         )
 
@@ -882,11 +987,11 @@
         1, q1, kv1, kv1p, probs1, attended1, attn_out1, mgrad1, after=None
     )
     dkvr1 = swap(dkvs1, "cols", 1)
-    keep1, send1 = kernel_call(
-        partial(one_split_body, 0),
+    keep1, table1, send1 = kernel_call(
+        first_body,
         [("p", keep1), ("v", recv1)],
-        [((8 * 2 * block, width), BF16)] * 2,
-        us=0.5,
+        [((8 * 2 * block, width), BF16), ((48, width), BF16), ((8 * 2 * block + 48, width), BF16)],
+        us=US["A1"],
         after=rows_a1,
     )
     recv1 = swap_by_core(send1, FIRST)
@@ -899,98 +1004,126 @@
             (tok, F32), ((16 * 3 * block, width), BF16), ((16 * 3 * block, width), BF16),
             ((8, width), F32),
         ],
-        us=6,
-        after=keep1,
+        us=US["middle"],
+        after=table1,
     )
     recv2 = swap(send2, "cols", 1)
-    keep1, send1 = kernel_call(
-        partial(one_split_body, 1),
-        [("p", keep1), ("v", recv1)],
-        [((4 * 2 * block, width), BF16)] * 2,
-        us=0.5,
-        after=rows_mid,
+    dq0, dkv0, gproj0, dkvs0, rows_a0 = attend_back(
+        0, q0, kv0, kv0p, probs0, attended0, attn_out0, mgrad0, after=None
+    )
+    dkvr0 = swap(dkvs0, "cols", 1)
+    keep1, pair1, send1 = kernel_call(
+        partial(first_pair_body, sums_a),
+        [("p", keep1), ("p", table1), ("v", recv1)],
+        [((4 * 2 * block, width), BF16), ((64, width), BF16), ((4 * 2 * block + 64, width), BF16)],
+        us=US["A2"],
+        after=rows_a0,
     )
     recv1 = swap_by_core(send1, SECOND)
-    dq0, dkv0, gproj0, dkvs0, rows_a0 = attend_back(
-        0, q0, kv0, kv0p, probs0, attended0, attn_out0, mgrad0, after=keep1
-    )
-    dkvr0 = swap(dkvs0, "cols", 1)
-    keep2, send2, *units1 = kernel_call(
+    whole_2, whole_r = keep2, recv2
+    keep2, send2 = kernel_call(
         second_body,
-        [("p", keep2), ("v", recv2), ("p", keep1), ("v", recv1)],
-        [((8 * 3 * block, width), BF16)] * 2 + [((2 * block, width), BF16)] * 4,
-        us=1,
-        after=rows_a0,
+        [("p", whole_2), ("v", whole_r)],
+        [((8 * 2 * block, width), BF16)] * 2,
+        us=US["A3"],
+        after=pair1,
     )
     recv2 = swap_by_core(send2, FIRST)
-    units1 = [units1[0]] + [swap(units1[k], "rows", k) for k in range(1, n_rows)]
-    keep3, send3, lgradt = kernel_call(
+    betas = kernel_call(
+        beta_body,
+        [("p", whole_2), ("v", whole_r)],
+        [((4 * block, width), BF16)] * 4,
+        us=US["A3b"],
+        after=keep2,
+    )
+    chips = betas[0]
+    betas = along_z(betas)
+    rows_3 = 16 * block + 32
+    keep3, send3, lgrads = kernel_call(
         last_body,
         [("s", offsets), ("p", state0), ("p", mgrad0), ("p", dq0), ("p", dkv0), ("v", dkvr0)]
-        + [("p", gproj0), ("p", mods), ("p", patches), ("v", patch_weight), ("p", cond)]
-        + [("p", a) for a in (rows_turn, rows_a1, rows_mid, rows_a0, gfinal, qkv)],
+        + [("p", gproj0), ("p", mods), ("p", patches), ("v", patch_weight)]
+        + [("p", a) for a in (rows_a1, rows_mid, rows_a0, qkv)],
+        [((rows_3, width), BF16), ((rows_3, width), BF16), ((2, tokens, 2 * lat_ch), F32)],
+        [pltpu.VMEM((8, width), F32), pltpu.VMEM((32, width), F32)],
+        us=US["last"],
+        after=chips,
+    )
+    recv3 = swap(send3, "cols", 1)
+    *ones, tiles = kernel_call(
+        partial(first_chip_body, sums_a),
+        [("p", keep1), ("p", pair1), ("v", recv1), ("p", preds), ("p", lgrads)],
+        [((2 * block + 48, width), BF16)] * 4 + [((4, 16, width), BF16)],
+        [pltpu.VMEM((4, ROWS, width), F32), pltpu.VMEM((sums_a, width), F32)],
+        us=US["A2b"],
+    )
+    ones = along_z(ones)
+    keep2, keepb, part = kernel_call(
+        third_body,
+        [("p", keep2), ("v", recv2), ("p", betas[0])] + [("v", beta) for beta in betas[1:]],
+        [((8 * block, width), BF16), ((2 * block, width), BF16), ((10 * block, width), BF16)],
+        [pltpu.VMEM((4 * block, width), BF16)],
+        us=US["A4"],
+        after=tiles,
+    )
+    keep3, table3, send = kernel_call(
+        third_send_body,
+        [("p", keep3), ("v", recv3), ("p", part)],
+        [((8 * block, width), BF16), ((32, width), BF16), ((18 * block + 32, width), BF16)],
+        us=US["A4b"],
+    )
+    recv = swap_by_core(send, SECOND)
+    whole2, keep3, keepb, pair3, send = kernel_call(
+        partial(fourth_body, sums_b),
+        [("p", keep2), ("p", keep3), ("p", keepb), ("p", table3), ("v", recv)],
         [
-            ((16 * block + 80, width), BF16), ((16 * block + 80, width), BF16),
-            ((4, wp, 4 * lat_ch * hp * 2), F32),
+            ((8 * block, width), BF16), ((4 * block, width), BF16), ((block, width), BF16),
+            ((48, width), BF16), ((5 * block + 48, width), BF16),
         ],
-        [
-            pltpu.VMEM((8, width), F32), pltpu.VMEM((2, tokens, 2 * lat_ch), F32),
-            pltpu.VMEM((80, width), F32),
-        ],
-        us=3,
-        after=keep2,
-    )
-    recv3 = swap(send3, "cols", 1)
-    keep2, keep3, table, unit1, send = kernel_call(
-        third_body,
-        [("p", keep2), ("v", recv2), ("p", keep3), ("v", recv3), ("p", units1[0])]
-        + [("v", u) for u in units1[1:]],
-        [
-            ((4 * 3 * block, width), BF16), ((8 * block, width), BF16), ((80, width), BF16),
-            ((2 * block, width), BF16), ((4 * 3 * block + 8 * block + 80, width), BF16),
-        ],
-        us=1,
-    )
-    recv = swap_by_core(send, SECOND)
-    unit1 = rest_sum(unit1)
-    ones = [unit1] + [swap(unit1, "wide", k) for k in range(1, 4)]
-    *twos, keep3, pair, send = kernel_call(
-        fourth_body,
-        [("p", keep2), ("p", keep3), ("p", table), ("v", recv)],
-        [((3 * block, width), BF16)] * 4
-        + [
-            ((4 * block, width), BF16), ((2 * ROWS + 48, width), BF16),
-            ((4 * block + 2 * ROWS + 48, width), BF16),
-        ],
-        us=1,
+        us=US["A5"],
     )
     recv = swap_by_core(send, FIRST)
-    twos = [twos[0]] + [swap(twos[k], "rows", k) for k in range(1, n_rows)]
-    threes = kernel_call(
-        fifth_body,
-        [("p", keep3), ("p", pair), ("v", recv), ("p", predt), ("p", lgradt)],
-        [((block + 2 * ROWS + 64, width), BF16)] * 4,
-        [pltpu.VMEM((4, ROWS, width), F32)],
-        us=1,
-    )
-    threes = [threes[0]] + [swap(threes[k], "rows", k) for k in range(1, n_rows)]
-    unit, rows, sums, tiles = kernel_call(
-        sixth_body,
-        [("v", t) for t in twos + threes],
-        [
-            ((4 * block, width), BF16), ((4 * 2 * ROWS, width), BF16), ((48, width), F32),
-            ((4, 16, width), BF16),
-        ],
-        us=1,
-    )
-    unit, sums = rest_sum(unit), rest_sum(sums)
-    others = [unit] + [swap(unit, "wide", k) for k in range(1, 4)]
-    rows_other = rest_gather(swap(rows, "cols", 1))
-    rows = rest_gather(rows)
+    pack = (8 * ROWS + 16, width)
+    unit1, pack_a = kernel_call(
+        partial(unit1_body, sums_a // 2),
+        [("p", ones[0])] + [("v", one) for one in ones[1:]],
+        [((2 * block, width), BF16), (pack, BF16)],
+        us=US["U1"],
+        after=pair3,
+    )
+    ones = along_wide(unit1)
+    *twos, unitb = kernel_call(
+        partial(fifth_body, sums_b),
+        [("p", whole2), ("p", keep3), ("p", keepb), ("p", pair3), ("v", recv), ("p", tiles)],
+        [((3 * block + 32 + 16, width), BF16)] * 4 + [((block, width), BF16)],
+        [pltpu.VMEM((4, ROWS, width), F32), pltpu.VMEM((sums_b, width), F32)],
+        us=US["A6"],
+        after=pack_a,
+    )
+    chips = twos[0]
+    twos = along_z(twos)
+    packs = both_halves(pack_a)
+    g_up, g_down = kernel_call(
+        first_spread_body,
+        [("p", ones[0])] + [("v", one) for one in ones[1:]],
+        [((2, block, ff), F32), ((2, ff // 8, width), F32)],
+        us=US["S1"],
+        after=chips,
+    )
+    unit2, pack_b, tiles = kernel_call(
+        partial(unit2_body, sums_b // 2),
+        [("p", twos[0])] + [("v", two) for two in twos[1:]] + [("p", unitb)],
+        [((4 * block, width), BF16), (pack, BF16), ((4, 16, width), BF16)],
+        us=US["U2"],
+        after=g_up,
+    )
+    twos = along_wide(unit2)
+    packs = packs + both_halves(pack_b)
+    samples = 2 * (packs[0].shape[0] - 16) // ROWS
     classes = label_table.shape[0]
     g_time_in, g_time_out, g_table, g_mod, g_final_mod, g_patch, g_final = kernel_call(
         sums_body,
-        [("v", rows), ("v", rows_other), ("v", sums)]
+        [("v", half) for half in packs]
         + [("p", a) for a in (modulation_v, final_mod_v, time_out_v)],
         [
             (shape, F32, 0)
@@ -1000,20 +1133,21 @@
             )
         ],
         [
-            pltpu.VMEM((width // 128, 2 * rows.shape[0], 128), F32),
-            pltpu.VMEM((width, 2 * rows.shape[0] // ROWS), F32),
+            pltpu.VMEM((2, width // 128, samples * ROWS, 128), F32),
+            pltpu.VMEM((width, samples), F32), pltpu.VMEM((sums_a, width), F32),
         ],
-        us=5,
+        us=US["sums"],
     )
     g_qkv, g_proj, g_up, g_down, prediction, latent_grad = kernel_call(
         spread_body,
-        [("v", a) for a in ones + others] + [("v", tiles)],
+        [("v", a) for a in twos] + [("p", tiles), ("p", g_up), ("p", g_down)],
         [
             ((2, block, 3 * width), F32, 0), ((2, block, width), F32, 0), ((2, block, ff), F32, 0),
             ((2, ff // 8, width), F32, 0), ((slots, out_ch, tile_h, tile_w), BF16, 0),
             (latent.shape, F32, 0),
         ],
-        us=2,
+        us=US["spread"],
+        after=g_patch,
     )
     return (
         prediction, latent_grad, g_patch, g_time_in, g_time_out, g_table, g_mod, g_qkv, g_proj,

time: 133 us -> 110 us (0.83)
  waiting for transfers between devices: 50.1 us -> 29.9 us
  starting transfers between devices: 34.9 us -> 30.5 us
    ppermute x26 -> x27, waiting for transfers between devices: 25.6 us -> 13.5 us  [swap(): return lax.ppermute(value, axis, [(i, i ^ bit) for i in range(count)])]
    ppermute x5, waiting for transfers between devices: 24.4 us -> 16.4 us  [swap_by_core(): return lax.ppermute(value, ('wide', 'cols'), pairs)]
    ppermute x26 -> x27, starting transfers between devices: 28 us -> 25.3 us  [swap(): return lax.ppermute(value, axis, [(i, i ^ bit) for i in range(count)])]
    ppermute x5, starting transfers between devices: 6.83 us -> 5.22 us  [swap_by_core(): return lax.ppermute(value, ('wide', 'cols'), pairs)]
    pallas_call x18 -> x23, Pallas kernels: 43.8 us -> 44.6 us  [kernel_call(): pl.pallas_call(kernel, in_specs=specs, out_specs=[pl.BlockSpec(memory_spa...]
    unnamed x22 -> x24, local copies, waits for them, and re-layouts: 2.71 us -> 3.45 us
  transfers between devices with their start and end apart: 31 -> 32, of which waited for: 13 -> 11; matrix products, arithmetic and copies ran while one was open for 1% -> 1% of each run, Pallas kernels for 15% -> 23%
where the time goes in v1:
time: 110 us
  Pallas kernels  44.6 us (41%)
  starting transfers between devices  30.5 us (28%)
  waiting for transfers between devices  29.9 us (27%)
  local copies, waits for them, and re-layouts  3.45 us (3%)
  between operations  1.61 us (1%)
    pallas_call x23, Pallas kernels, kernel_call(): pl.pallas_call(kernel, in_specs=specs, out_specs=[pl.BlockSpec(memory_spa...  44.6 us
    ppermute x27, starting transfers between devices, swap(): return lax.ppermute(value, axis, [(i, i ^ bit) for i in range(count)])  25.3 us
    ppermute x5, waiting for transfers between devices, swap_by_core(): return lax.ppermute(value, ('wide', 'cols'), pairs)  16.4 us
    ppermute x27, waiting for transfers between devices, swap(): return lax.ppermute(value, axis, [(i, i ^ bit) for i in range(count)])  13.5 us
    ppermute x5, starting transfers between devices, swap_by_core(): return lax.ppermute(value, ('wide', 'cols'), pairs)  5.22 us
    unnamed x24, local copies, waits for them, and re-layouts  3.45 us
  transfers between devices with their start and end apart: 32, of which 11 were waited for; matrix products, arithmetic and copies ran while one was open for 1% of the time, Pallas kernels for 23%

profile of v1, /device:TPU:0, one launch (start us, length us, event | category | flops | bytes accessed | tf_op | source)
XLA Modules:
  0.0 110.1 jit_solution(6985583184024368130)
XLA Ops:
  3.5 3.1 %collective-permute-start = (bf16[2,64,24]{2,1,0:T(8,128)(2,1)S(1)}, bf16[2,64,24]{2,1,0:T(8,128)(2,1)S(1)}, u32[]{:S(2)}, u32[]{:S(2)}) collective-permute-start(bf16[2,64,24]{2,1,0:T(8,128)(2,1)S(1)} %get-tuple-element.120), channel_id=1, source_target_pairs={{0,2},{2,0},{4,6},{6,4},{1,3},{3,1},{5,7},{7,5},{8,10},{10,8},{12,... | collective-permute-start | bytes 18440 | tf_op jit(solution)/shard_map/ppermute | solution.py:842
  6.6 2.6 %collective-permute-start.1 = (bf16[2,64,24]{2,1,0:T(8,128)(2,1)S(1)}, bf16[2,64,24]{2,1,0:T(8,128)(2,1)S(1)}, u32[]{:S(2)}, u32[]{:S(2)}) collective-permute-start(bf16[2,64,24]{2,1,0:T(8,128)(2,1)S(1)} %get-tuple-element.121), channel_id=1, source_target_pairs={{0,4},{2,6},{4,0},{6,2},{1,5},{3,7},{5,1},{7,3},{8,12},{10,14},{12... | collective-permute-start | bytes 18440 | tf_op jit(solution)/shard_map/ppermute | solution.py:842
  9.4 5.1 %shard_map.283 = (f32[3,8,384]{2,1,0:T(8,128)S(1)}, f32[8,384]{1,0:T(8,128)S(1)}, bf16[384,32]{1,0:T(8,128)(2,1)S(1)}, f32[256,384]{1,0:T(8,128)S(1)}, bf16[384,...) custom-call(s32[4]{0:T(128)S(1)} %copy-done.5, ...), custom_call_target="tpu_custom_call" | custom-call | flops 7500000256 | bytes 5000000 | tf_op jit(solution)/shard_map/pallas_call | solution.py:86
  16.5 1.7 %collective-permute-done.3.refs_3_.refs_2_ = bf16[256,768]{1,0:T(8,128)(2,1)S(1)} collective-permute-done((bf16[256,768]{1,0:T(8,128)(2,1)S(1)}, bf16[256,768]{1,0:T(8,128)(2,1)S(1)}, u32[]{:S(2)}, u32[]{:S(2)}) %collective-permute-start.3) | collective-permute-done | bytes 393248 | tf_op jit(solution)/shard_map/ppermute | solution.py:842
  18.2 5.5 %shard_map.285 = (f32[256,384]{1,0:T(8,128)S(1)}, bf16[256,384]{1,0:T(8,128)(2,1)S(1)}, bf16[256,768]{1,0:T(8,128)(2,1)S(1)}, bf16[6,2,256,256]{3,2,1,0:T(8,128)...) custom-call(f32[256,384]{1,0:T(8,128)S(1)} %get-tuple-element.126.re, ...), custom_call_target="tpu_custom_call" | custom-call | flops 8999999488 | bytes 6000000 | tf_op jit(solution)/shard_map/pallas_call | solution.py:86
  25.4 8.4 %shard_map.286 = (bf16[6,2,256,256]{3,2,1,0:T(8,128)(2,1)S(1)}, bf16[256,384]{1,0:T(8,128)(2,1)S(1)}, bf16[256,384]{1,0:T(8,128)(2,1)S(1)}, f32[256,384]{1,0:T(8...) custom-call(s32[4]{0:T(128)S(1)} %copy-done.7, ...), custom_call_target="tpu_custom_call" | custom-call | flops 13500000256 | bytes 9000000 | tf_op jit(solution)/shard_map/pallas_call | solution.py:86
  34.1 3.4 %shard_map.287 = (bf16[256,384]{1,0:T(8,128)(2,1)S(1)}, bf16[256,768]{1,0:T(8,128)(2,1)S(1)}, bf16[384,384]{1,0:T(8,128)(2,1)S(1)}, bf16[256,768]{1,0:T(8,128)(2,1)S(1)}, f32[8,384]{1,0:T(8,128)S(1)}) custom-call(bf16[256,384]{1,0:T(8,128)(2,1)S(1)} %get-tuple-element.133.refs_3_.refs_0_, bf16[256,768]{1,0:T(8,128)(2,1)S(1)} %get-tuple-element.134.refs_4_.refs_1_, ...), custom_call_target="tpu_custom_call" | custom-call | flops 30000001024 | bytes 20000000 | tf_op jit(solution)/shard_map/pallas_call | solution.py:86
  38.1 1.5 %collective-permute-start.8 = (bf16[816,384]{1,0:T(8,128)(2,1)S(1)}, bf16[816,384]{1,0:T(8,128)(2,1)S(1)}, u32[]{:S(2)}, u32[]{:S(2)}) collective-permute-start(bf16[816,384]{1,0:T(8,128)(2,1)S(1)} %get-tuple-element.157), channel_id=1, source_target_pairs={{0,8},{1,17},{8,0},{9,25},{16,24},{17,1},{24,16},{25,9},{2,10},{3,... | collective-permute-start | bytes 1880072 | tf_op jit(solution)/shard_map/ppermute | solution.py:850
  39.6 3.5 %shard_map.289 = (f32[256,384]{1,0:T(8,128)S(1)}, bf16[2304,384]{1,0:T(8,128)(2,1)S(1)}, bf16[2304,384]{1,0:T(8,128)(2,1)S(1)}, f32[8,384]{1,0:T(8,128)S(1)}) custom-call(f32[256,384]{1,0:T(8,128)S(1)} %get-tuple-element.132.refs_2_.refs_0_, f32[256,384]{1,0:T(8,128)S(1)} %get-tuple-element.138.refs_6_.refs_1_, ...), custom_call_target="tpu_custom_call" | custom-call | flops 6000000000 | bytes 4000000 | tf_op jit(solution)/shard_map/pallas_call | solution.py:86
  43.2 3.4 %shard_map.290 = (bf16[256,384]{1,0:T(8,128)(2,1)S(1)}, bf16[256,768]{1,0:T(8,128)(2,1)S(1)}, bf16[384,384]{1,0:T(8,128)(2,1)S(1)}, bf16[256,768]{1,0:T(8,128)(2,1)S(1)}, f32[8,384]{1,0:T(8,128)S(1)}) custom-call(bf16[256,384]{1,0:T(8,128)(2,1)S(1)} %get-tuple-element.127.refs_1_.refs_0_, bf16[256,768]{1,0:T(8,128)(2,1)S(1)} %get-tuple-element.128.refs_2_.refs_1_, ...), custom_call_target="tpu_custom_call" | custom-call | flops 30000001024 | bytes 20000000 | tf_op jit(solution)/shard_map/pallas_call | solution.py:86
  48.8 1.5 %collective-permute-start.9 = (bf16[768,384]{1,0:T(8,128)(2,1)S(1)}, bf16[768,384]{1,0:T(8,128)(2,1)S(1)}, u32[]{:S(2)}, u32[]{:S(2)}) collective-permute-start(bf16[768,384]{1,0:T(8,128)(2,1)S(1)} %get-tuple-element.165), channel_id=1, source_target_pairs={{0,8},{1,17},{8,0},{9,25},{16,24},{17,1},{24,16},{25,9},{2,10},{3,... | collective-permute-start | bytes 1769480 | tf_op jit(solution)/shard_map/ppermute | solution.py:850
  50.3 1.5 %collective-permute-start.13 = (bf16[448,384]{1,0:T(8,128)(2,1)S(1)}, bf16[448,384]{1,0:T(8,128)(2,1)S(1)}, u32[]{:S(2)}, u32[]{:S(2)}) collective-permute-start(bf16[448,384]{1,0:T(8,128)(2,1)S(1)} %get-tuple-element.171), channel_id=1, source_target_pairs={{0,16},{1,9},{8,24},{9,1},{16,0},{17,25},{24,8},{25,17},{2,18},{3,... | collective-permute-start | bytes 1032200 | tf_op jit(solution)/shard_map/ppermute | solution.py:850
  52.5 3.5 %collective-permute-start.11 = (bf16[192,384]{1,0:T(8,128)(2,1)S(1)}, bf16[192,384]{1,0:T(8,128)(2,1)S(1)}, u32[]{:S(2)}, u32[]{:S(2)}) collective-permute-start(bf16[192,384]{1,0:T(8,128)(2,1)S(1)} %get-tuple-element.168), channel_id=1, source_target_pairs={{0,4},{2,6},{4,0},{6,2},{1,5},{3,7},{5,1},{7,3},{8,12},{10,14},{12... | collective-permute-start | bytes 442376 | tf_op jit(solution)/shard_map/ppermute | solution.py:842
  56.4 2.3 %shard_map.294 = (bf16[800,384]{1,0:T(8,128)(2,1)S(1)}, bf16[800,384]{1,0:T(8,128)(2,1)S(1)}, f32[2,256,8]{2,1,0:T(8,128)S(1)}) custom-call(s32[4]{0:T(128)S(1)} %copy-done.7, f32[256,384]{1,0:T(8,128)S(1)} %get-tuple-element.126.refs_0_.refs_1_, f32[256,384]{1,0:T(8,128)S(1)} %get-tuple-element.161.refs_6_.refs_2_, ...), custom_call_target="tpu_custom_call" | custom-call | flops 6000000000 | bytes 4000000 | tf_op jit(solution)/shard_map/pallas_call | solution.py:86
  58.6 2.1 %collective-permute-done.13.refs_2_ = bf16[448,384]{1,0:T(8,128)(2,1)S(1)} collective-permute-done((bf16[448,384]{1,0:T(8,128)(2,1)S(1)}, bf16[448,384]{1,0:T(8,128)(2,1)S(1)}, u32[]{:S(2)}, u32[]{:S(2)}) %collective-permute-start.13) | collective-permute-done | bytes 344096 | tf_op jit(solution)/shard_map/ppermute | solution.py:850
  60.7 1.6 %shard_map.295 = (bf16[144,384]{1,0:T(8,128)(2,1)S(1)}, bf16[144,384]{1,0:T(8,128)(2,1)S(1)}, bf16[144,384]{1,0:T(8,128)(2,1)S(1)}, bf16[144,384]{1,0:T(8,128)(2,1)S(1)}, bf16[4,16,384]{2,1,0:T(8,128)(2,1)S(1)}) custom-call(bf16[384,384]{1,0:T(8,128)(2,1)S(1)} %get-tuple-element.170.refs_0_, bf16[64,384]{1,0:T(8,128)(2,1)S(1)} %get-tuple-element.163.refs_2_.refs_1_, ...), custom_call_target="tpu_custom_call" | custom-call | flops 75000000 | bytes 50000 | tf_op jit(solution)/shard_map/pallas_call | solution.py:86
  62.3 4.1 %collective-permute-done.11.refs_4_ = bf16[192,384]{1,0:T(8,128)(2,1)S(1)} collective-permute-done((bf16[192,384]{1,0:T(8,128)(2,1)S(1)}, bf16[192,384]{1,0:T(8,128)(2,1)S(1)}, u32[]{:S(2)}, u32[]{:S(2)}) %collective-permute-start.11) | collective-permute-done | bytes 147488 | tf_op jit(solution)/shard_map/ppermute | solution.py:842
  67.3 2.1 %collective-permute-start.18 = (bf16[144,384]{1,0:T(8,128)(2,1)S(1)}, bf16[144,384]{1,0:T(8,128)(2,1)S(1)}, u32[]{:S(2)}, u32[]{:S(2)}) collective-permute-start(bf16[144,384]{1,0:T(8,128)(2,1)S(1)} %get-tuple-element.194), channel_id=1, source_target_pairs={{0,2},{2,0},{4,6},{6,4},{1,3},{3,1},{5,7},{7,5},{8,10},{10,8},{12,... | collective-permute-start | bytes 331784 | tf_op jit(solution)/shard_map/ppermute | solution.py:842
  71.9 8.1 %collective-permute-done.16.refs_4_ = bf16[896,384]{1,0:T(8,128)(2,1)S(1)} collective-permute-done((bf16[896,384]{1,0:T(8,128)(2,1)S(1)}, bf16[896,384]{1,0:T(8,128)(2,1)S(1)}, u32[]{:S(2)}, u32[]{:S(2)}) %collective-permute-start.16) | collective-permute-done | bytes 688160 | tf_op jit(solution)/shard_map/ppermute | solution.py:850
  81.2 4.9 %collective-permute-done.17.refs_4_ = bf16[288,384]{1,0:T(8,128)(2,1)S(1)} collective-permute-done((bf16[288,384]{1,0:T(8,128)(2,1)S(1)}, bf16[288,384]{1,0:T(8,128)(2,1)S(1)}, u32[]{:S(2)}, u32[]{:S(2)}) %collective-permute-start.17) | collective-permute-done | bytes 221216 | tf_op jit(solution)/shard_map/ppermute | solution.py:850
  87.6 3.1 %collective-permute-start.23 = (bf16[192,384]{1,0:T(8,128)(2,1)S(1)}, bf16[192,384]{1,0:T(8,128)(2,1)S(1)}, u32[]{:S(2)}, u32[]{:S(2)}) collective-permute-start(bf16[192,384]{1,0:T(8,128)(2,1)S(1)} %get-tuple-element.201), channel_id=1, source_target_pairs={{0,6},{2,4},{4,2},{6,0},{1,7},{3,5},{5,3},{7,1},{8,14},{10,12},{12... | collective-permute-start | bytes 442376 | tf_op jit(solution)/shard_map/ppermute | solution.py:842
  90.7 4.3 %collective-permute-done.25.refs_2_ = bf16[96,384]{1,0:T(8,128)(2,1)S(1)} collective-permute-done((bf16[96,384]{1,0:T(8,128)(2,1)S(1)}, bf16[96,384]{1,0:T(8,128)(2,1)S(1)}, u32[]{:S(2)}, u32[]{:S(2)}) %collective-permute-start.25) | collective-permute-done | bytes 73760 | tf_op jit(solution)/shard_map/ppermute | solution.py:842
  100.3 5.0 %shard_map.303 = (f32[256,384]{1,0:T(8,128)}, f32[384,384]{1,0:T(8,128)}, f32[1001,384]{1,0:T(8,128)}, f32[2,48,2304]{2,1,0:T(8,128)}, f32[384,768]{1,0:T(8,128)...) custom-call(bf16[112,384]{1,0:T(8,128)(2,1)S(1)} %get-tuple-element.197.refs_6_.refs_0_, ...), custom_call_target="tpu_custom_call" | custom-call | flops 7500000256 | bytes 5000000 | tf_op jit(solution)/shard_map/pallas_call | solution.py:86
  107.4 2.7 %shard_map.304 = (f32[2,48,1152]{2,1,0:T(8,128)}, f32[2,48,384]{2,1,0:T(8,128)}, f32[2,48,1536]{2,1,0:T(8,128)}, f32[2,192,384]{2,1,0:T(8,128)}, bf16[4,8,16,16]...) custom-call(bf16[192,384]{1,0:T(8,128)(2,1)S(1)} %get-tuple-element.205.refs_0_, ...), custom_call_target="tpu_custom_call" | custom-call | flops 3000000000 | bytes 2000000 | tf_op jit(solution)/shard_map/pallas_call | solution.py:86
  (87 shorter events, 23.4 us)
Async XLA Ops:
  3.5 11.0 %collective-permute-start = (bf16[2,64,24]{2,1,0:T(8,128)(2,1)S(1)}, bf16[2,64,24]{2,1,0:T(8,128)(2,1)S(1)}, u32[]{:S(2)}, u32[]{:S(2)}) collective-permute-start(bf16[2,64,24]{2,1,0:T(8,128)(2,1)S(1)} %get-tuple-element.120), channel_id=1, source_target_pairs={{0,2},{2,0},{4,6},{6,4},{1,3},{3,1},{5,7},{7,5},{8,10},{10,8},{12,... | collective-permute-start | bytes 18440 | tf_op jit(solution)/shard_map/ppermute | solution.py:842
  6.6 7.9 %collective-permute-start.1 = (bf16[2,64,24]{2,1,0:T(8,128)(2,1)S(1)}, bf16[2,64,24]{2,1,0:T(8,128)(2,1)S(1)}, u32[]{:S(2)}, u32[]{:S(2)}) collective-permute-start(bf16[2,64,24]{2,1,0:T(8,128)(2,1)S(1)} %get-tuple-element.121), channel_id=1, source_target_pairs={{0,4},{2,6},{4,0},{6,2},{1,5},{3,7},{5,1},{7,3},{8,12},{10,14},{12... | collective-permute-start | bytes 18440 | tf_op jit(solution)/shard_map/ppermute | solution.py:842
  9.2 5.7 %collective-permute-start.2 = (bf16[2,64,24]{2,1,0:T(8,128)(2,1)S(1)}, bf16[2,64,24]{2,1,0:T(8,128)(2,1)S(1)}, u32[]{:S(2)}, u32[]{:S(2)}) collective-permute-start(bf16[2,64,24]{2,1,0:T(8,128)(2,1)S(1)} %get-tuple-element.122), channel_id=1, source_target_pairs={{0,6},{2,4},{4,2},{6,0},{1,7},{3,5},{5,3},{7,1},{8,14},{10,12},{12... | collective-permute-start | bytes 18440 | tf_op jit(solution)/shard_map/ppermute | solution.py:842
  38.1 10.3 %collective-permute-start.8 = (bf16[816,384]{1,0:T(8,128)(2,1)S(1)}, bf16[816,384]{1,0:T(8,128)(2,1)S(1)}, u32[]{:S(2)}, u32[]{:S(2)}) collective-permute-start(bf16[816,384]{1,0:T(8,128)(2,1)S(1)} %get-tuple-element.157), channel_id=1, source_target_pairs={{0,8},{1,17},{8,0},{9,25},{16,24},{17,1},{24,16},{25,9},{2,10},{3,... | collective-permute-start | bytes 1880072 | tf_op jit(solution)/shard_map/ppermute | solution.py:850
  43.1 5.4 %collective-permute-start.7 = (bf16[2304,384]{1,0:T(8,128)(2,1)S(1)}, bf16[2304,384]{1,0:T(8,128)(2,1)S(1)}, u32[]{:S(2)}, u32[]{:S(2)}) collective-permute-start(bf16[2304,384]{1,0:T(8,128)(2,1)S(1)} %get-tuple-element.155), channel_id=1, source_target_pairs={{0,1},{1,0},{2,3},{3,2},{4,5},{5,4},{6,7},{7,6},{8,9},{9,8},{10,11... | collective-permute-start | bytes 5308424 | tf_op jit(solution)/shard_map/ppermute | solution.py:842
  46.6 9.4 %collective-permute-start.14 = (bf16[256,768]{1,0:T(8,128)(2,1)S(1)}, bf16[256,768]{1,0:T(8,128)(2,1)S(1)}, u32[]{:S(2)}, u32[]{:S(2)}) collective-permute-start(bf16[256,768]{1,0:T(8,128)(2,1)S(1)} %get-tuple-element.175), channel_id=1, source_target_pairs={{0,1},{1,0},{2,3},{3,2},{4,5},{5,4},{6,7},{7,6},{8,9},{9,8},{10,11... | collective-permute-start | bytes 1179656 | tf_op jit(solution)/shard_map/ppermute | solution.py:842
  48.8 17.6 %collective-permute-start.9 = (bf16[768,384]{1,0:T(8,128)(2,1)S(1)}, bf16[768,384]{1,0:T(8,128)(2,1)S(1)}, u32[]{:S(2)}, u32[]{:S(2)}) collective-permute-start(bf16[768,384]{1,0:T(8,128)(2,1)S(1)} %get-tuple-element.165), channel_id=1, source_target_pairs={{0,8},{1,17},{8,0},{9,25},{16,24},{17,1},{24,16},{25,9},{2,10},{3,... | collective-permute-start | bytes 1769480 | tf_op jit(solution)/shard_map/ppermute | solution.py:850
  50.3 10.4 %collective-permute-start.13 = (bf16[448,384]{1,0:T(8,128)(2,1)S(1)}, bf16[448,384]{1,0:T(8,128)(2,1)S(1)}, u32[]{:S(2)}, u32[]{:S(2)}) collective-permute-start(bf16[448,384]{1,0:T(8,128)(2,1)S(1)} %get-tuple-element.171), channel_id=1, source_target_pairs={{0,16},{1,9},{8,24},{9,1},{16,0},{17,25},{24,8},{25,17},{2,18},{3,... | collective-permute-start | bytes 1032200 | tf_op jit(solution)/shard_map/ppermute | solution.py:850
  51.9 10.4 %collective-permute-start.10 = (bf16[192,384]{1,0:T(8,128)(2,1)S(1)}, bf16[192,384]{1,0:T(8,128)(2,1)S(1)}, u32[]{:S(2)}, u32[]{:S(2)}) collective-permute-start(bf16[192,384]{1,0:T(8,128)(2,1)S(1)} %get-tuple-element.167), channel_id=1, source_target_pairs={{0,2},{2,0},{4,6},{6,4},{1,3},{3,1},{5,7},{7,5},{8,10},{10,8},{12,... | collective-permute-start | bytes 442376 | tf_op jit(solution)/shard_map/ppermute | solution.py:842
  52.5 13.8 %collective-permute-start.11 = (bf16[192,384]{1,0:T(8,128)(2,1)S(1)}, bf16[192,384]{1,0:T(8,128)(2,1)S(1)}, u32[]{:S(2)}, u32[]{:S(2)}) collective-permute-start(bf16[192,384]{1,0:T(8,128)(2,1)S(1)} %get-tuple-element.168), channel_id=1, source_target_pairs={{0,4},{2,6},{4,0},{6,2},{1,5},{3,7},{5,1},{7,3},{8,12},{10,14},{12... | collective-permute-start | bytes 442376 | tf_op jit(solution)/shard_map/ppermute | solution.py:842
  56.0 10.4 %collective-permute-start.12 = (bf16[192,384]{1,0:T(8,128)(2,1)S(1)}, bf16[192,384]{1,0:T(8,128)(2,1)S(1)}, u32[]{:S(2)}, u32[]{:S(2)}) collective-permute-start(bf16[192,384]{1,0:T(8,128)(2,1)S(1)} %get-tuple-element.169), channel_id=1, source_target_pairs={{0,6},{2,4},{4,2},{6,0},{1,7},{3,5},{5,3},{7,1},{8,14},{10,12},{12... | collective-permute-start | bytes 442376 | tf_op jit(solution)/shard_map/ppermute | solution.py:842
  60.7 5.9 %collective-permute-start.15 = (bf16[800,384]{1,0:T(8,128)(2,1)S(1)}, bf16[800,384]{1,0:T(8,128)(2,1)S(1)}, u32[]{:S(2)}, u32[]{:S(2)}) collective-permute-start(bf16[800,384]{1,0:T(8,128)(2,1)S(1)} %get-tuple-element.182), channel_id=1, source_target_pairs={{0,1},{1,0},{2,3},{3,2},{4,5},{5,4},{6,7},{7,6},{8,9},{9,8},{10,11... | collective-permute-start | bytes 1843208 | tf_op jit(solution)/shard_map/ppermute | solution.py:842
  66.7 13.3 %collective-permute-start.16 = (bf16[896,384]{1,0:T(8,128)(2,1)S(1)}, bf16[896,384]{1,0:T(8,128)(2,1)S(1)}, u32[]{:S(2)}, u32[]{:S(2)}) collective-permute-start(bf16[896,384]{1,0:T(8,128)(2,1)S(1)} %get-tuple-element.187), channel_id=1, source_target_pairs={{0,16},{1,9},{8,24},{9,1},{16,0},{17,25},{24,8},{25,17},{2,18},{3,... | collective-permute-start | bytes 2064392 | tf_op jit(solution)/shard_map/ppermute | solution.py:850
  67.3 12.9 %collective-permute-start.18 = (bf16[144,384]{1,0:T(8,128)(2,1)S(1)}, bf16[144,384]{1,0:T(8,128)(2,1)S(1)}, u32[]{:S(2)}, u32[]{:S(2)}) collective-permute-start(bf16[144,384]{1,0:T(8,128)(2,1)S(1)} %get-tuple-element.194), channel_id=1, source_target_pairs={{0,2},{2,0},{4,6},{6,4},{1,3},{3,1},{5,7},{7,5},{8,10},{10,8},{12,... | collective-permute-start | bytes 331784 | tf_op jit(solution)/shard_map/ppermute | solution.py:842
  69.5 10.8 %collective-permute-start.19 = (bf16[144,384]{1,0:T(8,128)(2,1)S(1)}, bf16[144,384]{1,0:T(8,128)(2,1)S(1)}, u32[]{:S(2)}, u32[]{:S(2)}) collective-permute-start(bf16[144,384]{1,0:T(8,128)(2,1)S(1)} %get-tuple-element.195), channel_id=1, source_target_pairs={{0,4},{2,6},{4,0},{6,2},{1,5},{3,7},{5,1},{7,3},{8,12},{10,14},{12... | collective-permute-start | bytes 331784 | tf_op jit(solution)/shard_map/ppermute | solution.py:842
  70.5 9.8 %collective-permute-start.20 = (bf16[144,384]{1,0:T(8,128)(2,1)S(1)}, bf16[144,384]{1,0:T(8,128)(2,1)S(1)}, u32[]{:S(2)}, u32[]{:S(2)}) collective-permute-start(bf16[144,384]{1,0:T(8,128)(2,1)S(1)} %get-tuple-element.196), channel_id=1, source_target_pairs={{0,6},{2,4},{4,2},{6,0},{1,7},{3,5},{5,3},{7,1},{8,14},{10,12},{12... | collective-permute-start | bytes 331784 | tf_op jit(solution)/shard_map/ppermute | solution.py:842
  80.2 6.0 %collective-permute-start.17 = (bf16[288,384]{1,0:T(8,128)(2,1)S(1)}, bf16[288,384]{1,0:T(8,128)(2,1)S(1)}, u32[]{:S(2)}, u32[]{:S(2)}) collective-permute-start(bf16[288,384]{1,0:T(8,128)(2,1)S(1)} %get-tuple-element.192), channel_id=1, source_target_pairs={{0,8},{1,17},{8,0},{9,25},{16,24},{17,1},{24,16},{25,9},{2,10},{3,... | collective-permute-start | bytes 663560 | tf_op jit(solution)/shard_map/ppermute | solution.py:850
  80.3 10.4 %collective-permute-start.26 = (bf16[96,384]{1,0:T(8,128)(2,1)S(1)}, bf16[96,384]{1,0:T(8,128)(2,1)S(1)}, u32[]{:S(2)}, u32[]{:S(2)}) collective-permute-start(bf16[96,384]{1,0:T(8,128)(2,1)S(1)} %get-tuple-element.203.refs_0_), channel_id=1, source_target_pairs={{0,24},{8,16},{16,8},{24,0},{1,25},{9,17},{17,9},{25,1},{2,26},{10... | collective-permute-start | bytes 221192 | tf_op jit(solution)/shard_map/ppermute | solution.py:842
  86.2 8.9 %collective-permute-start.21 = (bf16[192,384]{1,0:T(8,128)(2,1)S(1)}, bf16[192,384]{1,0:T(8,128)(2,1)S(1)}, u32[]{:S(2)}, u32[]{:S(2)}) collective-permute-start(bf16[192,384]{1,0:T(8,128)(2,1)S(1)} %get-tuple-element.199), channel_id=1, source_target_pairs={{0,2},{2,0},{4,6},{6,4},{1,3},{3,1},{5,7},{7,5},{8,10},{10,8},{12,... | collective-permute-start | bytes 442376 | tf_op jit(solution)/shard_map/ppermute | solution.py:842
  86.3 10.3 %collective-permute-start.22 = (bf16[192,384]{1,0:T(8,128)(2,1)S(1)}, bf16[192,384]{1,0:T(8,128)(2,1)S(1)}, u32[]{:S(2)}, u32[]{:S(2)}) collective-permute-start(bf16[192,384]{1,0:T(8,128)(2,1)S(1)} %get-tuple-element.200), channel_id=1, source_target_pairs={{0,4},{2,6},{4,0},{6,2},{1,5},{3,7},{5,1},{7,3},{8,12},{10,14},{12... | collective-permute-start | bytes 442376 | tf_op jit(solution)/shard_map/ppermute | solution.py:842
  87.6 9.0 %collective-permute-start.23 = (bf16[192,384]{1,0:T(8,128)(2,1)S(1)}, bf16[192,384]{1,0:T(8,128)(2,1)S(1)}, u32[]{:S(2)}, u32[]{:S(2)}) collective-permute-start(bf16[192,384]{1,0:T(8,128)(2,1)S(1)} %get-tuple-element.201), channel_id=1, source_target_pairs={{0,6},{2,4},{4,2},{6,0},{1,7},{3,5},{5,3},{7,1},{8,14},{10,12},{12... | collective-permute-start | bytes 442376 | tf_op jit(solution)/shard_map/ppermute | solution.py:842
  96.8 9.3 %collective-permute-start.29 = (bf16[192,384]{1,0:T(8,128)(2,1)S(1)}, bf16[192,384]{1,0:T(8,128)(2,1)S(1)}, u32[]{:S(2)}, u32[]{:S(2)}) collective-permute-start(bf16[192,384]{1,0:T(8,128)(2,1)S(1)} %get-tuple-element.205.refs_0_), channel_id=1, source_target_pairs={{0,24},{8,16},{16,8},{24,0},{1,25},{9,17},{17,9},{25,1},{2,26},{10... | collective-permute-start | bytes 442376 | tf_op jit(solution)/shard_map/ppermute | solution.py:842
  97.6 9.1 %collective-permute-start.28 = (bf16[192,384]{1,0:T(8,128)(2,1)S(1)}, bf16[192,384]{1,0:T(8,128)(2,1)S(1)}, u32[]{:S(2)}, u32[]{:S(2)}) collective-permute-start(bf16[192,384]{1,0:T(8,128)(2,1)S(1)} %get-tuple-element.205.refs_0_), channel_id=1, source_target_pairs={{0,16},{8,24},{16,0},{24,8},{1,17},{9,25},{17,1},{25,9},{2,18},{10... | collective-permute-start | bytes 442376 | tf_op jit(solution)/shard_map/ppermute | solution.py:842
  98.9 7.8 %collective-permute-start.27 = (bf16[192,384]{1,0:T(8,128)(2,1)S(1)}, bf16[192,384]{1,0:T(8,128)(2,1)S(1)}, u32[]{:S(2)}, u32[]{:S(2)}) collective-permute-start(bf16[192,384]{1,0:T(8,128)(2,1)S(1)} %get-tuple-element.205.refs_0_), channel_id=1, source_target_pairs={{0,8},{8,0},{16,24},{24,16},{1,9},{9,1},{17,25},{25,17},{2,10},{10... | collective-permute-start | bytes 442376 | tf_op jit(solution)/shard_map/ppermute | solution.py:842
  (19 other events, 87.5 us)

commit v2 on v1

--- a/solution.py
+++ b/solution.py
@@ -19,9 +19,9 @@
 ROWS = 12
 ROW_SHARED, ROW_ACT, ROW_COND, ROW_HID, ROW_FEAT = 5, 6, 7, 8, 9
 US = {
-    "cond": 5, "embed": 2, "block": 6, "turn": 9, "back": 20, "middle": 4, "last": 4, "sums": 5, "spread": 2,
-    "A1": 0.05, "A2": 0.05, "A2b": 0.05, "A3": 0.05, "A3b": 0.05, "A4": 30, "A4b": 0.05, "A5": 0.05, "A6": 0.05, "S1": 0.05, "U2": 0.05,
-    "U1": 20,
+    "cond": 5, "embed": 2, "block": 6, "turn": 9, "back": 20, "middle": 4, "last": 4, "early": 0.05, "pack": 0.05, "join": 0.05, "U12": 0.05, "F3": 0.05, "sums": 5, "spread": 0.05,
+    "A1": 0.05, "A2": 0.05, "A2b": 0.05, "A3": 0.05, "A3b": 0.05, "A4": 30, "A4b": 0.05, "A5": 0.05, "A6": 0.05, "S1": 0.05, "U2": 3,
+    "U1": 1,
 }
 
 
@@ -68,7 +68,7 @@
     return (x * 8 + y * 4 + zz) if cc == 0 else (y * 8 + x * 4 + zz)
 
 
-def kernel_call(body, ins, outs, scratch=(), us=1.0, after=None):
+def kernel_call(body, ins, outs, scratch=(), us=1.0, after=None, aliases=()):
     spaces = {"v": pltpu.VMEM, "p": pltpu.VMEM, "s": pltpu.SMEM, "h": pltpu.HBM}
     specs, arrays = [], []
     for kind, array in ins:
@@ -86,8 +86,14 @@
     return pl.pallas_call(
         kernel,
         in_specs=specs,
-        out_specs=[pl.BlockSpec(memory_space=pltpu.VMEM)] * len(outs),
-        out_shape=[sds(o[0], o[1]) if len(o) > 2 else pltpu.VMEM(o[0], o[1]) for o in outs],
+        out_specs=[
+            pl.BlockSpec(memory_space=pltpu.HBM if "hbm" in o[2:] else pltpu.VMEM) for o in outs
+        ],
+        out_shape=[
+            pltpu.VMEM(o[0], o[1]) if len(o) < 3 else sds(o[0], o[1]) if o[2] == "any" else pltpu.HBM(o[0], o[1])
+            for o in outs
+        ],
+        input_output_aliases=dict(aliases),
         scratch_shapes=list(scratch),
         compiler_params=pltpu.CompilerParams(vmem_limit_bytes=24 * 1024 * 1024),
         cost_estimate=pl.CostEstimate(
@@ -121,7 +127,14 @@
     return pl.ds(pl.multiple_of(index * count, 16), count)
 
 
-def tiles_body(latent, pred_grad, *tiles):
+def tiles_body(latent_h, pred_h, *rest):
+    tiles, (latent, pred_grad, sem) = rest[:-3], rest[-3:]
+    copies = [
+        pltpu.make_async_copy(latent_h, latent, sem.at[0]),
+        pltpu.make_async_copy(pred_h, pred_grad, sem.at[1]),
+    ]
+    for copy in copies:
+        copy.start()
     z, _, _ = places()
     _, lat_ch, height, wide = latent.shape
     out_ch = pred_grad.shape[1]
@@ -143,6 +156,8 @@
         one_hot((chans * height, lanes), lambda v, lane: lane == lane_of(v // height, u))
         for u in range(2)
     ]
+    for copy in copies:
+        copy.wait()
     for k, tile in enumerate(tiles):
         image = jnp.concatenate(
             [
@@ -198,7 +213,9 @@
     sources, (mods, cond, final_copy, pos), held = rest[:7], rest[7:11], rest[11:18]
     sem = rest[18]
     final_copy[...] = final_weight[...]
-    sources, held = sources + (positions.at[lax.axis_index("cols")],), held + (pos,)
+    sources = sources[:3] + tuple(source.at[0] for source in sources[3:])
+    sources += (positions.at[lax.axis_index("cols")],)
+    held = held + (pos,)
     copies = [
         pltpu.make_async_copy(source, target, sem.at[i])
         for i, (source, target) in enumerate(zip(sources, held))
@@ -245,7 +262,7 @@
     width = state.shape[-1]
     normed, _ = layer_norm(state)
     inner = (normed * (1.0 + mods[layer, 1:2]) + mods[layer, 0:1]).astype(BF16)
-    projected = dot(inner, weight[layer]).astype(BF16)
+    projected = dot(inner, weight[...]).astype(BF16)
     return projected[:, :width], projected[:, width:]
 
 
@@ -276,14 +293,16 @@
         attended[:, at] = total.astype(BF16)
 
 
+CHUNK = 768
+
+
 def mlp_forward(middle, mods, layer, up, down, gp, act):
     normed, _ = layer_norm(middle)
     inner = (normed * (1.0 + mods[layer, 4:5]) + mods[layer, 3:4]).astype(BF16)
-    width = middle.shape[-1]
     branch = None
-    for i in range(up.shape[-1] // width):
-        at = slice(i * width, (i + 1) * width)
-        hidden = dot(inner, up[layer, :, at])
+    for start in range(0, up.shape[1], CHUNK):
+        at = slice(start, start + CHUNK)
+        hidden = dot(inner, up[:, at])
         square = hidden * hidden
         root = math.sqrt(2.0 / math.pi)
         bent = jnp.tanh(root * hidden * (1.0 + 0.044715 * square))
@@ -292,7 +311,7 @@
         act[:, at] = activated
         slope = half + 0.5 * hidden * (1.0 - bent * bent) * (root * (1.0 + 3 * 0.044715 * square))
         gp[:, at] = slope.astype(BF16)
-        part = dot(activated, down[layer, at, :])
+        part = dot(activated, down[at, :])
         branch = part if branch is None else branch + part
     return branch
 
@@ -306,29 +325,35 @@
     send[pl.ds(pl.multiple_of(other, 16), block), :] = jnp.where(first, pair[1], pair[0])
 
 
-def mlp_backward(grad, middle, branch, mods, layer, gp, act, up, down, keep, send, size, rows, first):
+def mlp_backward(
+    grad, middle, branch, mods, layer, gp, act, up, down, keep, send, size, flip, rows, first, low
+):
     width = middle.shape[-1]
     normed, inverse = layer_norm(middle)
     scale = 1.0 + mods[layer, 4:5]
     inner_t = (normed * scale + mods[layer, 3:4]).astype(BF16).T
     branch_grad = (mods[layer, 5:6] * grad).astype(BF16)
     inner_grad = None
-    pieces = up.shape[-1] // width
+    for start in range(0, up.shape[1], CHUNK):
+        at = slice(start, start + CHUNK)
+        act_grad = dot_nt(branch_grad, down[at, :])
+        hidden_grad = (act_grad * gp[:, at].astype(F32)).astype(BF16)
+        low[:, at] = hidden_grad
+        part = dot_nt(hidden_grad, up[:, at])
+        inner_grad = part if inner_grad is None else inner_grad + part
     block = width // 8
-    for i in range(pieces):
+    for i in range(up.shape[1] // width):
         at = slice(i * width, (i + 1) * width)
-        act_grad = dot_nt(branch_grad, down[layer, at, :])
-        hidden_grad = (act_grad * gp[:, at].astype(F32)).astype(BF16)
-        part = dot_nt(hidden_grad, up[layer, :, at])
-        inner_grad = part if inner_grad is None else inner_grad + part
-        grad_up = dot(inner_t, hidden_grad).astype(BF16)
+        grad_up = dot(inner_t, low[:, at]).astype(BF16)
         for b in range(4):
             pair = [grad_up[(2 * b + cc) * block : (2 * b + cc + 1) * block] for cc in range(2)]
-            put_units(keep, send, pair, [unit_place(b, i, cc) for cc in range(2)], size, 0)
+            place = [unit_place(b, i, cc ^ flip) for cc in range(2)]
+            put_units(keep, send, pair, place, size, 0)
         grad_down = dot_tn(act[:, at], branch_grad).astype(BF16)
         for j in range(4):
             pair = [grad_down[(4 * cc + j) * block : (4 * cc + j + 1) * block] for cc in range(2)]
-            put_units(keep, send, pair, [unit_place(i, j, cc) for cc in range(2)], size, block)
+            place = [unit_place(i, j, cc ^ flip) for cc in range(2)]
+            put_units(keep, send, pair, place, size, block)
     rows[first : first + 1, :] = token_sum(inner_grad)
     rows[first + 1 : first + 2, :] = token_sum(inner_grad * normed)
     rows[first + 2 : first + 3, :] = token_sum(grad * branch.astype(F32))
@@ -336,7 +361,7 @@
 
 
 def qkv_backward(
-    state, middle_grad, dq, dkv, dkvr, mods, layer, weight, gproj, keep, send, at_row, place_of, rows
+    state, middle_grad, dq, dkv, dkvr, mods, layer, weight, gproj, keep, send, shares, rows
 ):
     width = state.shape[-1]
     block = width // 8
@@ -350,11 +375,12 @@
     def put(values, i):
         for b in range(4):
             pair = [values[(2 * b + cc) * block : (2 * b + cc + 1) * block] for cc in range(2)]
-            place = [place_of(b, i, cc) for cc in range(2)]
-            put_units(keep, send, pair, place, block, at_row)
+            for start, end, place_of, size, at_row in shares:
+                place = [place_of(b, i, cc) for cc in range(2)]
+                put_units(keep, send, [part[start:end] for part in pair], place, size, at_row)
 
     for i, piece in enumerate(pieces):
-        part = dot_nt(piece, weight[layer, :, i * width : (i + 1) * width])
+        part = dot_nt(piece, weight[:, i * width : (i + 1) * width])
         inner_grad = part if inner_grad is None else inner_grad + part
         put(dot(inner_t, piece).astype(BF16), i)
     put(gproj[...], 3)
@@ -391,12 +417,20 @@
 
 
 def block_body(
-    state, q, kv, kvp, mods, proj, up, down, qkv,
-    state1, q1, kv1, probs, attended, attn_out, middle, gp, act, branch,
+    state, q, kv, kvp, mods, proj, up, down, *rest,
 ):
+    sources, rest = rest[:4], rest[4:]
+    state1, q1, kv1, probs, attended, attn_out, middle, gp, act, branch = rest[:10]
+    targets, sem = rest[10:14], rest[14]
+    copies = [
+        pltpu.make_async_copy(source.at[1], target, sem.at[i])
+        for i, (source, target) in enumerate(zip(sources, targets))
+    ]
+    for copy in copies:
+        copy.start()
     attend_forward(q, kv, kvp, probs, attended)
     m = mods
-    attn = dot(attended[...], proj[0])
+    attn = dot(attended[...], proj[...])
     attn_out[...] = attn.astype(BF16)
     mid = state[...] + m[0, 2:3] * attn
     middle[...] = mid
@@ -404,20 +438,23 @@
     branch[...] = out.astype(BF16)
     new = mid + m[0, 5:6] * out
     state1[...] = new
-    q1[...], kv1[...] = qkv_forward(new, m, 1, qkv)
+    copies[0].wait()
+    q1[...], kv1[...] = qkv_forward(new, m, 1, targets[0])
+    for copy in copies[1:]:
+        copy.wait()
 
 
 def turn_body(
     offsets, counts, state, q, kv, kvp, mods, cond, patches, final_weight, proj, up, down,
     probs, attended, attn_out, middle_grad, keep, send, preds,
-    gp, act, table,
+    gp, act, table, low,
 ):
     z, _, _ = places()
     offset = offsets[z]
     live = (z < counts[0]).astype(F32)
     attend_forward(q, kv, kvp, probs, attended)
     m = mods
-    attn = dot(attended[...], proj[1])
+    attn = dot(attended[...], proj[...])
     attn_out[...] = attn.astype(BF16)
     middle = state[...] + m[1, 2:3] * attn
     branch = mlp_forward(middle, m, 1, up, down, gp, act)
@@ -446,7 +483,7 @@
     grad = norm_back(inner_grad * scale, normed, inverse)
     size = 2 * (weight.shape[0] // 8)
     middle_grad[...] = mlp_backward(
-        grad, middle, branch, m, 1, gp, act, up, down, keep, send, size, table, 2
+        grad, middle, branch, m, 1, gp, act, up, down, keep, send, size, 0, table, 2, low
     )
     base = 4 * weight.shape[0]
     keep[base:] = table[...].astype(BF16)
@@ -459,7 +496,7 @@
 ):
     grad = middle_grad[...]
     attn_grad = (mods[layer, 2:3] * grad).astype(BF16)
-    attended_grad = dot_nt(attn_grad, proj[layer]).astype(BF16)
+    attended_grad = dot_nt(attn_grad, proj[...]).astype(BF16)
     masks = head_masks(BF16)
     width = q.shape[-1]
     for p in range(PAIRS):
@@ -469,10 +506,11 @@
         dop = attended_grad[:, at]
         ks, vs = (kv[:, at], kvp[:, at]), (kv[:, av], kvp[:, av])
         total = None
-        parts = [None] * 4
+        parts = [[], [], [], []]
+        q_t, do_t = qp.T, dop.T
         for h in range(2):
             doh = dop * masks[h]
-            qh = qp * masks[h]
+            own = slice(h * HEAD_DIM, (h + 1) * HEAD_DIM)
             ps = [probs[2 * p + h, i] for i in range(2)]
             dps = [dot_nt(doh, vs[i]) for i in range(2)]
             pfs = [ps[i].astype(F32) for i in range(2)]
@@ -481,14 +519,14 @@
                 ds = (pfs[i] * (dps[i] - inner)).astype(BF16)
                 part = dot(ds, ks[i] * masks[h])
                 total = part if total is None else total + part
-                dk, dv = dot_tn(ds, qh), dot_tn(ps[i], doh)
-                parts[2 * i] = dk if h == 0 else parts[2 * i] + dk
-                parts[2 * i + 1] = dv if h == 0 else parts[2 * i + 1] + dv
+                parts[2 * i].append(dot(q_t[own], ds))
+                parts[2 * i + 1].append(dot(do_t[own], ps[i]))
         dq[:, at] = (total * HEAD_DIM**-0.5).astype(BF16)
-        dkv[:, at] = parts[0].astype(BF16)
-        dkv[:, av] = parts[1].astype(BF16)
-        dkvs[:, at] = parts[2].astype(BF16)
-        dkvs[:, av] = parts[3].astype(BF16)
+        turned = [jnp.concatenate(part, axis=0).astype(BF16).T for part in parts]
+        dkv[:, at] = turned[0]
+        dkv[:, av] = turned[1]
+        dkvs[:, at] = turned[2]
+        dkvs[:, av] = turned[3]
     rows[...] = jnp.zeros_like(rows)
     rows[0:1, :] = token_sum(grad * attn_out[...].astype(F32))
     gproj[...] = dot_tn(attended[...], attn_grad).astype(BF16)
@@ -496,19 +534,20 @@
 
 def middle_body(
     state1, middle_grad1, dq, dkv, dkvr, gproj, middle, branch, gp, act, mods, qkv, up, down,
-    middle_grad, keep, send, rows,
+    middle_grad, keep, send, rows, low,
 ):
     width = dq.shape[-1]
-    size = 2 * (width // 8)
+    block = width // 8
+    size = 2 * block + 16
     rows[...] = jnp.zeros_like(rows)
     m = mods
     grad = qkv_backward(
         state1[...], middle_grad1[...], dq, dkv, dkvr, m, 1, qkv, gproj, keep, send,
-        16 * size, chip_place, rows,
+        ((0, 16, unit_place, size, 2 * block), (16, block, chip_place, block - 16, 16 * size)), rows,
     )
     middle_grad[...] = mlp_backward(
-        grad, middle[...], branch[...], m, 0, gp, act, up, down, keep, send, size,
-        rows, 2,
+        grad, middle[...], branch[...], m, 0, gp, act, up, down, keep, send, size, 0,
+        rows, 2, low,
     )
 
 
@@ -523,7 +562,7 @@
     block = width // 8
     grad = qkv_backward(
         state0[...], middle_grad[...], dq, dkv, dkvr, mods, 0, qkv, gproj, keep, send,
-        0, lambda zz, ww, cc: unit_place(zz, ww, 1 - cc), rows,
+        ((0, block, lambda zz, ww, cc: unit_place(zz, ww, 1 - cc), block, 0),), rows,
     )
     embed_grad = grad.astype(BF16)
     chosen = patches
@@ -610,7 +649,7 @@
 
 
 def first_chip_body(
-    sums, keep, pair, recv, preds, lgrads, z0, z1, z2, z3, tiles, four, total
+    sums, keep, pair, recv, z0, z1, z2, z3, four, total
 ):
     z, _, _ = places()
     size = keep.shape[0]
@@ -619,6 +658,16 @@
     for k, out in enumerate((z0, z1, z2, z3)):
         out[0:unit] = keep[rows_at(z ^ k, unit)] + recv[rows_at(z ^ k, unit)]
         out[unit:] = rows
+
+
+def unit1_body(sums, o0, o1, o2, o3, unit, pack):
+    ones = (o0, o1, o2, o3)
+    unit[...] = chip_sum(ones, slice(0, unit.shape[0])).astype(BF16)
+    chip_rows(sums, ones, unit.shape[0], pack)
+
+
+def pack_body(preds, lgrads, tiles):
+    z, _, _ = places()
     tok = preds.shape[1] // 4
     tiles[:, :, 256:] = jnp.zeros((4, 16, 128), BF16)
     for k in range(4):
@@ -664,10 +713,15 @@
     send[size + half3 :] = rows
 
 
-def fourth_body(sums, keep2, keep3, keepb, table, recv, whole2, keep3_out, keepb_out, pair_out, send):
+def fourth_body(
+    sums, keep2, keep3, keepb, table, recv, z0, z1, z2, z3, keep3_out, keepb_out, pair_out, send
+):
+    z, _, _ = places()
     size2, size3, sizeb = keep2.shape[0], keep3.shape[0], keepb.shape[0]
     half3, halfb = size3 // 2, sizeb // 2
-    whole2[...] = keep2[...] + recv[0:size2]
+    unit = size2 // 4
+    for k, out in enumerate((z0, z1, z2, z3)):
+        out[...] = keep2[rows_at(z ^ k, unit)] + recv[rows_at(z ^ k, unit)]
     bit = wide_bits()[0]
 
     def half(held, index, size, base):
@@ -683,18 +737,16 @@
     send[half3 + halfb :] = pair
 
 
-def fifth_body(sums, whole2, keep3, keepb, pair, recv, tiles, z0, z1, z2, z3, unitb, four, total):
+def fifth_body(sums, keep3, keepb, pair, recv, tiles, z0, z1, z2, z3, unitb, four, total):
     z, _, _ = places()
-    unit2, size3, sizeb = whole2.shape[0] // 4, keep3.shape[0], keepb.shape[0]
+    size3, sizeb = keep3.shape[0], keepb.shape[0]
     unit3 = size3 // 4
     other = recv[size3 + sizeb :].astype(F32)
     rows = half_of_four(pair[...].astype(F32), other, sums, 1, four, total)
-    start = unit2 + unit3
-    end = start + rows.shape[0]
+    end = unit3 + rows.shape[0]
     for k, out in enumerate((z0, z1, z2, z3)):
-        out[0:unit2] = whole2[rows_at(z ^ k, unit2)]
-        out[unit2:start] = keep3[rows_at(z ^ k, unit3)] + recv[rows_at(z ^ k, unit3)]
-        out[start:end] = rows
+        out[0:unit3] = keep3[rows_at(z ^ k, unit3)] + recv[rows_at(z ^ k, unit3)]
+        out[unit3:end] = rows
         out[end:] = tiles[k]
     unitb[...] = keepb[...] + recv[size3 : size3 + sizeb]
 
@@ -705,21 +757,33 @@
     pack[...] = padded(*[r[: 2 * ROWS] for r in rows], total)
 
 
-def unit1_body(sums, z0, z1, z2, z3, unit, pack):
+def unit12_body(unit1, t0, t1, t2, t3, unitb, unit):
+    size, end2 = unit1.shape[0], t0.shape[0]
+    unit[0:size] = unit1[...]
+    unit[size : size + end2] = chip_sum((t0, t1, t2, t3), slice(None)).astype(BF16)
+    unit[size + end2 :] = unitb[...]
+
+
+def join_body(own2, near2, own3, send):
+    size = own2.shape[0]
+    send[0:size] = own2[...]
+    send[size : 2 * size] = near2[...]
+    send[2 * size :] = own3[...]
+
+
+def unit3_body(sums, z0, z1, z2, z3, unit, pack, tiles):
     parts = (z0, z1, z2, z3)
     size = unit.shape[0]
     unit[...] = chip_sum(parts, slice(0, size)).astype(BF16)
     chip_rows(sums, parts, size, pack)
-
-
-def unit2_body(sums, z0, z1, z2, z3, unitb, unit, pack, tiles):
-    parts = (z0, z1, z2, z3)
-    size = unit.shape[0] - unitb.shape[0]
-    unit[0:size] = chip_sum(parts, slice(0, size)).astype(BF16)
-    unit[size:] = unitb[...]
-    chip_rows(sums, parts, size, pack)
     for k, part in enumerate(parts):
         tiles[k] = part[size + 32 :]
+
+
+def far_body(unit, recv, send):
+    size = unit.shape[0]
+    send[0:size] = unit[...]
+    send[size:] = recv[recv.shape[0] - size :]
 
 
 def silu_slope(values):
@@ -727,100 +791,94 @@
     return sigmoid * (1.0 + values * (1.0 - sigmoid))
 
 
+def sample_table(table, pack, other):
+    parts, half = table.shape[0], table.shape[1] // 2
+    for side, held in enumerate((pack, other)):
+        for i in range(parts):
+            at = slice(128 * i, 128 * (i + 1))
+            table[i, half * side : half * (side + 1)] = held[0:half, at].astype(F32)
+    samples = table.shape[1] // ROWS
+
+    def rows(r):
+        return jnp.concatenate(
+            [table[i, pl.ds(r, samples, stride=ROWS), :] for i in range(parts)], axis=-1
+        )
+
+    return rows
+
+
+def join_sums(out, pack, other):
+    c = lax.axis_index("cols")
+    count = out.shape[0] // 2
+    for side, held in enumerate((pack, other)):
+        at = pl.ds(pl.multiple_of((c ^ side) * count, 8), count)
+        out[at, :] = held[held.shape[0] - 16 :].astype(F32)[:count]
+
+
+def early_sums_body(
+    pack, other, final_mod,
+    g_final_mod, g_final, shared_t, slopes, base, high, act_t, feat_t, hot, table,
+):
+    rows = sample_table(table, pack, other)
+    join_sums(g_final, pack, other)
+    fmods = jnp.concatenate([rows(0), rows(1)], axis=-1).astype(BF16)
+    shared_t[...] = rows(ROW_SHARED).T
+    g_final_mod[...] = dot(shared_t[...].astype(BF16), fmods)
+    base[...] = dot_nt(fmods, final_mod[...])
+    slopes[0] = silu_slope(rows(ROW_COND))
+    slopes[1] = silu_slope(rows(ROW_HID))
+    for k in range(3):
+        high[k] = rows(2 + k)
+    act_t[...] = rows(ROW_ACT).T.astype(BF16)
+    feats = rows(ROW_FEAT)
+    count = feat_t.shape[0]
+    feat_t[...] = feats[:, :count].T.astype(BF16)
+    label = (feats[:, count : count + 1] * 32.0 + feats[:, count + 1 : count + 2]).astype(jnp.int32)
+    classes = hot.shape[0]
+    lane = lax.broadcasted_iota(jnp.int32, (feats.shape[0], (classes + 127) // 128 * 128), 1)
+    hot[...] = (lane == label).astype(F32).T[:classes].astype(BF16)
+
+
 def sums_body(
-    pack_a, other_a, pack_b, other_b, modulation, final_mod, time_out,
-    g_time_in, g_time_out, g_table, g_mod, g_final_mod, g_patch, g_final,
-    table, shared_t, total,
+    pack, other, modulation, time_out, shared_t, slopes, base, high, act_t, feat_t, hot, tiles,
+    g_time_in, g_time_out, g_table, g_mod, g_patch, prediction, latent_grad, token,
+    table, mod_v, table_v, time_out_v, time_in_v, sem,
 ):
     z, c, _ = places()
-    parts = table.shape[1]
-    half = table.shape[2] // 2
-    for which, pair in enumerate(((pack_a, other_a), (pack_b, other_b))):
-        for side, pack in enumerate(pair):
-            for i in range(parts):
-                at = slice(128 * i, 128 * (i + 1))
-                table[which, i, half * side : half * (side + 1)] = pack[0:half, at].astype(F32)
-    count = g_patch.shape[0] // 2
-    for side, pack in enumerate((pack_b, other_b)):
-        at = pl.ds(pl.multiple_of((c ^ side) * count, 8), count)
-        g_patch[at, :] = pack[half : half + 16].astype(F32)[:count]
-    count = total.shape[0] // 2
-    for side, pack in enumerate((pack_a, other_a)):
-        at = pl.ds(pl.multiple_of((c ^ side) * count, 8), count)
-        total[at, :] = pack[half : half + count].astype(F32)
-    g_final[...] = total[...].T
-    samples = table.shape[2] // ROWS
-
-    def rows(r, which=0):
-        pieces = [table[which, i, pl.ds(r, samples, stride=ROWS), :] for i in range(parts)]
-        return jnp.concatenate(pieces, axis=-1)
-
-    low = [rows(k, 1) for k in range(6)]
-    high = [rows(k, 1) for k in range(6, 9)] + [rows(k) for k in range(2, 5)]
-    mods = [jnp.concatenate(pieces, axis=-1).astype(BF16) for pieces in (low, high)]
-    fmods = jnp.concatenate([rows(0), rows(1)], axis=-1).astype(BF16)
-    shared_t[...] = rows(ROW_SHARED).T
-    block = g_mod.shape[1]
+    token[...] = jnp.zeros_like(token)
+    rows = sample_table(table, pack, other)
+    mods = [
+        jnp.concatenate([rows(k) for k in range(6)], axis=-1).astype(BF16),
+        jnp.concatenate(
+            [rows(k) for k in range(6, 9)] + [high[k] for k in range(3)], axis=-1
+        ).astype(BF16),
+    ]
+    block = mod_v.shape[1]
     start = pl.multiple_of((z * 2 + c) * block, 8)
     mine = shared_t[pl.ds(start, block), :].astype(BF16)
+    copies = []
+
+    def leave(source, target):
+        copies.append(pltpu.make_async_copy(source, target, sem.at[len(copies)]))
+        copies[-1].start()
+
     for layer in range(2):
-        g_mod[layer] = dot(mine, mods[layer])
-    g_final_mod[...] = dot(shared_t[...].astype(BF16), fmods)
-    shared_grad = dot_nt(fmods, final_mod[...])
+        mod_v[layer] = dot(mine, mods[layer])
+    leave(mod_v, g_mod)
+    shared_grad = base[...]
     for layer in range(2):
         shared_grad += dot_nt(mods[layer], modulation[layer])
-    cond_grad = shared_grad * silu_slope(rows(ROW_COND))
+    cond_grad = shared_grad * slopes[0]
     cond_low = cond_grad.astype(BF16)
-    feats = rows(ROW_FEAT)
-    count = g_time_in.shape[0]
-    label = (feats[:, count : count + 1] * 32.0 + feats[:, count + 1 : count + 2]).astype(jnp.int32)
-    classes = g_table.shape[0]
-    padded = (classes + 127) // 128 * 128
-    lane = lax.broadcasted_iota(jnp.int32, (samples, padded), 1)
-    hot = (lane == label).astype(F32).T[:classes].astype(BF16)
     cond_rest = (cond_grad - cond_low.astype(F32)).astype(BF16)
-    g_table[...] = dot(hot, cond_low) + dot(hot, cond_rest)
-    g_time_out[...] = dot(rows(ROW_ACT).T.astype(BF16), cond_low)
-    time_grad = dot_nt(cond_low, time_out[...]) * silu_slope(rows(ROW_HID))
-    g_time_in[...] = dot(feats[:, :count].T.astype(BF16), time_grad.astype(BF16))
-
-
-def place_mlp(g_up, g_down, layer, piece, unit):
-    block, width = g_up.shape[1], g_down.shape[2]
-    cols = pl.ds(pl.multiple_of(unit * width, 128), width)
-    g_up[layer, :, cols] = piece[0:block].astype(F32)
-    down_rows = pl.ds(pl.multiple_of(unit * block, 8), block)
-    g_down[layer, down_rows, :] = piece[block : 2 * block].astype(F32)
-
-
-def place_attn(g_qkv, g_proj, layer, piece, unit):
-    width = g_proj.shape[2]
-
-    @pl.when(unit < 3)
-    def _():
-        cols = pl.ds(pl.multiple_of(unit * width, 128), width)
-        g_qkv[layer, :, cols] = piece.astype(F32)
-
-    @pl.when(unit == 3)
-    def _():
-        g_proj[layer] = piece.astype(F32)
-
-
-def first_spread_body(*refs):
-    ones, (g_up, g_down) = refs[:4], refs[4:]
-    spot = lax.rem(lax.axis_index("wide"), 4)
-    for k in range(4):
-        place_mlp(g_up, g_down, 1, ones[k][...], spot ^ k)
-
-
-def spread_body(*refs):
-    twos, tiles, up, down = refs[:4], refs[4], refs[5], refs[6]
-    g_qkv, g_proj, g_up, g_down, prediction, latent_grad = refs[7:]
-    z, _, w = places()
-    block = g_proj.shape[1]
-    spot = lax.rem(w, 4)
-    g_up[1] = up[1]
-    g_down[1] = down[1]
+    table_v[...] = dot(hot[...], cond_low) + dot(hot[...], cond_rest)
+    leave(table_v, g_table)
+    time_out_v[...] = dot(act_t[...], cond_low)
+    leave(time_out_v, g_time_out)
+    time_grad = dot_nt(cond_low, time_out[...]) * slopes[1]
+    time_in_v[...] = dot(feat_t[...], time_grad.astype(BF16))
+    leave(time_in_v, g_time_in)
+    join_sums(g_patch, pack, other)
     _, out_ch, height, wide = prediction.shape
     lat_ch = latent_grad.shape[1]
     for k in range(4):
@@ -830,11 +888,57 @@
         image = unpacked_tile(tile[0:8, 0:128].astype(BF16), lat_ch, height, wide)
         image = image + unpacked_tile(tile[0:8, 128:256].astype(BF16), lat_ch, height, wide)
         latent_grad[z ^ k] = image.reshape(lat_ch, height, wide)
-    for k in range(4):
-        unit = spot ^ k
-        place_mlp(g_up, g_down, 0, twos[k][0 : 2 * block], unit)
-        place_attn(g_qkv, g_proj, 0, twos[k][2 * block : 3 * block], unit)
-        place_attn(g_qkv, g_proj, 1, twos[k][3 * block :], unit)
+    for copy in copies:
+        copy.wait()
+
+
+def place_mlp(up, down, piece, unit):
+    block, width = up.shape[0], down.shape[1]
+    cols = pl.ds(pl.multiple_of(unit * width, 128), width)
+    up[:, cols] = piece[0:block].astype(F32)
+    down_rows = pl.ds(pl.multiple_of(unit * block, 8), block)
+    down[down_rows, :] = piece[block : 2 * block].astype(F32)
+
+
+def place_attn(g_qkv, g_proj, layer, piece, unit):
+    width = g_proj.shape[2]
+
+    @pl.when(unit < 3)
+    def _():
+        cols = pl.ds(pl.multiple_of(unit * width, 128), width)
+        g_qkv[layer, :, cols] = piece.astype(F32)
+
+    @pl.when(unit == 3)
+    def _():
+        g_proj[layer] = piece.astype(F32)
+
+
+def spread_body(own2, near2, far, own3, near3, g_qkv, g_proj, g_up, g_down, up, down, sem):
+    _, c, w = places()
+    first = jnp.where(c == 0, 1, 2)
+    spot = lax.rem(w, 4)
+    spots = (spot, spot ^ first, spot ^ first ^ 3, spot ^ 3)
+    size2, size3 = own2.shape[0], own3.shape[0]
+    block = g_proj.shape[1]
+    size = 2 * block
+    twos = ((own2, 0), (near2, 0), (far, 0), (far, size2))
+    threes = ((own3, 0), (near3, 0), (far, 2 * size2), (near3, size3))
+    copies = []
+    for layer, start in ((1, 0), (0, size)):
+        for (ref, base), unit in zip(twos, spots):
+            piece = ref[base + start : base + start + size]
+            place_mlp(up.at[layer], down.at[layer], piece, unit)
+        for source, target in ((up, g_up), (down, g_down)):
+            copies.append(
+                pltpu.make_async_copy(source.at[layer], target.at[layer], sem.at[len(copies)])
+            )
+            copies[-1].start()
+    for (ref, base), unit in zip(twos, spots):
+        place_attn(g_qkv, g_proj, 1, ref[base + 2 * size : base + size2], unit)
+    for (ref, base), unit in zip(threes, spots):
+        place_attn(g_qkv, g_proj, 0, ref[base : base + size3], unit)
+    for copy in copies:
+        copy.wait()
 
 
 def swap(value, axis, bit):
@@ -904,15 +1008,18 @@
     tok, wide_tok, double = (tokens, width), (tokens, ff), (tokens, 2 * width)
 
     tiles = kernel_call(
-        tiles_body, [("v", latent), ("v", pred_grad)], [((2, tile_tok, lanes), BF16)] * n_rows, us=1
+        tiles_body,
+        [("h", latent), ("h", pred_grad)],
+        [((2, tile_tok, lanes), BF16)] * n_rows,
+        [
+            pltpu.VMEM(latent.shape, BF16), pltpu.VMEM(pred_grad.shape, BF16),
+            pltpu.SemaphoreType.DMA((2,)),
+        ],
+        us=1,
     )
 
     def along_z(parts):
         return [parts[0]] + [swap(parts[k], "rows", k) for k in range(1, n_rows)]
-
-    def along_wide(unit):
-        unit = rest_sum(unit)
-        return [unit] + [swap(unit, "wide", k) for k in range(1, 4)]
 
     def both_halves(pack):
         if lax.axis_size("wide") > 4:
@@ -924,14 +1031,19 @@
     half = time_in.shape[0] // 2
     freqs = np.exp(-math.log(10000.0) * np.arange(half, dtype=np.float32) / np.float32(half))
     positions = jnp.asarray(position_tables(n_rows * hp, wp, n_cols, width))
-    weights = (time_out, modulation, final_mod, qkv_weight, proj_weight, up_weight, down_weight)
-    mods, cond, final_v, pos, time_out_v, modulation_v, final_mod_v, qkv, proj, up, down = kernel_call(
+    blocks = (qkv_weight, proj_weight, up_weight, down_weight)
+    weights = (time_out, modulation, final_mod) + blocks
+    held = [(weight.shape[1:], BF16) for weight in blocks]
+    (
+        mods, cond, final_v, pos, time_out_v, modulation_v, final_mod_v, qkv0, proj0, up0, down0,
+    ) = kernel_call(
         cond_body,
         [("s", timesteps), ("s", labels), ("v", jnp.asarray(freqs.astype(np.float32))[None])]
         + [("v", label_table), ("v", time_in), ("v", final_weight), ("h", positions)]
         + [("h", weight) for weight in weights],
         [((3, 8, width), F32), ((8, width), F32), (final_weight.shape, BF16), (tok, F32)]
-        + [(weight.shape, BF16) for weight in weights],
+        + [(weight.shape, BF16) for weight in weights[:3]]
+        + held,
         [pltpu.SemaphoreType.DMA((len(weights) + 1,))],
         us=US["cond"],
     )
@@ -940,20 +1052,25 @@
         embed_body,
         [("s", offsets)]
         + [("v", t) for t in tiles]
-        + [("p", pos), ("p", mods), ("v", patch_weight), ("p", qkv)],
+        + [("p", pos), ("p", mods), ("v", patch_weight), ("p", qkv0)],
         [(tok, F32), (tok, BF16), (double, BF16), ((2, tokens, lanes), BF16)],
         [pltpu.VMEM((n_rows, 2, tile_tok, lanes), BF16)],
         us=US["embed"],
     )
     kv0p = swap(kv0, "cols", 1)
-    state1, q1, kv1, probs0, attended0, attn_out0, middle0, gp0, act0, branch0 = kernel_call(
+    (
+        state1, q1, kv1, probs0, attended0, attn_out0, middle0, gp0, act0, branch0, qkv1, proj1, up1, down1,
+    ) = kernel_call(
         block_body,
         [("p", state0), ("p", q0), ("p", kv0), ("v", kv0p)]
-        + [("p", a) for a in (mods, proj, up, down, qkv)],
+        + [("p", a) for a in (mods, proj0, up0, down0)]
+        + [("h", weight) for weight in blocks],
         [
             (tok, F32), (tok, BF16), (double, BF16), (probs_shape, BF16), (tok, BF16), (tok, BF16),
             (tok, F32), (wide_tok, BF16), (wide_tok, BF16), (tok, BF16),
-        ],
+        ]
+        + held,
+        [pltpu.SemaphoreType.DMA((4,))],
         us=US["block"],
     )
     kv1p = swap(kv1, "cols", 1)
@@ -962,12 +1079,15 @@
     probs1, attended1, attn_out1, mgrad1, keep1, send1, preds = kernel_call(
         turn_body,
         [("s", offsets), ("s", counts), ("p", state1), ("p", q1), ("p", kv1), ("v", kv1p)]
-        + [("p", a) for a in (mods, cond, patches, final_v, proj, up, down)],
+        + [("p", a) for a in (mods, cond, patches, final_v, proj1, up1, down1)],
         [
             (probs_shape, BF16), (tok, BF16), (tok, BF16), (tok, F32), ((rows_1, width), BF16),
             ((rows_1, width), BF16), ((2, tokens, 2 * out_ch), F32),
         ],
-        [pltpu.VMEM(wide_tok, BF16), pltpu.VMEM(wide_tok, BF16), pltpu.VMEM((48, width), F32)],
+        [
+            pltpu.VMEM(wide_tok, BF16), pltpu.VMEM(wide_tok, BF16), pltpu.VMEM((48, width), F32),
+            pltpu.VMEM(wide_tok, BF16),
+        ],
         us=US["turn"],
     )
     recv1 = swap(send1, "cols", 1)
@@ -975,7 +1095,7 @@
     def attend_back(layer, q, kv, kvp, *saved, after):
         return kernel_call(
             partial(attend_back_body, layer),
-            [("p", q), ("p", kv), ("v", kvp)] + [("p", a) for a in saved + (mods, proj)],
+            [("p", q), ("p", kv), ("v", kvp)] + [("p", a) for a in saved[:-1] + (mods, saved[-1])],
             [
                 (tok, BF16), (double, BF16), ((width, width), BF16), (double, BF16), ((8, width), F32),
             ],
@@ -984,7 +1104,7 @@
         )
 
     dq1, dkv1, gproj1, dkvs1, rows_a1 = attend_back(
-        1, q1, kv1, kv1p, probs1, attended1, attn_out1, mgrad1, after=None
+        1, q1, kv1, kv1p, probs1, attended1, attn_out1, mgrad1, proj1, after=None
     )
     dkvr1 = swap(dkvs1, "cols", 1)
     keep1, table1, send1 = kernel_call(
@@ -999,17 +1119,18 @@
         middle_body,
         [("p", a) for a in (state1, mgrad1, dq1, dkv1)]
         + [("v", dkvr1)]
-        + [("p", a) for a in (gproj1, middle0, branch0, gp0, act0, mods, qkv, up, down)],
+        + [("p", a) for a in (gproj1, middle0, branch0, gp0, act0, mods, qkv1, up0, down0)],
         [
             (tok, F32), ((16 * 3 * block, width), BF16), ((16 * 3 * block, width), BF16),
             ((8, width), F32),
         ],
+        [pltpu.VMEM(wide_tok, BF16)],
         us=US["middle"],
         after=table1,
     )
     recv2 = swap(send2, "cols", 1)
     dq0, dkv0, gproj0, dkvs0, rows_a0 = attend_back(
-        0, q0, kv0, kv0p, probs0, attended0, attn_out0, mgrad0, after=None
+        0, q0, kv0, kv0p, probs0, attended0, attn_out0, mgrad0, proj0, after=None
     )
     dkvr0 = swap(dkvs0, "cols", 1)
     keep1, pair1, send1 = kernel_call(
@@ -1020,11 +1141,13 @@
         after=rows_a0,
     )
     recv1 = swap_by_core(send1, SECOND)
+    alpha, beta = 2 * block + 16, block - 16
+    send_rows = 4 * alpha + 2 * beta + 8 * block + 32
     whole_2, whole_r = keep2, recv2
     keep2, send2 = kernel_call(
         second_body,
         [("p", whole_2), ("v", whole_r)],
-        [((8 * 2 * block, width), BF16)] * 2,
+        [((8 * alpha, width), BF16)] * 2,
         us=US["A3"],
         after=pair1,
     )
@@ -1032,7 +1155,7 @@
     betas = kernel_call(
         beta_body,
         [("p", whole_2), ("v", whole_r)],
-        [((4 * block, width), BF16)] * 4,
+        [((4 * beta, width), BF16)] * 4,
         us=US["A3b"],
         after=keep2,
     )
@@ -1043,46 +1166,56 @@
         last_body,
         [("s", offsets), ("p", state0), ("p", mgrad0), ("p", dq0), ("p", dkv0), ("v", dkvr0)]
         + [("p", gproj0), ("p", mods), ("p", patches), ("v", patch_weight)]
-        + [("p", a) for a in (rows_a1, rows_mid, rows_a0, qkv)],
+        + [("p", a) for a in (rows_a1, rows_mid, rows_a0, qkv0)],
         [((rows_3, width), BF16), ((rows_3, width), BF16), ((2, tokens, 2 * lat_ch), F32)],
         [pltpu.VMEM((8, width), F32), pltpu.VMEM((32, width), F32)],
         us=US["last"],
         after=chips,
     )
     recv3 = swap(send3, "cols", 1)
-    *ones, tiles = kernel_call(
+    (tiles,) = kernel_call(
+        pack_body, [("p", preds), ("p", lgrads)], [((4, 16, width), BF16)], us=US["pack"]
+    )
+    ones = kernel_call(
         partial(first_chip_body, sums_a),
-        [("p", keep1), ("p", pair1), ("v", recv1), ("p", preds), ("p", lgrads)],
-        [((2 * block + 48, width), BF16)] * 4 + [((4, 16, width), BF16)],
+        [("p", keep1), ("p", pair1), ("v", recv1)],
+        [((2 * block + 48, width), BF16)] * 4,
         [pltpu.VMEM((4, ROWS, width), F32), pltpu.VMEM((sums_a, width), F32)],
         us=US["A2b"],
-    )
+        after=tiles,
+    )
+    chips = ones[0]
     ones = along_z(ones)
     keep2, keepb, part = kernel_call(
         third_body,
         [("p", keep2), ("v", recv2), ("p", betas[0])] + [("v", beta) for beta in betas[1:]],
-        [((8 * block, width), BF16), ((2 * block, width), BF16), ((10 * block, width), BF16)],
-        [pltpu.VMEM((4 * block, width), BF16)],
+        [
+            ((4 * alpha, width), BF16), ((2 * beta, width), BF16),
+            ((4 * alpha + 2 * beta, width), BF16),
+        ],
+        [pltpu.VMEM((4 * beta, width), BF16)],
         us=US["A4"],
-        after=tiles,
+        after=chips,
     )
     keep3, table3, send = kernel_call(
         third_send_body,
         [("p", keep3), ("v", recv3), ("p", part)],
-        [((8 * block, width), BF16), ((32, width), BF16), ((18 * block + 32, width), BF16)],
+        [((8 * block, width), BF16), ((32, width), BF16), ((send_rows, width), BF16)],
         us=US["A4b"],
     )
     recv = swap_by_core(send, SECOND)
-    whole2, keep3, keepb, pair3, send = kernel_call(
+    *twos, keep3, keepb, pair3, send = kernel_call(
         partial(fourth_body, sums_b),
         [("p", keep2), ("p", keep3), ("p", keepb), ("p", table3), ("v", recv)],
-        [
-            ((8 * block, width), BF16), ((4 * block, width), BF16), ((block, width), BF16),
-            ((48, width), BF16), ((5 * block + 48, width), BF16),
+        [((alpha, width), BF16)] * 4
+        + [
+            ((4 * block, width), BF16), ((beta, width), BF16), ((48, width), BF16),
+            ((4 * block + beta + 48, width), BF16),
         ],
         us=US["A5"],
     )
     recv = swap_by_core(send, FIRST)
+    twos = along_z(twos)
     pack = (8 * ROWS + 16, width)
     unit1, pack_a = kernel_call(
         partial(unit1_body, sums_a // 2),
@@ -1091,67 +1224,95 @@
         us=US["U1"],
         after=pair3,
     )
-    ones = along_wide(unit1)
-    *twos, unitb = kernel_call(
+    packs = both_halves(pack_a)
+    *threes, unitb = kernel_call(
         partial(fifth_body, sums_b),
-        [("p", whole2), ("p", keep3), ("p", keepb), ("p", pair3), ("v", recv), ("p", tiles)],
-        [((3 * block + 32 + 16, width), BF16)] * 4 + [((block, width), BF16)],
+        [("p", keep3), ("p", keepb), ("p", pair3), ("v", recv), ("p", tiles)],
+        [((block + 32 + 16, width), BF16)] * 4 + [((beta, width), BF16)],
         [pltpu.VMEM((4, ROWS, width), F32), pltpu.VMEM((sums_b, width), F32)],
         us=US["A6"],
         after=pack_a,
     )
-    chips = twos[0]
-    twos = along_z(twos)
-    packs = both_halves(pack_a)
-    g_up, g_down = kernel_call(
-        first_spread_body,
-        [("p", ones[0])] + [("v", one) for one in ones[1:]],
-        [((2, block, ff), F32), ((2, ff // 8, width), F32)],
-        us=US["S1"],
-        after=chips,
-    )
-    unit2, pack_b, tiles = kernel_call(
-        partial(unit2_body, sums_b // 2),
-        [("p", twos[0])] + [("v", two) for two in twos[1:]] + [("p", unitb)],
-        [((4 * block, width), BF16), (pack, BF16), ((4, 16, width), BF16)],
-        us=US["U2"],
-        after=g_up,
-    )
-    twos = along_wide(unit2)
-    packs = packs + both_halves(pack_b)
+    threes = along_z(threes)
+    (unit2,) = kernel_call(
+        unit12_body,
+        [("p", unit1), ("p", twos[0])] + [("v", two) for two in twos[1:]] + [("p", unitb)],
+        [((2 * block + alpha + beta, width), BF16)],
+        us=US["U12"],
+    )
+    unit2 = rest_sum(unit2)
+    near2 = swap_by_core(unit2, FIRST)
     samples = 2 * (packs[0].shape[0] - 16) // ROWS
     classes = label_table.shape[0]
-    g_time_in, g_time_out, g_table, g_mod, g_final_mod, g_patch, g_final = kernel_call(
+    feat_count = time_in.shape[0]
+    g_final_mod, g_final, *early = kernel_call(
+        early_sums_body,
+        [("p", packs[0]), ("v", packs[1]), ("p", final_mod_v)],
+        [
+            (final_mod.shape, F32, "any"), ((sums_a, width), F32, "any"), ((width, samples), F32),
+            ((2, samples, width), F32), ((samples, width), F32), ((3, samples, width), F32),
+            ((width, samples), BF16), ((feat_count, samples), BF16), ((classes, samples), BF16),
+        ],
+        [pltpu.VMEM((width // 128, samples * ROWS, 128), F32)],
+        us=US["early"],
+        after=unit2,
+    )
+    unit3, pack_b, tiles = kernel_call(
+        partial(unit3_body, sums_b // 2),
+        [("p", threes[0])] + [("v", three) for three in threes[1:]],
+        [((block, width), BF16), (pack, BF16), ((4, 16, width), BF16)],
+        us=US["U2"],
+        after=early[0],
+    )
+    unit3 = rest_sum(unit3)
+    (send,) = kernel_call(
+        join_body,
+        [("p", unit2), ("v", near2), ("p", unit3)],
+        [((2 * unit2.shape[0] + block, width), BF16)],
+        us=US["join"],
+    )
+    far = swap_by_core(send, SECOND)
+    packs = both_halves(pack_b)
+    mod_shape = (2, block, 6 * width)
+    g_time_in, g_time_out, g_table, g_mod, g_patch, prediction, latent_grad, token = kernel_call(
         sums_body,
-        [("v", half) for half in packs]
-        + [("p", a) for a in (modulation_v, final_mod_v, time_out_v)],
+        [("p", packs[0]), ("v", packs[1])]
+        + [("p", a) for a in (modulation_v, time_out_v, *early, tiles)],
         [
-            (shape, F32, 0)
-            for shape in (
-                time_in.shape, time_out.shape, (classes, width), (2, block, 6 * width), final_mod.shape,
-                patch_weight.shape, final_weight.shape,
-            )
+            (time_in.shape, F32, "hbm"), (time_out.shape, F32, "hbm"), ((classes, width), F32, "hbm"),
+            (mod_shape, F32, "hbm"), (patch_weight.shape, F32, "any"),
+            ((slots, out_ch, tile_h, tile_w), BF16, "any"), (latent.shape, F32, "any"),
+            ((8, 128), F32),
         ],
         [
-            pltpu.VMEM((2, width // 128, samples * ROWS, 128), F32),
-            pltpu.VMEM((width, samples), F32), pltpu.VMEM((sums_a, width), F32),
+            pltpu.VMEM((width // 128, samples * ROWS, 128), F32), pltpu.VMEM(mod_shape, F32),
+            pltpu.VMEM((classes, width), F32), pltpu.VMEM(time_out.shape, F32),
+            pltpu.VMEM(time_in.shape, F32), pltpu.SemaphoreType.DMA((4,)),
         ],
         us=US["sums"],
     )
-    g_qkv, g_proj, g_up, g_down, prediction, latent_grad = kernel_call(
+    (send3,) = kernel_call(
+        far_body,
+        [("p", unit3), ("v", far)],
+        [((2 * block, width), BF16)],
+        us=US["F3"],
+        after=token,
+    )
+    near3 = swap_by_core(send3, FIRST)
+    up_shape, down_shape = (2, block, ff), (2, ff // 8, width)
+    g_qkv, g_proj, g_up, g_down = kernel_call(
         spread_body,
-        [("v", a) for a in twos] + [("p", tiles), ("p", g_up), ("p", g_down)],
+        [("p", unit2), ("v", near2), ("v", far), ("p", unit3), ("v", near3)],
         [
-            ((2, block, 3 * width), F32, 0), ((2, block, width), F32, 0), ((2, block, ff), F32, 0),
-            ((2, ff // 8, width), F32, 0), ((slots, out_ch, tile_h, tile_w), BF16, 0),
-            (latent.shape, F32, 0),
+            ((2, block, 3 * width), F32, "any"), ((2, block, width), F32, "any"),
+            (up_shape, F32, "hbm"), (down_shape, F32, "hbm"),
         ],
+        [pltpu.VMEM(up_shape, F32), pltpu.VMEM(down_shape, F32), pltpu.SemaphoreType.DMA((4,))],
         us=US["spread"],
-        after=g_patch,
     )
     return (
         prediction, latent_grad, g_patch, g_time_in, g_time_out, g_table, g_mod, g_qkv, g_proj,
-        g_up, g_down, g_final_mod, g_final,
+        g_up, g_down, g_final_mod, g_final.T,
     )
 
 

time: 110 us -> 107 us (0.973)
  starting transfers between devices: 30.5 us -> 34.9 us
  waiting for transfers between devices: 29.9 us -> 26.4 us
  local copies, waits for them, and re-layouts: 3.45 us -> 0.16 us
  Pallas kernels: 44.6 us -> 43.3 us
    ppermute x27 -> x24, waiting for transfers between devices: 13.5 us -> 8.19 us  [swap(): return lax.ppermute(value, axis, [(i, i ^ bit) for i in range(count)])]
    unnamed x24 -> x17, local copies, waits for them, and re-layouts: 3.45 us -> 0.16 us
    ppermute x5 -> x8, starting transfers between devices: 5.22 us -> 8.49 us  [swap_by_core(): return lax.ppermute(value, ('wide', 'cols'), pairs)]
    ppermute x5 -> x8, waiting for transfers between devices: 16.4 us -> 18.2 us  [swap_by_core(): return lax.ppermute(value, ('wide', 'cols'), pairs)]
    pallas_call x23 -> x27, Pallas kernels: 44.6 us -> 43.3 us  [kernel_call(): pl.pallas_call(kernel, in_specs=specs, out_specs=[pl.BlockSpec(memory_spa...]
    ppermute x27 -> x24, starting transfers between devices: 25.3 us -> 26.4 us  [swap(): return lax.ppermute(value, axis, [(i, i ^ bit) for i in range(count)])]
  transfers between devices with their start and end apart: 32 -> 32, of which waited for: 11 -> 14; matrix products, arithmetic and copies ran while one was open for 1% -> 0% of each run, Pallas kernels for 23% -> 23%
where the time goes in v2:
time: 107 us
  Pallas kernels  43.3 us (40%)
  starting transfers between devices  34.9 us (33%)
  waiting for transfers between devices  26.4 us (25%)
  between operations  1.8 us (2%)
    pallas_call x27, Pallas kernels, kernel_call(): pl.pallas_call(kernel, in_specs=specs, out_specs=[pl.BlockSpec(memory_spa...  43.3 us
    ppermute x24, starting transfers between devices, swap(): return lax.ppermute(value, axis, [(i, i ^ bit) for i in range(count)])  26.4 us
    ppermute x8, waiting for transfers between devices, swap_by_core(): return lax.ppermute(value, ('wide', 'cols'), pairs)  18.2 us
    ppermute x8, starting transfers between devices, swap_by_core(): return lax.ppermute(value, ('wide', 'cols'), pairs)  8.49 us
    ppermute x24, waiting for transfers between devices, swap(): return lax.ppermute(value, axis, [(i, i ^ bit) for i in range(count)])  8.19 us
  transfers between devices with their start and end apart: 32, of which 14 were waited for; matrix products, arithmetic and copies ran while one was open for 0% of the time, Pallas kernels for 23%

profile of v2, /device:TPU:0, one launch (start us, length us, event | category | flops | bytes accessed | tf_op | source)
XLA Modules:
  0.0 106.5 jit_solution(8717226602679636322)
XLA Ops:
  0.7 2.0 %shard_map.282 = (bf16[2,64,24]{2,1,0:T(8,128)(2,1)S(1)}, bf16[2,64,24]{2,1,0:T(8,128)(2,1)S(1)}, bf16[2,64,24]{2,1,0:T(8,128)(2,1)S(1)}, bf16[2,64,24]{2,1,0:T(8,128)(2,1)S(1)}) custom-call(bf16[4,4,16,16]{3,2,1,0:T(8,128)(2,1)} %refs_0_.5, bf16[4,8,16,16]{3,2,1,0:T(8,128)(2,1)} %refs_1_.3), custom_call_target="tpu_custom_call" | custom-call | flops 1500000000 | bytes 1000000 | tf_op jit(solution)/shard_map/pallas_call | solution.py:86
  2.7 3.1 %collective-permute-start = (bf16[2,64,24]{2,1,0:T(8,128)(2,1)S(1)}, bf16[2,64,24]{2,1,0:T(8,128)(2,1)S(1)}, u32[]{:S(2)}, u32[]{:S(2)}) collective-permute-start(bf16[2,64,24]{2,1,0:T(8,128)(2,1)S(1)} %get-tuple-element.132), channel_id=1, source_target_pairs={{0,2},{2,0},{4,6},{6,4},{1,3},{3,1},{5,7},{7,5},{8,10},{10,8},{12,... | collective-permute-start | bytes 18440 | tf_op jit(solution)/shard_map/ppermute | solution.py:946
  5.8 2.6 %collective-permute-start.1 = (bf16[2,64,24]{2,1,0:T(8,128)(2,1)S(1)}, bf16[2,64,24]{2,1,0:T(8,128)(2,1)S(1)}, u32[]{:S(2)}, u32[]{:S(2)}) collective-permute-start(bf16[2,64,24]{2,1,0:T(8,128)(2,1)S(1)} %get-tuple-element.133), channel_id=1, source_target_pairs={{0,4},{2,6},{4,0},{6,2},{1,5},{3,7},{5,1},{7,3},{8,12},{10,14},{12... | collective-permute-start | bytes 18440 | tf_op jit(solution)/shard_map/ppermute | solution.py:946
  8.6 4.0 %shard_map.283 = (f32[3,8,384]{2,1,0:T(8,128)S(1)}, f32[8,384]{1,0:T(8,128)S(1)}, bf16[384,32]{1,0:T(8,128)(2,1)S(1)}, f32[256,384]{1,0:T(8,128)S(1)}, bf16[384,...) custom-call(s32[4]{0:T(128)S(1)} %copy-done.3, ...), custom_call_target="tpu_custom_call" | custom-call | flops 7500000256 | bytes 5000000 | tf_op jit(solution)/shard_map/pallas_call | solution.py:86
  15.7 1.7 %collective-permute-done.3.refs_3_.refs_2_ = bf16[256,768]{1,0:T(8,128)(2,1)S(1)} collective-permute-done((bf16[256,768]{1,0:T(8,128)(2,1)S(1)}, bf16[256,768]{1,0:T(8,128)(2,1)S(1)}, u32[]{:S(2)}, u32[]{:S(2)}) %collective-permute-start.3) | collective-permute-done | bytes 393248 | tf_op jit(solution)/shard_map/ppermute | solution.py:946
  17.4 5.9 %shard_map.285 = (f32[256,384]{1,0:T(8,128)S(1)}, bf16[256,384]{1,0:T(8,128)(2,1)S(1)}, bf16[256,768]{1,0:T(8,128)(2,1)S(1)}, bf16[6,2,256,256]{3,2,1,0:T(8,128)...) custom-call(f32[256,384]{1,0:T(8,128)S(1)} %get-tuple-element.138.re, ...), custom_call_target="tpu_custom_call" | custom-call | flops 8999999488 | bytes 6000000 | tf_op jit(solution)/shard_map/pallas_call | solution.py:86
  25.1 7.4 %shard_map.286 = (bf16[6,2,256,256]{3,2,1,0:T(8,128)(2,1)S(1)}, bf16[256,384]{1,0:T(8,128)(2,1)S(1)}, bf16[256,384]{1,0:T(8,128)(2,1)S(1)}, f32[256,384]{1,0:T(8...) custom-call(s32[4]{0:T(128)S(1)} %copy-done.5, ...), custom_call_target="tpu_custom_call" | custom-call | flops 13500000256 | bytes 9000000 | tf_op jit(solution)/shard_map/pallas_call | solution.py:86
  32.7 3.2 %shard_map.287 = (bf16[256,384]{1,0:T(8,128)(2,1)S(1)}, bf16[256,768]{1,0:T(8,128)(2,1)S(1)}, bf16[384,384]{1,0:T(8,128)(2,1)S(1)}, bf16[256,768]{1,0:T(8,128)(2,1)S(1)}, f32[8,384]{1,0:T(8,128)S(1)}) custom-call(bf16[256,384]{1,0:T(8,128)(2,1)S(1)} %get-tuple-element.145.refs_3_.refs_0_, bf16[256,768]{1,0:T(8,128)(2,1)S(1)} %get-tuple-element.146.refs_4_.refs_1_, ...), custom_call_target="tpu_custom_call" | custom-call | flops 30000001024 | bytes 20000000 | tf_op jit(solution)/shard_map/pallas_call | solution.py:86
  38.0 3.0 %shard_map.289 = (f32[256,384]{1,0:T(8,128)S(1)}, bf16[2304,384]{1,0:T(8,128)(2,1)S(1)}, bf16[2304,384]{1,0:T(8,128)(2,1)S(1)}, f32[8,384]{1,0:T(8,128)S(1)}) custom-call(f32[256,384]{1,0:T(8,128)S(1)} %get-tuple-element.144.refs_2_.refs_0_, f32[256,384]{1,0:T(8,128)S(1)} %get-tuple-element.153.refs_6_.refs_1_, ...), custom_call_target="tpu_custom_call" | custom-call | flops 6000000000 | bytes 4000000 | tf_op jit(solution)/shard_map/pallas_call | solution.py:86
  41.1 3.2 %shard_map.290 = (bf16[256,384]{1,0:T(8,128)(2,1)S(1)}, bf16[256,768]{1,0:T(8,128)(2,1)S(1)}, bf16[384,384]{1,0:T(8,128)(2,1)S(1)}, bf16[256,768]{1,0:T(8,128)(2,1)S(1)}, f32[8,384]{1,0:T(8,128)S(1)}) custom-call(bf16[256,384]{1,0:T(8,128)(2,1)S(1)} %get-tuple-element.139.refs_1_.refs_0_, bf16[256,768]{1,0:T(8,128)(2,1)S(1)} %get-tuple-element.140.refs_2_.refs_1_, ...), custom_call_target="tpu_custom_call" | custom-call | flops 30000001024 | bytes 20000000 | tf_op jit(solution)/shard_map/pallas_call | solution.py:86
  44.9 1.9 %collective-permute-done.8.refs_2_ = bf16[816,384]{1,0:T(8,128)(2,1)S(1)} collective-permute-done((bf16[816,384]{1,0:T(8,128)(2,1)S(1)}, bf16[816,384]{1,0:T(8,128)(2,1)S(1)}, u32[]{:S(2)}, u32[]{:S(2)}) %collective-permute-start.8) | collective-permute-done | bytes 626720 | tf_op jit(solution)/shard_map/ppermute | solution.py:954
  50.4 2.9 %collective-permute-start.11 = (bf16[128,384]{1,0:T(8,128)(2,1)S(1)}, bf16[128,384]{1,0:T(8,128)(2,1)S(1)}, u32[]{:S(2)}, u32[]{:S(2)}) collective-permute-start(bf16[128,384]{1,0:T(8,128)(2,1)S(1)} %get-tuple-element.184), channel_id=1, source_target_pairs={{0,4},{2,6},{4,0},{6,2},{1,5},{3,7},{5,1},{7,3},{8,12},{10,14},{12... | collective-permute-start | bytes 294920 | tf_op jit(solution)/shard_map/ppermute | solution.py:946
  54.8 2.0 %shard_map.294 = (bf16[800,384]{1,0:T(8,128)(2,1)S(1)}, bf16[800,384]{1,0:T(8,128)(2,1)S(1)}, f32[2,256,8]{2,1,0:T(8,128)S(1)}) custom-call(s32[4]{0:T(128)S(1)} %copy-done.5, f32[256,384]{1,0:T(8,128)S(1)} %get-tuple-element.138.refs_0_.refs_1_, f32[256,384]{1,0:T(8,128)S(1)} %get-tuple-element.177.refs_6_.refs_2_, ...), custom_call_target="tpu_custom_call" | custom-call | flops 6000000000 | bytes 4000000 | tf_op jit(solution)/shard_map/pallas_call | solution.py:86
  56.8 1.6 %shard_map.295.refs_3_.refs_4_ = bf16[4,16,384]{2,1,0:T(8,128)(2,1)S(1)} custom-call(f32[2,256,16]{2,1,0:T(8,128)S(1)} %get-tuple-element.188.refs_0_, f32[2,256,8]{2,1,0:T(8,128)S(1)} %get-tuple-element.194.refs_1_), custom_call_target="tpu_custom_call" | custom-call | flops 75000000 | bytes 50000 | tf_op jit(solution)/shard_map/pallas_call | solution.py:86
  63.5 2.9 %collective-permute-start.19 = (bf16[144,384]{1,0:T(8,128)(2,1)S(1)}, bf16[144,384]{1,0:T(8,128)(2,1)S(1)}, u32[]{:S(2)}, u32[]{:S(2)}) collective-permute-start(bf16[144,384]{1,0:T(8,128)(2,1)S(1)} %get-tuple-element.209), channel_id=1, source_target_pairs={{0,4},{2,6},{4,0},{6,2},{1,5},{3,7},{5,1},{7,3},{8,12},{10,14},{12... | collective-permute-start | bytes 331784 | tf_op jit(solution)/shard_map/ppermute | solution.py:946
  67.9 5.3 %collective-permute-done.16.refs_4_ = bf16[928,384]{1,0:T(8,128)(2,1)S(1)} collective-permute-done((bf16[928,384]{1,0:T(8,128)(2,1)S(1)}, bf16[928,384]{1,0:T(8,128)(2,1)S(1)}, u32[]{:S(2)}, u32[]{:S(2)}) %collective-permute-start.16) | collective-permute-done | bytes 712736 | tf_op jit(solution)/shard_map/ppermute | solution.py:954
  74.7 2.9 %collective-permute-start.26 = (bf16[112,384]{1,0:T(8,128)(2,1)S(1)}, bf16[112,384]{1,0:T(8,128)(2,1)S(1)}, u32[]{:S(2)}, u32[]{:S(2)}) collective-permute-start(bf16[112,384]{1,0:T(8,128)(2,1)S(1)} %get-tuple-element.220), channel_id=1, source_target_pairs={{0,4},{2,6},{4,0},{6,2},{1,5},{3,7},{5,1},{7,3},{8,12},{10,14},{12... | collective-permute-start | bytes 258056 | tf_op jit(solution)/shard_map/ppermute | solution.py:946
  79.4 2.8 %collective-permute-start.22 = (bf16[96,384]{1,0:T(8,128)(2,1)S(1)}, bf16[96,384]{1,0:T(8,128)(2,1)S(1)}, u32[]{:S(2)}, u32[]{:S(2)}) collective-permute-start(bf16[96,384]{1,0:T(8,128)(2,1)S(1)} %get-tuple-element.214), channel_id=1, source_target_pairs={{0,4},{2,6},{4,0},{6,2},{1,5},{3,7},{5,1},{7,3},{8,12},{10,14},{12... | collective-permute-start | bytes 221192 | tf_op jit(solution)/shard_map/ppermute | solution.py:946
  83.5 2.9 %collective-permute-start.23 = (bf16[96,384]{1,0:T(8,128)(2,1)S(1)}, bf16[96,384]{1,0:T(8,128)(2,1)S(1)}, u32[]{:S(2)}, u32[]{:S(2)}) collective-permute-start(bf16[96,384]{1,0:T(8,128)(2,1)S(1)} %get-tuple-element.215), channel_id=1, source_target_pairs={{0,6},{2,4},{4,2},{6,0},{1,7},{3,5},{5,3},{7,1},{8,14},{10,12},{12... | collective-permute-start | bytes 221192 | tf_op jit(solution)/shard_map/ppermute | solution.py:946
  88.2 2.4 %collective-permute-done.22.refs_2_ = bf16[96,384]{1,0:T(8,128)(2,1)S(1)} collective-permute-done((bf16[96,384]{1,0:T(8,128)(2,1)S(1)}, bf16[96,384]{1,0:T(8,128)(2,1)S(1)}, u32[]{:S(2)}, u32[]{:S(2)}) %collective-permute-start.22) | collective-permute-done | bytes 73760 | tf_op jit(solution)/shard_map/ppermute | solution.py:946
  92.3 4.9 %shard_map.305 = (f32[256,384]{1,0:T(8,128)}, f32[384,384]{1,0:T(8,128)}, f32[1001,384]{1,0:T(8,128)}, f32[2,48,2304]{2,1,0:T(8,128)}, f32[16,384]{1,0:T(8,128)}...) custom-call(bf16[112,384]{1,0:T(8,128)(2,1)S(1)} %get-tuple-element.224.refs_0_, ...), custom_call_target="tpu_custom_call" | custom-call | flops 7500000256 | bytes 5000000 | tf_op jit(solution)/shard_map/pallas_call | solution.py:86
  97.2 2.8 %collective-permute-done.30.refs_1_.refs_2_ = bf16[528,384]{1,0:T(8,128)(2,1)S(1)} collective-permute-done((bf16[528,384]{1,0:T(8,128)(2,1)S(1)}, bf16[528,384]{1,0:T(8,128)(2,1)S(1)}, u32[]{:S(2)}, u32[]{:S(2)}) %collective-permute-start.30) | collective-permute-done | bytes 405536 | tf_op jit(solution)/shard_map/ppermute | solution.py:954
  100.4 4.1 %collective-permute-done.31.refs_4_ = bf16[96,384]{1,0:T(8,128)(2,1)S(1)} collective-permute-done((bf16[96,384]{1,0:T(8,128)(2,1)S(1)}, bf16[96,384]{1,0:T(8,128)(2,1)S(1)}, u32[]{:S(2)}, u32[]{:S(2)}) %collective-permute-start.31) | collective-permute-done | bytes 73760 | tf_op jit(solution)/shard_map/ppermute | solution.py:954
  104.5 1.9 %shard_map.308 = (f32[2,48,1152]{2,1,0:T(8,128)}, f32[2,48,384]{2,1,0:T(8,128)}, f32[2,48,1536]{2,1,0:T(8,128)}, f32[2,192,384]{2,1,0:T(8,128)}) custom-call(bf16[240,384]{1,0:T(8,128)(2,1)S(1)} %shard_map.302.refs_3_.refs_0_, bf16[240,384]{1,0:T(8,128)(2,1)S(1)} %collective-permute-done.29.refs_1_, ...), custom_call_target="tpu_custom_call" | custom-call | flops 75000000 | bytes 50000 | tf_op jit(solution)/shard_map/pallas_call | solution.py:86
  (84 shorter events, 27.4 us)
Async XLA Ops:
  2.7 9.9 %collective-permute-start = (bf16[2,64,24]{2,1,0:T(8,128)(2,1)S(1)}, bf16[2,64,24]{2,1,0:T(8,128)(2,1)S(1)}, u32[]{:S(2)}, u32[]{:S(2)}) collective-permute-start(bf16[2,64,24]{2,1,0:T(8,128)(2,1)S(1)} %get-tuple-element.132), channel_id=1, source_target_pairs={{0,2},{2,0},{4,6},{6,4},{1,3},{3,1},{5,7},{7,5},{8,10},{10,8},{12,... | collective-permute-start | bytes 18440 | tf_op jit(solution)/shard_map/ppermute | solution.py:946
  5.8 6.8 %collective-permute-start.1 = (bf16[2,64,24]{2,1,0:T(8,128)(2,1)S(1)}, bf16[2,64,24]{2,1,0:T(8,128)(2,1)S(1)}, u32[]{:S(2)}, u32[]{:S(2)}) collective-permute-start(bf16[2,64,24]{2,1,0:T(8,128)(2,1)S(1)} %get-tuple-element.133), channel_id=1, source_target_pairs={{0,4},{2,6},{4,0},{6,2},{1,5},{3,7},{5,1},{7,3},{8,12},{10,14},{12... | collective-permute-start | bytes 18440 | tf_op jit(solution)/shard_map/ppermute | solution.py:946
  8.4 5.7 %collective-permute-start.2 = (bf16[2,64,24]{2,1,0:T(8,128)(2,1)S(1)}, bf16[2,64,24]{2,1,0:T(8,128)(2,1)S(1)}, u32[]{:S(2)}, u32[]{:S(2)}) collective-permute-start(bf16[2,64,24]{2,1,0:T(8,128)(2,1)S(1)} %get-tuple-element.134), channel_id=1, source_target_pairs={{0,6},{2,4},{4,2},{6,0},{1,7},{3,5},{5,3},{7,1},{8,14},{10,12},{12... | collective-permute-start | bytes 18440 | tf_op jit(solution)/shard_map/ppermute | solution.py:946
  36.5 10.3 %collective-permute-start.8 = (bf16[816,384]{1,0:T(8,128)(2,1)S(1)}, bf16[816,384]{1,0:T(8,128)(2,1)S(1)}, u32[]{:S(2)}, u32[]{:S(2)}) collective-permute-start(bf16[816,384]{1,0:T(8,128)(2,1)S(1)} %get-tuple-element.173), channel_id=1, source_target_pairs={{0,8},{1,17},{8,0},{9,25},{16,24},{17,1},{24,16},{25,9},{2,10},{3,... | collective-permute-start | bytes 1880072 | tf_op jit(solution)/shard_map/ppermute | solution.py:954
  41.1 5.9 %collective-permute-start.7 = (bf16[2304,384]{1,0:T(8,128)(2,1)S(1)}, bf16[2304,384]{1,0:T(8,128)(2,1)S(1)}, u32[]{:S(2)}, u32[]{:S(2)}) collective-permute-start(bf16[2304,384]{1,0:T(8,128)(2,1)S(1)} %get-tuple-element.171), channel_id=1, source_target_pairs={{0,1},{1,0},{2,3},{3,2},{4,5},{5,4},{6,7},{7,6},{8,9},{9,8},{10,11... | collective-permute-start | bytes 5308424 | tf_op jit(solution)/shard_map/ppermute | solution.py:946
  44.3 9.0 %collective-permute-start.14 = (bf16[256,768]{1,0:T(8,128)(2,1)S(1)}, bf16[256,768]{1,0:T(8,128)(2,1)S(1)}, u32[]{:S(2)}, u32[]{:S(2)}) collective-permute-start(bf16[256,768]{1,0:T(8,128)(2,1)S(1)} %get-tuple-element.191), channel_id=1, source_target_pairs={{0,1},{1,0},{2,3},{3,2},{4,5},{5,4},{6,7},{7,6},{8,9},{9,8},{10,11... | collective-permute-start | bytes 1179656 | tf_op jit(solution)/shard_map/ppermute | solution.py:946
  47.2 14.3 %collective-permute-start.9 = (bf16[896,384]{1,0:T(8,128)(2,1)S(1)}, bf16[896,384]{1,0:T(8,128)(2,1)S(1)}, u32[]{:S(2)}, u32[]{:S(2)}) collective-permute-start(bf16[896,384]{1,0:T(8,128)(2,1)S(1)} %get-tuple-element.181), channel_id=1, source_target_pairs={{0,8},{1,17},{8,0},{9,25},{16,24},{17,1},{24,16},{25,9},{2,10},{3,... | collective-permute-start | bytes 2064392 | tf_op jit(solution)/shard_map/ppermute | solution.py:954
  48.7 11.0 %collective-permute-start.13 = (bf16[448,384]{1,0:T(8,128)(2,1)S(1)}, bf16[448,384]{1,0:T(8,128)(2,1)S(1)}, u32[]{:S(2)}, u32[]{:S(2)}) collective-permute-start(bf16[448,384]{1,0:T(8,128)(2,1)S(1)} %get-tuple-element.187), channel_id=1, source_target_pairs={{0,16},{1,9},{8,24},{9,1},{16,0},{17,25},{24,8},{25,17},{2,18},{3,... | collective-permute-start | bytes 1032200 | tf_op jit(solution)/shard_map/ppermute | solution.py:954
  50.3 9.5 %collective-permute-start.10 = (bf16[128,384]{1,0:T(8,128)(2,1)S(1)}, bf16[128,384]{1,0:T(8,128)(2,1)S(1)}, u32[]{:S(2)}, u32[]{:S(2)}) collective-permute-start(bf16[128,384]{1,0:T(8,128)(2,1)S(1)} %get-tuple-element.183), channel_id=1, source_target_pairs={{0,2},{2,0},{4,6},{6,4},{1,3},{3,1},{5,7},{7,5},{8,10},{10,8},{12,... | collective-permute-start | bytes 294920 | tf_op jit(solution)/shard_map/ppermute | solution.py:946
  50.4 9.7 %collective-permute-start.11 = (bf16[128,384]{1,0:T(8,128)(2,1)S(1)}, bf16[128,384]{1,0:T(8,128)(2,1)S(1)}, u32[]{:S(2)}, u32[]{:S(2)}) collective-permute-start(bf16[128,384]{1,0:T(8,128)(2,1)S(1)} %get-tuple-element.184), channel_id=1, source_target_pairs={{0,4},{2,6},{4,0},{6,2},{1,5},{3,7},{5,1},{7,3},{8,12},{10,14},{12... | collective-permute-start | bytes 294920 | tf_op jit(solution)/shard_map/ppermute | solution.py:946
  53.3 6.8 %collective-permute-start.12 = (bf16[128,384]{1,0:T(8,128)(2,1)S(1)}, bf16[128,384]{1,0:T(8,128)(2,1)S(1)}, u32[]{:S(2)}, u32[]{:S(2)}) collective-permute-start(bf16[128,384]{1,0:T(8,128)(2,1)S(1)} %get-tuple-element.185), channel_id=1, source_target_pairs={{0,6},{2,4},{4,2},{6,0},{1,7},{3,5},{5,3},{7,1},{8,14},{10,12},{12... | collective-permute-start | bytes 294920 | tf_op jit(solution)/shard_map/ppermute | solution.py:946
  61.9 11.3 %collective-permute-start.16 = (bf16[928,384]{1,0:T(8,128)(2,1)S(1)}, bf16[928,384]{1,0:T(8,128)(2,1)S(1)}, u32[]{:S(2)}, u32[]{:S(2)}) collective-permute-start(bf16[928,384]{1,0:T(8,128)(2,1)S(1)} %get-tuple-element.203), channel_id=1, source_target_pairs={{0,16},{1,9},{8,24},{9,1},{16,0},{17,25},{24,8},{25,17},{2,18},{3,... | collective-permute-start | bytes 2138120 | tf_op jit(solution)/shard_map/ppermute | solution.py:954
  63.5 11.2 %collective-permute-start.18 = (bf16[144,384]{1,0:T(8,128)(2,1)S(1)}, bf16[144,384]{1,0:T(8,128)(2,1)S(1)}, u32[]{:S(2)}, u32[]{:S(2)}) collective-permute-start(bf16[144,384]{1,0:T(8,128)(2,1)S(1)} %get-tuple-element.208), channel_id=1, source_target_pairs={{0,2},{2,0},{4,6},{6,4},{1,3},{3,1},{5,7},{7,5},{8,10},{10,8},{12,... | collective-permute-start | bytes 331784 | tf_op jit(solution)/shard_map/ppermute | solution.py:946
  63.5 14.1 %collective-permute-start.19 = (bf16[144,384]{1,0:T(8,128)(2,1)S(1)}, bf16[144,384]{1,0:T(8,128)(2,1)S(1)}, u32[]{:S(2)}, u32[]{:S(2)}) collective-permute-start(bf16[144,384]{1,0:T(8,128)(2,1)S(1)} %get-tuple-element.209), channel_id=1, source_target_pairs={{0,4},{2,6},{4,0},{6,2},{1,5},{3,7},{5,1},{7,3},{8,12},{10,14},{12... | collective-permute-start | bytes 331784 | tf_op jit(solution)/shard_map/ppermute | solution.py:946
  66.4 12.7 %collective-permute-start.20 = (bf16[144,384]{1,0:T(8,128)(2,1)S(1)}, bf16[144,384]{1,0:T(8,128)(2,1)S(1)}, u32[]{:S(2)}, u32[]{:S(2)}) collective-permute-start(bf16[144,384]{1,0:T(8,128)(2,1)S(1)} %get-tuple-element.210), channel_id=1, source_target_pairs={{0,6},{2,4},{4,2},{6,0},{1,7},{3,5},{5,3},{7,1},{8,14},{10,12},{12... | collective-permute-start | bytes 331784 | tf_op jit(solution)/shard_map/ppermute | solution.py:946
  73.3 5.9 %collective-permute-start.17 = (bf16[272,384]{1,0:T(8,128)(2,1)S(1)}, bf16[272,384]{1,0:T(8,128)(2,1)S(1)}, u32[]{:S(2)}, u32[]{:S(2)}) collective-permute-start(bf16[272,384]{1,0:T(8,128)(2,1)S(1)} %get-tuple-element.207), channel_id=1, source_target_pairs={{0,8},{1,17},{8,0},{9,25},{16,24},{17,1},{24,16},{25,9},{2,10},{3,... | collective-permute-start | bytes 626696 | tf_op jit(solution)/shard_map/ppermute | solution.py:954
  74.7 8.8 %collective-permute-start.26 = (bf16[112,384]{1,0:T(8,128)(2,1)S(1)}, bf16[112,384]{1,0:T(8,128)(2,1)S(1)}, u32[]{:S(2)}, u32[]{:S(2)}) collective-permute-start(bf16[112,384]{1,0:T(8,128)(2,1)S(1)} %get-tuple-element.220), channel_id=1, source_target_pairs={{0,4},{2,6},{4,0},{6,2},{1,5},{3,7},{5,1},{7,3},{8,12},{10,14},{12... | collective-permute-start | bytes 258056 | tf_op jit(solution)/shard_map/ppermute | solution.py:946
  77.6 8.8 %collective-permute-start.27 = (bf16[112,384]{1,0:T(8,128)(2,1)S(1)}, bf16[112,384]{1,0:T(8,128)(2,1)S(1)}, u32[]{:S(2)}, u32[]{:S(2)}) collective-permute-start(bf16[112,384]{1,0:T(8,128)(2,1)S(1)} %get-tuple-element.221), channel_id=1, source_target_pairs={{0,6},{2,4},{4,2},{6,0},{1,7},{3,5},{5,3},{7,1},{8,14},{10,12},{12... | collective-permute-start | bytes 258056 | tf_op jit(solution)/shard_map/ppermute | solution.py:946
  79.1 7.6 %collective-permute-start.24 = (bf16[112,384]{1,0:T(8,128)(2,1)S(1)}, bf16[112,384]{1,0:T(8,128)(2,1)S(1)}, u32[]{:S(2)}, u32[]{:S(2)}) collective-permute-start(bf16[112,384]{1,0:T(8,128)(2,1)S(1)} %get-tuple-element.211.refs_5_.refs_0_), channel_id=1, source_target_pairs={{0,1},{1,0},{2,3},{3,2},{4,5},{5,4},{6,7},{7,6},{8,9},{9,8},{10,11... | collective-permute-start | bytes 258056 | tf_op jit(solution)/shard_map/ppermute | solution.py:946
  79.3 8.9 %collective-permute-start.21 = (bf16[96,384]{1,0:T(8,128)(2,1)S(1)}, bf16[96,384]{1,0:T(8,128)(2,1)S(1)}, u32[]{:S(2)}, u32[]{:S(2)}) collective-permute-start(bf16[96,384]{1,0:T(8,128)(2,1)S(1)} %get-tuple-element.213), channel_id=1, source_target_pairs={{0,2},{2,0},{4,6},{6,4},{1,3},{3,1},{5,7},{7,5},{8,10},{10,8},{12,... | collective-permute-start | bytes 221192 | tf_op jit(solution)/shard_map/ppermute | solution.py:946
  79.4 11.1 %collective-permute-start.22 = (bf16[96,384]{1,0:T(8,128)(2,1)S(1)}, bf16[96,384]{1,0:T(8,128)(2,1)S(1)}, u32[]{:S(2)}, u32[]{:S(2)}) collective-permute-start(bf16[96,384]{1,0:T(8,128)(2,1)S(1)} %get-tuple-element.214), channel_id=1, source_target_pairs={{0,4},{2,6},{4,0},{6,2},{1,5},{3,7},{5,1},{7,3},{8,12},{10,14},{12... | collective-permute-start | bytes 221192 | tf_op jit(solution)/shard_map/ppermute | solution.py:946
  83.5 7.0 %collective-permute-start.23 = (bf16[96,384]{1,0:T(8,128)(2,1)S(1)}, bf16[96,384]{1,0:T(8,128)(2,1)S(1)}, u32[]{:S(2)}, u32[]{:S(2)}) collective-permute-start(bf16[96,384]{1,0:T(8,128)(2,1)S(1)} %get-tuple-element.215), channel_id=1, source_target_pairs={{0,6},{2,4},{4,2},{6,0},{1,7},{3,5},{5,3},{7,1},{8,14},{10,12},{12... | collective-permute-start | bytes 221192 | tf_op jit(solution)/shard_map/ppermute | solution.py:946
  86.4 5.6 %collective-permute-start.29 = (bf16[240,384]{1,0:T(8,128)(2,1)S(1)}, bf16[240,384]{1,0:T(8,128)(2,1)S(1)}, u32[]{:S(2)}, u32[]{:S(2)}) collective-permute-start(bf16[240,384]{1,0:T(8,128)(2,1)S(1)} %shard_map.302.refs_3_.refs_0_), channel_id=1, source_target_pairs={{0,8},{1,17},{8,0},{9,25},{16,24},{17,1},{24,16},{25,9},{2,10},{3,... | collective-permute-start | bytes 552968 | tf_op jit(solution)/shard_map/ppermute | solution.py:954
  92.1 8.0 %collective-permute-start.30 = (bf16[528,384]{1,0:T(8,128)(2,1)S(1)}, bf16[528,384]{1,0:T(8,128)(2,1)S(1)}, u32[]{:S(2)}, u32[]{:S(2)}) collective-permute-start(bf16[528,384]{1,0:T(8,128)(2,1)S(1)} %shard_map.306), channel_id=1, source_target_pairs={{0,16},{1,9},{8,24},{9,1},{16,0},{17,25},{24,8},{25,17},{2,18},{3,... | collective-permute-start | bytes 1216520 | tf_op jit(solution)/shard_map/ppermute | solution.py:954
  (16 other events, 80.9 us)

commit v3 on v2

--- a/solution.py
+++ b/solution.py
@@ -19,7 +19,7 @@
 ROWS = 12
 ROW_SHARED, ROW_ACT, ROW_COND, ROW_HID, ROW_FEAT = 5, 6, 7, 8, 9
 US = {
-    "cond": 5, "embed": 2, "block": 6, "turn": 9, "back": 20, "middle": 4, "last": 4, "early": 0.05, "pack": 0.05, "join": 0.05, "U12": 0.05, "F3": 0.05, "sums": 5, "spread": 0.05,
+    "cond": 5, "embed": 2, "block": 6, "turn": 9, "back": 20, "middle": 4, "last": 4, "early": 0.05, "pack": 0.05, "join": 0.05, "U12": 0.05, "F3": 0.05, "unpack": 0.05, "sums": 5, "spread": 0.05,
     "A1": 0.05, "A2": 0.05, "A2b": 0.05, "A3": 0.05, "A3b": 0.05, "A4": 30, "A4b": 0.05, "A5": 0.05, "A6": 0.05, "S1": 0.05, "U2": 3,
     "U1": 1,
 }
@@ -764,11 +764,10 @@
     unit[size + end2 :] = unitb[...]
 
 
-def join_body(own2, near2, own3, send):
-    size = own2.shape[0]
-    send[0:size] = own2[...]
-    send[size : 2 * size] = near2[...]
-    send[2 * size :] = own3[...]
+def join_body(own, near, send):
+    size = own.shape[0]
+    send[0:size] = own[...]
+    send[size:] = near[...]
 
 
 def unit3_body(sums, z0, z1, z2, z3, unit, pack, tiles):
@@ -778,12 +777,6 @@
     chip_rows(sums, parts, size, pack)
     for k, part in enumerate(parts):
         tiles[k] = part[size + 32 :]
-
-
-def far_body(unit, recv, send):
-    size = unit.shape[0]
-    send[0:size] = unit[...]
-    send[size:] = recv[recv.shape[0] - size :]
 
 
 def silu_slope(values):
@@ -840,8 +833,8 @@
 
 
 def sums_body(
-    pack, other, modulation, time_out, shared_t, slopes, base, high, act_t, feat_t, hot, tiles,
-    g_time_in, g_time_out, g_table, g_mod, g_patch, prediction, latent_grad, token,
+    pack, other, modulation, time_out, shared_t, slopes, base, high, act_t, feat_t, hot,
+    g_time_in, g_time_out, g_table, g_mod, g_patch, token,
     table, mod_v, table_v, time_out_v, time_in_v, sem,
 ):
     z, c, _ = places()
@@ -879,6 +872,13 @@
     time_in_v[...] = dot(feat_t[...], time_grad.astype(BF16))
     leave(time_in_v, g_time_in)
     join_sums(g_patch, pack, other)
+    for copy in copies:
+        copy.wait()
+
+
+def unpack_body(tiles, prediction, latent_grad, token):
+    z, _, _ = places()
+    token[...] = jnp.zeros_like(token)
     _, out_ch, height, wide = prediction.shape
     lat_ch = latent_grad.shape[1]
     for k in range(4):
@@ -888,8 +888,6 @@
         image = unpacked_tile(tile[0:8, 0:128].astype(BF16), lat_ch, height, wide)
         image = image + unpacked_tile(tile[0:8, 128:256].astype(BF16), lat_ch, height, wide)
         latent_grad[z ^ k] = image.reshape(lat_ch, height, wide)
-    for copy in copies:
-        copy.wait()
 
 
 def place_mlp(up, down, piece, unit):
@@ -900,43 +898,59 @@
     down[down_rows, :] = piece[block : 2 * block].astype(F32)
 
 
-def place_attn(g_qkv, g_proj, layer, piece, unit):
-    width = g_proj.shape[2]
+def place_attn(qkv, proj, piece, unit):
+    width = proj.shape[1]
 
     @pl.when(unit < 3)
     def _():
         cols = pl.ds(pl.multiple_of(unit * width, 128), width)
-        g_qkv[layer, :, cols] = piece.astype(F32)
+        qkv[:, cols] = piece.astype(F32)
 
     @pl.when(unit == 3)
     def _():
-        g_proj[layer] = piece.astype(F32)
-
-
-def spread_body(own2, near2, far, own3, near3, g_qkv, g_proj, g_up, g_down, up, down, sem):
+        proj[...] = piece.astype(F32)
+
+
+def wide_spots():
     _, c, w = places()
     first = jnp.where(c == 0, 1, 2)
     spot = lax.rem(w, 4)
-    spots = (spot, spot ^ first, spot ^ first ^ 3, spot ^ 3)
-    size2, size3 = own2.shape[0], own3.shape[0]
-    block = g_proj.shape[1]
+    return spot, spot ^ first, spot ^ first ^ 3, spot ^ 3
+
+
+def leave_all(pairs, sem, copies):
+    for source, target in pairs:
+        copies.append(pltpu.make_async_copy(source, target, sem.at[len(copies)]))
+        copies[-1].start()
+
+
+def spread_body(own, near, far, g_qkv, g_proj, g_up, g_down, up, down, qkv, proj, sem):
+    size2 = own.shape[0]
+    block = proj.shape[0]
     size = 2 * block
-    twos = ((own2, 0), (near2, 0), (far, 0), (far, size2))
-    threes = ((own3, 0), (near3, 0), (far, 2 * size2), (near3, size3))
+    units = ((own, 0), (near, 0), (far, 0), (far, size2))
     copies = []
     for layer, start in ((1, 0), (0, size)):
-        for (ref, base), unit in zip(twos, spots):
+        for (ref, base), unit in zip(units, wide_spots()):
             piece = ref[base + start : base + start + size]
             place_mlp(up.at[layer], down.at[layer], piece, unit)
-        for source, target in ((up, g_up), (down, g_down)):
-            copies.append(
-                pltpu.make_async_copy(source.at[layer], target.at[layer], sem.at[len(copies)])
-            )
-            copies[-1].start()
-    for (ref, base), unit in zip(twos, spots):
-        place_attn(g_qkv, g_proj, 1, ref[base + 2 * size : base + size2], unit)
-    for (ref, base), unit in zip(threes, spots):
-        place_attn(g_qkv, g_proj, 0, ref[base : base + size3], unit)
+        leave_all(
+            ((up.at[layer], g_up.at[layer]), (down.at[layer], g_down.at[layer])), sem, copies
+        )
+    for (ref, base), unit in zip(units, wide_spots()):
+        place_attn(qkv, proj, ref[base + 2 * size : base + size2], unit)
+    leave_all(((qkv, g_qkv.at[1]), (proj, g_proj.at[1])), sem, copies)
+    for copy in copies:
+        copy.wait()
+
+
+def last_spread_body(own, near, far, _q, _p, g_qkv, g_proj, qkv, proj, sem):
+    size = own.shape[0]
+    units = ((own, 0), (near, 0), (far, 0), (far, size))
+    for (ref, base), unit in zip(units, wide_spots()):
+        place_attn(qkv, proj, ref[base : base + size], unit)
+    copies = []
+    leave_all(((qkv, g_qkv.at[0]), (proj, g_proj.at[0])), sem, copies)
     for copy in copies:
         copy.wait()
 
@@ -1265,24 +1279,24 @@
         after=early[0],
     )
     unit3 = rest_sum(unit3)
-    (send,) = kernel_call(
+    near3 = swap_by_core(unit3, FIRST)
+    (send2,) = kernel_call(
         join_body,
-        [("p", unit2), ("v", near2), ("p", unit3)],
-        [((2 * unit2.shape[0] + block, width), BF16)],
+        [("p", unit2), ("v", near2)],
+        [((2 * unit2.shape[0], width), BF16)],
         us=US["join"],
-    )
-    far = swap_by_core(send, SECOND)
+        after=tiles,
+    )
+    far2 = swap_by_core(send2, SECOND)
     packs = both_halves(pack_b)
     mod_shape = (2, block, 6 * width)
-    g_time_in, g_time_out, g_table, g_mod, g_patch, prediction, latent_grad, token = kernel_call(
+    g_time_in, g_time_out, g_table, g_mod, g_patch, token = kernel_call(
         sums_body,
         [("p", packs[0]), ("v", packs[1])]
-        + [("p", a) for a in (modulation_v, time_out_v, *early, tiles)],
+        + [("p", a) for a in (modulation_v, time_out_v, *early)],
         [
             (time_in.shape, F32, "hbm"), (time_out.shape, F32, "hbm"), ((classes, width), F32, "hbm"),
-            (mod_shape, F32, "hbm"), (patch_weight.shape, F32, "any"),
-            ((slots, out_ch, tile_h, tile_w), BF16, "any"), (latent.shape, F32, "any"),
-            ((8, 128), F32),
+            (mod_shape, F32, "hbm"), (patch_weight.shape, F32, "any"), ((8, 128), F32),
         ],
         [
             pltpu.VMEM((width // 128, samples * ROWS, 128), F32), pltpu.VMEM(mod_shape, F32),
@@ -1292,23 +1306,40 @@
         us=US["sums"],
     )
     (send3,) = kernel_call(
-        far_body,
-        [("p", unit3), ("v", far)],
+        join_body,
+        [("p", unit3), ("v", near3)],
         [((2 * block, width), BF16)],
         us=US["F3"],
         after=token,
     )
-    near3 = swap_by_core(send3, FIRST)
+    far3 = swap_by_core(send3, SECOND)
+    prediction, latent_grad, token = kernel_call(
+        unpack_body,
+        [("p", tiles)],
+        [((slots, out_ch, tile_h, tile_w), BF16, "any"), (latent.shape, F32, "any"), ((8, 128), F32)],
+        us=US["unpack"],
+        after=send3,
+    )
     up_shape, down_shape = (2, block, ff), (2, ff // 8, width)
+    attn_scratch = [pltpu.VMEM((block, 3 * width), F32), pltpu.VMEM((block, width), F32)]
+    attn_shapes = [((2, block, 3 * width), F32, "hbm"), ((2, block, width), F32, "hbm")]
     g_qkv, g_proj, g_up, g_down = kernel_call(
         spread_body,
-        [("p", unit2), ("v", near2), ("v", far), ("p", unit3), ("v", near3)],
-        [
-            ((2, block, 3 * width), F32, "any"), ((2, block, width), F32, "any"),
-            (up_shape, F32, "hbm"), (down_shape, F32, "hbm"),
-        ],
-        [pltpu.VMEM(up_shape, F32), pltpu.VMEM(down_shape, F32), pltpu.SemaphoreType.DMA((4,))],
+        [("p", unit2), ("v", near2), ("v", far2)],
+        attn_shapes + [(up_shape, F32, "hbm"), (down_shape, F32, "hbm")],
+        [pltpu.VMEM(up_shape, F32), pltpu.VMEM(down_shape, F32)]
+        + attn_scratch
+        + [pltpu.SemaphoreType.DMA((6,))],
         us=US["spread"],
+        after=token,
+    )
+    g_qkv, g_proj = kernel_call(
+        last_spread_body,
+        [("p", unit3), ("v", near3), ("v", far3), ("h", g_qkv), ("h", g_proj)],
+        attn_shapes,
+        attn_scratch + [pltpu.SemaphoreType.DMA((2,))],
+        us=US["spread"],
+        aliases=((3, 0), (4, 1)),
     )
     return (
         prediction, latent_grad, g_patch, g_time_in, g_time_out, g_table, g_mod, g_qkv, g_proj,

time: 107 us -> 104 us (0.972)
  waiting for transfers between devices: 26.4 us -> 18.9 us
  starting transfers between devices: 34.9 us -> 37.1 us
  Pallas kernels: 43.3 us -> 45.3 us
    ppermute x8 -> x9, waiting for transfers between devices: 18.2 us -> 10.8 us  [swap_by_core(): return lax.ppermute(value, ('wide', 'cols'), pairs)]
    ppermute x8 -> x9, starting transfers between devices: 8.49 us -> 10.6 us  [swap_by_core(): return lax.ppermute(value, ('wide', 'cols'), pairs)]
    pallas_call x27 -> x29, Pallas kernels: 43.3 us -> 45.3 us  [kernel_call(): pl.pallas_call(kernel, in_specs=specs, out_specs=[pl.BlockSpec(memory_spa...]
  transfers between devices with their start and end apart: 32 -> 33, of which waited for: 14 -> 12; matrix products, arithmetic and copies ran while one was open for 0% -> 0% of each run, Pallas kernels for 23% -> 27%
where the time goes in v3:
time: 104 us; the launch traced here: 103 us
  Pallas kernels  45.3 us (44%)
  starting transfers between devices  37.1 us (36%)
  waiting for transfers between devices  18.9 us (18%)
  between operations  1.83 us (2%)
    pallas_call x29, Pallas kernels, kernel_call(): pl.pallas_call(kernel, in_specs=specs, out_specs=[pl.BlockSpec(memory_spa...  45.3 us
    ppermute x24, starting transfers between devices, swap(): return lax.ppermute(value, axis, [(i, i ^ bit) for i in range(count)])  26.5 us
    ppermute x9, waiting for transfers between devices, swap_by_core(): return lax.ppermute(value, ('wide', 'cols'), pairs)  10.8 us
    ppermute x9, starting transfers between devices, swap_by_core(): return lax.ppermute(value, ('wide', 'cols'), pairs)  10.6 us
    ppermute x24, waiting for transfers between devices, swap(): return lax.ppermute(value, axis, [(i, i ^ bit) for i in range(count)])  8.14 us
  transfers between devices with their start and end apart: 33, of which 12 were waited for; matrix products, arithmetic and copies ran while one was open for 0% of the time, Pallas kernels for 27%

profile of v3, /device:TPU:0, one launch (start us, length us, event | category | flops | bytes accessed | tf_op | source)
XLA Modules:
  0.0 103.3 jit_solution(7788935815426123842)
XLA Ops:
  0.7 2.0 %shard_map.282 = (bf16[2,64,24]{2,1,0:T(8,128)(2,1)S(1)}, bf16[2,64,24]{2,1,0:T(8,128)(2,1)S(1)}, bf16[2,64,24]{2,1,0:T(8,128)(2,1)S(1)}, bf16[2,64,24]{2,1,0:T(8,128)(2,1)S(1)}) custom-call(bf16[4,4,16,16]{3,2,1,0:T(8,128)(2,1)} %refs_0_.5, bf16[4,8,16,16]{3,2,1,0:T(8,128)(2,1)} %refs_1_.3), custom_call_target="tpu_custom_call" | custom-call | flops 1500000000 | bytes 1000000 | tf_op jit(solution)/shard_map/pallas_call | solution.py:86
  2.8 3.1 %collective-permute-start = (bf16[2,64,24]{2,1,0:T(8,128)(2,1)S(1)}, bf16[2,64,24]{2,1,0:T(8,128)(2,1)S(1)}, u32[]{:S(2)}, u32[]{:S(2)}) collective-permute-start(bf16[2,64,24]{2,1,0:T(8,128)(2,1)S(1)} %get-tuple-element.135), channel_id=1, source_target_pairs={{0,2},{2,0},{4,6},{6,4},{1,3},{3,1},{5,7},{7,5},{8,10},{10,8},{12,... | collective-permute-start | bytes 18440 | tf_op jit(solution)/shard_map/ppermute | solution.py:960
  5.8 2.6 %collective-permute-start.1 = (bf16[2,64,24]{2,1,0:T(8,128)(2,1)S(1)}, bf16[2,64,24]{2,1,0:T(8,128)(2,1)S(1)}, u32[]{:S(2)}, u32[]{:S(2)}) collective-permute-start(bf16[2,64,24]{2,1,0:T(8,128)(2,1)S(1)} %get-tuple-element.136), channel_id=1, source_target_pairs={{0,4},{2,6},{4,0},{6,2},{1,5},{3,7},{5,1},{7,3},{8,12},{10,14},{12... | collective-permute-start | bytes 18440 | tf_op jit(solution)/shard_map/ppermute | solution.py:960
  8.6 4.0 %shard_map.283 = (f32[3,8,384]{2,1,0:T(8,128)S(1)}, f32[8,384]{1,0:T(8,128)S(1)}, bf16[384,32]{1,0:T(8,128)(2,1)S(1)}, f32[256,384]{1,0:T(8,128)S(1)}, bf16[384,...) custom-call(s32[4]{0:T(128)S(1)} %copy-done.3, ...), custom_call_target="tpu_custom_call" | custom-call | flops 7500000256 | bytes 5000000 | tf_op jit(solution)/shard_map/pallas_call | solution.py:86
  15.7 1.7 %collective-permute-done.3.refs_3_.refs_2_ = bf16[256,768]{1,0:T(8,128)(2,1)S(1)} collective-permute-done((bf16[256,768]{1,0:T(8,128)(2,1)S(1)}, bf16[256,768]{1,0:T(8,128)(2,1)S(1)}, u32[]{:S(2)}, u32[]{:S(2)}) %collective-permute-start.3) | collective-permute-done | bytes 393248 | tf_op jit(solution)/shard_map/ppermute | solution.py:960
  17.4 5.9 %shard_map.285 = (f32[256,384]{1,0:T(8,128)S(1)}, bf16[256,384]{1,0:T(8,128)(2,1)S(1)}, bf16[256,768]{1,0:T(8,128)(2,1)S(1)}, bf16[6,2,256,256]{3,2,1,0:T(8,128)...) custom-call(f32[256,384]{1,0:T(8,128)S(1)} %get-tuple-element.141.re, ...), custom_call_target="tpu_custom_call" | custom-call | flops 8999999488 | bytes 6000000 | tf_op jit(solution)/shard_map/pallas_call | solution.py:86
  25.1 7.4 %shard_map.286 = (bf16[6,2,256,256]{3,2,1,0:T(8,128)(2,1)S(1)}, bf16[256,384]{1,0:T(8,128)(2,1)S(1)}, bf16[256,384]{1,0:T(8,128)(2,1)S(1)}, f32[256,384]{1,0:T(8...) custom-call(s32[4]{0:T(128)S(1)} %copy-done.5, ...), custom_call_target="tpu_custom_call" | custom-call | flops 13500000256 | bytes 9000000 | tf_op jit(solution)/shard_map/pallas_call | solution.py:86
  32.7 3.2 %shard_map.287 = (bf16[256,384]{1,0:T(8,128)(2,1)S(1)}, bf16[256,768]{1,0:T(8,128)(2,1)S(1)}, bf16[384,384]{1,0:T(8,128)(2,1)S(1)}, bf16[256,768]{1,0:T(8,128)(2,1)S(1)}, f32[8,384]{1,0:T(8,128)S(1)}) custom-call(bf16[256,384]{1,0:T(8,128)(2,1)S(1)} %get-tuple-element.148.refs_3_.refs_0_, bf16[256,768]{1,0:T(8,128)(2,1)S(1)} %get-tuple-element.149.refs_4_.refs_1_, ...), custom_call_target="tpu_custom_call" | custom-call | flops 30000001024 | bytes 20000000 | tf_op jit(solution)/shard_map/pallas_call | solution.py:86
  38.0 3.0 %shard_map.289 = (f32[256,384]{1,0:T(8,128)S(1)}, bf16[2304,384]{1,0:T(8,128)(2,1)S(1)}, bf16[2304,384]{1,0:T(8,128)(2,1)S(1)}, f32[8,384]{1,0:T(8,128)S(1)}) custom-call(f32[256,384]{1,0:T(8,128)S(1)} %get-tuple-element.147.refs_2_.refs_0_, f32[256,384]{1,0:T(8,128)S(1)} %get-tuple-element.156.refs_6_.refs_1_, ...), custom_call_target="tpu_custom_call" | custom-call | flops 6000000000 | bytes 4000000 | tf_op jit(solution)/shard_map/pallas_call | solution.py:86
  41.1 3.2 %shard_map.290 = (bf16[256,384]{1,0:T(8,128)(2,1)S(1)}, bf16[256,768]{1,0:T(8,128)(2,1)S(1)}, bf16[384,384]{1,0:T(8,128)(2,1)S(1)}, bf16[256,768]{1,0:T(8,128)(2,1)S(1)}, f32[8,384]{1,0:T(8,128)S(1)}) custom-call(bf16[256,384]{1,0:T(8,128)(2,1)S(1)} %get-tuple-element.142.refs_1_.refs_0_, bf16[256,768]{1,0:T(8,128)(2,1)S(1)} %get-tuple-element.143.refs_2_.refs_1_, ...), custom_call_target="tpu_custom_call" | custom-call | flops 30000001024 | bytes 20000000 | tf_op jit(solution)/shard_map/pallas_call | solution.py:86
  44.8 2.0 %collective-permute-done.8.refs_2_ = bf16[816,384]{1,0:T(8,128)(2,1)S(1)} collective-permute-done((bf16[816,384]{1,0:T(8,128)(2,1)S(1)}, bf16[816,384]{1,0:T(8,128)(2,1)S(1)}, u32[]{:S(2)}, u32[]{:S(2)}) %collective-permute-start.8) | collective-permute-done | bytes 626720 | tf_op jit(solution)/shard_map/ppermute | solution.py:968
  50.4 2.9 %collective-permute-start.11 = (bf16[128,384]{1,0:T(8,128)(2,1)S(1)}, bf16[128,384]{1,0:T(8,128)(2,1)S(1)}, u32[]{:S(2)}, u32[]{:S(2)}) collective-permute-start(bf16[128,384]{1,0:T(8,128)(2,1)S(1)} %get-tuple-element.187), channel_id=1, source_target_pairs={{0,4},{2,6},{4,0},{6,2},{1,5},{3,7},{5,1},{7,3},{8,12},{10,14},{12... | collective-permute-start | bytes 294920 | tf_op jit(solution)/shard_map/ppermute | solution.py:960
  54.8 2.0 %shard_map.294 = (bf16[800,384]{1,0:T(8,128)(2,1)S(1)}, bf16[800,384]{1,0:T(8,128)(2,1)S(1)}, f32[2,256,8]{2,1,0:T(8,128)S(1)}) custom-call(s32[4]{0:T(128)S(1)} %copy-done.5, f32[256,384]{1,0:T(8,128)S(1)} %get-tuple-element.141.refs_0_.refs_1_, f32[256,384]{1,0:T(8,128)S(1)} %get-tuple-element.180.refs_6_.refs_2_, ...), custom_call_target="tpu_custom_call" | custom-call | flops 6000000000 | bytes 4000000 | tf_op jit(solution)/shard_map/pallas_call | solution.py:86
  56.8 1.6 %shard_map.295.refs_3_.refs_4_ = bf16[4,16,384]{2,1,0:T(8,128)(2,1)S(1)} custom-call(f32[2,256,16]{2,1,0:T(8,128)S(1)} %get-tuple-element.191.refs_0_, f32[2,256,8]{2,1,0:T(8,128)S(1)} %get-tuple-element.197.refs_1_), custom_call_target="tpu_custom_call" | custom-call | flops 75000000 | bytes 50000 | tf_op jit(solution)/shard_map/pallas_call | solution.py:86
  61.9 1.6 %collective-permute-start.16 = (bf16[928,384]{1,0:T(8,128)(2,1)S(1)}, bf16[928,384]{1,0:T(8,128)(2,1)S(1)}, u32[]{:S(2)}, u32[]{:S(2)}) collective-permute-start(bf16[928,384]{1,0:T(8,128)(2,1)S(1)} %get-tuple-element.206), channel_id=1, source_target_pairs={{0,16},{1,9},{8,24},{9,1},{16,0},{17,25},{24,8},{25,17},{2,18},{3,... | collective-permute-start | bytes 2138120 | tf_op jit(solution)/shard_map/ppermute | solution.py:968
  63.5 2.9 %collective-permute-start.19 = (bf16[144,384]{1,0:T(8,128)(2,1)S(1)}, bf16[144,384]{1,0:T(8,128)(2,1)S(1)}, u32[]{:S(2)}, u32[]{:S(2)}) collective-permute-start(bf16[144,384]{1,0:T(8,128)(2,1)S(1)} %get-tuple-element.212), channel_id=1, source_target_pairs={{0,4},{2,6},{4,0},{6,2},{1,5},{3,7},{5,1},{7,3},{8,12},{10,14},{12... | collective-permute-start | bytes 331784 | tf_op jit(solution)/shard_map/ppermute | solution.py:960
  67.9 5.3 %collective-permute-done.16.refs_4_ = bf16[928,384]{1,0:T(8,128)(2,1)S(1)} collective-permute-done((bf16[928,384]{1,0:T(8,128)(2,1)S(1)}, bf16[928,384]{1,0:T(8,128)(2,1)S(1)}, u32[]{:S(2)}, u32[]{:S(2)}) %collective-permute-start.16) | collective-permute-done | bytes 712736 | tf_op jit(solution)/shard_map/ppermute | solution.py:968
  74.7 2.9 %collective-permute-start.26 = (bf16[112,384]{1,0:T(8,128)(2,1)S(1)}, bf16[112,384]{1,0:T(8,128)(2,1)S(1)}, u32[]{:S(2)}, u32[]{:S(2)}) collective-permute-start(bf16[112,384]{1,0:T(8,128)(2,1)S(1)} %get-tuple-element.223), channel_id=1, source_target_pairs={{0,4},{2,6},{4,0},{6,2},{1,5},{3,7},{5,1},{7,3},{8,12},{10,14},{12... | collective-permute-start | bytes 258056 | tf_op jit(solution)/shard_map/ppermute | solution.py:960
  79.4 2.9 %collective-permute-start.22 = (bf16[96,384]{1,0:T(8,128)(2,1)S(1)}, bf16[96,384]{1,0:T(8,128)(2,1)S(1)}, u32[]{:S(2)}, u32[]{:S(2)}) collective-permute-start(bf16[96,384]{1,0:T(8,128)(2,1)S(1)} %get-tuple-element.217), channel_id=1, source_target_pairs={{0,4},{2,6},{4,0},{6,2},{1,5},{3,7},{5,1},{7,3},{8,12},{10,14},{12... | collective-permute-start | bytes 221192 | tf_op jit(solution)/shard_map/ppermute | solution.py:960
  83.5 2.9 %collective-permute-start.23 = (bf16[96,384]{1,0:T(8,128)(2,1)S(1)}, bf16[96,384]{1,0:T(8,128)(2,1)S(1)}, u32[]{:S(2)}, u32[]{:S(2)}) collective-permute-start(bf16[96,384]{1,0:T(8,128)(2,1)S(1)} %get-tuple-element.218), channel_id=1, source_target_pairs={{0,6},{2,4},{4,2},{6,0},{1,7},{3,5},{5,3},{7,1},{8,14},{10,12},{12... | collective-permute-start | bytes 221192 | tf_op jit(solution)/shard_map/ppermute | solution.py:960
  88.2 2.3 %collective-permute-done.22.refs_2_ = bf16[96,384]{1,0:T(8,128)(2,1)S(1)} collective-permute-done((bf16[96,384]{1,0:T(8,128)(2,1)S(1)}, bf16[96,384]{1,0:T(8,128)(2,1)S(1)}, u32[]{:S(2)}, u32[]{:S(2)}) %collective-permute-start.22) | collective-permute-done | bytes 73760 | tf_op jit(solution)/shard_map/ppermute | solution.py:960
  92.3 4.9 %shard_map.305 = (f32[256,384]{1,0:T(8,128)}, f32[384,384]{1,0:T(8,128)}, f32[1001,384]{1,0:T(8,128)}, f32[2,48,2304]{2,1,0:T(8,128)}, f32[16,384]{1,0:T(8,128)}, /*index=5*/f32[8,128]{1,0:T(8,128)S(1)}) custom-call(bf16[112,384]{1,0:T(8,128)(2,1)S(1)} %get-tuple-element.229.refs_0_, bf16[112,384]{1,0:T(8,128)(2,1)S(1)} %collective-permute-done.29.refs_1_, ...), custom_call_target="tpu_custom_call" | custom-call | flops 7500000256 | bytes 5000000 | tf_op jit(solution)/shard_map/pallas_call | solution.py:86
  97.3 1.9 %collective-permute-start.30 = (bf16[96,384]{1,0:T(8,128)(2,1)S(1)}, bf16[96,384]{1,0:T(8,128)(2,1)S(1)}, u32[]{:S(2)}, u32[]{:S(2)}) collective-permute-start(bf16[96,384]{1,0:T(8,128)(2,1)S(1)} %shard_map.306.refs_1_), channel_id=1, source_target_pairs={{0,16},{1,9},{8,24},{9,1},{16,0},{17,25},{24,8},{25,17},{2,18},{3,... | collective-permute-start | bytes 221192 | tf_op jit(solution)/shard_map/ppermute | solution.py:968
  99.2 2.0 %shard_map.307 = (bf16[4,8,16,16]{3,2,1,0:T(8,128)(2,1)}, f32[4,4,16,16]{3,2,1,0:T(8,128)}, f32[8,128]{1,0:T(8,128)S(1)}) custom-call(bf16[4,16,384]{2,1,0:T(8,128)(2,1)S(1)} %get-tuple-element.227.refs_0_.refs_2_, bf16[96,384]{1,0:T(8,128)(2,1)S(1)} %shard_map.306.refs_1_), custom_call_target="tpu_custom_call" | custom-call | flops 75000000 | bytes 50000 | tf_op jit(solution)/shard_map/pallas_call | solution.py:86
  (88 shorter events, 27.3 us)
Async XLA Ops:
  2.8 9.9 %collective-permute-start = (bf16[2,64,24]{2,1,0:T(8,128)(2,1)S(1)}, bf16[2,64,24]{2,1,0:T(8,128)(2,1)S(1)}, u32[]{:S(2)}, u32[]{:S(2)}) collective-permute-start(bf16[2,64,24]{2,1,0:T(8,128)(2,1)S(1)} %get-tuple-element.135), channel_id=1, source_target_pairs={{0,2},{2,0},{4,6},{6,4},{1,3},{3,1},{5,7},{7,5},{8,10},{10,8},{12,... | collective-permute-start | bytes 18440 | tf_op jit(solution)/shard_map/ppermute | solution.py:960
  5.8 6.8 %collective-permute-start.1 = (bf16[2,64,24]{2,1,0:T(8,128)(2,1)S(1)}, bf16[2,64,24]{2,1,0:T(8,128)(2,1)S(1)}, u32[]{:S(2)}, u32[]{:S(2)}) collective-permute-start(bf16[2,64,24]{2,1,0:T(8,128)(2,1)S(1)} %get-tuple-element.136), channel_id=1, source_target_pairs={{0,4},{2,6},{4,0},{6,2},{1,5},{3,7},{5,1},{7,3},{8,12},{10,14},{12... | collective-permute-start | bytes 18440 | tf_op jit(solution)/shard_map/ppermute | solution.py:960
  8.4 5.7 %collective-permute-start.2 = (bf16[2,64,24]{2,1,0:T(8,128)(2,1)S(1)}, bf16[2,64,24]{2,1,0:T(8,128)(2,1)S(1)}, u32[]{:S(2)}, u32[]{:S(2)}) collective-permute-start(bf16[2,64,24]{2,1,0:T(8,128)(2,1)S(1)} %get-tuple-element.137), channel_id=1, source_target_pairs={{0,6},{2,4},{4,2},{6,0},{1,7},{3,5},{5,3},{7,1},{8,14},{10,12},{12... | collective-permute-start | bytes 18440 | tf_op jit(solution)/shard_map/ppermute | solution.py:960
  36.5 10.3 %collective-permute-start.8 = (bf16[816,384]{1,0:T(8,128)(2,1)S(1)}, bf16[816,384]{1,0:T(8,128)(2,1)S(1)}, u32[]{:S(2)}, u32[]{:S(2)}) collective-permute-start(bf16[816,384]{1,0:T(8,128)(2,1)S(1)} %get-tuple-element.176), channel_id=1, source_target_pairs={{0,8},{1,17},{8,0},{9,25},{16,24},{17,1},{24,16},{25,9},{2,10},{3,... | collective-permute-start | bytes 1880072 | tf_op jit(solution)/shard_map/ppermute | solution.py:968
  41.0 5.9 %collective-permute-start.7 = (bf16[2304,384]{1,0:T(8,128)(2,1)S(1)}, bf16[2304,384]{1,0:T(8,128)(2,1)S(1)}, u32[]{:S(2)}, u32[]{:S(2)}) collective-permute-start(bf16[2304,384]{1,0:T(8,128)(2,1)S(1)} %get-tuple-element.174), channel_id=1, source_target_pairs={{0,1},{1,0},{2,3},{3,2},{4,5},{5,4},{6,7},{7,6},{8,9},{9,8},{10,11... | collective-permute-start | bytes 5308424 | tf_op jit(solution)/shard_map/ppermute | solution.py:960
  44.3 9.0 %collective-permute-start.14 = (bf16[256,768]{1,0:T(8,128)(2,1)S(1)}, bf16[256,768]{1,0:T(8,128)(2,1)S(1)}, u32[]{:S(2)}, u32[]{:S(2)}) collective-permute-start(bf16[256,768]{1,0:T(8,128)(2,1)S(1)} %get-tuple-element.194), channel_id=1, source_target_pairs={{0,1},{1,0},{2,3},{3,2},{4,5},{5,4},{6,7},{7,6},{8,9},{9,8},{10,11... | collective-permute-start | bytes 1179656 | tf_op jit(solution)/shard_map/ppermute | solution.py:960
  47.2 14.2 %collective-permute-start.9 = (bf16[896,384]{1,0:T(8,128)(2,1)S(1)}, bf16[896,384]{1,0:T(8,128)(2,1)S(1)}, u32[]{:S(2)}, u32[]{:S(2)}) collective-permute-start(bf16[896,384]{1,0:T(8,128)(2,1)S(1)} %get-tuple-element.184), channel_id=1, source_target_pairs={{0,8},{1,17},{8,0},{9,25},{16,24},{17,1},{24,16},{25,9},{2,10},{3,... | collective-permute-start | bytes 2064392 | tf_op jit(solution)/shard_map/ppermute | solution.py:968
  48.7 11.0 %collective-permute-start.13 = (bf16[448,384]{1,0:T(8,128)(2,1)S(1)}, bf16[448,384]{1,0:T(8,128)(2,1)S(1)}, u32[]{:S(2)}, u32[]{:S(2)}) collective-permute-start(bf16[448,384]{1,0:T(8,128)(2,1)S(1)} %get-tuple-element.190), channel_id=1, source_target_pairs={{0,16},{1,9},{8,24},{9,1},{16,0},{17,25},{24,8},{25,17},{2,18},{3,... | collective-permute-start | bytes 1032200 | tf_op jit(solution)/shard_map/ppermute | solution.py:968
  50.3 9.5 %collective-permute-start.10 = (bf16[128,384]{1,0:T(8,128)(2,1)S(1)}, bf16[128,384]{1,0:T(8,128)(2,1)S(1)}, u32[]{:S(2)}, u32[]{:S(2)}) collective-permute-start(bf16[128,384]{1,0:T(8,128)(2,1)S(1)} %get-tuple-element.186), channel_id=1, source_target_pairs={{0,2},{2,0},{4,6},{6,4},{1,3},{3,1},{5,7},{7,5},{8,10},{10,8},{12,... | collective-permute-start | bytes 294920 | tf_op jit(solution)/shard_map/ppermute | solution.py:960
  50.4 9.7 %collective-permute-start.11 = (bf16[128,384]{1,0:T(8,128)(2,1)S(1)}, bf16[128,384]{1,0:T(8,128)(2,1)S(1)}, u32[]{:S(2)}, u32[]{:S(2)}) collective-permute-start(bf16[128,384]{1,0:T(8,128)(2,1)S(1)} %get-tuple-element.187), channel_id=1, source_target_pairs={{0,4},{2,6},{4,0},{6,2},{1,5},{3,7},{5,1},{7,3},{8,12},{10,14},{12... | collective-permute-start | bytes 294920 | tf_op jit(solution)/shard_map/ppermute | solution.py:960
  53.3 6.8 %collective-permute-start.12 = (bf16[128,384]{1,0:T(8,128)(2,1)S(1)}, bf16[128,384]{1,0:T(8,128)(2,1)S(1)}, u32[]{:S(2)}, u32[]{:S(2)}) collective-permute-start(bf16[128,384]{1,0:T(8,128)(2,1)S(1)} %get-tuple-element.188), channel_id=1, source_target_pairs={{0,6},{2,4},{4,2},{6,0},{1,7},{3,5},{5,3},{7,1},{8,14},{10,12},{12... | collective-permute-start | bytes 294920 | tf_op jit(solution)/shard_map/ppermute | solution.py:960
  61.9 11.3 %collective-permute-start.16 = (bf16[928,384]{1,0:T(8,128)(2,1)S(1)}, bf16[928,384]{1,0:T(8,128)(2,1)S(1)}, u32[]{:S(2)}, u32[]{:S(2)}) collective-permute-start(bf16[928,384]{1,0:T(8,128)(2,1)S(1)} %get-tuple-element.206), channel_id=1, source_target_pairs={{0,16},{1,9},{8,24},{9,1},{16,0},{17,25},{24,8},{25,17},{2,18},{3,... | collective-permute-start | bytes 2138120 | tf_op jit(solution)/shard_map/ppermute | solution.py:968
  63.5 11.2 %collective-permute-start.18 = (bf16[144,384]{1,0:T(8,128)(2,1)S(1)}, bf16[144,384]{1,0:T(8,128)(2,1)S(1)}, u32[]{:S(2)}, u32[]{:S(2)}) collective-permute-start(bf16[144,384]{1,0:T(8,128)(2,1)S(1)} %get-tuple-element.211), channel_id=1, source_target_pairs={{0,2},{2,0},{4,6},{6,4},{1,3},{3,1},{5,7},{7,5},{8,10},{10,8},{12,... | collective-permute-start | bytes 331784 | tf_op jit(solution)/shard_map/ppermute | solution.py:960
  63.5 14.1 %collective-permute-start.19 = (bf16[144,384]{1,0:T(8,128)(2,1)S(1)}, bf16[144,384]{1,0:T(8,128)(2,1)S(1)}, u32[]{:S(2)}, u32[]{:S(2)}) collective-permute-start(bf16[144,384]{1,0:T(8,128)(2,1)S(1)} %get-tuple-element.212), channel_id=1, source_target_pairs={{0,4},{2,6},{4,0},{6,2},{1,5},{3,7},{5,1},{7,3},{8,12},{10,14},{12... | collective-permute-start | bytes 331784 | tf_op jit(solution)/shard_map/ppermute | solution.py:960
  66.4 12.6 %collective-permute-start.20 = (bf16[144,384]{1,0:T(8,128)(2,1)S(1)}, bf16[144,384]{1,0:T(8,128)(2,1)S(1)}, u32[]{:S(2)}, u32[]{:S(2)}) collective-permute-start(bf16[144,384]{1,0:T(8,128)(2,1)S(1)} %get-tuple-element.213), channel_id=1, source_target_pairs={{0,6},{2,4},{4,2},{6,0},{1,7},{3,5},{5,3},{7,1},{8,14},{10,12},{12... | collective-permute-start | bytes 331784 | tf_op jit(solution)/shard_map/ppermute | solution.py:960
  73.3 5.9 %collective-permute-start.17 = (bf16[272,384]{1,0:T(8,128)(2,1)S(1)}, bf16[272,384]{1,0:T(8,128)(2,1)S(1)}, u32[]{:S(2)}, u32[]{:S(2)}) collective-permute-start(bf16[272,384]{1,0:T(8,128)(2,1)S(1)} %get-tuple-element.210), channel_id=1, source_target_pairs={{0,8},{1,17},{8,0},{9,25},{16,24},{17,1},{24,16},{25,9},{2,10},{3,... | collective-permute-start | bytes 626696 | tf_op jit(solution)/shard_map/ppermute | solution.py:968
  74.7 8.8 %collective-permute-start.26 = (bf16[112,384]{1,0:T(8,128)(2,1)S(1)}, bf16[112,384]{1,0:T(8,128)(2,1)S(1)}, u32[]{:S(2)}, u32[]{:S(2)}) collective-permute-start(bf16[112,384]{1,0:T(8,128)(2,1)S(1)} %get-tuple-element.223), channel_id=1, source_target_pairs={{0,4},{2,6},{4,0},{6,2},{1,5},{3,7},{5,1},{7,3},{8,12},{10,14},{12... | collective-permute-start | bytes 258056 | tf_op jit(solution)/shard_map/ppermute | solution.py:960
  77.6 8.8 %collective-permute-start.27 = (bf16[112,384]{1,0:T(8,128)(2,1)S(1)}, bf16[112,384]{1,0:T(8,128)(2,1)S(1)}, u32[]{:S(2)}, u32[]{:S(2)}) collective-permute-start(bf16[112,384]{1,0:T(8,128)(2,1)S(1)} %get-tuple-element.224), channel_id=1, source_target_pairs={{0,6},{2,4},{4,2},{6,0},{1,7},{3,5},{5,3},{7,1},{8,14},{10,12},{12... | collective-permute-start | bytes 258056 | tf_op jit(solution)/shard_map/ppermute | solution.py:960
  79.1 7.6 %collective-permute-start.24 = (bf16[112,384]{1,0:T(8,128)(2,1)S(1)}, bf16[112,384]{1,0:T(8,128)(2,1)S(1)}, u32[]{:S(2)}, u32[]{:S(2)}) collective-permute-start(bf16[112,384]{1,0:T(8,128)(2,1)S(1)} %get-tuple-element.214.refs_5_.refs_0_), channel_id=1, source_target_pairs={{0,1},{1,0},{2,3},{3,2},{4,5},{5,4},{6,7},{7,6},{8,9},{9,8},{10,11... | collective-permute-start | bytes 258056 | tf_op jit(solution)/shard_map/ppermute | solution.py:960
  79.3 8.9 %collective-permute-start.21 = (bf16[96,384]{1,0:T(8,128)(2,1)S(1)}, bf16[96,384]{1,0:T(8,128)(2,1)S(1)}, u32[]{:S(2)}, u32[]{:S(2)}) collective-permute-start(bf16[96,384]{1,0:T(8,128)(2,1)S(1)} %get-tuple-element.216), channel_id=1, source_target_pairs={{0,2},{2,0},{4,6},{6,4},{1,3},{3,1},{5,7},{7,5},{8,10},{10,8},{12,... | collective-permute-start | bytes 221192 | tf_op jit(solution)/shard_map/ppermute | solution.py:960
  79.4 11.1 %collective-permute-start.22 = (bf16[96,384]{1,0:T(8,128)(2,1)S(1)}, bf16[96,384]{1,0:T(8,128)(2,1)S(1)}, u32[]{:S(2)}, u32[]{:S(2)}) collective-permute-start(bf16[96,384]{1,0:T(8,128)(2,1)S(1)} %get-tuple-element.217), channel_id=1, source_target_pairs={{0,4},{2,6},{4,0},{6,2},{1,5},{3,7},{5,1},{7,3},{8,12},{10,14},{12... | collective-permute-start | bytes 221192 | tf_op jit(solution)/shard_map/ppermute | solution.py:960
  83.5 7.1 %collective-permute-start.23 = (bf16[96,384]{1,0:T(8,128)(2,1)S(1)}, bf16[96,384]{1,0:T(8,128)(2,1)S(1)}, u32[]{:S(2)}, u32[]{:S(2)}) collective-permute-start(bf16[96,384]{1,0:T(8,128)(2,1)S(1)} %get-tuple-element.218), channel_id=1, source_target_pairs={{0,6},{2,4},{4,2},{6,0},{1,7},{3,5},{5,3},{7,1},{8,14},{10,12},{12... | collective-permute-start | bytes 221192 | tf_op jit(solution)/shard_map/ppermute | solution.py:960
  90.7 6.6 %collective-permute-start.28 = (bf16[48,384]{1,0:T(8,128)(2,1)S(1)}, bf16[48,384]{1,0:T(8,128)(2,1)S(1)}, u32[]{:S(2)}, u32[]{:S(2)}) collective-permute-start(bf16[48,384]{1,0:T(8,128)(2,1)S(1)} %get-tuple-element.228.refs_0_), channel_id=1, source_target_pairs={{0,8},{1,17},{8,0},{9,25},{16,24},{17,1},{24,16},{25,9},{2,10},{3,... | collective-permute-start | bytes 110600 | tf_op jit(solution)/shard_map/ppermute | solution.py:968
  92.1 9.1 %collective-permute-start.32 = (bf16[480,384]{1,0:T(8,128)(2,1)S(1)}, bf16[480,384]{1,0:T(8,128)(2,1)S(1)}, u32[]{:S(2)}, u32[]{:S(2)}) collective-permute-start(bf16[480,384]{1,0:T(8,128)(2,1)S(1)} %shard_map.308), channel_id=1, source_target_pairs={{0,16},{1,9},{8,24},{9,1},{16,0},{17,25},{24,8},{25,17},{2,18},{3,... | collective-permute-start | bytes 1105928 | tf_op jit(solution)/shard_map/ppermute | solution.py:968
  (17 other events, 87.1 us)

commit v4 on v3

--- a/solution.py
+++ b/solution.py
@@ -834,11 +834,10 @@
 
 def sums_body(
     pack, other, modulation, time_out, shared_t, slopes, base, high, act_t, feat_t, hot,
-    g_time_in, g_time_out, g_table, g_mod, g_patch, token,
-    table, mod_v, table_v, time_out_v, time_in_v, sem,
+    time_in_v, time_out_v, table_v, mod_v, g_patch,
+    table,
 ):
     z, c, _ = places()
-    token[...] = jnp.zeros_like(token)
     rows = sample_table(table, pack, other)
     mods = [
         jnp.concatenate([rows(k) for k in range(6)], axis=-1).astype(BF16),
@@ -849,15 +848,8 @@
     block = mod_v.shape[1]
     start = pl.multiple_of((z * 2 + c) * block, 8)
     mine = shared_t[pl.ds(start, block), :].astype(BF16)
-    copies = []
-
-    def leave(source, target):
-        copies.append(pltpu.make_async_copy(source, target, sem.at[len(copies)]))
-        copies[-1].start()
-
     for layer in range(2):
         mod_v[layer] = dot(mine, mods[layer])
-    leave(mod_v, g_mod)
     shared_grad = base[...]
     for layer in range(2):
         shared_grad += dot_nt(mods[layer], modulation[layer])
@@ -865,18 +857,16 @@
     cond_low = cond_grad.astype(BF16)
     cond_rest = (cond_grad - cond_low.astype(F32)).astype(BF16)
     table_v[...] = dot(hot[...], cond_low) + dot(hot[...], cond_rest)
-    leave(table_v, g_table)
     time_out_v[...] = dot(act_t[...], cond_low)
-    leave(time_out_v, g_time_out)
     time_grad = dot_nt(cond_low, time_out[...]) * slopes[1]
     time_in_v[...] = dot(feat_t[...], time_grad.astype(BF16))
-    leave(time_in_v, g_time_in)
     join_sums(g_patch, pack, other)
-    for copy in copies:
-        copy.wait()
-
-
-def unpack_body(tiles, prediction, latent_grad, token):
+
+
+def unpack_body(tiles, *refs):
+    held, left, (prediction, latent_grad, token, sem) = refs[:5], refs[5:10], refs[10:]
+    copies = []
+    leave_all(tuple(zip(held, left)), sem, copies)
     z, _, _ = places()
     token[...] = jnp.zeros_like(token)
     _, out_ch, height, wide = prediction.shape
@@ -888,6 +878,8 @@
         image = unpacked_tile(tile[0:8, 0:128].astype(BF16), lat_ch, height, wide)
         image = image + unpacked_tile(tile[0:8, 128:256].astype(BF16), lat_ch, height, wide)
         latent_grad[z ^ k] = image.reshape(lat_ch, height, wide)
+    for copy in copies:
+        copy.wait()
 
 
 def place_mlp(up, down, piece, unit):
@@ -1147,14 +1139,6 @@
         0, q0, kv0, kv0p, probs0, attended0, attn_out0, mgrad0, proj0, after=None
     )
     dkvr0 = swap(dkvs0, "cols", 1)
-    keep1, pair1, send1 = kernel_call(
-        partial(first_pair_body, sums_a),
-        [("p", keep1), ("p", table1), ("v", recv1)],
-        [((4 * 2 * block, width), BF16), ((64, width), BF16), ((4 * 2 * block + 64, width), BF16)],
-        us=US["A2"],
-        after=rows_a0,
-    )
-    recv1 = swap_by_core(send1, SECOND)
     alpha, beta = 2 * block + 16, block - 16
     send_rows = 4 * alpha + 2 * beta + 8 * block + 32
     whole_2, whole_r = keep2, recv2
@@ -1163,15 +1147,23 @@
         [("p", whole_2), ("v", whole_r)],
         [((8 * alpha, width), BF16)] * 2,
         us=US["A3"],
-        after=pair1,
+        after=rows_a0,
     )
     recv2 = swap_by_core(send2, FIRST)
+    keep1, pair1, send1 = kernel_call(
+        partial(first_pair_body, sums_a),
+        [("p", keep1), ("p", table1), ("v", recv1)],
+        [((4 * 2 * block, width), BF16), ((64, width), BF16), ((4 * 2 * block + 64, width), BF16)],
+        us=US["A2"],
+        after=keep2,
+    )
+    recv1 = swap_by_core(send1, SECOND)
     betas = kernel_call(
         beta_body,
         [("p", whole_2), ("v", whole_r)],
         [((4 * beta, width), BF16)] * 4,
         us=US["A3b"],
-        after=keep2,
+        after=pair1,
     )
     chips = betas[0]
     betas = along_z(betas)
@@ -1289,20 +1281,14 @@
     )
     far2 = swap_by_core(send2, SECOND)
     packs = both_halves(pack_b)
-    mod_shape = (2, block, 6 * width)
-    g_time_in, g_time_out, g_table, g_mod, g_patch, token = kernel_call(
+    late_shapes = (
+        time_in.shape, time_out.shape, (classes, width), (2, block, 6 * width), patch_weight.shape,
+    )
+    late = kernel_call(
         sums_body,
-        [("p", packs[0]), ("v", packs[1])]
-        + [("p", a) for a in (modulation_v, time_out_v, *early)],
-        [
-            (time_in.shape, F32, "hbm"), (time_out.shape, F32, "hbm"), ((classes, width), F32, "hbm"),
-            (mod_shape, F32, "hbm"), (patch_weight.shape, F32, "any"), ((8, 128), F32),
-        ],
-        [
-            pltpu.VMEM((width // 128, samples * ROWS, 128), F32), pltpu.VMEM(mod_shape, F32),
-            pltpu.VMEM((classes, width), F32), pltpu.VMEM(time_out.shape, F32),
-            pltpu.VMEM(time_in.shape, F32), pltpu.SemaphoreType.DMA((4,)),
-        ],
+        [("p", packs[0]), ("v", packs[1])] + [("p", a) for a in (modulation_v, time_out_v, *early)],
+        [(shape, F32) for shape in late_shapes],
+        [pltpu.VMEM((width // 128, samples * ROWS, 128), F32)],
         us=US["sums"],
     )
     (send3,) = kernel_call(
@@ -1310,13 +1296,15 @@
         [("p", unit3), ("v", near3)],
         [((2 * block, width), BF16)],
         us=US["F3"],
-        after=token,
+        after=late[4],
     )
     far3 = swap_by_core(send3, SECOND)
-    prediction, latent_grad, token = kernel_call(
+    g_time_in, g_time_out, g_table, g_mod, g_patch, prediction, latent_grad, token = kernel_call(
         unpack_body,
-        [("p", tiles)],
-        [((slots, out_ch, tile_h, tile_w), BF16, "any"), (latent.shape, F32, "any"), ((8, 128), F32)],
+        [("p", tiles)] + [("p", a) for a in late],
+        [(shape, F32, "hbm") for shape in late_shapes]
+        + [((slots, out_ch, tile_h, tile_w), BF16, "any"), (latent.shape, F32, "any"), ((8, 128), F32)],
+        [pltpu.SemaphoreType.DMA((5,))],
         us=US["unpack"],
         after=send3,
     )

time: 104 us -> 102 us (0.981)
    ppermute x9, waiting for transfers between devices: 10.8 us -> 8.67 us  [swap_by_core(): return lax.ppermute(value, ('wide', 'cols'), pairs)]
    ppermute x24, waiting for transfers between devices: 8.14 us -> 9.68 us  [swap(): return lax.ppermute(value, axis, [(i, i ^ bit) for i in range(count)])]
  transfers between devices with their start and end apart: 33 -> 33, of which waited for: 12 -> 12; matrix products, arithmetic and copies ran while one was open for 0% -> 0% of each run, Pallas kernels for 27% -> 26%
where the time goes in v4:
time: 102 us
  Pallas kernels  44.3 us (43%)
  starting transfers between devices  37.6 us (37%)
  waiting for transfers between devices  18.3 us (18%)
  between operations  1.88 us (2%)
    pallas_call x29, Pallas kernels, kernel_call(): pl.pallas_call(kernel, in_specs=specs, out_specs=[pl.BlockSpec(memory_spa...  44.3 us
    ppermute x24, starting transfers between devices, swap(): return lax.ppermute(value, axis, [(i, i ^ bit) for i in range(count)])  26.3 us
    ppermute x9, starting transfers between devices, swap_by_core(): return lax.ppermute(value, ('wide', 'cols'), pairs)  11.3 us
    ppermute x24, waiting for transfers between devices, swap(): return lax.ppermute(value, axis, [(i, i ^ bit) for i in range(count)])  9.68 us
    ppermute x9, waiting for transfers between devices, swap_by_core(): return lax.ppermute(value, ('wide', 'cols'), pairs)  8.67 us
  transfers between devices with their start and end apart: 33, of which 12 were waited for; matrix products, arithmetic and copies ran while one was open for 0% of the time, Pallas kernels for 26%

profile of v4, /device:TPU:0, one launch (start us, length us, event | category | flops | bytes accessed | tf_op | source)
XLA Modules:
  0.0 102.3 jit_solution(1310180592902938070)
XLA Ops:
  0.7 2.0 %shard_map.282 = (bf16[2,64,24]{2,1,0:T(8,128)(2,1)S(1)}, bf16[2,64,24]{2,1,0:T(8,128)(2,1)S(1)}, bf16[2,64,24]{2,1,0:T(8,128)(2,1)S(1)}, bf16[2,64,24]{2,1,0:T(8,128)(2,1)S(1)}) custom-call(bf16[4,4,16,16]{3,2,1,0:T(8,128)(2,1)} %refs_0_.5, bf16[4,8,16,16]{3,2,1,0:T(8,128)(2,1)} %refs_1_.3), custom_call_target="tpu_custom_call" | custom-call | flops 1500000000 | bytes 1000000 | tf_op jit(solution)/shard_map/pallas_call | solution.py:86
  2.8 3.1 %collective-permute-start = (bf16[2,64,24]{2,1,0:T(8,128)(2,1)S(1)}, bf16[2,64,24]{2,1,0:T(8,128)(2,1)S(1)}, u32[]{:S(2)}, u32[]{:S(2)}) collective-permute-start(bf16[2,64,24]{2,1,0:T(8,128)(2,1)S(1)} %get-tuple-element.139), channel_id=1, source_target_pairs={{0,2},{2,0},{4,6},{6,4},{1,3},{3,1},{5,7},{7,5},{8,10},{10,8},{12,... | collective-permute-start | bytes 18440 | tf_op jit(solution)/shard_map/ppermute | solution.py:952
  5.8 2.6 %collective-permute-start.1 = (bf16[2,64,24]{2,1,0:T(8,128)(2,1)S(1)}, bf16[2,64,24]{2,1,0:T(8,128)(2,1)S(1)}, u32[]{:S(2)}, u32[]{:S(2)}) collective-permute-start(bf16[2,64,24]{2,1,0:T(8,128)(2,1)S(1)} %get-tuple-element.140), channel_id=1, source_target_pairs={{0,4},{2,6},{4,0},{6,2},{1,5},{3,7},{5,1},{7,3},{8,12},{10,14},{12... | collective-permute-start | bytes 18440 | tf_op jit(solution)/shard_map/ppermute | solution.py:952
  8.6 4.0 %shard_map.283 = (f32[3,8,384]{2,1,0:T(8,128)S(1)}, f32[8,384]{1,0:T(8,128)S(1)}, bf16[384,32]{1,0:T(8,128)(2,1)S(1)}, f32[256,384]{1,0:T(8,128)S(1)}, bf16[384,...) custom-call(s32[4]{0:T(128)S(1)} %copy-done.3, ...), custom_call_target="tpu_custom_call" | custom-call | flops 7500000256 | bytes 5000000 | tf_op jit(solution)/shard_map/pallas_call | solution.py:86
  15.7 1.7 %collective-permute-done.3.refs_3_.refs_2_ = bf16[256,768]{1,0:T(8,128)(2,1)S(1)} collective-permute-done((bf16[256,768]{1,0:T(8,128)(2,1)S(1)}, bf16[256,768]{1,0:T(8,128)(2,1)S(1)}, u32[]{:S(2)}, u32[]{:S(2)}) %collective-permute-start.3) | collective-permute-done | bytes 393248 | tf_op jit(solution)/shard_map/ppermute | solution.py:952
  17.4 5.9 %shard_map.285 = (f32[256,384]{1,0:T(8,128)S(1)}, bf16[256,384]{1,0:T(8,128)(2,1)S(1)}, bf16[256,768]{1,0:T(8,128)(2,1)S(1)}, bf16[6,2,256,256]{3,2,1,0:T(8,128)...) custom-call(f32[256,384]{1,0:T(8,128)S(1)} %get-tuple-element.145.re, ...), custom_call_target="tpu_custom_call" | custom-call | flops 8999999488 | bytes 6000000 | tf_op jit(solution)/shard_map/pallas_call | solution.py:86
  25.1 7.4 %shard_map.286 = (bf16[6,2,256,256]{3,2,1,0:T(8,128)(2,1)S(1)}, bf16[256,384]{1,0:T(8,128)(2,1)S(1)}, bf16[256,384]{1,0:T(8,128)(2,1)S(1)}, f32[256,384]{1,0:T(8...) custom-call(s32[4]{0:T(128)S(1)} %copy-done.5, ...), custom_call_target="tpu_custom_call" | custom-call | flops 13500000256 | bytes 9000000 | tf_op jit(solution)/shard_map/pallas_call | solution.py:86
  32.7 3.2 %shard_map.287 = (bf16[256,384]{1,0:T(8,128)(2,1)S(1)}, bf16[256,768]{1,0:T(8,128)(2,1)S(1)}, bf16[384,384]{1,0:T(8,128)(2,1)S(1)}, bf16[256,768]{1,0:T(8,128)(2,1)S(1)}, f32[8,384]{1,0:T(8,128)S(1)}) custom-call(bf16[256,384]{1,0:T(8,128)(2,1)S(1)} %get-tuple-element.152.refs_3_.refs_0_, bf16[256,768]{1,0:T(8,128)(2,1)S(1)} %get-tuple-element.153.refs_4_.refs_1_, ...), custom_call_target="tpu_custom_call" | custom-call | flops 30000001024 | bytes 20000000 | tf_op jit(solution)/shard_map/pallas_call | solution.py:86
  38.1 3.1 %shard_map.289 = (f32[256,384]{1,0:T(8,128)S(1)}, bf16[2304,384]{1,0:T(8,128)(2,1)S(1)}, bf16[2304,384]{1,0:T(8,128)(2,1)S(1)}, f32[8,384]{1,0:T(8,128)S(1)}) custom-call(f32[256,384]{1,0:T(8,128)S(1)} %get-tuple-element.151.refs_2_.refs_0_, f32[256,384]{1,0:T(8,128)S(1)} %get-tuple-element.160.refs_6_.refs_1_, ...), custom_call_target="tpu_custom_call" | custom-call | flops 6000000000 | bytes 4000000 | tf_op jit(solution)/shard_map/pallas_call | solution.py:86
  41.2 3.2 %shard_map.290 = (bf16[256,384]{1,0:T(8,128)(2,1)S(1)}, bf16[256,768]{1,0:T(8,128)(2,1)S(1)}, bf16[384,384]{1,0:T(8,128)(2,1)S(1)}, bf16[256,768]{1,0:T(8,128)(2,1)S(1)}, f32[8,384]{1,0:T(8,128)S(1)}) custom-call(bf16[256,384]{1,0:T(8,128)(2,1)S(1)} %get-tuple-element.146.refs_1_.refs_0_, bf16[256,768]{1,0:T(8,128)(2,1)S(1)} %get-tuple-element.147.refs_2_.refs_1_, ...), custom_call_target="tpu_custom_call" | custom-call | flops 30000001024 | bytes 20000000 | tf_op jit(solution)/shard_map/pallas_call | solution.py:86
  47.1 2.9 %collective-permute-start.11 = (bf16[128,384]{1,0:T(8,128)(2,1)S(1)}, bf16[128,384]{1,0:T(8,128)(2,1)S(1)}, u32[]{:S(2)}, u32[]{:S(2)}) collective-permute-start(bf16[128,384]{1,0:T(8,128)(2,1)S(1)} %get-tuple-element.191), channel_id=1, source_target_pairs={{0,4},{2,6},{4,0},{6,2},{1,5},{3,7},{5,1},{7,3},{8,12},{10,14},{12... | collective-permute-start | bytes 294920 | tf_op jit(solution)/shard_map/ppermute | solution.py:952
  53.0 2.1 %shard_map.294 = (bf16[800,384]{1,0:T(8,128)(2,1)S(1)}, bf16[800,384]{1,0:T(8,128)(2,1)S(1)}, f32[2,256,8]{2,1,0:T(8,128)S(1)}) custom-call(s32[4]{0:T(128)S(1)} %copy-done.5, f32[256,384]{1,0:T(8,128)S(1)} %get-tuple-element.145.refs_0_.refs_1_, f32[256,384]{1,0:T(8,128)S(1)} %get-tuple-element.182.refs_6_.refs_2_, ...), custom_call_target="tpu_custom_call" | custom-call | flops 6000000000 | bytes 4000000 | tf_op jit(solution)/shard_map/pallas_call | solution.py:86
  55.1 1.6 %shard_map.295.refs_3_.refs_4_ = bf16[4,16,384]{2,1,0:T(8,128)(2,1)S(1)} custom-call(f32[2,256,16]{2,1,0:T(8,128)S(1)} %get-tuple-element.195.refs_0_, f32[2,256,8]{2,1,0:T(8,128)S(1)} %get-tuple-element.201.refs_1_), custom_call_target="tpu_custom_call" | custom-call | flops 75000000 | bytes 50000 | tf_op jit(solution)/shard_map/pallas_call | solution.py:86
  56.7 2.3 %collective-permute-done.13.refs_2_ = bf16[448,384]{1,0:T(8,128)(2,1)S(1)} collective-permute-done((bf16[448,384]{1,0:T(8,128)(2,1)S(1)}, bf16[448,384]{1,0:T(8,128)(2,1)S(1)}, u32[]{:S(2)}, u32[]{:S(2)}) %collective-permute-start.13) | collective-permute-done | bytes 344096 | tf_op jit(solution)/shard_map/ppermute | solution.py:960
  61.5 1.8 %collective-permute-start.16 = (bf16[928,384]{1,0:T(8,128)(2,1)S(1)}, bf16[928,384]{1,0:T(8,128)(2,1)S(1)}, u32[]{:S(2)}, u32[]{:S(2)}) collective-permute-start(bf16[928,384]{1,0:T(8,128)(2,1)S(1)} %get-tuple-element.210), channel_id=1, source_target_pairs={{0,16},{1,9},{8,24},{9,1},{16,0},{17,25},{24,8},{25,17},{2,18},{3,... | collective-permute-start | bytes 2138120 | tf_op jit(solution)/shard_map/ppermute | solution.py:960
  63.3 2.9 %collective-permute-start.19 = (bf16[144,384]{1,0:T(8,128)(2,1)S(1)}, bf16[144,384]{1,0:T(8,128)(2,1)S(1)}, u32[]{:S(2)}, u32[]{:S(2)}) collective-permute-start(bf16[144,384]{1,0:T(8,128)(2,1)S(1)} %get-tuple-element.216), channel_id=1, source_target_pairs={{0,4},{2,6},{4,0},{6,2},{1,5},{3,7},{5,1},{7,3},{8,12},{10,14},{12... | collective-permute-start | bytes 331784 | tf_op jit(solution)/shard_map/ppermute | solution.py:952
  67.7 5.1 %collective-permute-done.16.refs_4_ = bf16[928,384]{1,0:T(8,128)(2,1)S(1)} collective-permute-done((bf16[928,384]{1,0:T(8,128)(2,1)S(1)}, bf16[928,384]{1,0:T(8,128)(2,1)S(1)}, u32[]{:S(2)}, u32[]{:S(2)}) %collective-permute-start.16) | collective-permute-done | bytes 712736 | tf_op jit(solution)/shard_map/ppermute | solution.py:960
  74.0 2.9 %collective-permute-start.26 = (bf16[112,384]{1,0:T(8,128)(2,1)S(1)}, bf16[112,384]{1,0:T(8,128)(2,1)S(1)}, u32[]{:S(2)}, u32[]{:S(2)}) collective-permute-start(bf16[112,384]{1,0:T(8,128)(2,1)S(1)} %get-tuple-element.227), channel_id=1, source_target_pairs={{0,4},{2,6},{4,0},{6,2},{1,5},{3,7},{5,1},{7,3},{8,12},{10,14},{12... | collective-permute-start | bytes 258056 | tf_op jit(solution)/shard_map/ppermute | solution.py:952
  79.5 2.3 %collective-permute-start.22 = (bf16[96,384]{1,0:T(8,128)(2,1)S(1)}, bf16[96,384]{1,0:T(8,128)(2,1)S(1)}, u32[]{:S(2)}, u32[]{:S(2)}) collective-permute-start(bf16[96,384]{1,0:T(8,128)(2,1)S(1)} %get-tuple-element.221), channel_id=1, source_target_pairs={{0,4},{2,6},{4,0},{6,2},{1,5},{3,7},{5,1},{7,3},{8,12},{10,14},{12... | collective-permute-start | bytes 221192 | tf_op jit(solution)/shard_map/ppermute | solution.py:952
  81.8 2.0 %collective-permute-done.26.refs_3_ = bf16[112,384]{1,0:T(8,128)(2,1)S(1)} collective-permute-done((bf16[112,384]{1,0:T(8,128)(2,1)S(1)}, bf16[112,384]{1,0:T(8,128)(2,1)S(1)}, u32[]{:S(2)}, u32[]{:S(2)}) %collective-permute-start.26) | collective-permute-done | bytes 86048 | tf_op jit(solution)/shard_map/ppermute | solution.py:952
  83.8 2.7 %collective-permute-start.23 = (bf16[96,384]{1,0:T(8,128)(2,1)S(1)}, bf16[96,384]{1,0:T(8,128)(2,1)S(1)}, u32[]{:S(2)}, u32[]{:S(2)}) collective-permute-start(bf16[96,384]{1,0:T(8,128)(2,1)S(1)} %get-tuple-element.222), channel_id=1, source_target_pairs={{0,6},{2,4},{4,2},{6,0},{1,7},{3,5},{5,3},{7,1},{8,14},{10,12},{12... | collective-permute-start | bytes 221192 | tf_op jit(solution)/shard_map/ppermute | solution.py:952
  92.3 2.6 %shard_map.305 = (f32[256,384]{1,0:T(8,128)S(1)}, f32[384,384]{1,0:T(8,128)S(1)}, f32[1001,384]{1,0:T(8,128)S(1)}, f32[2,48,2304]{2,1,0:T(8,128)S(1)}, f32[16,384]{1,0:T(8,128)S(1)}) custom-call(bf16[112,384]{1,0:T(8,128)(2,1)S(1)} %get-tuple-element.232.refs_0_, bf16[112,384]{1,0:T(8,128)(2,1)S(1)} %collective-permute-done.28.refs_1_, ...), custom_call_target="tpu_custom_call" | custom-call | flops 7500000256 | bytes 5000000 | tf_op jit(solution)/shard_map/pallas_call | solution.py:86
  95.0 2.1 %collective-permute-start.30 = (bf16[96,384]{1,0:T(8,128)(2,1)S(1)}, bf16[96,384]{1,0:T(8,128)(2,1)S(1)}, u32[]{:S(2)}, u32[]{:S(2)}) collective-permute-start(bf16[96,384]{1,0:T(8,128)(2,1)S(1)} %shard_map.306.refs_6_), channel_id=1, source_target_pairs={{0,16},{1,9},{8,24},{9,1},{16,0},{17,25},{24,8},{25,17},{2,18},{3,... | collective-permute-start | bytes 221192 | tf_op jit(solution)/shard_map/ppermute | solution.py:960
  97.1 3.0 %shard_map.307 = (f32[256,384]{1,0:T(8,128)}, f32[384,384]{1,0:T(8,128)}, f32[1001,384]{1,0:T(8,128)}, f32[2,48,2304]{2,1,0:T(8,128)}, f32[16,384]{1,0:T(8,128)}...) custom-call(bf16[4,16,384]{2,1,0:T(8,128)(2,1)S(1)} %get-tuple-element.231.refs_0_.refs_2_, ...), custom_call_target="tpu_custom_call" | custom-call | flops 75000000 | bytes 50000 | tf_op jit(solution)/shard_map/pallas_call | solution.py:86
  (88 shorter events, 28.0 us)
Async XLA Ops:
  2.8 9.9 %collective-permute-start = (bf16[2,64,24]{2,1,0:T(8,128)(2,1)S(1)}, bf16[2,64,24]{2,1,0:T(8,128)(2,1)S(1)}, u32[]{:S(2)}, u32[]{:S(2)}) collective-permute-start(bf16[2,64,24]{2,1,0:T(8,128)(2,1)S(1)} %get-tuple-element.139), channel_id=1, source_target_pairs={{0,2},{2,0},{4,6},{6,4},{1,3},{3,1},{5,7},{7,5},{8,10},{10,8},{12,... | collective-permute-start | bytes 18440 | tf_op jit(solution)/shard_map/ppermute | solution.py:952
  5.8 6.8 %collective-permute-start.1 = (bf16[2,64,24]{2,1,0:T(8,128)(2,1)S(1)}, bf16[2,64,24]{2,1,0:T(8,128)(2,1)S(1)}, u32[]{:S(2)}, u32[]{:S(2)}) collective-permute-start(bf16[2,64,24]{2,1,0:T(8,128)(2,1)S(1)} %get-tuple-element.140), channel_id=1, source_target_pairs={{0,4},{2,6},{4,0},{6,2},{1,5},{3,7},{5,1},{7,3},{8,12},{10,14},{12... | collective-permute-start | bytes 18440 | tf_op jit(solution)/shard_map/ppermute | solution.py:952
  8.4 5.7 %collective-permute-start.2 = (bf16[2,64,24]{2,1,0:T(8,128)(2,1)S(1)}, bf16[2,64,24]{2,1,0:T(8,128)(2,1)S(1)}, u32[]{:S(2)}, u32[]{:S(2)}) collective-permute-start(bf16[2,64,24]{2,1,0:T(8,128)(2,1)S(1)} %get-tuple-element.141), channel_id=1, source_target_pairs={{0,6},{2,4},{4,2},{6,0},{1,7},{3,5},{5,3},{7,1},{8,14},{10,12},{12... | collective-permute-start | bytes 18440 | tf_op jit(solution)/shard_map/ppermute | solution.py:952
  36.5 10.3 %collective-permute-start.9 = (bf16[816,384]{1,0:T(8,128)(2,1)S(1)}, bf16[816,384]{1,0:T(8,128)(2,1)S(1)}, u32[]{:S(2)}, u32[]{:S(2)}) collective-permute-start(bf16[816,384]{1,0:T(8,128)(2,1)S(1)} %get-tuple-element.187), channel_id=1, source_target_pairs={{0,8},{1,17},{8,0},{9,25},{16,24},{17,1},{24,16},{25,9},{2,10},{3,... | collective-permute-start | bytes 1880072 | tf_op jit(solution)/shard_map/ppermute | solution.py:960
  44.4 7.1 %collective-permute-start.14 = (bf16[256,768]{1,0:T(8,128)(2,1)S(1)}, bf16[256,768]{1,0:T(8,128)(2,1)S(1)}, u32[]{:S(2)}, u32[]{:S(2)}) collective-permute-start(bf16[256,768]{1,0:T(8,128)(2,1)S(1)} %get-tuple-element.198), channel_id=1, source_target_pairs={{0,1},{1,0},{2,3},{3,2},{4,5},{5,4},{6,7},{7,6},{8,9},{9,8},{10,11... | collective-permute-start | bytes 1179656 | tf_op jit(solution)/shard_map/ppermute | solution.py:952
  45.2 14.6 %collective-permute-start.8 = (bf16[896,384]{1,0:T(8,128)(2,1)S(1)}, bf16[896,384]{1,0:T(8,128)(2,1)S(1)}, u32[]{:S(2)}, u32[]{:S(2)}) collective-permute-start(bf16[896,384]{1,0:T(8,128)(2,1)S(1)} %get-tuple-element.185), channel_id=1, source_target_pairs={{0,8},{1,17},{8,0},{9,25},{16,24},{17,1},{24,16},{25,9},{2,10},{3,... | collective-permute-start | bytes 2064392 | tf_op jit(solution)/shard_map/ppermute | solution.py:960
  47.1 12.7 %collective-permute-start.10 = (bf16[128,384]{1,0:T(8,128)(2,1)S(1)}, bf16[128,384]{1,0:T(8,128)(2,1)S(1)}, u32[]{:S(2)}, u32[]{:S(2)}) collective-permute-start(bf16[128,384]{1,0:T(8,128)(2,1)S(1)} %get-tuple-element.190), channel_id=1, source_target_pairs={{0,2},{2,0},{4,6},{6,4},{1,3},{3,1},{5,7},{7,5},{8,10},{10,8},{12,... | collective-permute-start | bytes 294920 | tf_op jit(solution)/shard_map/ppermute | solution.py:952
  47.1 12.6 %collective-permute-start.11 = (bf16[128,384]{1,0:T(8,128)(2,1)S(1)}, bf16[128,384]{1,0:T(8,128)(2,1)S(1)}, u32[]{:S(2)}, u32[]{:S(2)}) collective-permute-start(bf16[128,384]{1,0:T(8,128)(2,1)S(1)} %get-tuple-element.191), channel_id=1, source_target_pairs={{0,4},{2,6},{4,0},{6,2},{1,5},{3,7},{5,1},{7,3},{8,12},{10,14},{12... | collective-permute-start | bytes 294920 | tf_op jit(solution)/shard_map/ppermute | solution.py:952
  50.0 9.7 %collective-permute-start.12 = (bf16[128,384]{1,0:T(8,128)(2,1)S(1)}, bf16[128,384]{1,0:T(8,128)(2,1)S(1)}, u32[]{:S(2)}, u32[]{:S(2)}) collective-permute-start(bf16[128,384]{1,0:T(8,128)(2,1)S(1)} %get-tuple-element.192), channel_id=1, source_target_pairs={{0,6},{2,4},{4,2},{6,0},{1,7},{3,5},{5,3},{7,1},{8,14},{10,12},{12... | collective-permute-start | bytes 294920 | tf_op jit(solution)/shard_map/ppermute | solution.py:952
  51.5 7.5 %collective-permute-start.13 = (bf16[448,384]{1,0:T(8,128)(2,1)S(1)}, bf16[448,384]{1,0:T(8,128)(2,1)S(1)}, u32[]{:S(2)}, u32[]{:S(2)}) collective-permute-start(bf16[448,384]{1,0:T(8,128)(2,1)S(1)} %get-tuple-element.194), channel_id=1, source_target_pairs={{0,16},{1,9},{8,24},{9,1},{16,0},{17,25},{24,8},{25,17},{2,18},{3,... | collective-permute-start | bytes 1032200 | tf_op jit(solution)/shard_map/ppermute | solution.py:960
  61.5 11.3 %collective-permute-start.16 = (bf16[928,384]{1,0:T(8,128)(2,1)S(1)}, bf16[928,384]{1,0:T(8,128)(2,1)S(1)}, u32[]{:S(2)}, u32[]{:S(2)}) collective-permute-start(bf16[928,384]{1,0:T(8,128)(2,1)S(1)} %get-tuple-element.210), channel_id=1, source_target_pairs={{0,16},{1,9},{8,24},{9,1},{16,0},{17,25},{24,8},{25,17},{2,18},{3,... | collective-permute-start | bytes 2138120 | tf_op jit(solution)/shard_map/ppermute | solution.py:960
  63.3 10.8 %collective-permute-start.18 = (bf16[144,384]{1,0:T(8,128)(2,1)S(1)}, bf16[144,384]{1,0:T(8,128)(2,1)S(1)}, u32[]{:S(2)}, u32[]{:S(2)}) collective-permute-start(bf16[144,384]{1,0:T(8,128)(2,1)S(1)} %get-tuple-element.215), channel_id=1, source_target_pairs={{0,2},{2,0},{4,6},{6,4},{1,3},{3,1},{5,7},{7,5},{8,10},{10,8},{12,... | collective-permute-start | bytes 331784 | tf_op jit(solution)/shard_map/ppermute | solution.py:952
  63.3 13.7 %collective-permute-start.19 = (bf16[144,384]{1,0:T(8,128)(2,1)S(1)}, bf16[144,384]{1,0:T(8,128)(2,1)S(1)}, u32[]{:S(2)}, u32[]{:S(2)}) collective-permute-start(bf16[144,384]{1,0:T(8,128)(2,1)S(1)} %get-tuple-element.216), channel_id=1, source_target_pairs={{0,4},{2,6},{4,0},{6,2},{1,5},{3,7},{5,1},{7,3},{8,12},{10,14},{12... | collective-permute-start | bytes 331784 | tf_op jit(solution)/shard_map/ppermute | solution.py:952
  66.2 12.2 %collective-permute-start.20 = (bf16[144,384]{1,0:T(8,128)(2,1)S(1)}, bf16[144,384]{1,0:T(8,128)(2,1)S(1)}, u32[]{:S(2)}, u32[]{:S(2)}) collective-permute-start(bf16[144,384]{1,0:T(8,128)(2,1)S(1)} %get-tuple-element.217), channel_id=1, source_target_pairs={{0,6},{2,4},{4,2},{6,0},{1,7},{3,5},{5,3},{7,1},{8,14},{10,12},{12... | collective-permute-start | bytes 331784 | tf_op jit(solution)/shard_map/ppermute | solution.py:952
  72.9 5.9 %collective-permute-start.17 = (bf16[272,384]{1,0:T(8,128)(2,1)S(1)}, bf16[272,384]{1,0:T(8,128)(2,1)S(1)}, u32[]{:S(2)}, u32[]{:S(2)}) collective-permute-start(bf16[272,384]{1,0:T(8,128)(2,1)S(1)} %get-tuple-element.214), channel_id=1, source_target_pairs={{0,8},{1,17},{8,0},{9,25},{16,24},{17,1},{24,16},{25,9},{2,10},{3,... | collective-permute-start | bytes 626696 | tf_op jit(solution)/shard_map/ppermute | solution.py:960
  74.0 9.8 %collective-permute-start.26 = (bf16[112,384]{1,0:T(8,128)(2,1)S(1)}, bf16[112,384]{1,0:T(8,128)(2,1)S(1)}, u32[]{:S(2)}, u32[]{:S(2)}) collective-permute-start(bf16[112,384]{1,0:T(8,128)(2,1)S(1)} %get-tuple-element.227), channel_id=1, source_target_pairs={{0,4},{2,6},{4,0},{6,2},{1,5},{3,7},{5,1},{7,3},{8,12},{10,14},{12... | collective-permute-start | bytes 258056 | tf_op jit(solution)/shard_map/ppermute | solution.py:952
  77.0 9.6 %collective-permute-start.27 = (bf16[112,384]{1,0:T(8,128)(2,1)S(1)}, bf16[112,384]{1,0:T(8,128)(2,1)S(1)}, u32[]{:S(2)}, u32[]{:S(2)}) collective-permute-start(bf16[112,384]{1,0:T(8,128)(2,1)S(1)} %get-tuple-element.228), channel_id=1, source_target_pairs={{0,6},{2,4},{4,2},{6,0},{1,7},{3,5},{5,3},{7,1},{8,14},{10,12},{12... | collective-permute-start | bytes 258056 | tf_op jit(solution)/shard_map/ppermute | solution.py:952
  78.5 9.1 %collective-permute-start.24 = (bf16[112,384]{1,0:T(8,128)(2,1)S(1)}, bf16[112,384]{1,0:T(8,128)(2,1)S(1)}, u32[]{:S(2)}, u32[]{:S(2)}) collective-permute-start(bf16[112,384]{1,0:T(8,128)(2,1)S(1)} %get-tuple-element.218.refs_5_.refs_0_), channel_id=1, source_target_pairs={{0,1},{1,0},{2,3},{3,2},{4,5},{5,4},{6,7},{7,6},{8,9},{9,8},{10,11... | collective-permute-start | bytes 258056 | tf_op jit(solution)/shard_map/ppermute | solution.py:952
  78.8 10.2 %collective-permute-start.21 = (bf16[96,384]{1,0:T(8,128)(2,1)S(1)}, bf16[96,384]{1,0:T(8,128)(2,1)S(1)}, u32[]{:S(2)}, u32[]{:S(2)}) collective-permute-start(bf16[96,384]{1,0:T(8,128)(2,1)S(1)} %get-tuple-element.220), channel_id=1, source_target_pairs={{0,2},{2,0},{4,6},{6,4},{1,3},{3,1},{5,7},{7,5},{8,10},{10,8},{12,... | collective-permute-start | bytes 221192 | tf_op jit(solution)/shard_map/ppermute | solution.py:952
  79.5 11.0 %collective-permute-start.22 = (bf16[96,384]{1,0:T(8,128)(2,1)S(1)}, bf16[96,384]{1,0:T(8,128)(2,1)S(1)}, u32[]{:S(2)}, u32[]{:S(2)}) collective-permute-start(bf16[96,384]{1,0:T(8,128)(2,1)S(1)} %get-tuple-element.221), channel_id=1, source_target_pairs={{0,4},{2,6},{4,0},{6,2},{1,5},{3,7},{5,1},{7,3},{8,12},{10,14},{12... | collective-permute-start | bytes 221192 | tf_op jit(solution)/shard_map/ppermute | solution.py:952
  83.8 6.7 %collective-permute-start.23 = (bf16[96,384]{1,0:T(8,128)(2,1)S(1)}, bf16[96,384]{1,0:T(8,128)(2,1)S(1)}, u32[]{:S(2)}, u32[]{:S(2)}) collective-permute-start(bf16[96,384]{1,0:T(8,128)(2,1)S(1)} %get-tuple-element.222), channel_id=1, source_target_pairs={{0,6},{2,4},{4,2},{6,0},{1,7},{3,5},{5,3},{7,1},{8,14},{10,12},{12... | collective-permute-start | bytes 221192 | tf_op jit(solution)/shard_map/ppermute | solution.py:952
  86.6 5.6 %collective-permute-start.31 = (bf16[240,384]{1,0:T(8,128)(2,1)S(1)}, bf16[240,384]{1,0:T(8,128)(2,1)S(1)}, u32[]{:S(2)}, u32[]{:S(2)}) collective-permute-start(bf16[240,384]{1,0:T(8,128)(2,1)S(1)} %shard_map.302.refs_3_.refs_0_), channel_id=1, source_target_pairs={{0,8},{1,17},{8,0},{9,25},{16,24},{17,1},{24,16},{25,9},{2,10},{3,... | collective-permute-start | bytes 552968 | tf_op jit(solution)/shard_map/ppermute | solution.py:960
  92.2 7.9 %collective-permute-start.32 = (bf16[480,384]{1,0:T(8,128)(2,1)S(1)}, bf16[480,384]{1,0:T(8,128)(2,1)S(1)}, u32[]{:S(2)}, u32[]{:S(2)}) collective-permute-start(bf16[480,384]{1,0:T(8,128)(2,1)S(1)} %shard_map.308), channel_id=1, source_target_pairs={{0,16},{1,9},{8,24},{9,1},{16,0},{17,25},{24,8},{25,17},{2,18},{3,... | collective-permute-start | bytes 1105928 | tf_op jit(solution)/shard_map/ppermute | solution.py:960
  95.0 6.3 %collective-permute-start.30 = (bf16[96,384]{1,0:T(8,128)(2,1)S(1)}, bf16[96,384]{1,0:T(8,128)(2,1)S(1)}, u32[]{:S(2)}, u32[]{:S(2)}) collective-permute-start(bf16[96,384]{1,0:T(8,128)(2,1)S(1)} %shard_map.306.refs_6_), channel_id=1, source_target_pairs={{0,16},{1,9},{8,24},{9,1},{16,0},{17,25},{24,8},{25,17},{2,18},{3,... | collective-permute-start | bytes 221192 | tf_op jit(solution)/shard_map/ppermute | solution.py:960
  (17 other events, 85.7 us)

commit v5 on v4

--- a/solution.py
+++ b/solution.py
@@ -19,7 +19,7 @@
 ROWS = 12
 ROW_SHARED, ROW_ACT, ROW_COND, ROW_HID, ROW_FEAT = 5, 6, 7, 8, 9
 US = {
-    "cond": 5, "embed": 2, "block": 6, "turn": 9, "back": 20, "middle": 4, "last": 4, "early": 0.05, "pack": 0.05, "join": 0.05, "U12": 0.05, "F3": 0.05, "unpack": 0.05, "sums": 5, "spread": 0.05,
+    "cond": 5, "embed": 2, "block": 6, "turn": 9, "back": 20, "middle": 4, "last": 4, "early": 0.05, "pack": 0.05, "join": 0.05, "U12": 0.05, "F3": 0.05, "unpack": 0.05, "relay": 0.05, "sums": 5, "spread": 0.05,
     "A1": 0.05, "A2": 0.05, "A2b": 0.05, "A3": 0.05, "A3b": 0.05, "A4": 30, "A4b": 0.05, "A5": 0.05, "A6": 0.05, "S1": 0.05, "U2": 3,
     "U1": 1,
 }
@@ -395,8 +395,8 @@
 ):
     z, _, _ = places()
     offset = offsets[z]
-    for k, tile in enumerate((t0, t1, t2, t3)):
-        tiles[k] = tile[...]
+    for i, tile in enumerate((t0, t1, t2, t3)):
+        tiles[-i % 4] = tile[...]
     count = tiles.shape[0]
     even = jnp.concatenate([tiles[z ^ t, 0] for t in range(count)], axis=0).astype(F32)
     odd = jnp.concatenate([tiles[z ^ t, 1] for t in range(count)], axis=0).astype(F32)
@@ -538,12 +538,12 @@
 ):
     width = dq.shape[-1]
     block = width // 8
-    size = 2 * block + 16
+    size = 2 * block
     rows[...] = jnp.zeros_like(rows)
     m = mods
     grad = qkv_backward(
         state1[...], middle_grad1[...], dq, dkv, dkvr, m, 1, qkv, gproj, keep, send,
-        ((0, 16, unit_place, size, 2 * block), (16, block, chip_place, block - 16, 16 * size)), rows,
+        ((0, block, chip_place, block, 16 * size),), rows,
     )
     middle_grad[...] = mlp_backward(
         grad, middle[...], branch[...], m, 0, gp, act, up, down, keep, send, size, 0,
@@ -624,7 +624,7 @@
     at = slice(2 * ROWS, 2 * ROWS + sums)
     total[...] = mine[at] + other[at]
     half = sums // 2
-    return padded(four[2 * c], four[2 * c + 1], total[pl.ds(pl.multiple_of(c * half, 8), half), :])
+    return four[2 * c], four[2 * c + 1], total[pl.ds(pl.multiple_of(c * half, 8), half), :]
 
 
 def first_body(keep, recv, keep_out, table, send):
@@ -649,7 +649,7 @@
 
 
 def first_chip_body(
-    sums, keep, pair, recv, z0, z1, z2, z3, four, total
+    sums, keep, pair, recv, tiles, z0, z1, z2, z3, four, total
 ):
     z, _, _ = places()
     size = keep.shape[0]
@@ -657,33 +657,25 @@
     rows = half_of_four(pair[...].astype(F32), recv[size:].astype(F32), sums, 0, four, total)
     for k, out in enumerate((z0, z1, z2, z3)):
         out[0:unit] = keep[rows_at(z ^ k, unit)] + recv[rows_at(z ^ k, unit)]
-        out[unit:] = rows
-
-
-def unit1_body(sums, o0, o1, o2, o3, unit, pack):
+        out[unit:] = padded(*rows, tiles[k])
+
+
+def unit1_body(sums, o0, o1, o2, o3, unit, pack, tiles):
     ones = (o0, o1, o2, o3)
     unit[...] = chip_sum(ones, slice(0, unit.shape[0])).astype(BF16)
     chip_rows(sums, ones, unit.shape[0], pack)
+    for i, one in enumerate(ones):
+        tiles[-i % 4] = one[unit.shape[0] + 32 :].astype(F32)[8:]
 
 
 def pack_body(preds, lgrads, tiles):
     z, _, _ = places()
     tok = preds.shape[1] // 4
-    tiles[:, :, 256:] = jnp.zeros((4, 16, 128), BF16)
     for k in range(4):
         cut = pl.ds(pl.multiple_of((z ^ k) * tok, 8), tok)
-        parts = [lgrads[0, cut, :], lgrads[1, cut, :]]
-        leading = [part.astype(BF16).astype(F32) for part in parts]
-        chans = lgrads.shape[2]
-        latents = jnp.concatenate(
-            [
-                packed_tile(leading, chans, 8),
-                packed_tile([a - b for a, b in zip(parts, leading)], chans, 8),
-            ],
-            axis=1,
-        )
+        latents = packed_tile([lgrads[0, cut, :], lgrads[1, cut, :]], lgrads.shape[2], 8)
         predicted = packed_tile([preds[0, cut, :], preds[1, cut, :]], preds.shape[2], 8)
-        tiles[k, :, 0:256] = jnp.concatenate([latents, predicted], axis=0).astype(BF16)
+        tiles[k] = jnp.concatenate([latents, predicted], axis=1)
 
 
 def chip_sum(parts, at):
@@ -737,17 +729,15 @@
     send[half3 + halfb :] = pair
 
 
-def fifth_body(sums, keep3, keepb, pair, recv, tiles, z0, z1, z2, z3, unitb, four, total):
+def fifth_body(sums, keep3, keepb, pair, recv, z0, z1, z2, z3, unitb, four, total):
     z, _, _ = places()
     size3, sizeb = keep3.shape[0], keepb.shape[0]
     unit3 = size3 // 4
     other = recv[size3 + sizeb :].astype(F32)
-    rows = half_of_four(pair[...].astype(F32), other, sums, 1, four, total)
-    end = unit3 + rows.shape[0]
+    rows = padded(*half_of_four(pair[...].astype(F32), other, sums, 1, four, total))
     for k, out in enumerate((z0, z1, z2, z3)):
         out[0:unit3] = keep3[rows_at(z ^ k, unit3)] + recv[rows_at(z ^ k, unit3)]
-        out[unit3:end] = rows
-        out[end:] = tiles[k]
+        out[unit3:] = rows
     unitb[...] = keepb[...] + recv[size3 : size3 + sizeb]
 
 
@@ -770,13 +760,11 @@
     send[size:] = near[...]
 
 
-def unit3_body(sums, z0, z1, z2, z3, unit, pack, tiles):
+def unit3_body(sums, z0, z1, z2, z3, unit, pack):
     parts = (z0, z1, z2, z3)
     size = unit.shape[0]
     unit[...] = chip_sum(parts, slice(0, size)).astype(BF16)
     chip_rows(sums, parts, size, pack)
-    for k, part in enumerate(parts):
-        tiles[k] = part[size + 32 :]
 
 
 def silu_slope(values):
@@ -872,11 +860,10 @@
     _, out_ch, height, wide = prediction.shape
     lat_ch = latent_grad.shape[1]
     for k in range(4):
-        tile = tiles[k].astype(F32)
-        image = unpacked_tile(tile[8:16, 0:256].astype(BF16), out_ch, height, wide)
+        split = tiles.shape[2] // 3
+        image = unpacked_tile(tiles[k, :, split:].astype(BF16), out_ch, height, wide)
         prediction[z ^ k] = image.astype(BF16).reshape(out_ch, height, wide)
-        image = unpacked_tile(tile[0:8, 0:128].astype(BF16), lat_ch, height, wide)
-        image = image + unpacked_tile(tile[0:8, 128:256].astype(BF16), lat_ch, height, wide)
+        image = unpacked_tile(tiles[k, :, :split].astype(BF16), lat_ch, height, wide)
         latent_grad[z ^ k] = image.reshape(lat_ch, height, wide)
     for copy in copies:
         copy.wait()
@@ -1025,7 +1012,7 @@
     )
 
     def along_z(parts):
-        return [parts[0]] + [swap(parts[k], "rows", k) for k in range(1, n_rows)]
+        return [parts[0]] + [swap(parts[k], "rows", k) for k in reversed(range(1, n_rows))]
 
     def both_halves(pack):
         if lax.axis_size("wide") > 4:
@@ -1139,7 +1126,7 @@
         0, q0, kv0, kv0p, probs0, attended0, attn_out0, mgrad0, proj0, after=None
     )
     dkvr0 = swap(dkvs0, "cols", 1)
-    alpha, beta = 2 * block + 16, block - 16
+    alpha, beta = 2 * block, block
     send_rows = 4 * alpha + 2 * beta + 8 * block + 32
     whole_2, whole_r = keep2, recv2
     keep2, send2 = kernel_call(
@@ -1180,15 +1167,14 @@
     )
     recv3 = swap(send3, "cols", 1)
     (tiles,) = kernel_call(
-        pack_body, [("p", preds), ("p", lgrads)], [((4, 16, width), BF16)], us=US["pack"]
+        pack_body, [("p", preds), ("p", lgrads)], [((4, 8, width), F32)], us=US["pack"]
     )
     ones = kernel_call(
         partial(first_chip_body, sums_a),
-        [("p", keep1), ("p", pair1), ("v", recv1)],
+        [("p", keep1), ("p", pair1), ("v", recv1), ("p", tiles)],
         [((2 * block + 48, width), BF16)] * 4,
         [pltpu.VMEM((4, ROWS, width), F32), pltpu.VMEM((sums_a, width), F32)],
         us=US["A2b"],
-        after=tiles,
     )
     chips = ones[0]
     ones = along_z(ones)
@@ -1223,18 +1209,18 @@
     recv = swap_by_core(send, FIRST)
     twos = along_z(twos)
     pack = (8 * ROWS + 16, width)
-    unit1, pack_a = kernel_call(
+    unit1, pack_a, tiles = kernel_call(
         partial(unit1_body, sums_a // 2),
         [("p", ones[0])] + [("v", one) for one in ones[1:]],
-        [((2 * block, width), BF16), (pack, BF16)],
+        [((2 * block, width), BF16), (pack, BF16), ((4, 8, width), F32)],
         us=US["U1"],
         after=pair3,
     )
     packs = both_halves(pack_a)
     *threes, unitb = kernel_call(
         partial(fifth_body, sums_b),
-        [("p", keep3), ("p", keepb), ("p", pair3), ("v", recv), ("p", tiles)],
-        [((block + 32 + 16, width), BF16)] * 4 + [((beta, width), BF16)],
+        [("p", keep3), ("p", keepb), ("p", pair3), ("v", recv)],
+        [((block + 32, width), BF16)] * 4 + [((beta, width), BF16)],
         [pltpu.VMEM((4, ROWS, width), F32), pltpu.VMEM((sums_b, width), F32)],
         us=US["A6"],
         after=pack_a,
@@ -1263,10 +1249,10 @@
         us=US["early"],
         after=unit2,
     )
-    unit3, pack_b, tiles = kernel_call(
+    unit3, pack_b = kernel_call(
         partial(unit3_body, sums_b // 2),
         [("p", threes[0])] + [("v", three) for three in threes[1:]],
-        [((block, width), BF16), (pack, BF16), ((4, 16, width), BF16)],
+        [((block, width), BF16), (pack, BF16)],
         us=US["U2"],
         after=early[0],
     )
@@ -1277,7 +1263,7 @@
         [("p", unit2), ("v", near2)],
         [((2 * unit2.shape[0], width), BF16)],
         us=US["join"],
-        after=tiles,
+        after=pack_b,
     )
     far2 = swap_by_core(send2, SECOND)
     packs = both_halves(pack_b)

time: 102 us -> 99.3 us (0.974)
  starting transfers between devices: 37.6 us -> 35.8 us
    ppermute x24, starting transfers between devices: 26.3 us -> 24.2 us  [swap(): return lax.ppermute(value, axis, [(i, i ^ bit) for i in range(count)])]
  transfers between devices with their start and end apart: 33 -> 33, of which waited for: 12 -> 9; matrix products, arithmetic and copies ran while one was open for 0% -> 0% of each run, Pallas kernels for 26% -> 26%
where the time goes in v5:
time: 99.3 us; the launch traced here: 99.2 us
  Pallas kernels  43.8 us (44%)
  starting transfers between devices  35.8 us (36%)
  waiting for transfers between devices  17.5 us (18%)
  between operations  1.87 us (2%)
    pallas_call x29, Pallas kernels, kernel_call(): pl.pallas_call(kernel, in_specs=specs, out_specs=[pl.BlockSpec(memory_spa...  43.8 us
    ppermute x24, starting transfers between devices, swap(): return lax.ppermute(value, axis, [(i, i ^ bit) for i in range(count)])  24.2 us
    ppermute x9, starting transfers between devices, swap_by_core(): return lax.ppermute(value, ('wide', 'cols'), pairs)  11.6 us
    ppermute x24, waiting for transfers between devices, swap(): return lax.ppermute(value, axis, [(i, i ^ bit) for i in range(count)])  9.39 us
    ppermute x9, waiting for transfers between devices, swap_by_core(): return lax.ppermute(value, ('wide', 'cols'), pairs)  8.11 us
  transfers between devices with their start and end apart: 33, of which 9 were waited for; matrix products, arithmetic and copies ran while one was open for 0% of the time, Pallas kernels for 26%

profile of v5, /device:TPU:0, one launch (start us, length us, event | category | flops | bytes accessed | tf_op | source)
XLA Modules:
  0.0 99.2 jit_solution(9954096268988772065)
XLA Ops:
  0.7 2.0 %shard_map.282 = (bf16[2,64,24]{2,1,0:T(8,128)(2,1)S(1)}, bf16[2,64,24]{2,1,0:T(8,128)(2,1)S(1)}, bf16[2,64,24]{2,1,0:T(8,128)(2,1)S(1)}, bf16[2,64,24]{2,1,0:T(8,128)(2,1)S(1)}) custom-call(bf16[4,4,16,16]{3,2,1,0:T(8,128)(2,1)} %refs_0_.5, bf16[4,8,16,16]{3,2,1,0:T(8,128)(2,1)} %refs_1_.3), custom_call_target="tpu_custom_call" | custom-call | flops 1500000000 | bytes 1000000 | tf_op jit(solution)/shard_map/pallas_call | solution.py:86
  2.8 5.1 %collective-permute-start = (bf16[2,64,24]{2,1,0:T(8,128)(2,1)S(1)}, bf16[2,64,24]{2,1,0:T(8,128)(2,1)S(1)}, u32[]{:S(2)}, u32[]{:S(2)}) collective-permute-start(bf16[2,64,24]{2,1,0:T(8,128)(2,1)S(1)} %get-tuple-element.139), channel_id=1, source_target_pairs={{0,6},{2,4},{4,2},{6,0},{1,7},{3,5},{5,3},{7,1},{8,14},{10,12},{12... | collective-permute-start | bytes 18440 | tf_op jit(solution)/shard_map/ppermute | solution.py:939
  8.7 4.0 %shard_map.283 = (f32[3,8,384]{2,1,0:T(8,128)S(1)}, f32[8,384]{1,0:T(8,128)S(1)}, bf16[384,32]{1,0:T(8,128)(2,1)S(1)}, f32[256,384]{1,0:T(8,128)S(1)}, bf16[384,...) custom-call(s32[4]{0:T(128)S(1)} %copy-done.3, ...), custom_call_target="tpu_custom_call" | custom-call | flops 7500000256 | bytes 5000000 | tf_op jit(solution)/shard_map/pallas_call | solution.py:86
  14.3 1.7 %collective-permute-done.3.refs_3_.refs_2_ = bf16[256,768]{1,0:T(8,128)(2,1)S(1)} collective-permute-done((bf16[256,768]{1,0:T(8,128)(2,1)S(1)}, bf16[256,768]{1,0:T(8,128)(2,1)S(1)}, u32[]{:S(2)}, u32[]{:S(2)}) %collective-permute-start.3) | collective-permute-done | bytes 393248 | tf_op jit(solution)/shard_map/ppermute | solution.py:939
  16.0 5.9 %shard_map.285 = (f32[256,384]{1,0:T(8,128)S(1)}, bf16[256,384]{1,0:T(8,128)(2,1)S(1)}, bf16[256,768]{1,0:T(8,128)(2,1)S(1)}, bf16[6,2,256,256]{3,2,1,0:T(8,128)...) custom-call(f32[256,384]{1,0:T(8,128)S(1)} %get-tuple-element.145.re, ...), custom_call_target="tpu_custom_call" | custom-call | flops 8999999488 | bytes 6000000 | tf_op jit(solution)/shard_map/pallas_call | solution.py:86
  23.7 7.4 %shard_map.286 = (bf16[6,2,256,256]{3,2,1,0:T(8,128)(2,1)S(1)}, bf16[256,384]{1,0:T(8,128)(2,1)S(1)}, bf16[256,384]{1,0:T(8,128)(2,1)S(1)}, f32[256,384]{1,0:T(8...) custom-call(s32[4]{0:T(128)S(1)} %copy-done.5, ...), custom_call_target="tpu_custom_call" | custom-call | flops 13500000256 | bytes 9000000 | tf_op jit(solution)/shard_map/pallas_call | solution.py:86
  31.3 3.2 %shard_map.287 = (bf16[256,384]{1,0:T(8,128)(2,1)S(1)}, bf16[256,768]{1,0:T(8,128)(2,1)S(1)}, bf16[384,384]{1,0:T(8,128)(2,1)S(1)}, bf16[256,768]{1,0:T(8,128)(2,1)S(1)}, f32[8,384]{1,0:T(8,128)S(1)}) custom-call(bf16[256,384]{1,0:T(8,128)(2,1)S(1)} %get-tuple-element.152.refs_3_.refs_0_, bf16[256,768]{1,0:T(8,128)(2,1)S(1)} %get-tuple-element.153.refs_4_.refs_1_, ...), custom_call_target="tpu_custom_call" | custom-call | flops 30000001024 | bytes 20000000 | tf_op jit(solution)/shard_map/pallas_call | solution.py:86
  35.1 1.7 %collective-permute-start.6 = (bf16[816,384]{1,0:T(8,128)(2,1)S(1)}, bf16[816,384]{1,0:T(8,128)(2,1)S(1)}, u32[]{:S(2)}, u32[]{:S(2)}) collective-permute-start(bf16[816,384]{1,0:T(8,128)(2,1)S(1)} %get-tuple-element.169), channel_id=1, source_target_pairs={{0,8},{1,17},{8,0},{9,25},{16,24},{17,1},{24,16},{25,9},{2,10},{3,... | collective-permute-start | bytes 1880072 | tf_op jit(solution)/shard_map/ppermute | solution.py:947
  36.8 3.1 %shard_map.289 = (f32[256,384]{1,0:T(8,128)S(1)}, bf16[2304,384]{1,0:T(8,128)(2,1)S(1)}, bf16[2304,384]{1,0:T(8,128)(2,1)S(1)}, f32[8,384]{1,0:T(8,128)S(1)}) custom-call(f32[256,384]{1,0:T(8,128)S(1)} %get-tuple-element.151.refs_2_.refs_0_, f32[256,384]{1,0:T(8,128)S(1)} %get-tuple-element.165.refs_6_.refs_1_, ...), custom_call_target="tpu_custom_call" | custom-call | flops 6000000000 | bytes 4000000 | tf_op jit(solution)/shard_map/pallas_call | solution.py:86
  40.0 3.2 %shard_map.290 = (bf16[256,384]{1,0:T(8,128)(2,1)S(1)}, bf16[256,768]{1,0:T(8,128)(2,1)S(1)}, bf16[384,384]{1,0:T(8,128)(2,1)S(1)}, bf16[256,768]{1,0:T(8,128)(2,1)S(1)}, f32[8,384]{1,0:T(8,128)S(1)}) custom-call(bf16[256,384]{1,0:T(8,128)(2,1)S(1)} %get-tuple-element.146.refs_1_.refs_0_, bf16[256,768]{1,0:T(8,128)(2,1)S(1)} %get-tuple-element.147.refs_2_.refs_1_, ...), custom_call_target="tpu_custom_call" | custom-call | flops 30000001024 | bytes 20000000 | tf_op jit(solution)/shard_map/pallas_call | solution.py:86
  45.7 3.8 %collective-permute-start.15 = (bf16[192,384]{1,0:T(8,128)(2,1)S(1)}, bf16[192,384]{1,0:T(8,128)(2,1)S(1)}, u32[]{:S(2)}, u32[]{:S(2)}) collective-permute-start(bf16[192,384]{1,0:T(8,128)(2,1)S(1)} %get-tuple-element.203), channel_id=1, source_target_pairs={{0,6},{2,4},{4,2},{6,0},{1,7},{3,5},{5,3},{7,1},{8,14},{10,12},{12... | collective-permute-start | bytes 442376 | tf_op jit(solution)/shard_map/ppermute | solution.py:939
  50.1 1.7 %collective-permute-start.9 = (bf16[448,384]{1,0:T(8,128)(2,1)S(1)}, bf16[448,384]{1,0:T(8,128)(2,1)S(1)}, u32[]{:S(2)}, u32[]{:S(2)}) collective-permute-start(bf16[448,384]{1,0:T(8,128)(2,1)S(1)} %get-tuple-element.189), channel_id=1, source_target_pairs={{0,16},{1,9},{8,24},{9,1},{16,0},{17,25},{24,8},{25,17},{2,18},{3,... | collective-permute-start | bytes 1032200 | tf_op jit(solution)/shard_map/ppermute | solution.py:947
  51.8 2.1 %shard_map.294 = (bf16[800,384]{1,0:T(8,128)(2,1)S(1)}, bf16[800,384]{1,0:T(8,128)(2,1)S(1)}, f32[2,256,8]{2,1,0:T(8,128)S(1)}) custom-call(s32[4]{0:T(128)S(1)} %copy-done.5, f32[256,384]{1,0:T(8,128)S(1)} %get-tuple-element.145.refs_0_.refs_1_, f32[256,384]{1,0:T(8,128)S(1)} %get-tuple-element.184.refs_6_.refs_2_, ...), custom_call_target="tpu_custom_call" | custom-call | flops 6000000000 | bytes 4000000 | tf_op jit(solution)/shard_map/pallas_call | solution.py:86
  55.2 2.2 %collective-permute-done.9.refs_2_ = bf16[448,384]{1,0:T(8,128)(2,1)S(1)} collective-permute-done((bf16[448,384]{1,0:T(8,128)(2,1)S(1)}, bf16[448,384]{1,0:T(8,128)(2,1)S(1)}, u32[]{:S(2)}, u32[]{:S(2)}) %collective-permute-start.9) | collective-permute-done | bytes 344096 | tf_op jit(solution)/shard_map/ppermute | solution.py:947
  57.6 3.9 %collective-permute-done.16.refs_4_ = bf16[192,384]{1,0:T(8,128)(2,1)S(1)} collective-permute-done((bf16[192,384]{1,0:T(8,128)(2,1)S(1)}, bf16[192,384]{1,0:T(8,128)(2,1)S(1)}, u32[]{:S(2)}, u32[]{:S(2)}) %collective-permute-start.16) | collective-permute-done | bytes 147488 | tf_op jit(solution)/shard_map/ppermute | solution.py:939
  63.1 2.4 %collective-permute-start.11 = (bf16[144,384]{1,0:T(8,128)(2,1)S(1)}, bf16[144,384]{1,0:T(8,128)(2,1)S(1)}, u32[]{:S(2)}, u32[]{:S(2)}) collective-permute-start(bf16[144,384]{1,0:T(8,128)(2,1)S(1)} %get-tuple-element.199), channel_id=1, source_target_pairs={{0,6},{2,4},{4,2},{6,0},{1,7},{3,5},{5,3},{7,1},{8,14},{10,12},{12... | collective-permute-start | bytes 331784 | tf_op jit(solution)/shard_map/ppermute | solution.py:939
  65.4 2.0 %collective-permute-start.13 = (bf16[144,384]{1,0:T(8,128)(2,1)S(1)}, bf16[144,384]{1,0:T(8,128)(2,1)S(1)}, u32[]{:S(2)}, u32[]{:S(2)}) collective-permute-start(bf16[144,384]{1,0:T(8,128)(2,1)S(1)} %get-tuple-element.201), channel_id=1, source_target_pairs={{0,2},{2,0},{4,6},{6,4},{1,3},{3,1},{5,7},{7,5},{8,10},{10,8},{12,... | collective-permute-start | bytes 331784 | tf_op jit(solution)/shard_map/ppermute | solution.py:939
  67.5 5.4 %collective-permute-done.19.refs_4_ = bf16[896,384]{1,0:T(8,128)(2,1)S(1)} collective-permute-done((bf16[896,384]{1,0:T(8,128)(2,1)S(1)}, bf16[896,384]{1,0:T(8,128)(2,1)S(1)}, u32[]{:S(2)}, u32[]{:S(2)}) %collective-permute-start.19) | collective-permute-done | bytes 688160 | tf_op jit(solution)/shard_map/ppermute | solution.py:947
  74.4 2.4 %collective-permute-start.25 = (bf16[96,384]{1,0:T(8,128)(2,1)S(1)}, bf16[96,384]{1,0:T(8,128)(2,1)S(1)}, u32[]{:S(2)}, u32[]{:S(2)}) collective-permute-start(bf16[96,384]{1,0:T(8,128)(2,1)S(1)} %get-tuple-element.227), channel_id=1, source_target_pairs={{0,6},{2,4},{4,2},{6,0},{1,7},{3,5},{5,3},{7,1},{8,14},{10,12},{12... | collective-permute-start | bytes 221192 | tf_op jit(solution)/shard_map/ppermute | solution.py:939
  77.0 2.1 %collective-permute-start.27 = (bf16[96,384]{1,0:T(8,128)(2,1)S(1)}, bf16[96,384]{1,0:T(8,128)(2,1)S(1)}, u32[]{:S(2)}, u32[]{:S(2)}) collective-permute-start(bf16[96,384]{1,0:T(8,128)(2,1)S(1)} %get-tuple-element.229), channel_id=1, source_target_pairs={{0,2},{2,0},{4,6},{6,4},{1,3},{3,1},{5,7},{7,5},{8,10},{10,8},{12,... | collective-permute-start | bytes 221192 | tf_op jit(solution)/shard_map/ppermute | solution.py:939
  79.1 2.4 %collective-permute-start.21 = (bf16[80,384]{1,0:T(8,128)(2,1)S(1)}, bf16[80,384]{1,0:T(8,128)(2,1)S(1)}, u32[]{:S(2)}, u32[]{:S(2)}) collective-permute-start(bf16[80,384]{1,0:T(8,128)(2,1)S(1)} %get-tuple-element.221), channel_id=1, source_target_pairs={{0,6},{2,4},{4,2},{6,0},{1,7},{3,5},{5,3},{7,1},{8,14},{10,12},{12... | collective-permute-start | bytes 184328 | tf_op jit(solution)/shard_map/ppermute | solution.py:939
  86.4 1.6 %collective-permute-done.22.refs_2_ = bf16[80,384]{1,0:T(8,128)(2,1)S(1)} collective-permute-done((bf16[80,384]{1,0:T(8,128)(2,1)S(1)}, bf16[80,384]{1,0:T(8,128)(2,1)S(1)}, u32[]{:S(2)}, u32[]{:S(2)}) %collective-permute-start.22) | collective-permute-done | bytes 61472 | tf_op jit(solution)/shard_map/ppermute | solution.py:939
  90.6 2.6 %shard_map.305 = (f32[256,384]{1,0:T(8,128)S(1)}, f32[384,384]{1,0:T(8,128)S(1)}, f32[1001,384]{1,0:T(8,128)S(1)}, f32[2,48,2304]{2,1,0:T(8,128)S(1)}, f32[16,384]{1,0:T(8,128)S(1)}) custom-call(bf16[112,384]{1,0:T(8,128)(2,1)S(1)} %get-tuple-element.232.refs_0_.refs_2_, bf16[112,384]{1,0:T(8,128)(2,1)S(1)} %collective-permute-done.28.refs_1_, ...), custom_call_target="tpu_custom_call" | custom-call | flops 7500000256 | bytes 5000000 | tf_op jit(solution)/shard_map/pallas_call | solution.py:86
  94.1 2.9 %shard_map.307 = (f32[256,384]{1,0:T(8,128)}, f32[384,384]{1,0:T(8,128)}, f32[1001,384]{1,0:T(8,128)}, f32[2,48,2304]{2,1,0:T(8,128)}, f32[16,384]{1,0:T(8,128)}...) custom-call(f32[4,8,384]{2,1,0:T(8,128)S(1)} %get-tuple-element.215.refs_0_, ...), custom_call_target="tpu_custom_call" | custom-call | flops 75000000 | bytes 50000 | tf_op jit(solution)/shard_map/pallas_call | solution.py:86
  (88 shorter events, 22.6 us)
Async XLA Ops:
  2.8 10.0 %collective-permute-start = (bf16[2,64,24]{2,1,0:T(8,128)(2,1)S(1)}, bf16[2,64,24]{2,1,0:T(8,128)(2,1)S(1)}, u32[]{:S(2)}, u32[]{:S(2)}) collective-permute-start(bf16[2,64,24]{2,1,0:T(8,128)(2,1)S(1)} %get-tuple-element.139), channel_id=1, source_target_pairs={{0,6},{2,4},{4,2},{6,0},{1,7},{3,5},{5,3},{7,1},{8,14},{10,12},{12... | collective-permute-start | bytes 18440 | tf_op jit(solution)/shard_map/ppermute | solution.py:939
  35.1 10.3 %collective-permute-start.6 = (bf16[816,384]{1,0:T(8,128)(2,1)S(1)}, bf16[816,384]{1,0:T(8,128)(2,1)S(1)}, u32[]{:S(2)}, u32[]{:S(2)}) collective-permute-start(bf16[816,384]{1,0:T(8,128)(2,1)S(1)} %get-tuple-element.169), channel_id=1, source_target_pairs={{0,8},{1,17},{8,0},{9,25},{16,24},{17,1},{24,16},{25,9},{2,10},{3,... | collective-permute-start | bytes 1880072 | tf_op jit(solution)/shard_map/ppermute | solution.py:947
  43.1 7.0 %collective-permute-start.10 = (bf16[256,768]{1,0:T(8,128)(2,1)S(1)}, bf16[256,768]{1,0:T(8,128)(2,1)S(1)}, u32[]{:S(2)}, u32[]{:S(2)}) collective-permute-start(bf16[256,768]{1,0:T(8,128)(2,1)S(1)} %get-tuple-element.193), channel_id=1, source_target_pairs={{0,1},{1,0},{2,3},{3,2},{4,5},{5,4},{6,7},{7,6},{8,9},{9,8},{10,11... | collective-permute-start | bytes 1179656 | tf_op jit(solution)/shard_map/ppermute | solution.py:939
  43.9 17.6 %collective-permute-start.14 = (bf16[768,384]{1,0:T(8,128)(2,1)S(1)}, bf16[768,384]{1,0:T(8,128)(2,1)S(1)}, u32[]{:S(2)}, u32[]{:S(2)}) collective-permute-start(bf16[768,384]{1,0:T(8,128)(2,1)S(1)} %get-tuple-element.202), channel_id=1, source_target_pairs={{0,8},{1,17},{8,0},{9,25},{16,24},{17,1},{24,16},{25,9},{2,10},{3,... | collective-permute-start | bytes 1769480 | tf_op jit(solution)/shard_map/ppermute | solution.py:947
  45.7 11.9 %collective-permute-start.15 = (bf16[192,384]{1,0:T(8,128)(2,1)S(1)}, bf16[192,384]{1,0:T(8,128)(2,1)S(1)}, u32[]{:S(2)}, u32[]{:S(2)}) collective-permute-start(bf16[192,384]{1,0:T(8,128)(2,1)S(1)} %get-tuple-element.203), channel_id=1, source_target_pairs={{0,6},{2,4},{4,2},{6,0},{1,7},{3,5},{5,3},{7,1},{8,14},{10,12},{12... | collective-permute-start | bytes 442376 | tf_op jit(solution)/shard_map/ppermute | solution.py:939
  49.5 12.0 %collective-permute-start.16 = (bf16[192,384]{1,0:T(8,128)(2,1)S(1)}, bf16[192,384]{1,0:T(8,128)(2,1)S(1)}, u32[]{:S(2)}, u32[]{:S(2)}) collective-permute-start(bf16[192,384]{1,0:T(8,128)(2,1)S(1)} %get-tuple-element.204), channel_id=1, source_target_pairs={{0,4},{2,6},{4,0},{6,2},{1,5},{3,7},{5,1},{7,3},{8,12},{10,14},{12... | collective-permute-start | bytes 442376 | tf_op jit(solution)/shard_map/ppermute | solution.py:939
  49.5 12.0 %collective-permute-start.17 = (bf16[192,384]{1,0:T(8,128)(2,1)S(1)}, bf16[192,384]{1,0:T(8,128)(2,1)S(1)}, u32[]{:S(2)}, u32[]{:S(2)}) collective-permute-start(bf16[192,384]{1,0:T(8,128)(2,1)S(1)} %get-tuple-element.205), channel_id=1, source_target_pairs={{0,2},{2,0},{4,6},{6,4},{1,3},{3,1},{5,7},{7,5},{8,10},{10,8},{12,... | collective-permute-start | bytes 442376 | tf_op jit(solution)/shard_map/ppermute | solution.py:939
  50.1 7.3 %collective-permute-start.9 = (bf16[448,384]{1,0:T(8,128)(2,1)S(1)}, bf16[448,384]{1,0:T(8,128)(2,1)S(1)}, u32[]{:S(2)}, u32[]{:S(2)}) collective-permute-start(bf16[448,384]{1,0:T(8,128)(2,1)S(1)} %get-tuple-element.189), channel_id=1, source_target_pairs={{0,16},{1,9},{8,24},{9,1},{16,0},{17,25},{24,8},{25,17},{2,18},{3,... | collective-permute-start | bytes 1032200 | tf_op jit(solution)/shard_map/ppermute | solution.py:947
  61.9 11.0 %collective-permute-start.19 = (bf16[896,384]{1,0:T(8,128)(2,1)S(1)}, bf16[896,384]{1,0:T(8,128)(2,1)S(1)}, u32[]{:S(2)}, u32[]{:S(2)}) collective-permute-start(bf16[896,384]{1,0:T(8,128)(2,1)S(1)} %get-tuple-element.213), channel_id=1, source_target_pairs={{0,16},{1,9},{8,24},{9,1},{16,0},{17,25},{24,8},{25,17},{2,18},{3,... | collective-permute-start | bytes 2064392 | tf_op jit(solution)/shard_map/ppermute | solution.py:947
  63.1 13.8 %collective-permute-start.11 = (bf16[144,384]{1,0:T(8,128)(2,1)S(1)}, bf16[144,384]{1,0:T(8,128)(2,1)S(1)}, u32[]{:S(2)}, u32[]{:S(2)}) collective-permute-start(bf16[144,384]{1,0:T(8,128)(2,1)S(1)} %get-tuple-element.199), channel_id=1, source_target_pairs={{0,6},{2,4},{4,2},{6,0},{1,7},{3,5},{5,3},{7,1},{8,14},{10,12},{12... | collective-permute-start | bytes 331784 | tf_op jit(solution)/shard_map/ppermute | solution.py:939
  65.4 11.4 %collective-permute-start.12 = (bf16[144,384]{1,0:T(8,128)(2,1)S(1)}, bf16[144,384]{1,0:T(8,128)(2,1)S(1)}, u32[]{:S(2)}, u32[]{:S(2)}) collective-permute-start(bf16[144,384]{1,0:T(8,128)(2,1)S(1)} %get-tuple-element.200), channel_id=1, source_target_pairs={{0,4},{2,6},{4,0},{6,2},{1,5},{3,7},{5,1},{7,3},{8,12},{10,14},{12... | collective-permute-start | bytes 331784 | tf_op jit(solution)/shard_map/ppermute | solution.py:939
  65.4 11.4 %collective-permute-start.13 = (bf16[144,384]{1,0:T(8,128)(2,1)S(1)}, bf16[144,384]{1,0:T(8,128)(2,1)S(1)}, u32[]{:S(2)}, u32[]{:S(2)}) collective-permute-start(bf16[144,384]{1,0:T(8,128)(2,1)S(1)} %get-tuple-element.201), channel_id=1, source_target_pairs={{0,2},{2,0},{4,6},{6,4},{1,3},{3,1},{5,7},{7,5},{8,10},{10,8},{12,... | collective-permute-start | bytes 331784 | tf_op jit(solution)/shard_map/ppermute | solution.py:939
  73.0 6.0 %collective-permute-start.20 = (bf16[288,384]{1,0:T(8,128)(2,1)S(1)}, bf16[288,384]{1,0:T(8,128)(2,1)S(1)}, u32[]{:S(2)}, u32[]{:S(2)}) collective-permute-start(bf16[288,384]{1,0:T(8,128)(2,1)S(1)} %get-tuple-element.218), channel_id=1, source_target_pairs={{0,8},{1,17},{8,0},{9,25},{16,24},{17,1},{24,16},{25,9},{2,10},{3,... | collective-permute-start | bytes 663560 | tf_op jit(solution)/shard_map/ppermute | solution.py:947
  74.4 7.1 %collective-permute-start.25 = (bf16[96,384]{1,0:T(8,128)(2,1)S(1)}, bf16[96,384]{1,0:T(8,128)(2,1)S(1)}, u32[]{:S(2)}, u32[]{:S(2)}) collective-permute-start(bf16[96,384]{1,0:T(8,128)(2,1)S(1)} %get-tuple-element.227), channel_id=1, source_target_pairs={{0,6},{2,4},{4,2},{6,0},{1,7},{3,5},{5,3},{7,1},{8,14},{10,12},{12... | collective-permute-start | bytes 221192 | tf_op jit(solution)/shard_map/ppermute | solution.py:939
  76.8 5.9 %collective-permute-start.26 = (bf16[96,384]{1,0:T(8,128)(2,1)S(1)}, bf16[96,384]{1,0:T(8,128)(2,1)S(1)}, u32[]{:S(2)}, u32[]{:S(2)}) collective-permute-start(bf16[96,384]{1,0:T(8,128)(2,1)S(1)} %get-tuple-element.228), channel_id=1, source_target_pairs={{0,4},{2,6},{4,0},{6,2},{1,5},{3,7},{5,1},{7,3},{8,12},{10,14},{12... | collective-permute-start | bytes 221192 | tf_op jit(solution)/shard_map/ppermute | solution.py:939
  76.9 8.1 %collective-permute-start.24 = (bf16[112,384]{1,0:T(8,128)(2,1)S(1)}, bf16[112,384]{1,0:T(8,128)(2,1)S(1)}, u32[]{:S(2)}, u32[]{:S(2)}) collective-permute-start(bf16[112,384]{1,0:T(8,128)(2,1)S(1)} %get-tuple-element.219.refs_4_.refs_0_), channel_id=1, source_target_pairs={{0,1},{1,0},{2,3},{3,2},{4,5},{5,4},{6,7},{7,6},{8,9},{9,8},{10,11... | collective-permute-start | bytes 258056 | tf_op jit(solution)/shard_map/ppermute | solution.py:939
  77.0 6.6 %collective-permute-start.27 = (bf16[96,384]{1,0:T(8,128)(2,1)S(1)}, bf16[96,384]{1,0:T(8,128)(2,1)S(1)}, u32[]{:S(2)}, u32[]{:S(2)}) collective-permute-start(bf16[96,384]{1,0:T(8,128)(2,1)S(1)} %get-tuple-element.229), channel_id=1, source_target_pairs={{0,2},{2,0},{4,6},{6,4},{1,3},{3,1},{5,7},{7,5},{8,10},{10,8},{12,... | collective-permute-start | bytes 221192 | tf_op jit(solution)/shard_map/ppermute | solution.py:939
  79.1 7.3 %collective-permute-start.21 = (bf16[80,384]{1,0:T(8,128)(2,1)S(1)}, bf16[80,384]{1,0:T(8,128)(2,1)S(1)}, u32[]{:S(2)}, u32[]{:S(2)}) collective-permute-start(bf16[80,384]{1,0:T(8,128)(2,1)S(1)} %get-tuple-element.221), channel_id=1, source_target_pairs={{0,6},{2,4},{4,2},{6,0},{1,7},{3,5},{5,3},{7,1},{8,14},{10,12},{12... | collective-permute-start | bytes 184328 | tf_op jit(solution)/shard_map/ppermute | solution.py:939
  81.5 6.5 %collective-permute-start.22 = (bf16[80,384]{1,0:T(8,128)(2,1)S(1)}, bf16[80,384]{1,0:T(8,128)(2,1)S(1)}, u32[]{:S(2)}, u32[]{:S(2)}) collective-permute-start(bf16[80,384]{1,0:T(8,128)(2,1)S(1)} %get-tuple-element.222), channel_id=1, source_target_pairs={{0,4},{2,6},{4,0},{6,2},{1,5},{3,7},{5,1},{7,3},{8,12},{10,14},{12... | collective-permute-start | bytes 184328 | tf_op jit(solution)/shard_map/ppermute | solution.py:939
  82.7 5.4 %collective-permute-start.23 = (bf16[80,384]{1,0:T(8,128)(2,1)S(1)}, bf16[80,384]{1,0:T(8,128)(2,1)S(1)}, u32[]{:S(2)}, u32[]{:S(2)}) collective-permute-start(bf16[80,384]{1,0:T(8,128)(2,1)S(1)} %get-tuple-element.223), channel_id=1, source_target_pairs={{0,2},{2,0},{4,6},{6,4},{1,3},{3,1},{5,7},{7,5},{8,10},{10,8},{12,... | collective-permute-start | bytes 184328 | tf_op jit(solution)/shard_map/ppermute | solution.py:939
  83.6 5.6 %collective-permute-start.31 = (bf16[240,384]{1,0:T(8,128)(2,1)S(1)}, bf16[240,384]{1,0:T(8,128)(2,1)S(1)}, u32[]{:S(2)}, u32[]{:S(2)}) collective-permute-start(bf16[240,384]{1,0:T(8,128)(2,1)S(1)} %shard_map.302.refs_3_.refs_0_), channel_id=1, source_target_pairs={{0,8},{1,17},{8,0},{9,25},{16,24},{17,1},{24,16},{25,9},{2,10},{3,... | collective-permute-start | bytes 552968 | tf_op jit(solution)/shard_map/ppermute | solution.py:947
  88.2 5.0 %collective-permute-start.29 = (bf16[48,384]{1,0:T(8,128)(2,1)S(1)}, bf16[48,384]{1,0:T(8,128)(2,1)S(1)}, u32[]{:S(2)}, u32[]{:S(2)}) collective-permute-start(bf16[48,384]{1,0:T(8,128)(2,1)S(1)} %get-tuple-element.246.refs_0_), channel_id=1, source_target_pairs={{0,8},{1,17},{8,0},{9,25},{16,24},{17,1},{24,16},{25,9},{2,10},{3,... | collective-permute-start | bytes 110600 | tf_op jit(solution)/shard_map/ppermute | solution.py:947
  89.3 7.7 %collective-permute-start.32 = (bf16[480,384]{1,0:T(8,128)(2,1)S(1)}, bf16[480,384]{1,0:T(8,128)(2,1)S(1)}, u32[]{:S(2)}, u32[]{:S(2)}) collective-permute-start(bf16[480,384]{1,0:T(8,128)(2,1)S(1)} %shard_map.308), channel_id=1, source_target_pairs={{0,16},{1,9},{8,24},{9,1},{16,0},{17,25},{24,8},{25,17},{2,18},{3,... | collective-permute-start | bytes 1105928 | tf_op jit(solution)/shard_map/ppermute | solution.py:947
  93.3 4.9 %collective-permute-start.30 = (bf16[96,384]{1,0:T(8,128)(2,1)S(1)}, bf16[96,384]{1,0:T(8,128)(2,1)S(1)}, u32[]{:S(2)}, u32[]{:S(2)}) collective-permute-start(bf16[96,384]{1,0:T(8,128)(2,1)S(1)} %shard_map.306.refs_6_), channel_id=1, source_target_pairs={{0,16},{1,9},{8,24},{9,1},{16,0},{17,25},{24,8},{25,17},{2,18},{3,... | collective-permute-start | bytes 221192 | tf_op jit(solution)/shard_map/ppermute | solution.py:947
  (17 other events, 85.9 us)

commit v6 on v5

--- a/solution.py
+++ b/solution.py
@@ -294,6 +294,7 @@
 
 
 CHUNK = 768
+BACK_CHUNK = 1536
 
 
 def mlp_forward(middle, mods, layer, up, down, gp, act):
@@ -334,8 +335,8 @@
     inner_t = (normed * scale + mods[layer, 3:4]).astype(BF16).T
     branch_grad = (mods[layer, 5:6] * grad).astype(BF16)
     inner_grad = None
-    for start in range(0, up.shape[1], CHUNK):
-        at = slice(start, start + CHUNK)
+    for start in range(0, up.shape[1], BACK_CHUNK):
+        at = slice(start, start + BACK_CHUNK)
         act_grad = dot_nt(branch_grad, down[at, :])
         hidden_grad = (act_grad * gp[:, at].astype(F32)).astype(BF16)
         low[:, at] = hidden_grad

time: 99.3 us -> 99.4 us (level)
  no operation moved by 1% of the time
where the time goes in v6:
time: 99.4 us; the launch traced here: 99.2 us
  Pallas kernels  43.8 us (44%)
  starting transfers between devices  35.8 us (36%)
  waiting for transfers between devices  17.5 us (18%)
  between operations  1.87 us (2%)
    pallas_call x29, Pallas kernels, kernel_call(): pl.pallas_call(kernel, in_specs=specs, out_specs=[pl.BlockSpec(memory_spa...  43.8 us
    ppermute x24, starting transfers between devices, swap(): return lax.ppermute(value, axis, [(i, i ^ bit) for i in range(count)])  24.2 us
    ppermute x9, starting transfers between devices, swap_by_core(): return lax.ppermute(value, ('wide', 'cols'), pairs)  11.7 us
    ppermute x24, waiting for transfers between devices, swap(): return lax.ppermute(value, axis, [(i, i ^ bit) for i in range(count)])  9.38 us
    ppermute x9, waiting for transfers between devices, swap_by_core(): return lax.ppermute(value, ('wide', 'cols'), pairs)  8.11 us
  transfers between devices with their start and end apart: 33, of which 9 were waited for; matrix products, arithmetic and copies ran while one was open for 0% of the time, Pallas kernels for 26%

profile of v6, /device:TPU:0, one launch (start us, length us, event | category | flops | bytes accessed | tf_op | source)
XLA Modules:
  0.0 99.2 jit_solution(848742858717989270)
XLA Ops:
  0.7 2.0 %shard_map.282 = (bf16[2,64,24]{2,1,0:T(8,128)(2,1)S(1)}, bf16[2,64,24]{2,1,0:T(8,128)(2,1)S(1)}, bf16[2,64,24]{2,1,0:T(8,128)(2,1)S(1)}, bf16[2,64,24]{2,1,0:T(8,128)(2,1)S(1)}) custom-call(bf16[4,4,16,16]{3,2,1,0:T(8,128)(2,1)} %refs_0_.5, bf16[4,8,16,16]{3,2,1,0:T(8,128)(2,1)} %refs_1_.3), custom_call_target="tpu_custom_call" | custom-call | flops 1500000000 | bytes 1000000 | tf_op jit(solution)/shard_map/pallas_call | solution.py:86
  2.8 5.1 %collective-permute-start = (bf16[2,64,24]{2,1,0:T(8,128)(2,1)S(1)}, bf16[2,64,24]{2,1,0:T(8,128)(2,1)S(1)}, u32[]{:S(2)}, u32[]{:S(2)}) collective-permute-start(bf16[2,64,24]{2,1,0:T(8,128)(2,1)S(1)} %get-tuple-element.139), channel_id=1, source_target_pairs={{0,6},{2,4},{4,2},{6,0},{1,7},{3,5},{5,3},{7,1},{8,14},{10,12},{12... | collective-permute-start | bytes 18440 | tf_op jit(solution)/shard_map/ppermute | solution.py:940
  8.7 4.0 %shard_map.283 = (f32[3,8,384]{2,1,0:T(8,128)S(1)}, f32[8,384]{1,0:T(8,128)S(1)}, bf16[384,32]{1,0:T(8,128)(2,1)S(1)}, f32[256,384]{1,0:T(8,128)S(1)}, bf16[384,...) custom-call(s32[4]{0:T(128)S(1)} %copy-done.3, ...), custom_call_target="tpu_custom_call" | custom-call | flops 7500000256 | bytes 5000000 | tf_op jit(solution)/shard_map/pallas_call | solution.py:86
  14.3 1.7 %collective-permute-done.3.refs_3_.refs_2_ = bf16[256,768]{1,0:T(8,128)(2,1)S(1)} collective-permute-done((bf16[256,768]{1,0:T(8,128)(2,1)S(1)}, bf16[256,768]{1,0:T(8,128)(2,1)S(1)}, u32[]{:S(2)}, u32[]{:S(2)}) %collective-permute-start.3) | collective-permute-done | bytes 393248 | tf_op jit(solution)/shard_map/ppermute | solution.py:940
  16.0 5.9 %shard_map.285 = (f32[256,384]{1,0:T(8,128)S(1)}, bf16[256,384]{1,0:T(8,128)(2,1)S(1)}, bf16[256,768]{1,0:T(8,128)(2,1)S(1)}, bf16[6,2,256,256]{3,2,1,0:T(8,128)...) custom-call(f32[256,384]{1,0:T(8,128)S(1)} %get-tuple-element.145.re, ...), custom_call_target="tpu_custom_call" | custom-call | flops 8999999488 | bytes 6000000 | tf_op jit(solution)/shard_map/pallas_call | solution.py:86
  23.7 7.4 %shard_map.286 = (bf16[6,2,256,256]{3,2,1,0:T(8,128)(2,1)S(1)}, bf16[256,384]{1,0:T(8,128)(2,1)S(1)}, bf16[256,384]{1,0:T(8,128)(2,1)S(1)}, f32[256,384]{1,0:T(8...) custom-call(s32[4]{0:T(128)S(1)} %copy-done.5, ...), custom_call_target="tpu_custom_call" | custom-call | flops 13500000256 | bytes 9000000 | tf_op jit(solution)/shard_map/pallas_call | solution.py:86
  31.3 3.2 %shard_map.287 = (bf16[256,384]{1,0:T(8,128)(2,1)S(1)}, bf16[256,768]{1,0:T(8,128)(2,1)S(1)}, bf16[384,384]{1,0:T(8,128)(2,1)S(1)}, bf16[256,768]{1,0:T(8,128)(2,1)S(1)}, f32[8,384]{1,0:T(8,128)S(1)}) custom-call(bf16[256,384]{1,0:T(8,128)(2,1)S(1)} %get-tuple-element.152.refs_3_.refs_0_, bf16[256,768]{1,0:T(8,128)(2,1)S(1)} %get-tuple-element.153.refs_4_.refs_1_, ...), custom_call_target="tpu_custom_call" | custom-call | flops 30000001024 | bytes 20000000 | tf_op jit(solution)/shard_map/pallas_call | solution.py:86
  35.1 1.7 %collective-permute-start.6 = (bf16[816,384]{1,0:T(8,128)(2,1)S(1)}, bf16[816,384]{1,0:T(8,128)(2,1)S(1)}, u32[]{:S(2)}, u32[]{:S(2)}) collective-permute-start(bf16[816,384]{1,0:T(8,128)(2,1)S(1)} %get-tuple-element.169), channel_id=1, source_target_pairs={{0,8},{1,17},{8,0},{9,25},{16,24},{17,1},{24,16},{25,9},{2,10},{3,... | collective-permute-start | bytes 1880072 | tf_op jit(solution)/shard_map/ppermute | solution.py:948
  36.8 3.1 %shard_map.289 = (f32[256,384]{1,0:T(8,128)S(1)}, bf16[2304,384]{1,0:T(8,128)(2,1)S(1)}, bf16[2304,384]{1,0:T(8,128)(2,1)S(1)}, f32[8,384]{1,0:T(8,128)S(1)}) custom-call(f32[256,384]{1,0:T(8,128)S(1)} %get-tuple-element.151.refs_2_.refs_0_, f32[256,384]{1,0:T(8,128)S(1)} %get-tuple-element.165.refs_6_.refs_1_, ...), custom_call_target="tpu_custom_call" | custom-call | flops 6000000000 | bytes 4000000 | tf_op jit(solution)/shard_map/pallas_call | solution.py:86
  40.0 3.2 %shard_map.290 = (bf16[256,384]{1,0:T(8,128)(2,1)S(1)}, bf16[256,768]{1,0:T(8,128)(2,1)S(1)}, bf16[384,384]{1,0:T(8,128)(2,1)S(1)}, bf16[256,768]{1,0:T(8,128)(2,1)S(1)}, f32[8,384]{1,0:T(8,128)S(1)}) custom-call(bf16[256,384]{1,0:T(8,128)(2,1)S(1)} %get-tuple-element.146.refs_1_.refs_0_, bf16[256,768]{1,0:T(8,128)(2,1)S(1)} %get-tuple-element.147.refs_2_.refs_1_, ...), custom_call_target="tpu_custom_call" | custom-call | flops 30000001024 | bytes 20000000 | tf_op jit(solution)/shard_map/pallas_call | solution.py:86
  45.7 3.8 %collective-permute-start.15 = (bf16[192,384]{1,0:T(8,128)(2,1)S(1)}, bf16[192,384]{1,0:T(8,128)(2,1)S(1)}, u32[]{:S(2)}, u32[]{:S(2)}) collective-permute-start(bf16[192,384]{1,0:T(8,128)(2,1)S(1)} %get-tuple-element.203), channel_id=1, source_target_pairs={{0,6},{2,4},{4,2},{6,0},{1,7},{3,5},{5,3},{7,1},{8,14},{10,12},{12... | collective-permute-start | bytes 442376 | tf_op jit(solution)/shard_map/ppermute | solution.py:940
  50.1 1.7 %collective-permute-start.9 = (bf16[448,384]{1,0:T(8,128)(2,1)S(1)}, bf16[448,384]{1,0:T(8,128)(2,1)S(1)}, u32[]{:S(2)}, u32[]{:S(2)}) collective-permute-start(bf16[448,384]{1,0:T(8,128)(2,1)S(1)} %get-tuple-element.189), channel_id=1, source_target_pairs={{0,16},{1,9},{8,24},{9,1},{16,0},{17,25},{24,8},{25,17},{2,18},{3,... | collective-permute-start | bytes 1032200 | tf_op jit(solution)/shard_map/ppermute | solution.py:948
  51.8 2.1 %shard_map.294 = (bf16[800,384]{1,0:T(8,128)(2,1)S(1)}, bf16[800,384]{1,0:T(8,128)(2,1)S(1)}, f32[2,256,8]{2,1,0:T(8,128)S(1)}) custom-call(s32[4]{0:T(128)S(1)} %copy-done.5, f32[256,384]{1,0:T(8,128)S(1)} %get-tuple-element.145.refs_0_.refs_1_, f32[256,384]{1,0:T(8,128)S(1)} %get-tuple-element.184.refs_6_.refs_2_, ...), custom_call_target="tpu_custom_call" | custom-call | flops 6000000000 | bytes 4000000 | tf_op jit(solution)/shard_map/pallas_call | solution.py:86
  55.2 2.2 %collective-permute-done.9.refs_2_ = bf16[448,384]{1,0:T(8,128)(2,1)S(1)} collective-permute-done((bf16[448,384]{1,0:T(8,128)(2,1)S(1)}, bf16[448,384]{1,0:T(8,128)(2,1)S(1)}, u32[]{:S(2)}, u32[]{:S(2)}) %collective-permute-start.9) | collective-permute-done | bytes 344096 | tf_op jit(solution)/shard_map/ppermute | solution.py:948
  57.6 3.9 %collective-permute-done.16.refs_4_ = bf16[192,384]{1,0:T(8,128)(2,1)S(1)} collective-permute-done((bf16[192,384]{1,0:T(8,128)(2,1)S(1)}, bf16[192,384]{1,0:T(8,128)(2,1)S(1)}, u32[]{:S(2)}, u32[]{:S(2)}) %collective-permute-start.16) | collective-permute-done | bytes 147488 | tf_op jit(solution)/shard_map/ppermute | solution.py:940
  63.1 2.4 %collective-permute-start.11 = (bf16[144,384]{1,0:T(8,128)(2,1)S(1)}, bf16[144,384]{1,0:T(8,128)(2,1)S(1)}, u32[]{:S(2)}, u32[]{:S(2)}) collective-permute-start(bf16[144,384]{1,0:T(8,128)(2,1)S(1)} %get-tuple-element.199), channel_id=1, source_target_pairs={{0,6},{2,4},{4,2},{6,0},{1,7},{3,5},{5,3},{7,1},{8,14},{10,12},{12... | collective-permute-start | bytes 331784 | tf_op jit(solution)/shard_map/ppermute | solution.py:940
  65.4 2.0 %collective-permute-start.13 = (bf16[144,384]{1,0:T(8,128)(2,1)S(1)}, bf16[144,384]{1,0:T(8,128)(2,1)S(1)}, u32[]{:S(2)}, u32[]{:S(2)}) collective-permute-start(bf16[144,384]{1,0:T(8,128)(2,1)S(1)} %get-tuple-element.201), channel_id=1, source_target_pairs={{0,2},{2,0},{4,6},{6,4},{1,3},{3,1},{5,7},{7,5},{8,10},{10,8},{12,... | collective-permute-start | bytes 331784 | tf_op jit(solution)/shard_map/ppermute | solution.py:940
  67.5 5.4 %collective-permute-done.19.refs_4_ = bf16[896,384]{1,0:T(8,128)(2,1)S(1)} collective-permute-done((bf16[896,384]{1,0:T(8,128)(2,1)S(1)}, bf16[896,384]{1,0:T(8,128)(2,1)S(1)}, u32[]{:S(2)}, u32[]{:S(2)}) %collective-permute-start.19) | collective-permute-done | bytes 688160 | tf_op jit(solution)/shard_map/ppermute | solution.py:948
  74.5 2.4 %collective-permute-start.25 = (bf16[96,384]{1,0:T(8,128)(2,1)S(1)}, bf16[96,384]{1,0:T(8,128)(2,1)S(1)}, u32[]{:S(2)}, u32[]{:S(2)}) collective-permute-start(bf16[96,384]{1,0:T(8,128)(2,1)S(1)} %get-tuple-element.227), channel_id=1, source_target_pairs={{0,6},{2,4},{4,2},{6,0},{1,7},{3,5},{5,3},{7,1},{8,14},{10,12},{12... | collective-permute-start | bytes 221192 | tf_op jit(solution)/shard_map/ppermute | solution.py:940
  77.0 2.1 %collective-permute-start.27 = (bf16[96,384]{1,0:T(8,128)(2,1)S(1)}, bf16[96,384]{1,0:T(8,128)(2,1)S(1)}, u32[]{:S(2)}, u32[]{:S(2)}) collective-permute-start(bf16[96,384]{1,0:T(8,128)(2,1)S(1)} %get-tuple-element.229), channel_id=1, source_target_pairs={{0,2},{2,0},{4,6},{6,4},{1,3},{3,1},{5,7},{7,5},{8,10},{10,8},{12,... | collective-permute-start | bytes 221192 | tf_op jit(solution)/shard_map/ppermute | solution.py:940
  79.1 2.5 %collective-permute-start.21 = (bf16[80,384]{1,0:T(8,128)(2,1)S(1)}, bf16[80,384]{1,0:T(8,128)(2,1)S(1)}, u32[]{:S(2)}, u32[]{:S(2)}) collective-permute-start(bf16[80,384]{1,0:T(8,128)(2,1)S(1)} %get-tuple-element.221), channel_id=1, source_target_pairs={{0,6},{2,4},{4,2},{6,0},{1,7},{3,5},{5,3},{7,1},{8,14},{10,12},{12... | collective-permute-start | bytes 184328 | tf_op jit(solution)/shard_map/ppermute | solution.py:940
  86.5 1.6 %collective-permute-done.22.refs_2_ = bf16[80,384]{1,0:T(8,128)(2,1)S(1)} collective-permute-done((bf16[80,384]{1,0:T(8,128)(2,1)S(1)}, bf16[80,384]{1,0:T(8,128)(2,1)S(1)}, u32[]{:S(2)}, u32[]{:S(2)}) %collective-permute-start.22) | collective-permute-done | bytes 61472 | tf_op jit(solution)/shard_map/ppermute | solution.py:940
  90.6 2.6 %shard_map.305 = (f32[256,384]{1,0:T(8,128)S(1)}, f32[384,384]{1,0:T(8,128)S(1)}, f32[1001,384]{1,0:T(8,128)S(1)}, f32[2,48,2304]{2,1,0:T(8,128)S(1)}, f32[16,384]{1,0:T(8,128)S(1)}) custom-call(bf16[112,384]{1,0:T(8,128)(2,1)S(1)} %get-tuple-element.232.refs_0_.refs_2_, bf16[112,384]{1,0:T(8,128)(2,1)S(1)} %collective-permute-done.28.refs_1_, ...), custom_call_target="tpu_custom_call" | custom-call | flops 7500000256 | bytes 5000000 | tf_op jit(solution)/shard_map/pallas_call | solution.py:86
  94.1 2.9 %shard_map.307 = (f32[256,384]{1,0:T(8,128)}, f32[384,384]{1,0:T(8,128)}, f32[1001,384]{1,0:T(8,128)}, f32[2,48,2304]{2,1,0:T(8,128)}, f32[16,384]{1,0:T(8,128)}...) custom-call(f32[4,8,384]{2,1,0:T(8,128)S(1)} %get-tuple-element.215.refs_0_, ...), custom_call_target="tpu_custom_call" | custom-call | flops 75000000 | bytes 50000 | tf_op jit(solution)/shard_map/pallas_call | solution.py:86
  (88 shorter events, 22.6 us)
Async XLA Ops:
  2.8 10.0 %collective-permute-start = (bf16[2,64,24]{2,1,0:T(8,128)(2,1)S(1)}, bf16[2,64,24]{2,1,0:T(8,128)(2,1)S(1)}, u32[]{:S(2)}, u32[]{:S(2)}) collective-permute-start(bf16[2,64,24]{2,1,0:T(8,128)(2,1)S(1)} %get-tuple-element.139), channel_id=1, source_target_pairs={{0,6},{2,4},{4,2},{6,0},{1,7},{3,5},{5,3},{7,1},{8,14},{10,12},{12... | collective-permute-start | bytes 18440 | tf_op jit(solution)/shard_map/ppermute | solution.py:940
  35.1 10.3 %collective-permute-start.6 = (bf16[816,384]{1,0:T(8,128)(2,1)S(1)}, bf16[816,384]{1,0:T(8,128)(2,1)S(1)}, u32[]{:S(2)}, u32[]{:S(2)}) collective-permute-start(bf16[816,384]{1,0:T(8,128)(2,1)S(1)} %get-tuple-element.169), channel_id=1, source_target_pairs={{0,8},{1,17},{8,0},{9,25},{16,24},{17,1},{24,16},{25,9},{2,10},{3,... | collective-permute-start | bytes 1880072 | tf_op jit(solution)/shard_map/ppermute | solution.py:948
  43.2 7.0 %collective-permute-start.10 = (bf16[256,768]{1,0:T(8,128)(2,1)S(1)}, bf16[256,768]{1,0:T(8,128)(2,1)S(1)}, u32[]{:S(2)}, u32[]{:S(2)}) collective-permute-start(bf16[256,768]{1,0:T(8,128)(2,1)S(1)} %get-tuple-element.193), channel_id=1, source_target_pairs={{0,1},{1,0},{2,3},{3,2},{4,5},{5,4},{6,7},{7,6},{8,9},{9,8},{10,11... | collective-permute-start | bytes 1179656 | tf_op jit(solution)/shard_map/ppermute | solution.py:940
  43.9 17.6 %collective-permute-start.14 = (bf16[768,384]{1,0:T(8,128)(2,1)S(1)}, bf16[768,384]{1,0:T(8,128)(2,1)S(1)}, u32[]{:S(2)}, u32[]{:S(2)}) collective-permute-start(bf16[768,384]{1,0:T(8,128)(2,1)S(1)} %get-tuple-element.202), channel_id=1, source_target_pairs={{0,8},{1,17},{8,0},{9,25},{16,24},{17,1},{24,16},{25,9},{2,10},{3,... | collective-permute-start | bytes 1769480 | tf_op jit(solution)/shard_map/ppermute | solution.py:948
  45.7 11.9 %collective-permute-start.15 = (bf16[192,384]{1,0:T(8,128)(2,1)S(1)}, bf16[192,384]{1,0:T(8,128)(2,1)S(1)}, u32[]{:S(2)}, u32[]{:S(2)}) collective-permute-start(bf16[192,384]{1,0:T(8,128)(2,1)S(1)} %get-tuple-element.203), channel_id=1, source_target_pairs={{0,6},{2,4},{4,2},{6,0},{1,7},{3,5},{5,3},{7,1},{8,14},{10,12},{12... | collective-permute-start | bytes 442376 | tf_op jit(solution)/shard_map/ppermute | solution.py:940
  49.5 12.0 %collective-permute-start.16 = (bf16[192,384]{1,0:T(8,128)(2,1)S(1)}, bf16[192,384]{1,0:T(8,128)(2,1)S(1)}, u32[]{:S(2)}, u32[]{:S(2)}) collective-permute-start(bf16[192,384]{1,0:T(8,128)(2,1)S(1)} %get-tuple-element.204), channel_id=1, source_target_pairs={{0,4},{2,6},{4,0},{6,2},{1,5},{3,7},{5,1},{7,3},{8,12},{10,14},{12... | collective-permute-start | bytes 442376 | tf_op jit(solution)/shard_map/ppermute | solution.py:940
  49.5 12.0 %collective-permute-start.17 = (bf16[192,384]{1,0:T(8,128)(2,1)S(1)}, bf16[192,384]{1,0:T(8,128)(2,1)S(1)}, u32[]{:S(2)}, u32[]{:S(2)}) collective-permute-start(bf16[192,384]{1,0:T(8,128)(2,1)S(1)} %get-tuple-element.205), channel_id=1, source_target_pairs={{0,2},{2,0},{4,6},{6,4},{1,3},{3,1},{5,7},{7,5},{8,10},{10,8},{12,... | collective-permute-start | bytes 442376 | tf_op jit(solution)/shard_map/ppermute | solution.py:940
  50.1 7.3 %collective-permute-start.9 = (bf16[448,384]{1,0:T(8,128)(2,1)S(1)}, bf16[448,384]{1,0:T(8,128)(2,1)S(1)}, u32[]{:S(2)}, u32[]{:S(2)}) collective-permute-start(bf16[448,384]{1,0:T(8,128)(2,1)S(1)} %get-tuple-element.189), channel_id=1, source_target_pairs={{0,16},{1,9},{8,24},{9,1},{16,0},{17,25},{24,8},{25,17},{2,18},{3,... | collective-permute-start | bytes 1032200 | tf_op jit(solution)/shard_map/ppermute | solution.py:948
  61.9 11.0 %collective-permute-start.19 = (bf16[896,384]{1,0:T(8,128)(2,1)S(1)}, bf16[896,384]{1,0:T(8,128)(2,1)S(1)}, u32[]{:S(2)}, u32[]{:S(2)}) collective-permute-start(bf16[896,384]{1,0:T(8,128)(2,1)S(1)} %get-tuple-element.213), channel_id=1, source_target_pairs={{0,16},{1,9},{8,24},{9,1},{16,0},{17,25},{24,8},{25,17},{2,18},{3,... | collective-permute-start | bytes 2064392 | tf_op jit(solution)/shard_map/ppermute | solution.py:948
  63.1 13.8 %collective-permute-start.11 = (bf16[144,384]{1,0:T(8,128)(2,1)S(1)}, bf16[144,384]{1,0:T(8,128)(2,1)S(1)}, u32[]{:S(2)}, u32[]{:S(2)}) collective-permute-start(bf16[144,384]{1,0:T(8,128)(2,1)S(1)} %get-tuple-element.199), channel_id=1, source_target_pairs={{0,6},{2,4},{4,2},{6,0},{1,7},{3,5},{5,3},{7,1},{8,14},{10,12},{12... | collective-permute-start | bytes 331784 | tf_op jit(solution)/shard_map/ppermute | solution.py:940
  65.4 11.4 %collective-permute-start.12 = (bf16[144,384]{1,0:T(8,128)(2,1)S(1)}, bf16[144,384]{1,0:T(8,128)(2,1)S(1)}, u32[]{:S(2)}, u32[]{:S(2)}) collective-permute-start(bf16[144,384]{1,0:T(8,128)(2,1)S(1)} %get-tuple-element.200), channel_id=1, source_target_pairs={{0,4},{2,6},{4,0},{6,2},{1,5},{3,7},{5,1},{7,3},{8,12},{10,14},{12... | collective-permute-start | bytes 331784 | tf_op jit(solution)/shard_map/ppermute | solution.py:940
  65.4 11.4 %collective-permute-start.13 = (bf16[144,384]{1,0:T(8,128)(2,1)S(1)}, bf16[144,384]{1,0:T(8,128)(2,1)S(1)}, u32[]{:S(2)}, u32[]{:S(2)}) collective-permute-start(bf16[144,384]{1,0:T(8,128)(2,1)S(1)} %get-tuple-element.201), channel_id=1, source_target_pairs={{0,2},{2,0},{4,6},{6,4},{1,3},{3,1},{5,7},{7,5},{8,10},{10,8},{12,... | collective-permute-start | bytes 331784 | tf_op jit(solution)/shard_map/ppermute | solution.py:940
  73.0 6.0 %collective-permute-start.20 = (bf16[288,384]{1,0:T(8,128)(2,1)S(1)}, bf16[288,384]{1,0:T(8,128)(2,1)S(1)}, u32[]{:S(2)}, u32[]{:S(2)}) collective-permute-start(bf16[288,384]{1,0:T(8,128)(2,1)S(1)} %get-tuple-element.218), channel_id=1, source_target_pairs={{0,8},{1,17},{8,0},{9,25},{16,24},{17,1},{24,16},{25,9},{2,10},{3,... | collective-permute-start | bytes 663560 | tf_op jit(solution)/shard_map/ppermute | solution.py:948
  74.5 7.1 %collective-permute-start.25 = (bf16[96,384]{1,0:T(8,128)(2,1)S(1)}, bf16[96,384]{1,0:T(8,128)(2,1)S(1)}, u32[]{:S(2)}, u32[]{:S(2)}) collective-permute-start(bf16[96,384]{1,0:T(8,128)(2,1)S(1)} %get-tuple-element.227), channel_id=1, source_target_pairs={{0,6},{2,4},{4,2},{6,0},{1,7},{3,5},{5,3},{7,1},{8,14},{10,12},{12... | collective-permute-start | bytes 221192 | tf_op jit(solution)/shard_map/ppermute | solution.py:940
  76.8 5.8 %collective-permute-start.26 = (bf16[96,384]{1,0:T(8,128)(2,1)S(1)}, bf16[96,384]{1,0:T(8,128)(2,1)S(1)}, u32[]{:S(2)}, u32[]{:S(2)}) collective-permute-start(bf16[96,384]{1,0:T(8,128)(2,1)S(1)} %get-tuple-element.228), channel_id=1, source_target_pairs={{0,4},{2,6},{4,0},{6,2},{1,5},{3,7},{5,1},{7,3},{8,12},{10,14},{12... | collective-permute-start | bytes 221192 | tf_op jit(solution)/shard_map/ppermute | solution.py:940
  76.9 8.1 %collective-permute-start.24 = (bf16[112,384]{1,0:T(8,128)(2,1)S(1)}, bf16[112,384]{1,0:T(8,128)(2,1)S(1)}, u32[]{:S(2)}, u32[]{:S(2)}) collective-permute-start(bf16[112,384]{1,0:T(8,128)(2,1)S(1)} %get-tuple-element.219.refs_4_.refs_0_), channel_id=1, source_target_pairs={{0,1},{1,0},{2,3},{3,2},{4,5},{5,4},{6,7},{7,6},{8,9},{9,8},{10,11... | collective-permute-start | bytes 258056 | tf_op jit(solution)/shard_map/ppermute | solution.py:940
  77.0 6.6 %collective-permute-start.27 = (bf16[96,384]{1,0:T(8,128)(2,1)S(1)}, bf16[96,384]{1,0:T(8,128)(2,1)S(1)}, u32[]{:S(2)}, u32[]{:S(2)}) collective-permute-start(bf16[96,384]{1,0:T(8,128)(2,1)S(1)} %get-tuple-element.229), channel_id=1, source_target_pairs={{0,2},{2,0},{4,6},{6,4},{1,3},{3,1},{5,7},{7,5},{8,10},{10,8},{12,... | collective-permute-start | bytes 221192 | tf_op jit(solution)/shard_map/ppermute | solution.py:940
  79.1 7.3 %collective-permute-start.21 = (bf16[80,384]{1,0:T(8,128)(2,1)S(1)}, bf16[80,384]{1,0:T(8,128)(2,1)S(1)}, u32[]{:S(2)}, u32[]{:S(2)}) collective-permute-start(bf16[80,384]{1,0:T(8,128)(2,1)S(1)} %get-tuple-element.221), channel_id=1, source_target_pairs={{0,6},{2,4},{4,2},{6,0},{1,7},{3,5},{5,3},{7,1},{8,14},{10,12},{12... | collective-permute-start | bytes 184328 | tf_op jit(solution)/shard_map/ppermute | solution.py:940
  81.6 6.5 %collective-permute-start.22 = (bf16[80,384]{1,0:T(8,128)(2,1)S(1)}, bf16[80,384]{1,0:T(8,128)(2,1)S(1)}, u32[]{:S(2)}, u32[]{:S(2)}) collective-permute-start(bf16[80,384]{1,0:T(8,128)(2,1)S(1)} %get-tuple-element.222), channel_id=1, source_target_pairs={{0,4},{2,6},{4,0},{6,2},{1,5},{3,7},{5,1},{7,3},{8,12},{10,14},{12... | collective-permute-start | bytes 184328 | tf_op jit(solution)/shard_map/ppermute | solution.py:940
  82.7 5.4 %collective-permute-start.23 = (bf16[80,384]{1,0:T(8,128)(2,1)S(1)}, bf16[80,384]{1,0:T(8,128)(2,1)S(1)}, u32[]{:S(2)}, u32[]{:S(2)}) collective-permute-start(bf16[80,384]{1,0:T(8,128)(2,1)S(1)} %get-tuple-element.223), channel_id=1, source_target_pairs={{0,2},{2,0},{4,6},{6,4},{1,3},{3,1},{5,7},{7,5},{8,10},{10,8},{12,... | collective-permute-start | bytes 184328 | tf_op jit(solution)/shard_map/ppermute | solution.py:940
  83.7 5.6 %collective-permute-start.31 = (bf16[240,384]{1,0:T(8,128)(2,1)S(1)}, bf16[240,384]{1,0:T(8,128)(2,1)S(1)}, u32[]{:S(2)}, u32[]{:S(2)}) collective-permute-start(bf16[240,384]{1,0:T(8,128)(2,1)S(1)} %shard_map.302.refs_3_.refs_0_), channel_id=1, source_target_pairs={{0,8},{1,17},{8,0},{9,25},{16,24},{17,1},{24,16},{25,9},{2,10},{3,... | collective-permute-start | bytes 552968 | tf_op jit(solution)/shard_map/ppermute | solution.py:948
  88.2 5.0 %collective-permute-start.29 = (bf16[48,384]{1,0:T(8,128)(2,1)S(1)}, bf16[48,384]{1,0:T(8,128)(2,1)S(1)}, u32[]{:S(2)}, u32[]{:S(2)}) collective-permute-start(bf16[48,384]{1,0:T(8,128)(2,1)S(1)} %get-tuple-element.246.refs_0_), channel_id=1, source_target_pairs={{0,8},{1,17},{8,0},{9,25},{16,24},{17,1},{24,16},{25,9},{2,10},{3,... | collective-permute-start | bytes 110600 | tf_op jit(solution)/shard_map/ppermute | solution.py:948
  89.3 7.7 %collective-permute-start.32 = (bf16[480,384]{1,0:T(8,128)(2,1)S(1)}, bf16[480,384]{1,0:T(8,128)(2,1)S(1)}, u32[]{:S(2)}, u32[]{:S(2)}) collective-permute-start(bf16[480,384]{1,0:T(8,128)(2,1)S(1)} %shard_map.308), channel_id=1, source_target_pairs={{0,16},{1,9},{8,24},{9,1},{16,0},{17,25},{24,8},{25,17},{2,18},{3,... | collective-permute-start | bytes 1105928 | tf_op jit(solution)/shard_map/ppermute | solution.py:948
  93.3 5.0 %collective-permute-start.30 = (bf16[96,384]{1,0:T(8,128)(2,1)S(1)}, bf16[96,384]{1,0:T(8,128)(2,1)S(1)}, u32[]{:S(2)}, u32[]{:S(2)}) collective-permute-start(bf16[96,384]{1,0:T(8,128)(2,1)S(1)} %shard_map.306.refs_6_), channel_id=1, source_target_pairs={{0,16},{1,9},{8,24},{9,1},{16,0},{17,25},{24,8},{25,17},{2,18},{3,... | collective-permute-start | bytes 221192 | tf_op jit(solution)/shard_map/ppermute | solution.py:948
  (17 other events, 85.9 us)
